TPU v7x, 512 devices: a whole 4x4x16 slice. The times are simulated.
512 devices in a mesh: pipe: 16 (over y, z_lo), expert: 32 (over x, z_hi, core).
Axes of the slice: x: 4, y: 4, z: 16 (z_hi: 4, z_lo: 4; z = z_hi * 4 + z_lo), core: 2. Of those that a mesh axis runs over, the one named last changes fastest.
Arguments:
- forward_input: bfloat16 [16, 512, 3584], P('pipe', 'expert'), may hold values from -6 to 6
- backward_input: bfloat16 [16, 512, 3584], P('pipe', 'expert'), may hold values from -6 to 6
- backward_grad: bfloat16 [16, 512, 3584], P('pipe', 'expert'), may hold values from -6 to 6
- gate_up_weight: bfloat16 [16, 3584, 8192], P('pipe', None, 'expert'), may hold values from -0.09375 to 0.09375
- down_weight: bfloat16 [16, 4096, 3584], P('pipe', 'expert'), may hold values from -0.1875 to 0.1875
- forward_routes: int32 [16, 512, 2], P('pipe', 'expert'), may hold values from 0 to 3, all different within a row; in each aligned block of 16 rows (0 to 15, 16 to 31, ..., all dimensions but the last counted through in order) at most 12 rows name the same one
- backward_routes: int32 [16, 512, 2], P('pipe', 'expert'), may hold values from 0 to 3, all different within a row; in each aligned block of 16 rows (0 to 15, 16 to 31, ..., all dimensions but the last counted through in order) at most 12 rows name the same one
- forward_gates: float32 [16, 512, 2], P('pipe', 'expert'), may hold values from 0.1 to 1
- backward_gates: float32 [16, 512, 2], P('pipe', 'expert'), may hold values from 0.1 to 1
Outputs:
- forward_next: bfloat16 [16, 512, 3584], P('pipe', 'expert')
- backward_next: bfloat16 [16, 512, 3584], P('pipe', 'expert')
Inputs may be any that keep to these rules, and one draw needn't show every extreme that they name: `forward_routes`: A token names 2 different experts. Within the 16 tokens of one device at one section no expert is named more than 12 times, and in some such blocks one expert is named exactly 12 times. `backward_routes`: as for forward_routes.
All inputs are finite; a program needn't handle non-finite values.
Results may differ from a plain program's by a relative error of at most 0.0041.
Values may be sent and summed in bfloat16 or wider, within the bound.
No kernel may reach another device: no remote copies, remote signals or barrier semaphores. Data moves between devices by JAX's collectives and lax.ppermute only.
A program may use at most 128 MiB of HBM per device.

v0:
```python
import jax
import jax.numpy as jnp
from jax import lax
from jax.sharding import PartitionSpec as P

EXPERTS = 4
CAP = 12


def from_behind(block, axis, distance):
    devices = range(lax.axis_size(axis))
    route = [(i - distance, i) for i in devices if i - distance in devices]
    return lax.ppermute(block, axis, route)


def route_tables(routes, gate_share, capacity):
    tok_count = routes.shape[0]
    top_count = routes.shape[1]
    flat_routes = routes.reshape(-1)
    expert_hot = (flat_routes[:, None] == jnp.arange(EXPERTS, dtype=jnp.int32)[None, :]).astype(
        jnp.int32
    )
    earlier = jnp.cumsum(expert_hot, axis=0) - expert_hot
    slot_of = jnp.sum(earlier * expert_hot, axis=1)
    position = flat_routes * capacity + slot_of
    placed = (jnp.arange(EXPERTS * capacity, dtype=jnp.int32)[:, None] == position[None, :]).astype(
        jnp.float32
    )
    placed = placed.reshape(EXPERTS * capacity, tok_count, top_count)
    dispatch = jnp.sum(placed, axis=2).astype(jnp.bfloat16)
    combine = jnp.sum(placed * gate_share.reshape(1, tok_count, top_count), axis=2)
    return (dispatch, combine)


def fan_out(dispatch, tokens, slices):
    packed = jnp.dot(dispatch, tokens, preferred_element_type=jnp.float32).astype(jnp.bfloat16)
    capacity = packed.shape[0] // EXPERTS
    spread = jnp.broadcast_to(
        packed.reshape(EXPERTS, 1, capacity, packed.shape[1]),
        (EXPERTS, slices, capacity, packed.shape[1]),
    )
    return spread.reshape(EXPERTS * slices, capacity, packed.shape[1])


def fold_slices(returned, combine, tokens, slices):
    capacity = returned.shape[1]
    summed = jnp.sum(
        returned.reshape(EXPERTS, slices, capacity, returned.shape[2]).astype(jnp.float32), axis=1
    )
    summed = summed.reshape(EXPERTS * capacity, returned.shape[2])
    mixture = jnp.dot(
        combine.T, summed, precision=lax.Precision.HIGHEST, preferred_element_type=jnp.float32
    )
    return (tokens.astype(jnp.float32) + mixture).astype(jnp.bfloat16)


def forward_rows_work(flat_rows, gate_weight, up_weight, local_down):
    gate_val = jnp.dot(flat_rows, gate_weight, preferred_element_type=jnp.float32)
    up_val = jnp.dot(flat_rows, up_weight, preferred_element_type=jnp.float32)
    hidden = (jax.nn.silu(gate_val) * up_val).astype(jnp.bfloat16)
    return jnp.dot(hidden, local_down, preferred_element_type=jnp.float32).astype(jnp.bfloat16)


def backward_rows_work(flat_saved, flat_grad, gate_weight, up_weight, local_down):
    contract = (((1,), (1,)), ((), ()))
    gate_val = jnp.dot(flat_saved, gate_weight, preferred_element_type=jnp.float32)
    up_val = jnp.dot(flat_saved, up_weight, preferred_element_type=jnp.float32)
    hidden_grad = lax.dot_general(
        flat_grad, local_down, contract, preferred_element_type=jnp.float32
    )
    sigmoid_val = jax.nn.sigmoid(gate_val)
    gate_grad = (
        hidden_grad * up_val * sigmoid_val * (1.0 + gate_val * (1.0 - sigmoid_val))
    ).astype(jnp.bfloat16)
    up_grad = (hidden_grad * gate_val * sigmoid_val).astype(jnp.bfloat16)
    partial_in = lax.dot_general(
        gate_grad, gate_weight, contract, preferred_element_type=jnp.float32
    )
    partial_in = partial_in + lax.dot_general(
        up_grad, up_weight, contract, preferred_element_type=jnp.float32
    )
    return partial_in.astype(jnp.bfloat16)


def forward_section(tokens, routes, gate_share, gate_weight, up_weight, local_down, slices):
    dispatch, combine = route_tables(routes, gate_share, CAP)
    outgoing = fan_out(dispatch, tokens, slices)
    arrived = lax.all_to_all(outgoing, "expert", split_axis=0, concat_axis=0, tiled=True)
    item_count = arrived.shape[1]
    flat_rows = arrived.reshape(-1, arrived.shape[2])
    partial_out = forward_rows_work(flat_rows, gate_weight, up_weight, local_down)
    partial_out = partial_out.reshape(arrived.shape[0], item_count, arrived.shape[2])
    returned = lax.all_to_all(partial_out, "expert", split_axis=0, concat_axis=0, tiled=True)
    return fold_slices(returned, combine, tokens, slices)


def backward_section(
    tokens, upstream, routes, gate_share, gate_weight, up_weight, local_down, slices
):
    dispatch, combine = route_tables(routes, gate_share, CAP)
    out_tokens = fan_out(dispatch, tokens, slices)
    out_grads = fan_out(dispatch, upstream, slices)
    saved_rows = lax.all_to_all(out_tokens, "expert", split_axis=0, concat_axis=0, tiled=True)
    incoming = lax.all_to_all(out_grads, "expert", split_axis=0, concat_axis=0, tiled=True)
    item_count = saved_rows.shape[1]
    flat_saved = saved_rows.reshape(-1, saved_rows.shape[2])
    flat_grad = incoming.reshape(-1, incoming.shape[2])
    partial_in = backward_rows_work(flat_saved, flat_grad, gate_weight, up_weight, local_down)
    partial_in = partial_in.reshape(saved_rows.shape[0], item_count, saved_rows.shape[2])
    returned = lax.all_to_all(partial_in, "expert", split_axis=0, concat_axis=0, tiled=True)
    return fold_slices(returned, combine, upstream, slices)


def on_device(
    forward_input,
    backward_input,
    backward_grad,
    gate_up_weight,
    down_weight,
    forward_routes,
    backward_routes,
    forward_gates,
    backward_gates,
):
    slices = lax.axis_size("expert") // EXPERTS
    half_cols = gate_up_weight.shape[2] // 2
    gate_weight = gate_up_weight[0, :, :half_cols]
    up_weight = gate_up_weight[0, :, half_cols:]
    local_down = down_weight[0]
    forward_out = forward_section(
        forward_input[0],
        forward_routes[0],
        forward_gates[0],
        gate_weight,
        up_weight,
        local_down,
        slices,
    )
    backward_out = backward_section(
        backward_input[0],
        backward_grad[0],
        backward_routes[0],
        backward_gates[0],
        gate_weight,
        up_weight,
        local_down,
        slices,
    )
    forward_next = from_behind(forward_out[None], "pipe", 1)
    backward_next = from_behind(backward_out[None], "pipe", -1)
    return (forward_next, backward_next)


def solution(mesh):
    return jax.shard_map(
        on_device,
        mesh=mesh,
        in_specs=(
            P("pipe", "expert", None),
            P("pipe", "expert", None),
            P("pipe", "expert", None),
            P("pipe", None, "expert"),
            P("pipe", "expert", None),
            P("pipe", "expert", None),
            P("pipe", "expert", None),
            P("pipe", "expert", None),
            P("pipe", "expert", None),
        ),
        out_specs=(P("pipe", "expert", None), P("pipe", "expert", None)),
        check_vma=False,
    )
```

profile of v0, /device:TPU:24, one launch (start us, length us, event | category | flops | bytes accessed | tf_op | source)
XLA Modules:
  0.0 905.1 jit_solution(10571637790764326861)
XLA Ops:
  0.6 0.8 copy.27
  1.5 0.1 eq.59
  1.7 0.2 select_reduce_fusion.3
  2.0 0.1 copy.28
  2.1 0.7 bitcast_add_fusion.1
  2.8 0.8 convert_reduce_fusion.3
  3.5 1.2 convolution_convert_fusion.3
  4.7 0.1 broadcast_in_dim.16
  4.8 2.3 broadcast_in_dim.34
  7.0 18.2 %all-to-all-start = ((bf16[32,12,3584]{2,1,0:T(8,128)(2,1)}), bf16[32,12,3584]{2,1,0:T(8,128)(2,1)}, u32[]{:S(2)}, u32[]{:S(2)}) async-start(bf16[32,12,3584]{2,1,0:T(8,128)(2,1)} %bitcast.63), calls=%async_computation | async-start | bytes 7340032 | tf_op jit(solution)/shard_map/all_to_all | solution.py:88
  25.3 0.1 copy.29
  25.3 0.1 eq.66
  25.6 0.2 select_reduce_fusion.1
  25.8 0.1 copy.30
  26.0 0.3 convolution_convert_fusion.2
  26.3 0.1 broadcast_in_dim.36
  26.4 163.3 %all-to-all-done = bf16[32,12,3584]{2,1,0:T(8,128)(2,1)} async-done(((bf16[32,12,3584]{2,1,0:T(8,128)(2,1)}), bf16[32,12,3584]{2,1,0:T(8,128)(2,1)}, u32[]{:S(2)}, u32[]{:S(2)}) %all-to-all-start) | async-done | bytes 2752544 | tf_op jit(solution)/shard_map/all_to_all | solution.py:88
  189.7 2.3 broadcast_in_dim.37
  192.0 9.5 %all-to-all-start.2 = ((bf16[32,12,3584]{2,1,0:T(8,128)(2,1)}), bf16[32,12,3584]{2,1,0:T(8,128)(2,1)}, u32[]{:S(2)}, u32[]{:S(2)}) async-start(bf16[32,12,3584]{2,1,0:T(8,128)(2,1)} %bitcast.65), calls=%async_computation.2 | async-start | bytes 7340032 | tf_op jit(solution)/shard_map/all_to_all | solution.py:104
  201.5 0.3 convolution_convert_fusion.1
  201.9 164.2 %all-to-all-done.2 = bf16[32,12,3584]{2,1,0:T(8,128)(2,1)} async-done(((bf16[32,12,3584]{2,1,0:T(8,128)(2,1)}), bf16[32,12,3584]{2,1,0:T(8,128)(2,1)}, u32[]{:S(2)}, u32[]{:S(2)}) %all-to-all-start.2) | async-done | bytes 2752544 | tf_op jit(solution)/shard_map/all_to_all | solution.py:104
  366.1 2.3 broadcast_in_dim.39
  368.3 10.2 %all-to-all-start.3 = ((bf16[32,12,3584]{2,1,0:T(8,128)(2,1)}), bf16[32,12,3584]{2,1,0:T(8,128)(2,1)}, u32[]{:S(2)}, u32[]{:S(2)}) async-start(bf16[32,12,3584]{2,1,0:T(8,128)(2,1)} %bitcast.64), calls=%async_computation.3 | async-start | bytes 7340032 | tf_op jit(solution)/shard_map/all_to_all | solution.py:103
  378.5 5.5 reshape.89
  384.0 2.6 fusion.21
  386.7 6.3 convolution_convert_fusion
  393.0 5.3 reshape.90
  398.3 144.2 %all-to-all-done.3 = bf16[32,12,3584]{2,1,0:T(8,128)(2,1)} async-done(((bf16[32,12,3584]{2,1,0:T(8,128)(2,1)}), bf16[32,12,3584]{2,1,0:T(8,128)(2,1)}, u32[]{:S(2)}, u32[]{:S(2)}) %all-to-all-start.3) | async-done | bytes 2752544 | tf_op jit(solution)/shard_map/all_to_all | solution.py:103
  542.5 11.2 %all-to-all-start.1 = ((bf16[32,12,3584]{2,1,0:T(8,128)(2,1)}), bf16[32,12,3584]{2,1,0:T(8,128)(2,1)}, u32[]{:S(2)}, u32[]{:S(2)}) async-start(bf16[32,12,3584]{2,1,0:T(8,128)(2,1)} %reshape.90), calls=%async_computation.1 | async-start | bytes 7340032 | tf_op jit(solution)/shard_map/all_to_all | solution.py:93
  553.8 5.3 reshape.93
  559.1 5.4 reshape.95
  564.5 2.8 fusion.10
  567.3 0.9 fusion.19
  568.2 7.3 fusion.9
  575.4 5.0 fusion
  580.4 5.4 reshape.96
  585.7 135.1 %all-to-all-done.1 = bf16[32,12,3584]{2,1,0:T(8,128)(2,1)} async-done(((bf16[32,12,3584]{2,1,0:T(8,128)(2,1)}), bf16[32,12,3584]{2,1,0:T(8,128)(2,1)}, u32[]{:S(2)}, u32[]{:S(2)}) %all-to-all-start.1) | async-done | bytes 2752544 | tf_op jit(solution)/shard_map/all_to_all | solution.py:93
  720.9 5.5 all-to-all-start.4
  726.4 2.7 convert_reduce_fusion.1
  729.3 0.5 fusion.4
  729.7 1.9 collective-permute-start
  731.7 162.2 %all-to-all-done.4 = bf16[32,12,3584]{2,1,0:T(8,128)(2,1)} async-done(((bf16[32,12,3584]{2,1,0:T(8,128)(2,1)}), bf16[32,12,3584]{2,1,0:T(8,128)(2,1)}, u32[]{:S(2)}, u32[]{:S(2)}) %all-to-all-start.4) | async-done | bytes 2752544 | tf_op jit(solution)/shard_map/all_to_all | solution.py:110
  893.8 2.7 convert_reduce_fusion
  896.7 0.5 fusion.3
  897.1 1.9 collective-permute-start.1
  899.1 4.7 collective-permute-done.1
  903.8 0.6 copy.33
  904.4 0.6 copy.34
  (28 shorter events, 0.8 us)
Async XLA Ops:
  0.6 386.0 %copy-start = (bf16[1,128,3584]{2,1,0:T(8,128)(2,1)S(1)}, bf16[1,128,3584]{2,1,0:T(8,128)(2,1)}, u32[]{:S(2)}) copy-start(bf16[1,128,3584]{2,1,0:T(8,128)(2,1)} %param.13) | copy-start | bytes 2752516
  7.0 18.2 %copy-start.6 = (s32[1,16,2]{1,2,0:T(2,128)S(1)}, s32[1,16,2]{1,2,0:T(2,128)}, u32[]{:S(2)}) copy-start(s32[1,16,2]{1,2,0:T(2,128)} %param.15) | copy-start | bytes 388
  7.0 18.9 %copy-start.7 = (f32[1,16,2]{1,2,0:T(2,128)S(1)}, f32[1,16,2]{1,2,0:T(2,128)}, u32[]{:S(2)}) copy-start(f32[1,16,2]{1,2,0:T(2,128)} %param.17) | copy-start | bytes 388
  7.0 19.0 %copy-start.4 = (bf16[1,16,3584]{2,1,0:T(8,128)(2,1)S(1)}, bf16[1,16,3584]{2,1,0:T(8,128)(2,1)}, u32[]{:S(2)}) copy-start(bf16[1,16,3584]{2,1,0:T(8,128)(2,1)} %param.11) | copy-start | bytes 344068
  7.0 182.7 %all-to-all-start = ((bf16[32,12,3584]{2,1,0:T(8,128)(2,1)}), bf16[32,12,3584]{2,1,0:T(8,128)(2,1)}, u32[]{:S(2)}, u32[]{:S(2)}) async-start(bf16[32,12,3584]{2,1,0:T(8,128)(2,1)} %bitcast.63), calls=%async_computation | async-start | bytes 7340032 | tf_op jit(solution)/shard_map/all_to_all | solution.py:88
  192.0 9.6 %copy-start.5 = (bf16[1,16,3584]{2,1,0:T(8,128)(2,1)S(1)}, bf16[1,16,3584]{2,1,0:T(8,128)(2,1)}, u32[]{:S(2)}) copy-start(bf16[1,16,3584]{2,1,0:T(8,128)(2,1)} %param.10) | copy-start | bytes 344068
  192.0 174.1 %all-to-all-start.2 = ((bf16[32,12,3584]{2,1,0:T(8,128)(2,1)}), bf16[32,12,3584]{2,1,0:T(8,128)(2,1)}, u32[]{:S(2)}, u32[]{:S(2)}) async-start(bf16[32,12,3584]{2,1,0:T(8,128)(2,1)} %bitcast.65), calls=%async_computation.2 | async-start | bytes 7340032 | tf_op jit(solution)/shard_map/all_to_all | solution.py:104
  368.3 174.2 %all-to-all-start.3 = ((bf16[32,12,3584]{2,1,0:T(8,128)(2,1)}), bf16[32,12,3584]{2,1,0:T(8,128)(2,1)}, u32[]{:S(2)}, u32[]{:S(2)}) async-start(bf16[32,12,3584]{2,1,0:T(8,128)(2,1)} %bitcast.64), calls=%async_computation.3 | async-start | bytes 7340032 | tf_op jit(solution)/shard_map/all_to_all | solution.py:103
  378.5 5.5 copy-start.2
  542.5 178.4 %all-to-all-start.1 = ((bf16[32,12,3584]{2,1,0:T(8,128)(2,1)}), bf16[32,12,3584]{2,1,0:T(8,128)(2,1)}, u32[]{:S(2)}, u32[]{:S(2)}) async-start(bf16[32,12,3584]{2,1,0:T(8,128)(2,1)} %reshape.90), calls=%async_computation.1 | async-start | bytes 7340032 | tf_op jit(solution)/shard_map/all_to_all | solution.py:93
  564.5 2.8 copy-start.1
  720.9 172.9 %all-to-all-start.4 = ((bf16[32,12,3584]{2,1,0:T(8,128)(2,1)}), bf16[32,12,3584]{2,1,0:T(8,128)(2,1)}, u32[]{:S(2)}, u32[]{:S(2)}) async-start(bf16[32,12,3584]{2,1,0:T(8,128)(2,1)} %reshape.96), calls=%async_computation.4 | async-start | bytes 7340032 | tf_op jit(solution)/shard_map/all_to_all | solution.py:110
  726.4 2.9 copy-start.3
  729.7 169.3 %collective-permute-start = (bf16[1,16,3584]{2,1,0:T(8,128)(2,1)S(1)}, bf16[1,16,3584]{2,1,0:T(8,128)(2,1)S(1)}, u32[]{:S(2)}, u32[]{:S(2)}) collective-permute-start(bf16[1,16,3584]{2,1,0:T(8,128)(2,1)S(1)} %fusion.4), channel_id=1, source_target_pairs={{0,32},{32,64},{64,96},{96,128},{128,160},{160,192},{192,224},{224... | collective-permute-start | bytes 344072 | tf_op jit(solution)/shard_map/ppermute | solution.py:13
  897.1 6.7 collective-permute-start.1
where the time goes:
time: 907 us; the launch traced here: 905 us
  waiting for transfers between devices  774 us (85%)
  starting transfers between devices  58.5 us (6%)
  local copies, waits for them, and re-layouts  36.8 us (4%)
  matrix products  27.4 us (3%)
    all_to_all x1, waiting for transfers between devices, backward_section(): lax.all_to_all(out_grads, 'expert', split_axis=0, concat_axis=0, tiled=True)  164 us
    all_to_all x1, waiting for transfers between devices, forward_section(): lax.all_to_all(outgoing, 'expert', split_axis=0, concat_axis=0, tiled=True)  163 us
    all_to_all x1, waiting for transfers between devices, backward_section(): lax.all_to_all(partial_in, 'expert', split_axis=0, concat_axis=0, tiled=T...  162 us
    all_to_all x1, waiting for transfers between devices, backward_section(): lax.all_to_all(out_tokens, 'expert', split_axis=0, concat_axis=0, tiled=T...  144 us
    all_to_all x1, waiting for transfers between devices, forward_section(): lax.all_to_all(partial_out, 'expert', split_axis=0, concat_axis=0, tiled=...  135 us
    all_to_all x1, starting transfers between devices, forward_section(): lax.all_to_all(outgoing, 'expert', split_axis=0, concat_axis=0, tiled=True)  18.2 us
  transfers between devices with their start and end apart: 7, of which 6 were waited for; matrix products, arithmetic and copies ran while one was open for 7% of the time, Pallas kernels for 0%

commit v1 on v0

v1 whole, which is shorter than its diff:
```python
import jax
import jax.numpy as jnp
from jax import lax
from jax.sharding import PartitionSpec as P

EXPERTS = 4
Z = 4
CORES = 2
LANES = 128


def expert_index(x, z, core):
    return (x * Z + z) * CORES + core


def expert_route(move):
    return [
        (expert_index(x, z, c), expert_index(*move(x, z, c)))
        for x in range(EXPERTS)
        for z in range(Z)
        for c in range(CORES)
    ]


def along_x(block, distance):
    route = expert_route(lambda x, z, c: ((x + distance) % EXPERTS, z, c))
    return lax.ppermute(block, "expert", route)


def along_z(block, distance):
    route = expert_route(lambda x, z, c: (x, (z + distance) % Z, c))
    return lax.ppermute(block, "expert", route)


def other_core(block):
    return lax.ppermute(block, "expert", expert_route(lambda x, z, c: (x, z, 1 - c)))


def to_section(block, step, distance):
    sections = lax.axis_size("pipe")
    width = EXPERTS * Z * CORES
    route = [
        (p * width + source, (p + step) * width + target)
        for p in range(sections)
        if 0 <= p + step < sections
        for source, target in expert_route(lambda x, z, c: (x, (z + distance) % Z, c))
    ]
    return lax.ppermute(block, ("pipe", "expert"), route)


def expert_shares(routes, gates):
    hot = routes[:, :, None] == jnp.arange(EXPERTS, dtype=jnp.int32)
    return jnp.sum(jnp.where(hot, gates[:, :, None], 0.0), axis=1)


def share_columns(shares):
    first = lax.reduce_precision(shares, 8, 7)
    second = lax.reduce_precision(shares - first, 8, 7)
    third = shares - first - second
    parts = jnp.concatenate([first, second, third], axis=1)
    parts = jnp.pad(parts, ((0, 0), (0, LANES - parts.shape[1])))
    return parts.astype(jnp.bfloat16)


def shares_of(columns, width):
    parts = columns.astype(jnp.float32)
    return parts[:, :width] + parts[:, width : 2 * width] + parts[:, 2 * width : 3 * width]


def dot(a, b):
    return jnp.dot(a, b, preferred_element_type=jnp.float32)


def dot_t(a, b):
    return lax.dot_general(a, b, (((1,), (1,)), ((), ())), preferred_element_type=jnp.float32)


def forward_rows(rows, gate_ups, down):
    hidden = []
    for gate_up in gate_ups:
        both = dot(rows, gate_up)
        gate_val, up_val = jnp.split(both, 2, axis=1)
        hidden.append((jax.nn.silu(gate_val) * up_val).astype(jnp.bfloat16))
    return dot(jnp.concatenate(hidden, axis=1), down).astype(jnp.bfloat16)


def backward_rows(rows, grads, gate_ups, down):
    hidden_grads = jnp.split(dot_t(grads, down), len(gate_ups), axis=1)
    total = None
    for gate_up, hidden_grad in zip(gate_ups, hidden_grads):
        both = dot(rows, gate_up)
        gate_val, up_val = jnp.split(both, 2, axis=1)
        sig = jax.nn.sigmoid(gate_val)
        gate_grad = hidden_grad * up_val * sig * (1.0 + gate_val * (1.0 - sig))
        up_grad = hidden_grad * gate_val * sig
        grad = jnp.concatenate([gate_grad, up_grad], axis=1).astype(jnp.bfloat16)
        term = dot_t(grad, gate_up)
        total = term if total is None else total + term
    return total.astype(jnp.bfloat16)


def gated_sum(parts, shares):
    me = lax.axis_index("expert") // (Z * CORES)
    total = 0.0
    for d, part in enumerate(parts):
        hot = jnp.arange(EXPERTS, dtype=jnp.int32) == lax.rem(me + d, EXPERTS)
        share = jnp.sum(jnp.where(hot[None, :], shares, 0.0), axis=1, keepdims=True)
        total = total + share * part.astype(jnp.float32)
    return total


def send_home(mixture, residual, step):
    rows = residual.shape[0]
    total = 0.0
    for k in range(Z):
        term = mixture[k * rows : (k + 1) * rows]
        if k == 0:
            term = term + residual.astype(jnp.float32)
        total = total + to_section(term.astype(jnp.bfloat16), step, -k).astype(jnp.float32)
    return total.astype(jnp.bfloat16)


def on_device(
    forward_input,
    backward_input,
    backward_grad,
    gate_up_weight,
    down_weight,
    forward_routes,
    backward_routes,
    forward_gates,
    backward_gates,
):
    tokens, saved, upstream = forward_input[0], backward_input[0], backward_grad[0]
    rows, model = tokens.shape
    shares = jnp.concatenate(
        [
            expert_shares(forward_routes[0], forward_gates[0]),
            expert_shares(backward_routes[0], backward_gates[0]),
        ],
        axis=1,
    )
    with jax.named_scope("gather_z"):
        first = jnp.concatenate([tokens, share_columns(shares)], axis=1)
        first = [first] + [along_z(first, d) for d in range(1, Z)]
        second = jnp.concatenate([saved, upstream], axis=0)
        second = [second] + [along_z(second, d) for d in range(1, Z)]
    with jax.named_scope("swap_weights"):
        gate_up, down = gate_up_weight[0], down_weight[0]
        gate_ups = [gate_up, other_core(gate_up)]
        down = jnp.concatenate([down, other_core(down)], axis=0)
    with jax.named_scope("gather_x"):
        forward_block = jnp.concatenate([part[:, :model] for part in first], axis=0)
        all_shares = jnp.concatenate([part[:, model:] for part in first], axis=0)
        all_shares = shares_of(all_shares, 2 * EXPERTS)
        forward_parts = [forward_block] + [along_x(forward_block, d) for d in range(1, EXPERTS)]
        backward_block = jnp.concatenate(
            [part[:rows] for part in second] + [part[rows:] for part in second], axis=0
        )
        backward_parts = [backward_block] + [along_x(backward_block, d) for d in range(1, EXPERTS)]
    half = Z * rows
    with jax.named_scope("forward_experts"):
        outs = [forward_rows(part, gate_ups, down) for part in forward_parts]
        outs = [outs[0]] + [along_x(outs[d], -d) for d in range(1, EXPERTS)]
        mixture = gated_sum(outs, all_shares[:, :EXPERTS])
        forward_next = send_home(mixture, tokens, 1)
    with jax.named_scope("backward_experts"):
        outs = [backward_rows(part[:half], part[half:], gate_ups, down) for part in backward_parts]
        outs = [outs[0]] + [along_x(outs[d], -d) for d in range(1, EXPERTS)]
        mixture = gated_sum(outs, all_shares[:, EXPERTS:])
        backward_next = send_home(mixture, upstream, -1)
    return (forward_next[None], backward_next[None])


def solution(mesh):
    by_token = P("pipe", "expert", None)
    return jax.shard_map(
        on_device,
        mesh=mesh,
        in_specs=(by_token,) * 3 + (P("pipe", None, "expert"),) + (by_token,) * 5,
        out_specs=(by_token, by_token),
        check_vma=False,
    )
```

time: 907 us -> 263 us (0.29)
  waiting for transfers between devices: 774 us -> 56 us
  starting transfers between devices: 58.5 us -> 156 us
  local copies, waits for them, and re-layouts: 36.8 us -> 9.62 us
    all_to_all x5 -> x0, waiting for transfers between devices: 769 us -> none  [the longest x1 164 us: backward_section(): lax.all_to_all(out_grads, 'expert', split_axis=0, concat_axis=0, tiled=True)]
    ppermute x2 -> x28, starting transfers between devices: 3.84 us -> 156 us  [the longest x8 70.3 us: to_section(): return lax.ppermute(block, ('pipe', 'expert'), route)]
    all_to_all x5 -> x0, starting transfers between devices: 54.7 us -> none  [the longest x1 18.2 us: forward_section(): lax.all_to_all(outgoing, 'expert', split_axis=0, concat_axis=0, tiled=True)]
    ppermute x2 -> x28, waiting for transfers between devices: 4.75 us -> 56 us  [the longest x12 31.9 us: along_x(): return lax.ppermute(block, 'expert', route)]
    reshape x7 -> x0, local copies, waits for them, and re-layouts: 27 us -> none  [the longest x1 5.47 us: forward_section(): flat_rows = arrived.reshape(-1, arrived.shape[2])]
    dot_general x11 -> x32, matrix products: 27.4 us -> 28.7 us  [the longest x20 15.9 us: dot(): return jnp.dot(a, b, preferred_element_type=jnp.float32)]
  transfers between devices with their start and end apart: 7 -> 28, of which waited for: 6 -> 5; matrix products, arithmetic and copies ran while one was open for 7% -> 16% of each run, Pallas kernels for 0% -> 0%
where the time goes in v1:
time: 263 us; the launch traced here: 261 us
  starting transfers between devices  156 us (59%)
  waiting for transfers between devices  56 us (21%)
  matrix products  28.7 us (11%)
  local copies, waits for them, and re-layouts  9.62 us (4%)
  other arithmetic  9.09 us (3%)
    ppermute x8, starting transfers between devices, to_section(): return lax.ppermute(block, ('pipe', 'expert'), route)  70.3 us
    ppermute x12, starting transfers between devices, along_x(): return lax.ppermute(block, 'expert', route)  42.2 us
    ppermute x6, starting transfers between devices, along_z(): return lax.ppermute(block, 'expert', route)  38.9 us
    ppermute x12, waiting for transfers between devices, along_x(): return lax.ppermute(block, 'expert', route)  31.9 us
    dot_general x20, matrix products, dot(): return jnp.dot(a, b, preferred_element_type=jnp.float32)  15.9 us
    dot_general x12, matrix products, dot_t(): lax.dot_general(a, b, (((1,), (1,)), ((), ())), preferred_element_type=jn...  12.9 us
    ppermute x8, waiting for transfers between devices, to_section(): return lax.ppermute(block, ('pipe', 'expert'), route)  12.7 us
    ppermute x6, waiting for transfers between devices, along_z(): return lax.ppermute(block, 'expert', route)  11.4 us
  transfers between devices with their start and end apart: 28, of which 5 were waited for; matrix products, arithmetic and copies ran while one was open for 16% of the time, Pallas kernels for 0%

profile of v1, /device:TPU:24, one launch (start us, length us, event | category | flops | bytes accessed | tf_op | source)
XLA Modules:
  0.0 260.5 jit_solution(10660145774743833487)
XLA Ops:
  1.5 1.6 pad_maximum_fusion.4
  3.1 12.7 %collective-permute-start.2 = (bf16[16,3712]{1,0:T(8,128)(2,1)}, bf16[16,3712]{1,0:T(8,128)(2,1)S(1)}, u32[]{:S(2)}, u32[]{:S(2)}) collective-permute-start(bf16[16,3712]{1,0:T(8,128)(2,1)} %pad_maximum_fusion.4), channel_id=1, source_target_pairs={{0,6},{1,7},{2,0},{3,1},{4,2},{5,3},{6,4},{7,5},{8,14},{9,15},{10,... | collective-permute-start | bytes 356360 | tf_op jit(solution)/shard_map/gather_z/ppermute | solution.py:32
  15.8 4.9 %collective-permute-start.1 = (bf16[16,3712]{1,0:T(8,128)(2,1)}, bf16[16,3712]{1,0:T(8,128)(2,1)S(1)}, u32[]{:S(2)}, u32[]{:S(2)}) collective-permute-start(bf16[16,3712]{1,0:T(8,128)(2,1)} %pad_maximum_fusion.4), channel_id=1, source_target_pairs={{0,4},{1,5},{2,6},{3,7},{4,0},{5,1},{6,2},{7,3},{8,12},{9,13},{10,... | collective-permute-start | bytes 356360 | tf_op jit(solution)/shard_map/gather_z/ppermute | solution.py:32
  20.7 7.8 %collective-permute-start = (bf16[16,3712]{1,0:T(8,128)(2,1)}, bf16[16,3712]{1,0:T(8,128)(2,1)}, u32[]{:S(2)}, u32[]{:S(2)}) collective-permute-start(bf16[16,3712]{1,0:T(8,128)(2,1)} %pad_maximum_fusion.4), channel_id=1, source_target_pairs={{0,2},{1,3},{2,4},{3,5},{4,6},{5,7},{6,0},{7,1},{8,10},{9,11},{10,... | collective-permute-start | bytes 356360 | tf_op jit(solution)/shard_map/gather_z/ppermute | solution.py:32
  28.6 1.0 pad_maximum_fusion.3
  29.6 4.3 %collective-permute-start.15 = (bf16[32,3584]{1,0:T(8,128)(2,1)S(1)}, bf16[32,3584]{1,0:T(8,128)(2,1)S(1)}, u32[]{:S(2)}, u32[]{:S(2)}) collective-permute-start(bf16[32,3584]{1,0:T(8,128)(2,1)S(1)} %pad_maximum_fusion.3), channel_id=1, source_target_pairs={{0,2},{1,3},{2,4},{3,5},{4,6},{5,7},{6,0},{7,1},{8,10},{9,11},{10,... | collective-permute-start | bytes 688136 | tf_op jit(solution)/shard_map/gather_z/ppermute | solution.py:32
  33.8 4.9 %collective-permute-start.16 = (bf16[32,3584]{1,0:T(8,128)(2,1)S(1)}, bf16[32,3584]{1,0:T(8,128)(2,1)S(1)}, u32[]{:S(2)}, u32[]{:S(2)}) collective-permute-start(bf16[32,3584]{1,0:T(8,128)(2,1)S(1)} %pad_maximum_fusion.3), channel_id=1, source_target_pairs={{0,4},{1,5},{2,6},{3,7},{4,0},{5,1},{6,2},{7,3},{8,12},{9,13},{10,... | collective-permute-start | bytes 688136 | tf_op jit(solution)/shard_map/gather_z/ppermute | solution.py:32
  38.8 1.6 constant_dynamic-update-slice_fusion.7
  40.9 4.3 %collective-permute-start.17 = (bf16[32,3584]{1,0:T(8,128)(2,1)S(1)}, bf16[32,3584]{1,0:T(8,128)(2,1)S(1)}, u32[]{:S(2)}, u32[]{:S(2)}) collective-permute-start(bf16[32,3584]{1,0:T(8,128)(2,1)S(1)} %pad_maximum_fusion.3), channel_id=1, source_target_pairs={{0,6},{1,7},{2,0},{3,1},{4,2},{5,3},{6,4},{7,5},{8,14},{9,15},{10,... | collective-permute-start | bytes 688136 | tf_op jit(solution)/shard_map/gather_z/ppermute | solution.py:32
  45.3 1.9 collective-permute-start.3
  47.3 2.4 collective-permute-start.4
  49.7 0.9 slice.137
  50.6 0.8 pad_maximum_fusion.1
  51.4 2.6 %fusion.154 = f32[64,256]{1,0:T(8,128)} fusion(bf16[1,3584,256]{2,1,0:T(8,128)(2,1)} %param.12, bf16[16,3584]{1,0:T(8,128)(2,1)S(1)} %slice.139, bf16[16,3584]{1,0:T(8,128)(2,1)S(1)} %slice.138, bf16[16,3584]{1,0:T(8,128)(2,1)S(1)} %slice.137, bf16[16,3584]{1,0:T(8,128)(2,1)S(1)} %bitcast.64), kind=kOutput, calls=%fused_computation.237 | convolution fusion | flops 119275520 | bytes 2359296 | tf_op jit(solution)/shard_map/forward_experts/dot_general | solution.py:71
  55.7 0.9 fusion.124
  58.2 4.7 %collective-permute-start.9 = (bf16[64,3584]{1,0:T(8,128)(2,1)}, bf16[64,3584]{1,0:T(8,128)(2,1)S(1)}, u32[]{:S(2)}, u32[]{:S(2)}) collective-permute-start(bf16[64,3584]{1,0:T(8,128)(2,1)} %pad_maximum_fusion.1), channel_id=1, source_target_pairs={{0,24},{1,25},{2,26},{3,27},{4,28},{5,29},{6,30},{7,31},{8,0},{9,1... | collective-permute-start | bytes 1376264 | tf_op jit(solution)/shard_map/gather_x/ppermute | solution.py:27
  63.5 3.9 %collective-permute-start.7 = (bf16[64,3584]{1,0:T(8,128)(2,1)}, bf16[64,3584]{1,0:T(8,128)(2,1)S(1)}, u32[]{:S(2)}, u32[]{:S(2)}) collective-permute-start(bf16[64,3584]{1,0:T(8,128)(2,1)} %pad_maximum_fusion.1), channel_id=1, source_target_pairs={{0,16},{1,17},{2,18},{3,19},{4,20},{5,21},{6,22},{7,23},{8,24},{9,... | collective-permute-start | bytes 1376264 | tf_op jit(solution)/shard_map/gather_x/ppermute | solution.py:27
  68.1 11.4 %collective-permute-done.17 = bf16[32,3584]{1,0:T(8,128)(2,1)S(1)} collective-permute-done((bf16[32,3584]{1,0:T(8,128)(2,1)S(1)}, bf16[32,3584]{1,0:T(8,128)(2,1)S(1)}, u32[]{:S(2)}, u32[]{:S(2)}) %collective-permute-start.17) | collective-permute-done | bytes 229408 | tf_op jit(solution)/shard_map/gather_z/ppermute | solution.py:32
  79.5 3.4 %collective-permute-start.5 = (bf16[64,3584]{1,0:T(8,128)(2,1)}, bf16[64,3584]{1,0:T(8,128)(2,1)S(1)}, u32[]{:S(2)}, u32[]{:S(2)}) collective-permute-start(bf16[64,3584]{1,0:T(8,128)(2,1)} %pad_maximum_fusion.1), channel_id=1, source_target_pairs={{0,8},{1,9},{2,10},{3,11},{4,12},{5,13},{6,14},{7,15},{8,16},{9,17... | collective-permute-start | bytes 1376264 | tf_op jit(solution)/shard_map/gather_x/ppermute | solution.py:27
  87.4 3.6 %collective-permute-start.22 = (bf16[128,3584]{1,0:T(8,128)(2,1)S(1)}, bf16[128,3584]{1,0:T(8,128)(2,1)S(1)}, u32[]{:S(2)}, u32[]{:S(2)}) collective-permute-start(bf16[128,3584]{1,0:T(8,128)(2,1)S(1)} %copy-done.6), channel_id=1, source_target_pairs={{0,24},{1,25},{2,26},{3,27},{4,28},{5,29},{6,30},{7,31},{8,0},{9,1... | collective-permute-start | bytes 2752520 | tf_op jit(solution)/shard_map/gather_x/ppermute | solution.py:27
  91.5 3.7 %collective-permute-start.20 = (bf16[128,3584]{1,0:T(8,128)(2,1)S(1)}, bf16[128,3584]{1,0:T(8,128)(2,1)S(1)}, u32[]{:S(2)}, u32[]{:S(2)}) collective-permute-start(bf16[128,3584]{1,0:T(8,128)(2,1)S(1)} %copy-done.6), channel_id=1, source_target_pairs={{0,16},{1,17},{2,18},{3,19},{4,20},{5,21},{6,22},{7,23},{8,24},{9,... | collective-permute-start | bytes 2752520 | tf_op jit(solution)/shard_map/gather_x/ppermute | solution.py:27
  95.7 2.6 %collective-permute-start.18 = (bf16[128,3584]{1,0:T(8,128)(2,1)S(1)}, bf16[128,3584]{1,0:T(8,128)(2,1)S(1)}, u32[]{:S(2)}, u32[]{:S(2)}) collective-permute-start(bf16[128,3584]{1,0:T(8,128)(2,1)S(1)} %copy-done.6), channel_id=1, source_target_pairs={{0,8},{1,9},{2,10},{3,11},{4,12},{5,13},{6,14},{7,15},{8,16},{9,17... | collective-permute-start | bytes 2752520 | tf_op jit(solution)/shard_map/gather_x/ppermute | solution.py:27
  98.9 1.8 fusion.20
  100.7 29.5 %collective-permute-done.22 = bf16[128,3584]{1,0:T(8,128)(2,1)S(1)} collective-permute-done((bf16[128,3584]{1,0:T(8,128)(2,1)S(1)}, bf16[128,3584]{1,0:T(8,128)(2,1)S(1)}, u32[]{:S(2)}, u32[]{:S(2)}) %collective-permute-start.22) | collective-permute-done | bytes 917536 | tf_op jit(solution)/shard_map/gather_x/ppermute | solution.py:27
  130.2 1.8 fusion.14
  132.1 1.8 fusion.16
  133.9 2.3 collective-permute-done.18
  136.3 1.8 fusion.18
  139.9 1.6 convolution_convert_fusion
  141.6 2.3 collective-permute-start.10
  144.3 1.6 convolution_convert_fusion.1
  145.9 4.4 %collective-permute-start.8 = (bf16[64,3584]{1,0:T(8,128)(2,1)S(1)}, bf16[64,3584]{1,0:T(8,128)(2,1)S(1)}, u32[]{:S(2)}, u32[]{:S(2)}) collective-permute-start(bf16[64,3584]{1,0:T(8,128)(2,1)S(1)} %convolution_convert_fusion.1), channel_id=1, source_target_pairs={{0,16},{1,17},{2,18},{3,19},{4,20},{5,21},{6,22},{7,23},{8,24},{9,... | collective-permute-start | bytes 1376264 | tf_op jit(solution)/shard_map/forward_experts/ppermute | solution.py:27
  150.8 1.6 convolution_convert_fusion.2
  152.4 3.5 %collective-permute-start.6 = (bf16[64,3584]{1,0:T(8,128)(2,1)S(1)}, bf16[64,3584]{1,0:T(8,128)(2,1)S(1)}, u32[]{:S(2)}, u32[]{:S(2)}) collective-permute-start(bf16[64,3584]{1,0:T(8,128)(2,1)S(1)} %convolution_convert_fusion.2), channel_id=1, source_target_pairs={{0,24},{1,25},{2,26},{3,27},{4,28},{5,29},{6,30},{7,31},{8,0},{9,1... | collective-permute-start | bytes 1376264 | tf_op jit(solution)/shard_map/forward_experts/ppermute | solution.py:27
  157.8 2.3 collective-permute-start.23
  162.0 3.2 %collective-permute-start.21 = (bf16[64,3584]{1,0:T(8,128)(2,1)S(1)}, bf16[64,3584]{1,0:T(8,128)(2,1)S(1)}, u32[]{:S(2)}, u32[]{:S(2)}) collective-permute-start(bf16[64,3584]{1,0:T(8,128)(2,1)S(1)} %fusion.7), channel_id=1, source_target_pairs={{0,16},{1,17},{2,18},{3,19},{4,20},{5,21},{6,22},{7,23},{8,24},{9,... | collective-permute-start | bytes 1376264 | tf_op jit(solution)/shard_map/backward_experts/ppermute | solution.py:27
  168.7 4.5 %collective-permute-start.19 = (bf16[64,3584]{1,0:T(8,128)(2,1)S(1)}, bf16[64,3584]{1,0:T(8,128)(2,1)S(1)}, u32[]{:S(2)}, u32[]{:S(2)}) collective-permute-start(bf16[64,3584]{1,0:T(8,128)(2,1)S(1)} %fusion.6), channel_id=1, source_target_pairs={{0,24},{1,25},{2,26},{3,27},{4,28},{5,29},{6,30},{7,31},{8,0},{9,1... | collective-permute-start | bytes 1376264 | tf_op jit(solution)/shard_map/backward_experts/ppermute | solution.py:27
  173.3 1.8 fusion.159
  175.1 16.0 %collective-permute-start.14 = (bf16[16,3584]{1,0:T(8,128)(2,1)S(1)}, bf16[16,3584]{1,0:T(8,128)(2,1)S(1)}, u32[]{:S(2)}, u32[]{:S(2)}) collective-permute-start(bf16[16,3584]{1,0:T(8,128)(2,1)S(1)} %get-tuple-element.22), channel_id=1, source_target_pairs={{0,34},{1,35},{2,36},{3,37},{4,38},{5,39},{6,32},{7,33},{8,42},{9,... | collective-permute-start | bytes 344072 | tf_op jit(solution)/shard_map/forward_experts/ppermute | solution.py:48
  191.1 5.8 %collective-permute-start.13 = (bf16[16,3584]{1,0:T(8,128)(2,1)S(1)}, bf16[16,3584]{1,0:T(8,128)(2,1)S(1)}, u32[]{:S(2)}, u32[]{:S(2)}) collective-permute-start(bf16[16,3584]{1,0:T(8,128)(2,1)S(1)} %get-tuple-element.23), channel_id=1, source_target_pairs={{0,36},{1,37},{2,38},{3,39},{4,32},{5,33},{6,34},{7,35},{8,44},{9,... | collective-permute-start | bytes 344072 | tf_op jit(solution)/shard_map/forward_experts/ppermute | solution.py:48
  197.0 26.3 %collective-permute-start.12 = (bf16[16,3584]{1,0:T(8,128)(2,1)S(1)}, bf16[16,3584]{1,0:T(8,128)(2,1)S(1)}, u32[]{:S(2)}, u32[]{:S(2)}) collective-permute-start(bf16[16,3584]{1,0:T(8,128)(2,1)S(1)} %get-tuple-element.21), channel_id=1, source_target_pairs={{0,38},{1,39},{2,32},{3,33},{4,34},{5,35},{6,36},{7,37},{8,46},{9,... | collective-permute-start | bytes 344072 | tf_op jit(solution)/shard_map/forward_experts/ppermute | solution.py:48
  223.3 1.9 collective-permute-start.11
  226.0 9.3 %collective-permute-start.27 = (bf16[16,3584]{1,0:T(8,128)(2,1)S(1)}, bf16[16,3584]{1,0:T(8,128)(2,1)S(1)}, u32[]{:S(2)}, u32[]{:S(2)}) collective-permute-start(bf16[16,3584]{1,0:T(8,128)(2,1)S(1)} %get-tuple-element.19), channel_id=1, source_target_pairs={{32,2},{33,3},{34,4},{35,5},{36,6},{37,7},{38,0},{39,1},{40,10},{4... | collective-permute-start | bytes 344072 | tf_op jit(solution)/shard_map/backward_experts/ppermute | solution.py:48
  235.3 1.9 collective-permute-start.26
  237.3 1.9 collective-permute-start.25
  239.2 7.2 %collective-permute-start.24 = (bf16[16,3584]{1,0:T(8,128)(2,1)S(1)}, bf16[16,3584]{1,0:T(8,128)(2,1)S(1)}, u32[]{:S(2)}, u32[]{:S(2)}) collective-permute-start(bf16[16,3584]{1,0:T(8,128)(2,1)S(1)} %fusion.40), channel_id=1, source_target_pairs={{32,0},{33,1},{34,2},{35,3},{36,4},{37,5},{38,6},{39,7},{40,8},{41... | collective-permute-start | bytes 344072 | tf_op jit(solution)/shard_map/backward_experts/ppermute | solution.py:48
  247.1 6.9 %collective-permute-done.27 = bf16[16,3584]{1,0:T(8,128)(2,1)S(1)} collective-permute-done((bf16[16,3584]{1,0:T(8,128)(2,1)S(1)}, bf16[16,3584]{1,0:T(8,128)(2,1)S(1)}, u32[]{:S(2)}, u32[]{:S(2)}) %collective-permute-start.27) | collective-permute-done | bytes 114720 | tf_op jit(solution)/shard_map/backward_experts/ppermute | solution.py:48
  254.0 5.8 %collective-permute-done.26 = bf16[16,3584]{1,0:T(8,128)(2,1)S(1)} collective-permute-done((bf16[16,3584]{1,0:T(8,128)(2,1)S(1)}, bf16[16,3584]{1,0:T(8,128)(2,1)S(1)}, u32[]{:S(2)}, u32[]{:S(2)}) %collective-permute-start.26) | collective-permute-done | bytes 114720 | tf_op jit(solution)/shard_map/backward_experts/ppermute | solution.py:48
  (104 shorter events, 24.1 us)
Async XLA Ops:
  0.6 49.9 %copy-start.2 = (bf16[1,16,3584]{2,1,0:T(8,128)(2,1)S(1)}, bf16[1,16,3584]{2,1,0:T(8,128)(2,1)}, u32[]{:S(2)}) copy-start(bf16[1,16,3584]{2,1,0:T(8,128)(2,1)} %param.9) | copy-start | bytes 344068
  3.1 37.9 %collective-permute-start.2 = (bf16[16,3712]{1,0:T(8,128)(2,1)}, bf16[16,3712]{1,0:T(8,128)(2,1)S(1)}, u32[]{:S(2)}, u32[]{:S(2)}) collective-permute-start(bf16[16,3712]{1,0:T(8,128)(2,1)} %pad_maximum_fusion.4), channel_id=1, source_target_pairs={{0,6},{1,7},{2,0},{3,1},{4,2},{5,3},{6,4},{7,5},{8,14},{9,15},{10,... | collective-permute-start | bytes 356360 | tf_op jit(solution)/shard_map/gather_z/ppermute | solution.py:32
  15.8 29.4 %collective-permute-start.1 = (bf16[16,3712]{1,0:T(8,128)(2,1)}, bf16[16,3712]{1,0:T(8,128)(2,1)S(1)}, u32[]{:S(2)}, u32[]{:S(2)}) collective-permute-start(bf16[16,3712]{1,0:T(8,128)(2,1)} %pad_maximum_fusion.4), channel_id=1, source_target_pairs={{0,4},{1,5},{2,6},{3,7},{4,0},{5,1},{6,2},{7,3},{8,12},{9,13},{10,... | collective-permute-start | bytes 356360 | tf_op jit(solution)/shard_map/gather_z/ppermute | solution.py:32
  20.7 26.5 %collective-permute-start = (bf16[16,3712]{1,0:T(8,128)(2,1)}, bf16[16,3712]{1,0:T(8,128)(2,1)}, u32[]{:S(2)}, u32[]{:S(2)}) collective-permute-start(bf16[16,3712]{1,0:T(8,128)(2,1)} %pad_maximum_fusion.4), channel_id=1, source_target_pairs={{0,2},{1,3},{2,4},{3,5},{4,6},{5,7},{6,0},{7,1},{8,10},{9,11},{10,... | collective-permute-start | bytes 356360 | tf_op jit(solution)/shard_map/gather_z/ppermute | solution.py:32
  29.6 28.6 %collective-permute-start.15 = (bf16[32,3584]{1,0:T(8,128)(2,1)S(1)}, bf16[32,3584]{1,0:T(8,128)(2,1)S(1)}, u32[]{:S(2)}, u32[]{:S(2)}) collective-permute-start(bf16[32,3584]{1,0:T(8,128)(2,1)S(1)} %pad_maximum_fusion.3), channel_id=1, source_target_pairs={{0,2},{1,3},{2,4},{3,5},{4,6},{5,7},{6,0},{7,1},{8,10},{9,11},{10,... | collective-permute-start | bytes 688136 | tf_op jit(solution)/shard_map/gather_z/ppermute | solution.py:32
  33.8 29.7 %collective-permute-start.16 = (bf16[32,3584]{1,0:T(8,128)(2,1)S(1)}, bf16[32,3584]{1,0:T(8,128)(2,1)S(1)}, u32[]{:S(2)}, u32[]{:S(2)}) collective-permute-start(bf16[32,3584]{1,0:T(8,128)(2,1)S(1)} %pad_maximum_fusion.3), channel_id=1, source_target_pairs={{0,4},{1,5},{2,6},{3,7},{4,0},{5,1},{6,2},{7,3},{8,12},{9,13},{10,... | collective-permute-start | bytes 688136 | tf_op jit(solution)/shard_map/gather_z/ppermute | solution.py:32
  40.9 4.3 %copy-start.4 = (bf16[16,3712]{1,0:T(8,128)(2,1)}, bf16[16,3712]{1,0:T(8,128)(2,1)S(1)}, u32[]{:S(2)}) copy-start(bf16[16,3712]{1,0:T(8,128)(2,1)S(1)} %collective-permute-done.2) | copy-start | bytes 356356
  40.9 38.6 %collective-permute-start.17 = (bf16[32,3584]{1,0:T(8,128)(2,1)S(1)}, bf16[32,3584]{1,0:T(8,128)(2,1)S(1)}, u32[]{:S(2)}, u32[]{:S(2)}) collective-permute-start(bf16[32,3584]{1,0:T(8,128)(2,1)S(1)} %pad_maximum_fusion.3), channel_id=1, source_target_pairs={{0,6},{1,7},{2,0},{3,1},{4,2},{5,3},{6,4},{7,5},{8,14},{9,15},{10,... | collective-permute-start | bytes 688136 | tf_op jit(solution)/shard_map/gather_z/ppermute | solution.py:32
  45.3 2.0 copy-start.5
  45.3 94.2 %collective-permute-start.3 = (bf16[3584,256]{1,0:T(8,128)(2,1)}, bf16[3584,256]{1,0:T(8,128)(2,1)S(1)}, u32[]{:S(2)}, u32[]{:S(2)}) collective-permute-start(bf16[3584,256]{1,0:T(8,128)(2,1)} %bitcast.59), channel_id=1, source_target_pairs={{0,1},{1,0},{2,3},{3,2},{4,5},{5,4},{6,7},{7,6},{8,9},{9,8},{10,11... | collective-permute-start | bytes 5505032 | tf_op jit(solution)/shard_map/swap_weights/ppermute | solution.py:36
  47.3 51.6 %collective-permute-start.4 = (bf16[128,3584]{1,0:T(8,128)(2,1)}, bf16[128,3584]{1,0:T(8,128)(2,1)}, u32[]{:S(2)}, u32[]{:S(2)}) collective-permute-start(bf16[128,3584]{1,0:T(8,128)(2,1)} %bitcast.73), channel_id=1, source_target_pairs={{0,1},{1,0},{2,3},{3,2},{4,5},{5,4},{6,7},{7,6},{8,9},{9,8},{10,11... | collective-permute-start | bytes 2752520 | tf_op jit(solution)/shard_map/swap_weights/ppermute | solution.py:36
  50.6 3.5 %slice-start = ((bf16[16,3712]{1,0:T(8,128)(2,1)}), bf16[16,128]{1,0:T(8,128)(2,1)S(1)}, s32[]{:S(2)}) async-start(bf16[16,3712]{1,0:T(8,128)(2,1)} %copy-done.4), calls=%async_computation | async-start | bytes 8192 | tf_op jit(solution)/shard_map/gather_x/slice | solution.py:154
  50.6 3.6 %slice-start.1 = ((bf16[16,3712]{1,0:T(8,128)(2,1)}), bf16[16,128]{1,0:T(8,128)(2,1)S(1)}, s32[]{:S(2)}) async-start(bf16[16,3712]{1,0:T(8,128)(2,1)} %copy-done.5), calls=%async_computation.1 | async-start | bytes 8192 | tf_op jit(solution)/shard_map/gather_x/slice | solution.py:154
  51.4 32.2 %copy-start.1 = (bf16[1,16,3584]{2,1,0:T(8,128)(2,1)S(1)}, bf16[1,16,3584]{2,1,0:T(8,128)(2,1)}, u32[]{:S(2)}) copy-start(bf16[1,16,3584]{2,1,0:T(8,128)(2,1)} %param.11) | copy-start | bytes 344068
  54.0 32.2 %copy-start.3 = (bf16[1,16,3584]{2,1,0:T(8,128)(2,1)S(1)}, bf16[1,16,3584]{2,1,0:T(8,128)(2,1)}, u32[]{:S(2)}) copy-start(bf16[1,16,3584]{2,1,0:T(8,128)(2,1)} %param.10) | copy-start | bytes 344068
  55.7 30.5 %copy-start = (bf16[1,3584,256]{2,1,0:T(8,128)(2,1)S(1)}, bf16[1,3584,256]{2,1,0:T(8,128)(2,1)}, u32[]{:S(2)}) copy-start(bf16[1,3584,256]{2,1,0:T(8,128)(2,1)} %param.12) | copy-start | bytes 5505028
  58.2 28.5 %collective-permute-start.9 = (bf16[64,3584]{1,0:T(8,128)(2,1)}, bf16[64,3584]{1,0:T(8,128)(2,1)S(1)}, u32[]{:S(2)}, u32[]{:S(2)}) collective-permute-start(bf16[64,3584]{1,0:T(8,128)(2,1)} %pad_maximum_fusion.1), channel_id=1, source_target_pairs={{0,24},{1,25},{2,26},{3,27},{4,28},{5,29},{6,30},{7,31},{8,0},{9,1... | collective-permute-start | bytes 1376264 | tf_op jit(solution)/shard_map/gather_x/ppermute | solution.py:27
  63.5 28.0 %collective-permute-start.7 = (bf16[64,3584]{1,0:T(8,128)(2,1)}, bf16[64,3584]{1,0:T(8,128)(2,1)S(1)}, u32[]{:S(2)}, u32[]{:S(2)}) collective-permute-start(bf16[64,3584]{1,0:T(8,128)(2,1)} %pad_maximum_fusion.1), channel_id=1, source_target_pairs={{0,16},{1,17},{2,18},{3,19},{4,20},{5,21},{6,22},{7,23},{8,24},{9,... | collective-permute-start | bytes 1376264 | tf_op jit(solution)/shard_map/gather_x/ppermute | solution.py:27
  79.5 16.2 %collective-permute-start.5 = (bf16[64,3584]{1,0:T(8,128)(2,1)}, bf16[64,3584]{1,0:T(8,128)(2,1)S(1)}, u32[]{:S(2)}, u32[]{:S(2)}) collective-permute-start(bf16[64,3584]{1,0:T(8,128)(2,1)} %pad_maximum_fusion.1), channel_id=1, source_target_pairs={{0,8},{1,9},{2,10},{3,11},{4,12},{5,13},{6,14},{7,15},{8,16},{9,17... | collective-permute-start | bytes 1376264 | tf_op jit(solution)/shard_map/gather_x/ppermute | solution.py:27
  86.2 1.2 copy-start.6
  87.4 42.8 %collective-permute-start.22 = (bf16[128,3584]{1,0:T(8,128)(2,1)S(1)}, bf16[128,3584]{1,0:T(8,128)(2,1)S(1)}, u32[]{:S(2)}, u32[]{:S(2)}) collective-permute-start(bf16[128,3584]{1,0:T(8,128)(2,1)S(1)} %copy-done.6), channel_id=1, source_target_pairs={{0,24},{1,25},{2,26},{3,27},{4,28},{5,29},{6,30},{7,31},{8,0},{9,1... | collective-permute-start | bytes 2752520 | tf_op jit(solution)/shard_map/gather_x/ppermute | solution.py:27
  91.5 40.6 %collective-permute-start.20 = (bf16[128,3584]{1,0:T(8,128)(2,1)S(1)}, bf16[128,3584]{1,0:T(8,128)(2,1)S(1)}, u32[]{:S(2)}, u32[]{:S(2)}) collective-permute-start(bf16[128,3584]{1,0:T(8,128)(2,1)S(1)} %copy-done.6), channel_id=1, source_target_pairs={{0,16},{1,17},{2,18},{3,19},{4,20},{5,21},{6,22},{7,23},{8,24},{9,... | collective-permute-start | bytes 2752520 | tf_op jit(solution)/shard_map/gather_x/ppermute | solution.py:27
  95.7 3.2 %copy-start.7 = (bf16[1,128,3584]{2,1,0:T(8,128)(2,1)S(1)}, bf16[1,128,3584]{2,1,0:T(8,128)(2,1)}, u32[]{:S(2)}) copy-start(bf16[1,128,3584]{2,1,0:T(8,128)(2,1)} %param.13) | copy-start | bytes 2752516
  95.7 40.6 %collective-permute-start.18 = (bf16[128,3584]{1,0:T(8,128)(2,1)S(1)}, bf16[128,3584]{1,0:T(8,128)(2,1)S(1)}, u32[]{:S(2)}, u32[]{:S(2)}) collective-permute-start(bf16[128,3584]{1,0:T(8,128)(2,1)S(1)} %copy-done.6), channel_id=1, source_target_pairs={{0,8},{1,9},{2,10},{3,11},{4,12},{5,13},{6,14},{7,15},{8,16},{9,17... | collective-permute-start | bytes 2752520 | tf_op jit(solution)/shard_map/gather_x/ppermute | solution.py:27
  141.6 27.2 %collective-permute-start.10 = (bf16[64,3584]{1,0:T(8,128)(2,1)S(1)}, bf16[64,3584]{1,0:T(8,128)(2,1)S(1)}, u32[]{:S(2)}, u32[]{:S(2)}) collective-permute-start(bf16[64,3584]{1,0:T(8,128)(2,1)S(1)} %convolution_convert_fusion), channel_id=1, source_target_pairs={{0,8},{1,9},{2,10},{3,11},{4,12},{5,13},{6,14},{7,15},{8,16},{9,17... | collective-permute-start | bytes 1376264 | tf_op jit(solution)/shard_map/forward_experts/ppermute | solution.py:27
  145.9 27.3 %collective-permute-start.8 = (bf16[64,3584]{1,0:T(8,128)(2,1)S(1)}, bf16[64,3584]{1,0:T(8,128)(2,1)S(1)}, u32[]{:S(2)}, u32[]{:S(2)}) collective-permute-start(bf16[64,3584]{1,0:T(8,128)(2,1)S(1)} %convolution_convert_fusion.1), channel_id=1, source_target_pairs={{0,16},{1,17},{2,18},{3,19},{4,20},{5,21},{6,22},{7,23},{8,24},{9,... | collective-permute-start | bytes 1376264 | tf_op jit(solution)/shard_map/forward_experts/ppermute | solution.py:27
  152.4 20.9 %collective-permute-start.6 = (bf16[64,3584]{1,0:T(8,128)(2,1)S(1)}, bf16[64,3584]{1,0:T(8,128)(2,1)S(1)}, u32[]{:S(2)}, u32[]{:S(2)}) collective-permute-start(bf16[64,3584]{1,0:T(8,128)(2,1)S(1)} %convolution_convert_fusion.2), channel_id=1, source_target_pairs={{0,24},{1,25},{2,26},{3,27},{4,28},{5,29},{6,30},{7,31},{8,0},{9,1... | collective-permute-start | bytes 1376264 | tf_op jit(solution)/shard_map/forward_experts/ppermute | solution.py:27
  157.8 39.1 %collective-permute-start.23 = (bf16[64,3584]{1,0:T(8,128)(2,1)S(1)}, bf16[64,3584]{1,0:T(8,128)(2,1)S(1)}, u32[]{:S(2)}, u32[]{:S(2)}) collective-permute-start(bf16[64,3584]{1,0:T(8,128)(2,1)S(1)} %fusion.8), channel_id=1, source_target_pairs={{0,8},{1,9},{2,10},{3,11},{4,12},{5,13},{6,14},{7,15},{8,16},{9,17... | collective-permute-start | bytes 1376264 | tf_op jit(solution)/shard_map/backward_experts/ppermute | solution.py:27
  162.0 61.3 %collective-permute-start.21 = (bf16[64,3584]{1,0:T(8,128)(2,1)S(1)}, bf16[64,3584]{1,0:T(8,128)(2,1)S(1)}, u32[]{:S(2)}, u32[]{:S(2)}) collective-permute-start(bf16[64,3584]{1,0:T(8,128)(2,1)S(1)} %fusion.7), channel_id=1, source_target_pairs={{0,16},{1,17},{2,18},{3,19},{4,20},{5,21},{6,22},{7,23},{8,24},{9,... | collective-permute-start | bytes 1376264 | tf_op jit(solution)/shard_map/backward_experts/ppermute | solution.py:27
  168.7 56.5 %collective-permute-start.19 = (bf16[64,3584]{1,0:T(8,128)(2,1)S(1)}, bf16[64,3584]{1,0:T(8,128)(2,1)S(1)}, u32[]{:S(2)}, u32[]{:S(2)}) collective-permute-start(bf16[64,3584]{1,0:T(8,128)(2,1)S(1)} %fusion.6), channel_id=1, source_target_pairs={{0,24},{1,25},{2,26},{3,27},{4,28},{5,29},{6,30},{7,31},{8,0},{9,1... | collective-permute-start | bytes 1376264 | tf_op jit(solution)/shard_map/backward_experts/ppermute | solution.py:27
  175.1 60.2 %collective-permute-start.14 = (bf16[16,3584]{1,0:T(8,128)(2,1)S(1)}, bf16[16,3584]{1,0:T(8,128)(2,1)S(1)}, u32[]{:S(2)}, u32[]{:S(2)}) collective-permute-start(bf16[16,3584]{1,0:T(8,128)(2,1)S(1)} %get-tuple-element.22), channel_id=1, source_target_pairs={{0,34},{1,35},{2,36},{3,37},{4,38},{5,39},{6,32},{7,33},{8,42},{9,... | collective-permute-start | bytes 344072 | tf_op jit(solution)/shard_map/forward_experts/ppermute | solution.py:48
  191.1 46.1 %collective-permute-start.13 = (bf16[16,3584]{1,0:T(8,128)(2,1)S(1)}, bf16[16,3584]{1,0:T(8,128)(2,1)S(1)}, u32[]{:S(2)}, u32[]{:S(2)}) collective-permute-start(bf16[16,3584]{1,0:T(8,128)(2,1)S(1)} %get-tuple-element.23), channel_id=1, source_target_pairs={{0,36},{1,37},{2,38},{3,39},{4,32},{5,33},{6,34},{7,35},{8,44},{9,... | collective-permute-start | bytes 344072 | tf_op jit(solution)/shard_map/forward_experts/ppermute | solution.py:48
  197.0 42.2 %collective-permute-start.12 = (bf16[16,3584]{1,0:T(8,128)(2,1)S(1)}, bf16[16,3584]{1,0:T(8,128)(2,1)S(1)}, u32[]{:S(2)}, u32[]{:S(2)}) collective-permute-start(bf16[16,3584]{1,0:T(8,128)(2,1)S(1)} %get-tuple-element.21), channel_id=1, source_target_pairs={{0,38},{1,39},{2,32},{3,33},{4,34},{5,35},{6,36},{7,37},{8,46},{9,... | collective-permute-start | bytes 344072 | tf_op jit(solution)/shard_map/forward_experts/ppermute | solution.py:48
  223.3 23.1 %collective-permute-start.11 = (bf16[16,3584]{1,0:T(8,128)(2,1)S(1)}, bf16[16,3584]{1,0:T(8,128)(2,1)S(1)}, u32[]{:S(2)}, u32[]{:S(2)}) collective-permute-start(bf16[16,3584]{1,0:T(8,128)(2,1)S(1)} %fusion.41), channel_id=1, source_target_pairs={{0,32},{1,33},{2,34},{3,35},{4,36},{5,37},{6,38},{7,39},{8,40},{9,... | collective-permute-start | bytes 344072 | tf_op jit(solution)/shard_map/forward_experts/ppermute | solution.py:48
  226.0 28.0 %collective-permute-start.27 = (bf16[16,3584]{1,0:T(8,128)(2,1)S(1)}, bf16[16,3584]{1,0:T(8,128)(2,1)S(1)}, u32[]{:S(2)}, u32[]{:S(2)}) collective-permute-start(bf16[16,3584]{1,0:T(8,128)(2,1)S(1)} %get-tuple-element.19), channel_id=1, source_target_pairs={{32,2},{33,3},{34,4},{35,5},{36,6},{37,7},{38,0},{39,1},{40,10},{4... | collective-permute-start | bytes 344072 | tf_op jit(solution)/shard_map/backward_experts/ppermute | solution.py:48
  235.3 24.5 %collective-permute-start.26 = (bf16[16,3584]{1,0:T(8,128)(2,1)S(1)}, bf16[16,3584]{1,0:T(8,128)(2,1)S(1)}, u32[]{:S(2)}, u32[]{:S(2)}) collective-permute-start(bf16[16,3584]{1,0:T(8,128)(2,1)S(1)} %get-tuple-element.20), channel_id=1, source_target_pairs={{32,4},{33,5},{34,6},{35,7},{36,0},{37,1},{38,2},{39,3},{40,12},{4... | collective-permute-start | bytes 344072 | tf_op jit(solution)/shard_map/backward_experts/ppermute | solution.py:48
  237.3 22.6 %collective-permute-start.25 = (bf16[16,3584]{1,0:T(8,128)(2,1)S(1)}, bf16[16,3584]{1,0:T(8,128)(2,1)S(1)}, u32[]{:S(2)}, u32[]{:S(2)}) collective-permute-start(bf16[16,3584]{1,0:T(8,128)(2,1)S(1)} %get-tuple-element.18), channel_id=1, source_target_pairs={{32,6},{33,7},{34,0},{35,1},{36,2},{37,3},{38,4},{39,5},{40,14},{4... | collective-permute-start | bytes 344072 | tf_op jit(solution)/shard_map/backward_experts/ppermute | solution.py:48
  239.2 20.6 %collective-permute-start.24 = (bf16[16,3584]{1,0:T(8,128)(2,1)S(1)}, bf16[16,3584]{1,0:T(8,128)(2,1)S(1)}, u32[]{:S(2)}, u32[]{:S(2)}) collective-permute-start(bf16[16,3584]{1,0:T(8,128)(2,1)S(1)} %fusion.40), channel_id=1, source_target_pairs={{32,0},{33,1},{34,2},{35,3},{36,4},{37,5},{38,6},{39,7},{40,8},{41... | collective-permute-start | bytes 344072 | tf_op jit(solution)/shard_map/backward_experts/ppermute | solution.py:48

commit v2 on v1

v2 whole, which is shorter than its diff:
```python
import jax
import jax.numpy as jnp
from jax import lax
from jax.sharding import PartitionSpec as P

EXPERTS = 4
Z = 4
CORES = 2
LANES = 128
CAP = 12


def expert_index(x, z, core):
    return (x * Z + z) * CORES + core


def expert_route(move):
    return [
        (expert_index(x, z, c), expert_index(*move(x, z, c)))
        for x in range(EXPERTS)
        for z in range(Z)
        for c in range(CORES)
    ]


def across_x(blocks):
    groups = [
        [expert_index(x, z, c) for x in range(EXPERTS)] for z in range(Z) for c in range(CORES)
    ]
    return lax.all_to_all(blocks, "expert", 0, 0, axis_index_groups=groups, tiled=True)


def along_z(block, distance):
    route = expert_route(lambda x, z, c: (x, (z + distance) % Z, c))
    return lax.ppermute(block, "expert", route)


def other_core(block):
    return lax.ppermute(block, "expert", expert_route(lambda x, z, c: (x, z, 1 - c)))


def to_section(block, step, distance):
    sections = lax.axis_size("pipe")
    width = EXPERTS * Z * CORES
    route = [
        (p * width + source, (p + step) * width + target)
        for p in range(sections)
        if 0 <= p + step < sections
        for source, target in expert_route(lambda x, z, c: (x, (z + distance) % Z, c))
    ]
    return lax.ppermute(block, ("pipe", "expert"), route)


def after(values, *others):
    return lax.optimization_barrier((values, others))[0]


def expert_hot(routes):
    return routes[:, :, None] == jnp.arange(EXPERTS, dtype=jnp.int32)


def expert_shares(hot, gates):
    return jnp.sum(jnp.where(hot, gates[:, :, None], 0.0), axis=1)


def expert_slots(hot):
    named = jnp.any(hot, axis=1)
    count = named.astype(jnp.int32)
    earlier = jnp.cumsum(count, axis=0) - count
    return jnp.where(named, earlier, -1).astype(jnp.float32)


def three_parts(values):
    first = lax.reduce_precision(values, 8, 7)
    second = lax.reduce_precision(values - first, 8, 7)
    return [part.astype(jnp.bfloat16) for part in (first, second, values - first - second)]


def side_columns(shares, slots):
    parts = jnp.concatenate(three_parts(shares) + [slots.astype(jnp.bfloat16)], axis=1)
    return jnp.pad(parts, ((0, 0), (0, LANES - parts.shape[1])))


def side_values(columns):
    width = 2 * EXPERTS
    parts = columns[:, : 4 * width].astype(jnp.float32)
    first, second, third, slots = jnp.split(parts, 4, axis=1)
    return first + second + third, slots


def placement(slots, rows):
    place = jnp.arange(EXPERTS * Z * CAP, dtype=jnp.int32)
    block = jnp.arange(slots.shape[0], dtype=jnp.int32) // rows
    expert, source, slot = place // (Z * CAP), place // CAP % Z, place % CAP
    wanted = jnp.repeat(slots, Z * CAP, axis=1)
    return (block[:, None] == source[None, :]) & (wanted == slot.astype(jnp.float32)[None, :])


def dot(a, b):
    return jnp.dot(a, b, preferred_element_type=jnp.float32)


def dot_t(a, b):
    return lax.dot_general(a, b, (((1,), (1,)), ((), ())), preferred_element_type=jnp.float32)


def pack(places, block):
    packed = lax.dot_general(
        places.astype(jnp.bfloat16),
        block,
        (((0,), (0,)), ((), ())),
        preferred_element_type=jnp.float32,
    )
    return packed.astype(jnp.bfloat16)


def forward_rows(rows, gate_ups, down):
    hidden = []
    for gate_up in gate_ups:
        both = dot(rows, gate_up)
        gate_val, up_val = jnp.split(both, 2, axis=1)
        hidden.append((jax.nn.silu(gate_val) * up_val).astype(jnp.bfloat16))
    return dot(jnp.concatenate(hidden, axis=1), down).astype(jnp.bfloat16)


def backward_rows(rows, grads, gate_ups, down):
    hidden_grads = jnp.split(dot_t(grads, down), len(gate_ups), axis=1)
    total = None
    for gate_up, hidden_grad in zip(gate_ups, hidden_grads):
        both = dot(rows, gate_up)
        gate_val, up_val = jnp.split(both, 2, axis=1)
        sig = jax.nn.sigmoid(gate_val)
        gate_grad = hidden_grad * up_val * sig * (1.0 + gate_val * (1.0 - sig))
        up_grad = hidden_grad * gate_val * sig
        grad = jnp.concatenate([gate_grad, up_grad], axis=1).astype(jnp.bfloat16)
        term = dot_t(grad, gate_up)
        total = term if total is None else total + term
    return total.astype(jnp.bfloat16)


def gated_sum(parts, places, shares):
    weights = jnp.where(places, jnp.repeat(shares, Z * CAP, axis=1), 0.0)
    return sum(dot(weight, parts) for weight in three_parts(weights))


def send_home(mixture, residual, step):
    rows = residual.shape[0]
    own = mixture[:rows] + residual.astype(jnp.float32)
    parts = [
        to_section(mixture[k * rows : (k + 1) * rows].astype(jnp.bfloat16), step, -k)
        for k in range(1, Z)
    ]
    total = to_section(own, step, 0)
    for part in parts:
        total = total + part.astype(jnp.float32)
    return total.astype(jnp.bfloat16)


def on_device(
    forward_input,
    backward_input,
    backward_grad,
    gate_up_weight,
    down_weight,
    forward_routes,
    backward_routes,
    forward_gates,
    backward_gates,
):
    tokens, saved, upstream = forward_input[0], backward_input[0], backward_grad[0]
    rows, model = tokens.shape
    with jax.named_scope("gather_z"):
        hots = [expert_hot(forward_routes[0]), expert_hot(backward_routes[0])]
        shares = [
            expert_shares(hots[0], forward_gates[0]),
            expert_shares(hots[1], backward_gates[0]),
        ]
        slots = [expert_slots(hot) for hot in hots]
        side = side_columns(jnp.concatenate(shares, axis=1), jnp.concatenate(slots, axis=1))
        mine = jnp.concatenate([tokens, saved, upstream, side], axis=1)
        parts = [mine] + [along_z(mine, d) for d in range(1, Z)]
    with jax.named_scope("swap_weights"):
        gate_up, down = gate_up_weight[0], down_weight[0]
        gate_ups = [gate_up, other_core(gate_up)]
        down_other = other_core(down)
        down = jnp.concatenate([down, down_other], axis=0)
    with jax.named_scope("gather_x"):
        block = jnp.concatenate([part[:, : 3 * model] for part in parts], axis=0)
        side = jnp.concatenate([part[:, 3 * model :] for part in parts], axis=0)
        shares, slots = side_values(side)
        places = placement(slots[:, :EXPERTS], rows)
        back_places = placement(slots[:, EXPERTS:], rows)
        packed = [pack(places, block[:, :model]), pack(back_places, block[:, model:])]
        inbound = across_x(jnp.concatenate(packed, axis=1))
    with jax.named_scope("experts"):
        outs = forward_rows(inbound[:, :model], gate_ups, down)
        back = backward_rows(
            inbound[:, model : 2 * model], inbound[:, 2 * model :], gate_ups, down
        )
        outs = across_x(jnp.concatenate([outs, back], axis=1))
    with jax.named_scope("home"):
        mixture = gated_sum(outs[:, :model], places, shares[:, :EXPERTS])
        forward_next = send_home(mixture, tokens, 1)
        mixture = gated_sum(outs[:, model:], back_places, shares[:, EXPERTS:])
        backward_next = send_home(mixture, upstream, -1)
    return (forward_next[None], backward_next[None])


def solution(mesh):
    by_token = P("pipe", "expert", None)
    return jax.shard_map(
        on_device,
        mesh=mesh,
        in_specs=(by_token,) * 3 + (P("pipe", None, "expert"),) + (by_token,) * 5,
        out_specs=(by_token, by_token),
        check_vma=False,
    )
```

time: 263 us -> 256 us (0.973)
  waiting for transfers between devices: 56 us -> 143 us
  starting transfers between devices: 156 us -> 81.2 us
  matrix products: 28.7 us -> 20 us
  local copies, waits for them, and re-layouts: 9.62 us -> 1.01 us
    all_to_all x0 -> x2, waiting for transfers between devices: none -> 77 us  [across_x(): lax.all_to_all(blocks, 'expert', 0, 0, axis_index_groups=groups, tiled=True)]
    ppermute x12 -> x0, starting transfers between devices: 42.2 us -> none  [along_x(): return lax.ppermute(block, 'expert', route)]
    ppermute x6 -> x3, waiting for transfers between devices: 11.4 us -> 52.1 us  [along_z(): return lax.ppermute(block, 'expert', route)]
    ppermute x12 -> x0, waiting for transfers between devices: 31.9 us -> none  [along_x(): return lax.ppermute(block, 'expert', route)]
    ppermute x8, starting transfers between devices: 70.3 us -> 42.7 us  [to_section(): return lax.ppermute(block, ('pipe', 'expert'), route)]
    ppermute x6 -> x3, starting transfers between devices: 38.9 us -> 25.5 us  [along_z(): return lax.ppermute(block, 'expert', route)]
    all_to_all x0 -> x2, starting transfers between devices: none -> 8.63 us  [across_x(): lax.all_to_all(blocks, 'expert', 0, 0, axis_index_groups=groups, tiled=True)]
    dot_general x12 -> x3, matrix products: 12.9 us -> 5.64 us  [dot_t(): lax.dot_general(a, b, (((1,), (1,)), ((), ())), preferred_element_type=jn...]
  transfers between devices with their start and end apart: 28 -> 15, of which waited for: 5 -> 7; matrix products, arithmetic and copies ran while one was open for 16% -> 4% of each run, Pallas kernels for 0% -> 0%
where the time goes in v2:
time: 256 us; the launch traced here: 255 us
  waiting for transfers between devices  143 us (56%)
  starting transfers between devices  81.2 us (32%)
  matrix products  20 us (8%)
  other arithmetic  9.46 us (4%)
    all_to_all x2, waiting for transfers between devices, across_x(): lax.all_to_all(blocks, 'expert', 0, 0, axis_index_groups=groups, tiled=True)  77 us
    ppermute x3, waiting for transfers between devices, along_z(): return lax.ppermute(block, 'expert', route)  52.1 us
    ppermute x8, starting transfers between devices, to_section(): return lax.ppermute(block, ('pipe', 'expert'), route)  42.7 us
    ppermute x3, starting transfers between devices, along_z(): return lax.ppermute(block, 'expert', route)  25.5 us
    ppermute x8, waiting for transfers between devices, to_section(): return lax.ppermute(block, ('pipe', 'expert'), route)  13.5 us
    dot_general x11, matrix products, dot(): return jnp.dot(a, b, preferred_element_type=jnp.float32)  13 us
    all_to_all x2, starting transfers between devices, across_x(): lax.all_to_all(blocks, 'expert', 0, 0, axis_index_groups=groups, tiled=True)  8.63 us
    dot_general x3, matrix products, dot_t(): lax.dot_general(a, b, (((1,), (1,)), ((), ())), preferred_element_type=jn...  5.64 us
  transfers between devices with their start and end apart: 15, of which 7 were waited for; matrix products, arithmetic and copies ran while one was open for 4% of the time, Pallas kernels for 0%

profile of v2, /device:TPU:24, one launch (start us, length us, event | category | flops | bytes accessed | tf_op | source)
XLA Modules:
  0.0 255.4 jit_solution(7322994064685375456)
XLA Ops:
  0.7 0.7 fusion.56
  1.6 0.7 fusion.55
  2.5 0.7 select_reduce_fusion
  3.5 1.1 pad_maximum_fusion.15
  4.5 9.1 %collective-permute-start = (bf16[16,10880]{1,0:T(8,128)(2,1)S(1)}, bf16[16,10880]{1,0:T(8,128)(2,1)S(1)}, u32[]{:S(2)}, u32[]{:S(2)}) collective-permute-start(bf16[16,10880]{1,0:T(8,128)(2,1)S(1)} %pad_maximum_fusion.15), channel_id=1, source_target_pairs={{0,2},{1,3},{2,4},{3,5},{4,6},{5,7},{6,0},{7,1},{8,10},{9,11},{10,... | collective-permute-start | bytes 1044488 | tf_op jit(solution)/shard_map/gather_z/ppermute | solution.py:35
  13.6 10.9 %collective-permute-start.1 = (bf16[16,10880]{1,0:T(8,128)(2,1)S(1)}, bf16[16,10880]{1,0:T(8,128)(2,1)S(1)}, u32[]{:S(2)}, u32[]{:S(2)}) collective-permute-start(bf16[16,10880]{1,0:T(8,128)(2,1)S(1)} %pad_maximum_fusion.15), channel_id=1, source_target_pairs={{0,4},{1,5},{2,6},{3,7},{4,0},{5,1},{6,2},{7,3},{8,12},{9,13},{10,... | collective-permute-start | bytes 1044488 | tf_op jit(solution)/shard_map/gather_z/ppermute | solution.py:35
  24.5 5.5 %collective-permute-start.2 = (bf16[16,10880]{1,0:T(8,128)(2,1)S(1)}, bf16[16,10880]{1,0:T(8,128)(2,1)S(1)}, u32[]{:S(2)}, u32[]{:S(2)}) collective-permute-start(bf16[16,10880]{1,0:T(8,128)(2,1)S(1)} %pad_maximum_fusion.15), channel_id=1, source_target_pairs={{0,6},{1,7},{2,0},{3,1},{4,2},{5,3},{6,4},{7,5},{8,14},{9,15},{10,... | collective-permute-start | bytes 1044488 | tf_op jit(solution)/shard_map/gather_z/ppermute | solution.py:35
  30.0 0.9 collective-permute-done
  31.1 26.3 %collective-permute-done.1 = bf16[16,10880]{1,0:T(8,128)(2,1)S(1)} collective-permute-done((bf16[16,10880]{1,0:T(8,128)(2,1)S(1)}, bf16[16,10880]{1,0:T(8,128)(2,1)S(1)}, u32[]{:S(2)}, u32[]{:S(2)}) %collective-permute-start.1) | collective-permute-done | bytes 348192 | tf_op jit(solution)/shard_map/gather_z/ppermute | solution.py:35
  57.4 0.1 copy.57
  57.5 24.9 %collective-permute-done.2 = bf16[16,10880]{1,0:T(8,128)(2,1)S(1)} collective-permute-done((bf16[16,10880]{1,0:T(8,128)(2,1)S(1)}, bf16[16,10880]{1,0:T(8,128)(2,1)S(1)}, u32[]{:S(2)}, u32[]{:S(2)}) %collective-permute-start.2) | collective-permute-done | bytes 348192 | tf_op jit(solution)/shard_map/gather_z/ppermute | solution.py:35
  82.7 0.2 fusion.34
  83.0 0.8 convolution_convert_fusion
  83.9 0.5 convolution_convert_fusion.2
  84.4 2.2 pad_maximum_fusion
  86.6 5.0 %all-to-all-start = ((bf16[4,48,10752]{2,1,0:T(8,128)(2,1)}), bf16[4,48,10752]{2,1,0:T(8,128)(2,1)}, u32[]{:S(2)}, u32[]{:S(2)}) async-start(bf16[4,48,10752]{2,1,0:T(8,128)(2,1)} %bitcast.72), calls=%async_computation | async-start | bytes 8257536 | tf_op jit(solution)/shard_map/gather_x/all_to_all | solution.py:30
  91.6 1.9 collective-permute-start.3
  93.5 2.4 collective-permute-start.4
  95.9 44.2 %all-to-all-done = bf16[4,48,10752]{2,1,0:T(8,128)(2,1)} async-done(((bf16[4,48,10752]{2,1,0:T(8,128)(2,1)}), bf16[4,48,10752]{2,1,0:T(8,128)(2,1)}, u32[]{:S(2)}, u32[]{:S(2)}) %all-to-all-start) | async-done | bytes 4128800 | tf_op jit(solution)/shard_map/gather_x/all_to_all | solution.py:30
  140.1 1.9 fusion.9
  142.0 2.4 fusion.7
  144.6 1.9 fusion.5
  146.4 2.4 fusion.3
  148.9 2.6 %fusion.1 = f32[192,256]{1,0:T(8,128)S(1)} fusion(bf16[192,10752]{1,0:T(8,128)(2,1)} %bitcast.11, bf16[128,3584]{1,0:T(8,128)(2,1)} %collective-permute-done.4, bf16[128,3584]{1,0:T(8,128)(2,1)} %bitcast.13), kind=kOutput, calls=%fused_computation.12 | convolution fusion | flops 355991552 | bytes 3407872 | tf_op jit(solution)/shard_map/experts/dot_general | solution.py:104
  151.6 0.8 fusion.46
  152.4 2.0 convolution_convert_fusion.1
  154.4 2.3 fusion
  156.7 1.8 pad_maximum_fusion.1
  158.5 3.7 %all-to-all-start.1 = ((bf16[4,48,7168]{2,1,0:T(8,128)(2,1)}), bf16[4,48,7168]{2,1,0:T(8,128)(2,1)S(1)}, u32[]{:S(2)}, u32[]{:S(2)}) async-start(bf16[4,48,7168]{2,1,0:T(8,128)(2,1)} %bitcast.73), calls=%async_computation.1 | async-start | bytes 5505024 | tf_op jit(solution)/shard_map/experts/all_to_all | solution.py:30
  162.3 32.8 %all-to-all-done.1 = bf16[4,48,7168]{2,1,0:T(8,128)(2,1)S(1)} async-done(((bf16[4,48,7168]{2,1,0:T(8,128)(2,1)}), bf16[4,48,7168]{2,1,0:T(8,128)(2,1)S(1)}, u32[]{:S(2)}, u32[]{:S(2)}) %all-to-all-start.1) | async-done | bytes 2752544 | tf_op jit(solution)/shard_map/experts/all_to_all | solution.py:30
  195.1 0.4 fusion.13
  195.5 0.4 convolution_add_fusion.2
  195.9 0.4 fusion.74
  196.3 4.9 %collective-permute-start.10 = (bf16[16,3584]{1,0:T(8,128)(2,1)S(1)}, bf16[16,3584]{1,0:T(8,128)(2,1)S(1)}, u32[]{:S(2)}, u32[]{:S(2)}) collective-permute-start(bf16[16,3584]{1,0:T(8,128)(2,1)S(1)} %get-tuple-element.8), channel_id=1, source_target_pairs={{32,6},{33,7},{34,0},{35,1},{36,2},{37,3},{38,4},{39,5},{40,14},{4... | collective-permute-start | bytes 344072 | tf_op jit(solution)/shard_map/home/ppermute | solution.py:51
  201.2 9.7 %collective-permute-start.11 = (bf16[16,3584]{1,0:T(8,128)(2,1)S(1)}, bf16[16,3584]{1,0:T(8,128)(2,1)S(1)}, u32[]{:S(2)}, u32[]{:S(2)}) collective-permute-start(bf16[16,3584]{1,0:T(8,128)(2,1)S(1)} %get-tuple-element.10), channel_id=1, source_target_pairs={{32,4},{33,5},{34,6},{35,7},{36,0},{37,1},{38,2},{39,3},{40,12},{4... | collective-permute-start | bytes 344072 | tf_op jit(solution)/shard_map/home/ppermute | solution.py:51
  210.9 5.0 %collective-permute-start.12 = (bf16[16,3584]{1,0:T(8,128)(2,1)S(1)}, bf16[16,3584]{1,0:T(8,128)(2,1)S(1)}, u32[]{:S(2)}, u32[]{:S(2)}) collective-permute-start(bf16[16,3584]{1,0:T(8,128)(2,1)S(1)} %get-tuple-element.9), channel_id=1, source_target_pairs={{32,2},{33,3},{34,4},{35,5},{36,6},{37,7},{38,0},{39,1},{40,10},{4... | collective-permute-start | bytes 344072 | tf_op jit(solution)/shard_map/home/ppermute | solution.py:51
  216.0 4.9 %collective-permute-start.9 = (f32[16,3584]{1,0:T(8,128)S(1)}, f32[16,3584]{1,0:T(8,128)S(1)}, u32[]{:S(2)}, u32[]{:S(2)}) collective-permute-start(f32[16,3584]{1,0:T(8,128)S(1)} %slice_add_fusion), channel_id=1, source_target_pairs={{32,0},{33,1},{34,2},{35,3},{36,4},{37,5},{38,6},{39,7},{40,8},{41... | collective-permute-start | bytes 688136 | tf_op jit(solution)/shard_map/home/ppermute | solution.py:51
  221.0 0.4 fusion.17
  221.4 0.4 convolution_add_fusion.4
  221.8 0.4 fusion.73
  222.2 4.2 %collective-permute-start.6 = (bf16[16,3584]{1,0:T(8,128)(2,1)S(1)}, bf16[16,3584]{1,0:T(8,128)(2,1)S(1)}, u32[]{:S(2)}, u32[]{:S(2)}) collective-permute-start(bf16[16,3584]{1,0:T(8,128)(2,1)S(1)} %get-tuple-element.11), channel_id=1, source_target_pairs={{0,38},{1,39},{2,32},{3,33},{4,34},{5,35},{6,36},{7,37},{8,46},{9,... | collective-permute-start | bytes 344072 | tf_op jit(solution)/shard_map/home/ppermute | solution.py:51
  226.5 5.7 %collective-permute-start.7 = (bf16[16,3584]{1,0:T(8,128)(2,1)S(1)}, bf16[16,3584]{1,0:T(8,128)(2,1)S(1)}, u32[]{:S(2)}, u32[]{:S(2)}) collective-permute-start(bf16[16,3584]{1,0:T(8,128)(2,1)S(1)} %get-tuple-element.13), channel_id=1, source_target_pairs={{0,36},{1,37},{2,38},{3,39},{4,32},{5,33},{6,34},{7,35},{8,44},{9,... | collective-permute-start | bytes 344072 | tf_op jit(solution)/shard_map/home/ppermute | solution.py:51
  232.2 2.2 collective-permute-start.8
  234.5 6.0 %collective-permute-start.5 = (f32[16,3584]{1,0:T(8,128)S(1)}, f32[16,3584]{1,0:T(8,128)S(1)}, u32[]{:S(2)}, u32[]{:S(2)}) collective-permute-start(f32[16,3584]{1,0:T(8,128)S(1)} %slice_add_fusion.1), channel_id=1, source_target_pairs={{0,32},{1,33},{2,34},{3,35},{4,36},{5,37},{6,38},{7,39},{8,40},{9,... | collective-permute-start | bytes 688136 | tf_op jit(solution)/shard_map/home/ppermute | solution.py:51
  240.5 0.7 fusion.32
  241.2 8.7 %collective-permute-done.6 = bf16[16,3584]{1,0:T(8,128)(2,1)S(1)} collective-permute-done((bf16[16,3584]{1,0:T(8,128)(2,1)S(1)}, bf16[16,3584]{1,0:T(8,128)(2,1)S(1)}, u32[]{:S(2)}, u32[]{:S(2)}) %collective-permute-start.6) | collective-permute-done | bytes 114720 | tf_op jit(solution)/shard_map/home/ppermute | solution.py:51
  249.9 4.8 %collective-permute-done.5 = f32[16,3584]{1,0:T(8,128)S(1)} collective-permute-done((f32[16,3584]{1,0:T(8,128)S(1)}, f32[16,3584]{1,0:T(8,128)S(1)}, u32[]{:S(2)}, u32[]{:S(2)}) %collective-permute-start.5) | collective-permute-done | bytes 229408 | tf_op jit(solution)/shard_map/home/ppermute | solution.py:51
  254.7 0.7 fusion.31
  (52 shorter events, 1.5 us)
Async XLA Ops:
  0.6 82.4 %copy-start.2 = (bf16[1,16,3584]{2,1,0:T(8,128)(2,1)S(1)}, bf16[1,16,3584]{2,1,0:T(8,128)(2,1)}, u32[]{:S(2)}) copy-start(bf16[1,16,3584]{2,1,0:T(8,128)(2,1)} %param.9) | copy-start | bytes 344068
  0.6 82.4 %copy-start.3 = (bf16[1,16,3584]{2,1,0:T(8,128)(2,1)S(1)}, bf16[1,16,3584]{2,1,0:T(8,128)(2,1)}, u32[]{:S(2)}) copy-start(bf16[1,16,3584]{2,1,0:T(8,128)(2,1)} %param.10) | copy-start | bytes 344068
  0.7 82.4 %copy-start.1 = (bf16[1,16,3584]{2,1,0:T(8,128)(2,1)S(1)}, bf16[1,16,3584]{2,1,0:T(8,128)(2,1)}, u32[]{:S(2)}) copy-start(bf16[1,16,3584]{2,1,0:T(8,128)(2,1)} %param.11) | copy-start | bytes 344068
  4.5 26.4 %collective-permute-start = (bf16[16,10880]{1,0:T(8,128)(2,1)S(1)}, bf16[16,10880]{1,0:T(8,128)(2,1)S(1)}, u32[]{:S(2)}, u32[]{:S(2)}) collective-permute-start(bf16[16,10880]{1,0:T(8,128)(2,1)S(1)} %pad_maximum_fusion.15), channel_id=1, source_target_pairs={{0,2},{1,3},{2,4},{3,5},{4,6},{5,7},{6,0},{7,1},{8,10},{9,11},{10,... | collective-permute-start | bytes 1044488 | tf_op jit(solution)/shard_map/gather_z/ppermute | solution.py:35
  13.6 43.7 %collective-permute-start.1 = (bf16[16,10880]{1,0:T(8,128)(2,1)S(1)}, bf16[16,10880]{1,0:T(8,128)(2,1)S(1)}, u32[]{:S(2)}, u32[]{:S(2)}) collective-permute-start(bf16[16,10880]{1,0:T(8,128)(2,1)S(1)} %pad_maximum_fusion.15), channel_id=1, source_target_pairs={{0,4},{1,5},{2,6},{3,7},{4,0},{5,1},{6,2},{7,3},{8,12},{9,13},{10,... | collective-permute-start | bytes 1044488 | tf_op jit(solution)/shard_map/gather_z/ppermute | solution.py:35
  24.5 57.9 %collective-permute-start.2 = (bf16[16,10880]{1,0:T(8,128)(2,1)S(1)}, bf16[16,10880]{1,0:T(8,128)(2,1)S(1)}, u32[]{:S(2)}, u32[]{:S(2)}) collective-permute-start(bf16[16,10880]{1,0:T(8,128)(2,1)S(1)} %pad_maximum_fusion.15), channel_id=1, source_target_pairs={{0,6},{1,7},{2,0},{3,1},{4,2},{5,3},{6,4},{7,5},{8,14},{9,15},{10,... | collective-permute-start | bytes 1044488 | tf_op jit(solution)/shard_map/gather_z/ppermute | solution.py:35
  86.6 5.0 %copy-start = (bf16[1,3584,256]{2,1,0:T(8,128)(2,1)S(1)}, bf16[1,3584,256]{2,1,0:T(8,128)(2,1)}, u32[]{:S(2)}) copy-start(bf16[1,3584,256]{2,1,0:T(8,128)(2,1)} %param.12) | copy-start | bytes 5505028
  86.6 53.5 %all-to-all-start = ((bf16[4,48,10752]{2,1,0:T(8,128)(2,1)}), bf16[4,48,10752]{2,1,0:T(8,128)(2,1)}, u32[]{:S(2)}, u32[]{:S(2)}) async-start(bf16[4,48,10752]{2,1,0:T(8,128)(2,1)} %bitcast.72), calls=%async_computation | async-start | bytes 8257536 | tf_op jit(solution)/shard_map/gather_x/all_to_all | solution.py:30
  91.6 50.4 %collective-permute-start.3 = (bf16[3584,256]{1,0:T(8,128)(2,1)S(1)}, bf16[3584,256]{1,0:T(8,128)(2,1)}, u32[]{:S(2)}, u32[]{:S(2)}) collective-permute-start(bf16[3584,256]{1,0:T(8,128)(2,1)S(1)} %bitcast.74), channel_id=1, source_target_pairs={{0,1},{1,0},{2,3},{3,2},{4,5},{5,4},{6,7},{7,6},{8,9},{9,8},{10,11... | collective-permute-start | bytes 5505032 | tf_op jit(solution)/shard_map/swap_weights/ppermute | solution.py:39
  93.5 55.4 %collective-permute-start.4 = (bf16[128,3584]{1,0:T(8,128)(2,1)}, bf16[128,3584]{1,0:T(8,128)(2,1)}, u32[]{:S(2)}, u32[]{:S(2)}) collective-permute-start(bf16[128,3584]{1,0:T(8,128)(2,1)} %bitcast.13), channel_id=1, source_target_pairs={{0,1},{1,0},{2,3},{3,2},{4,5},{5,4},{6,7},{7,6},{8,9},{9,8},{10,11... | collective-permute-start | bytes 2752520 | tf_op jit(solution)/shard_map/swap_weights/ppermute | solution.py:39
  158.5 36.5 %all-to-all-start.1 = ((bf16[4,48,7168]{2,1,0:T(8,128)(2,1)}), bf16[4,48,7168]{2,1,0:T(8,128)(2,1)S(1)}, u32[]{:S(2)}, u32[]{:S(2)}) async-start(bf16[4,48,7168]{2,1,0:T(8,128)(2,1)} %bitcast.73), calls=%async_computation.1 | async-start | bytes 5505024 | tf_op jit(solution)/shard_map/experts/all_to_all | solution.py:30
  196.3 30.1 %collective-permute-start.10 = (bf16[16,3584]{1,0:T(8,128)(2,1)S(1)}, bf16[16,3584]{1,0:T(8,128)(2,1)S(1)}, u32[]{:S(2)}, u32[]{:S(2)}) collective-permute-start(bf16[16,3584]{1,0:T(8,128)(2,1)S(1)} %get-tuple-element.8), channel_id=1, source_target_pairs={{32,6},{33,7},{34,0},{35,1},{36,2},{37,3},{38,4},{39,5},{40,14},{4... | collective-permute-start | bytes 344072 | tf_op jit(solution)/shard_map/home/ppermute | solution.py:51
  201.2 31.0 %collective-permute-start.11 = (bf16[16,3584]{1,0:T(8,128)(2,1)S(1)}, bf16[16,3584]{1,0:T(8,128)(2,1)S(1)}, u32[]{:S(2)}, u32[]{:S(2)}) collective-permute-start(bf16[16,3584]{1,0:T(8,128)(2,1)S(1)} %get-tuple-element.10), channel_id=1, source_target_pairs={{32,4},{33,5},{34,6},{35,7},{36,0},{37,1},{38,2},{39,3},{40,12},{4... | collective-permute-start | bytes 344072 | tf_op jit(solution)/shard_map/home/ppermute | solution.py:51
  210.9 23.5 %collective-permute-start.12 = (bf16[16,3584]{1,0:T(8,128)(2,1)S(1)}, bf16[16,3584]{1,0:T(8,128)(2,1)S(1)}, u32[]{:S(2)}, u32[]{:S(2)}) collective-permute-start(bf16[16,3584]{1,0:T(8,128)(2,1)S(1)} %get-tuple-element.9), channel_id=1, source_target_pairs={{32,2},{33,3},{34,4},{35,5},{36,6},{37,7},{38,0},{39,1},{40,10},{4... | collective-permute-start | bytes 344072 | tf_op jit(solution)/shard_map/home/ppermute | solution.py:51
  216.0 24.5 %collective-permute-start.9 = (f32[16,3584]{1,0:T(8,128)S(1)}, f32[16,3584]{1,0:T(8,128)S(1)}, u32[]{:S(2)}, u32[]{:S(2)}) collective-permute-start(f32[16,3584]{1,0:T(8,128)S(1)} %slice_add_fusion), channel_id=1, source_target_pairs={{32,0},{33,1},{34,2},{35,3},{36,4},{37,5},{38,6},{39,7},{40,8},{41... | collective-permute-start | bytes 688136 | tf_op jit(solution)/shard_map/home/ppermute | solution.py:51
  222.2 27.7 %collective-permute-start.6 = (bf16[16,3584]{1,0:T(8,128)(2,1)S(1)}, bf16[16,3584]{1,0:T(8,128)(2,1)S(1)}, u32[]{:S(2)}, u32[]{:S(2)}) collective-permute-start(bf16[16,3584]{1,0:T(8,128)(2,1)S(1)} %get-tuple-element.11), channel_id=1, source_target_pairs={{0,38},{1,39},{2,32},{3,33},{4,34},{5,35},{6,36},{7,37},{8,46},{9,... | collective-permute-start | bytes 344072 | tf_op jit(solution)/shard_map/home/ppermute | solution.py:51
  226.5 23.4 %collective-permute-start.7 = (bf16[16,3584]{1,0:T(8,128)(2,1)S(1)}, bf16[16,3584]{1,0:T(8,128)(2,1)S(1)}, u32[]{:S(2)}, u32[]{:S(2)}) collective-permute-start(bf16[16,3584]{1,0:T(8,128)(2,1)S(1)} %get-tuple-element.13), channel_id=1, source_target_pairs={{0,36},{1,37},{2,38},{3,39},{4,32},{5,33},{6,34},{7,35},{8,44},{9,... | collective-permute-start | bytes 344072 | tf_op jit(solution)/shard_map/home/ppermute | solution.py:51
  232.2 17.7 %collective-permute-start.8 = (bf16[16,3584]{1,0:T(8,128)(2,1)S(1)}, bf16[16,3584]{1,0:T(8,128)(2,1)S(1)}, u32[]{:S(2)}, u32[]{:S(2)}) collective-permute-start(bf16[16,3584]{1,0:T(8,128)(2,1)S(1)} %get-tuple-element.12), channel_id=1, source_target_pairs={{0,34},{1,35},{2,36},{3,37},{4,38},{5,39},{6,32},{7,33},{8,42},{9,... | collective-permute-start | bytes 344072 | tf_op jit(solution)/shard_map/home/ppermute | solution.py:51
  234.5 20.2 %collective-permute-start.5 = (f32[16,3584]{1,0:T(8,128)S(1)}, f32[16,3584]{1,0:T(8,128)S(1)}, u32[]{:S(2)}, u32[]{:S(2)}) collective-permute-start(f32[16,3584]{1,0:T(8,128)S(1)} %slice_add_fusion.1), channel_id=1, source_target_pairs={{0,32},{1,33},{2,34},{3,35},{4,36},{5,37},{6,38},{7,39},{8,40},{9,... | collective-permute-start | bytes 688136 | tf_op jit(solution)/shard_map/home/ppermute | solution.py:51

commit v3 on v2

--- a/solution.py
+++ b/solution.py
@@ -8,6 +8,7 @@
 CORES = 2
 LANES = 128
 CAP = 12
+OWNERS = (0, -1, 1, -2)
 
 
 def expert_index(x, z, core):
@@ -30,8 +31,12 @@
     return lax.all_to_all(blocks, "expert", 0, 0, axis_index_groups=groups, tiled=True)
 
 
+def turn(core):
+    return 1 - 2 * core
+
+
 def along_z(block, distance):
-    route = expert_route(lambda x, z, c: (x, (z + distance) % Z, c))
+    route = expert_route(lambda x, z, c: (x, (z + distance * turn(c)) % Z, c))
     return lax.ppermute(block, "expert", route)
 
 
@@ -46,13 +51,13 @@
         (p * width + source, (p + step) * width + target)
         for p in range(sections)
         if 0 <= p + step < sections
-        for source, target in expert_route(lambda x, z, c: (x, (z + distance) % Z, c))
+        for source, target in expert_route(lambda x, z, c: (x, (z + distance * turn(c)) % Z, c))
     ]
     return lax.ppermute(block, ("pipe", "expert"), route)
 
 
-def after(values, *others):
-    return lax.optimization_barrier((values, others))[0]
+def together(*values):
+    return lax.optimization_barrier(values)
 
 
 def expert_hot(routes):
@@ -147,8 +152,8 @@
     rows = residual.shape[0]
     own = mixture[:rows] + residual.astype(jnp.float32)
     parts = [
-        to_section(mixture[k * rows : (k + 1) * rows].astype(jnp.bfloat16), step, -k)
-        for k in range(1, Z)
+        to_section(mixture[k * rows : (k + 1) * rows].astype(jnp.bfloat16), step, distance)
+        for k, distance in enumerate(OWNERS) if k > 0
     ]
     total = to_section(own, step, 0)
     for part in parts:
@@ -177,31 +182,38 @@
         ]
         slots = [expert_slots(hot) for hot in hots]
         side = side_columns(jnp.concatenate(shares, axis=1), jnp.concatenate(slots, axis=1))
-        mine = jnp.concatenate([tokens, saved, upstream, side], axis=1)
-        parts = [mine] + [along_z(mine, d) for d in range(1, Z)]
-    with jax.named_scope("swap_weights"):
+        mine = jnp.concatenate([tokens, side], axis=1)
+        near, far = along_z(mine, 1), along_z(mine, -1)
         gate_up, down = gate_up_weight[0], down_weight[0]
-        gate_ups = [gate_up, other_core(gate_up)]
-        down_other = other_core(down)
-        down = jnp.concatenate([down, down_other], axis=0)
+        gate_up_2, down_2 = other_core(gate_up), other_core(down)
+        near, far, gate_up_2, down_2 = together(near, far, gate_up_2, down_2)
+        back_mine = jnp.concatenate([saved, upstream], axis=1)
+        both = along_z(jnp.concatenate([near, back_mine], axis=1), 1)
+        both, back_far = together(both, along_z(back_mine, -1))
+        opposite, back_near = both[:, : mine.shape[1]], both[:, mine.shape[1] :]
+        parts = [mine, near, far, opposite]
+        gate_ups, down = [gate_up, gate_up_2], jnp.concatenate([down, down_2], axis=0)
     with jax.named_scope("gather_x"):
-        block = jnp.concatenate([part[:, : 3 * model] for part in parts], axis=0)
-        side = jnp.concatenate([part[:, 3 * model :] for part in parts], axis=0)
-        shares, slots = side_values(side)
+        block = jnp.concatenate([part[:, :model] for part in parts], axis=0)
+        shares, slots = side_values(jnp.concatenate([part[:, model:] for part in parts], axis=0))
         places = placement(slots[:, :EXPERTS], rows)
         back_places = placement(slots[:, EXPERTS:], rows)
-        packed = [pack(places, block[:, :model]), pack(back_places, block[:, model:])]
-        inbound = across_x(jnp.concatenate(packed, axis=1))
-    with jax.named_scope("experts"):
-        outs = forward_rows(inbound[:, :model], gate_ups, down)
-        back = backward_rows(
-            inbound[:, model : 2 * model], inbound[:, 2 * model :], gate_ups, down
-        )
-        outs = across_x(jnp.concatenate([outs, back], axis=1))
-    with jax.named_scope("home"):
-        mixture = gated_sum(outs[:, :model], places, shares[:, :EXPERTS])
+        token_rows = across_x(pack(places, block))
+        token_rows, back_opposite = together(token_rows, along_z(back_near, 1))
+        back_block = jnp.concatenate([back_mine, back_near, back_far, back_opposite], axis=0)
+        back_rows = across_x(pack(back_places, back_block))
+    with jax.named_scope("forward_experts"):
+        outs = forward_rows(token_rows, gate_ups, down)
+        outs, back_rows = together(outs, back_rows)
+        outs = across_x(outs)
+    with jax.named_scope("backward_experts"):
+        back_outs = backward_rows(back_rows[:, :model], back_rows[:, model:], gate_ups, down)
+        back_outs = across_x(back_outs)
+    with jax.named_scope("forward_home"):
+        mixture = gated_sum(outs, places, shares[:, :EXPERTS])
         forward_next = send_home(mixture, tokens, 1)
-        mixture = gated_sum(outs[:, model:], back_places, shares[:, EXPERTS:])
+    with jax.named_scope("backward_home"):
+        mixture = gated_sum(back_outs, back_places, shares[:, EXPERTS:])
         backward_next = send_home(mixture, upstream, -1)
     return (forward_next[None], backward_next[None])
 

time: 256 us -> 229 us (0.89)
  the two profiles are of different devices: /device:TPU:24 before, /device:TPU:98 now
where the time goes in v3:
time: 229 us; the launch traced here: 228 us
  starting transfers between devices  97.6 us (43%)
  waiting for transfers between devices  85.8 us (37%)
  matrix products  21 us (9%)
  other arithmetic  11.3 us (5%)
  local copies, waits for them, and re-layouts  10.8 us (5%)
    ppermute x8, starting transfers between devices, to_section(): return lax.ppermute(block, ('pipe', 'expert'), route)  48.6 us
    ppermute x5, waiting for transfers between devices, along_z(): return lax.ppermute(block, 'expert', route)  40.9 us
    all_to_all x4, waiting for transfers between devices, across_x(): lax.all_to_all(blocks, 'expert', 0, 0, axis_index_groups=groups, tiled=True)  27.4 us
    ppermute x5, starting transfers between devices, along_z(): return lax.ppermute(block, 'expert', route)  24.7 us
    all_to_all x4, starting transfers between devices, across_x(): lax.all_to_all(blocks, 'expert', 0, 0, axis_index_groups=groups, tiled=True)  20 us
    ppermute x8, waiting for transfers between devices, to_section(): return lax.ppermute(block, ('pipe', 'expert'), route)  17.5 us
    dot_general x11, matrix products, dot(): return jnp.dot(a, b, preferred_element_type=jnp.float32)  10.1 us
    dot_general x2, matrix products, pack(): lax.dot_general(places.astype(jnp.bfloat16), block, (((0,), (0,)), ((), (...  5.86 us
  transfers between devices with their start and end apart: 19, of which 10 were waited for; matrix products, arithmetic and copies ran while one was open for 10% of the time, Pallas kernels for 0%

profile of v3, /device:TPU:98, one launch (start us, length us, event | category | flops | bytes accessed | tf_op | source)
XLA Modules:
  0.0 227.6 jit_solution(9109651781481676375)
XLA Ops:
  0.6 1.9 collective-permute-start.2
  2.6 2.4 %collective-permute-start.3 = (bf16[128,3584]{1,0:T(8,128)(2,1)}, bf16[128,3584]{1,0:T(8,128)(2,1)S(1)}, u32[]{:S(2)}, u32[]{:S(2)}) collective-permute-start(bf16[128,3584]{1,0:T(8,128)(2,1)} %bitcast.87), channel_id=1, source_target_pairs={{0,1},{1,0},{2,3},{3,2},{4,5},{5,4},{6,7},{7,6},{8,9},{9,8},{10,11... | collective-permute-start | bytes 2752520 | tf_op jit(solution)/shard_map/gather_z/ppermute | solution.py:44
  7.7 0.9 pad_maximum_fusion.5
  8.6 10.0 %collective-permute-start.1 = (bf16[16,3712]{1,0:T(8,128)(2,1)S(1)}, bf16[16,3712]{1,0:T(8,128)(2,1)S(1)}, u32[]{:S(2)}, u32[]{:S(2)}) collective-permute-start(bf16[16,3712]{1,0:T(8,128)(2,1)S(1)} %pad_maximum_fusion.5), channel_id=1, source_target_pairs={{0,6},{1,3},{2,0},{3,5},{4,2},{5,7},{6,4},{7,1},{8,14},{9,11},{10,... | collective-permute-start | bytes 356360 | tf_op jit(solution)/shard_map/gather_z/ppermute | solution.py:40
  18.7 1.9 collective-permute-start
  20.6 0.8 collective-permute-done.1
  21.4 10.2 %collective-permute-done = bf16[16,3712]{1,0:T(8,128)(2,1)S(1)} collective-permute-done((bf16[16,3712]{1,0:T(8,128)(2,1)S(1)}, bf16[16,3712]{1,0:T(8,128)(2,1)S(1)}, u32[]{:S(2)}, u32[]{:S(2)}) %collective-permute-start) | collective-permute-done | bytes 118816 | tf_op jit(solution)/shard_map/gather_z/ppermute | solution.py:40
  31.7 0.9 copy-done.16
  32.6 1.7 pad_maximum_fusion.3
  34.3 3.6 %collective-permute-start.4 = (bf16[16,10880]{1,0:T(8,128)(2,1)}, bf16[16,10880]{1,0:T(8,128)(2,1)S(1)}, u32[]{:S(2)}, u32[]{:S(2)}) collective-permute-start(bf16[16,10880]{1,0:T(8,128)(2,1)} %pad_maximum_fusion.3), channel_id=1, source_target_pairs={{0,2},{1,7},{2,4},{3,1},{4,6},{5,3},{6,0},{7,5},{8,10},{9,15},{10,... | collective-permute-start | bytes 1044488 | tf_op jit(solution)/shard_map/gather_z/ppermute | solution.py:40
  37.9 1.7 pad_maximum_fusion.4
  39.6 6.1 %collective-permute-start.5 = (bf16[16,7168]{1,0:T(8,128)(2,1)}, bf16[16,7168]{1,0:T(8,128)(2,1)}, u32[]{:S(2)}, u32[]{:S(2)}) collective-permute-start(bf16[16,7168]{1,0:T(8,128)(2,1)} %pad_maximum_fusion.4), channel_id=1, source_target_pairs={{0,6},{1,3},{2,0},{3,5},{4,2},{5,7},{6,4},{7,1},{8,14},{9,11},{10,... | collective-permute-start | bytes 688136 | tf_op jit(solution)/shard_map/gather_z/ppermute | solution.py:40
  46.8 1.3 copy.50
  48.2 1.4 slice.100
  49.6 19.0 %collective-permute-done.5 = bf16[16,7168]{1,0:T(8,128)(2,1)} collective-permute-done((bf16[16,7168]{1,0:T(8,128)(2,1)}, bf16[16,7168]{1,0:T(8,128)(2,1)}, u32[]{:S(2)}, u32[]{:S(2)}) %collective-permute-start.5) | collective-permute-done | bytes 229408 | tf_op jit(solution)/shard_map/gather_z/ppermute | solution.py:40
  69.3 2.3 %copy.51 = bf16[16,10880]{0,1:T(8,128)(2,1)S(1)} copy(bf16[16,10880]{1,0:T(8,128)(2,1)S(1)} %collective-permute-done.4) | data formatting | bytes 696320 | tf_op jit(solution)/shard_map/gather_z/optimization_barrier | solution.py:60
  72.2 0.8 maximum_convert_fusion
  73.1 0.8 compare_and_fusion
  73.9 2.5 %convolution_convert_fusion.2 = bf16[192,3584]{1,0:T(8,128)(2,1)} fusion(pred[64,192]{0,1:T(32,128)(4,1)S(1)} %get-tuple-element.44, bf16[16,3584]{1,0:T(8,128)(2,1)} %slice.85, bf16[16,3584]{1,0:T(8,128)(2,1)S(1)} %slice-done.1, bf16[16,3584]{1,0:T(8,128)(2,1)S(1)} %slice-done, bf16[16,3584]{1,0:T(8,128)(2,1)S(1)} %bitcast.74), kind=kOutput, calls=%fused_computation.4 | convolution fusion | flops 90603520 | bytes 1847296 | tf_op jit(solution)/shard_map/gather_x/dot_general | solution.py:113
  76.4 5.0 %all-to-all-start = ((bf16[4,48,3584]{2,1,0:T(8,128)(2,1)}), bf16[4,48,3584]{2,1,0:T(8,128)(2,1)S(1)}, u32[]{:S(2)}, u32[]{:S(2)}) async-start(bf16[4,48,3584]{2,1,0:T(8,128)(2,1)} %bitcast.10), calls=%async_computation | async-start | bytes 2752512 | tf_op jit(solution)/shard_map/gather_x/all_to_all | solution.py:31
  81.4 3.0 %collective-permute-start.6 = (bf16[16,7168]{1,0:T(8,128)(2,1)S(1)}, bf16[16,7168]{1,0:T(8,128)(2,1)S(1)}, u32[]{:S(2)}, u32[]{:S(2)}) collective-permute-start(bf16[16,7168]{1,0:T(8,128)(2,1)S(1)} %slice.86), channel_id=1, source_target_pairs={{0,2},{1,7},{2,4},{3,1},{4,6},{5,3},{6,0},{7,5},{8,10},{9,15},{10,... | collective-permute-start | bytes 688136 | tf_op jit(solution)/shard_map/gather_x/ppermute | solution.py:40
  84.4 10.9 %collective-permute-done.6 = bf16[16,7168]{1,0:T(8,128)(2,1)S(1)} collective-permute-done((bf16[16,7168]{1,0:T(8,128)(2,1)S(1)}, bf16[16,7168]{1,0:T(8,128)(2,1)S(1)}, u32[]{:S(2)}, u32[]{:S(2)}) %collective-permute-start.6) | collective-permute-done | bytes 229408 | tf_op jit(solution)/shard_map/gather_x/ppermute | solution.py:40
  95.3 3.3 %convolution_convert_fusion = bf16[192,7168]{1,0:T(8,128)(2,1)} fusion(pred[64,192]{0,1:T(32,128)(4,1)S(1)} %get-tuple-element.43, bf16[16,7168]{1,0:T(8,128)(2,1)S(1)} %collective-permute-done.6, bf16[16,7168]{1,0:T(8,128)(2,1)} %collective-permute-done.5, bf16[16,7168]{1,0:T(8,128)(2,1)S(1)} %slice.86, bf16[16,3584]{1,0:T(8,128)(2,1)S(1)} %bitcast.77, ...), kind=kOutput, calls=%fused_computation | convolution fusion | flops 182124544 | bytes 3682304 | tf_op jit(solution)/shard_map/gather_x/dot_general | solution.py:113
  98.6 4.9 %all-to-all-start.1 = ((bf16[4,48,7168]{2,1,0:T(8,128)(2,1)}), bf16[4,48,7168]{2,1,0:T(8,128)(2,1)}, u32[]{:S(2)}, u32[]{:S(2)}) async-start(bf16[4,48,7168]{2,1,0:T(8,128)(2,1)} %bitcast.72), calls=%async_computation.1 | async-start | bytes 5505024 | tf_op jit(solution)/shard_map/gather_x/all_to_all | solution.py:31
  103.6 0.8 fusion.87
  105.0 0.9 copy-done.3
  107.4 1.7 convolution_convert_fusion.1
  109.0 15.7 %all-to-all-done.1 = bf16[4,48,7168]{2,1,0:T(8,128)(2,1)} async-done(((bf16[4,48,7168]{2,1,0:T(8,128)(2,1)}), bf16[4,48,7168]{2,1,0:T(8,128)(2,1)}, u32[]{:S(2)}, u32[]{:S(2)}) %all-to-all-start.1) | async-done | bytes 2752544 | tf_op jit(solution)/shard_map/gather_x/all_to_all | solution.py:31
  124.8 2.4 %fusion.7 = f32[192,256]{1,0:T(8,128)S(1)} fusion(bf16[3584,256]{1,0:T(8,128)(2,1)} %copy-done.2, bf16[192,7168]{1,0:T(8,128)(2,1)} %bitcast.14), kind=kOutput, calls=%fused_computation.18 | convolution fusion | flops 352321536 | bytes 3407872 | tf_op jit(solution)/shard_map/backward_experts/dot_general | solution.py:105
  127.2 1.9 fusion.9
  129.1 5.1 %all-to-all-start.2 = ((bf16[4,48,3584]{2,1,0:T(8,128)(2,1)}), bf16[4,48,3584]{2,1,0:T(8,128)(2,1)S(1)}, u32[]{:S(2)}, u32[]{:S(2)}) async-start(bf16[4,48,3584]{2,1,0:T(8,128)(2,1)} %bitcast.15), calls=%async_computation.2 | async-start | bytes 2752512 | tf_op jit(solution)/shard_map/forward_experts/all_to_all | solution.py:31
  134.2 2.5 %fusion.5 = f32[192,256]{1,0:T(8,128)S(1)} fusion(bf16[192,7168]{1,0:T(8,128)(2,1)} %bitcast.14, bf16[128,3584]{1,0:T(8,128)(2,1)} %copy-done.16, bf16[128,3584]{1,0:T(8,128)(2,1)S(1)} %bitcast.89), kind=kOutput, calls=%fused_computation.16 | convolution fusion | flops 355991552 | bytes 3407872 | tf_op jit(solution)/shard_map/backward_experts/dot_general | solution.py:109
  136.8 0.8 fusion.42
  138.3 1.9 fusion
  140.2 11.7 %all-to-all-done.2 = bf16[4,48,3584]{2,1,0:T(8,128)(2,1)S(1)} async-done(((bf16[4,48,3584]{2,1,0:T(8,128)(2,1)}), bf16[4,48,3584]{2,1,0:T(8,128)(2,1)S(1)}, u32[]{:S(2)}, u32[]{:S(2)}) %all-to-all-start.2) | async-done | bytes 1376288 | tf_op jit(solution)/shard_map/forward_experts/all_to_all | solution.py:31
  151.9 5.0 %all-to-all-start.3 = ((bf16[4,48,3584]{2,1,0:T(8,128)(2,1)}), bf16[4,48,3584]{2,1,0:T(8,128)(2,1)S(1)}, u32[]{:S(2)}, u32[]{:S(2)}) async-start(bf16[4,48,3584]{2,1,0:T(8,128)(2,1)} %bitcast.71), calls=%async_computation.3 | async-start | bytes 2752512 | tf_op jit(solution)/shard_map/backward_experts/all_to_all | solution.py:31
  158.4 15.4 %collective-permute-start.8 = (bf16[16,3584]{1,0:T(8,128)(2,1)S(1)}, bf16[16,3584]{1,0:T(8,128)(2,1)S(1)}, u32[]{:S(2)}, u32[]{:S(2)}) collective-permute-start(bf16[16,3584]{1,0:T(8,128)(2,1)S(1)} %get-tuple-element.27), channel_id=1, source_target_pairs={{0,38},{1,35},{2,32},{3,37},{4,34},{5,39},{6,36},{7,33},{8,46},{9,... | collective-permute-start | bytes 344072 | tf_op jit(solution)/shard_map/forward_home/ppermute | solution.py:56
  173.9 4.1 %collective-permute-start.10 = (bf16[16,3584]{1,0:T(8,128)(2,1)S(1)}, bf16[16,3584]{1,0:T(8,128)(2,1)S(1)}, u32[]{:S(2)}, u32[]{:S(2)}) collective-permute-start(bf16[16,3584]{1,0:T(8,128)(2,1)S(1)} %get-tuple-element.28), channel_id=1, source_target_pairs={{0,36},{1,37},{2,38},{3,39},{4,32},{5,33},{6,34},{7,35},{8,44},{9,... | collective-permute-start | bytes 344072 | tf_op jit(solution)/shard_map/forward_home/ppermute | solution.py:56
  177.9 8.7 %collective-permute-start.9 = (bf16[16,3584]{1,0:T(8,128)(2,1)S(1)}, bf16[16,3584]{1,0:T(8,128)(2,1)S(1)}, u32[]{:S(2)}, u32[]{:S(2)}) collective-permute-start(bf16[16,3584]{1,0:T(8,128)(2,1)S(1)} %get-tuple-element.29), channel_id=1, source_target_pairs={{0,34},{1,39},{2,36},{3,33},{4,38},{5,35},{6,32},{7,37},{8,42},{9,... | collective-permute-start | bytes 344072 | tf_op jit(solution)/shard_map/forward_home/ppermute | solution.py:56
  186.7 3.9 %collective-permute-start.7 = (f32[16,3584]{1,0:T(8,128)S(1)}, f32[16,3584]{1,0:T(8,128)S(1)}, u32[]{:S(2)}, u32[]{:S(2)}) collective-permute-start(f32[16,3584]{1,0:T(8,128)S(1)} %slice_add_fusion.1), channel_id=1, source_target_pairs={{0,32},{1,33},{2,34},{3,35},{4,36},{5,37},{6,38},{7,39},{8,40},{9,... | collective-permute-start | bytes 688136 | tf_op jit(solution)/shard_map/forward_home/ppermute | solution.py:56
  192.1 1.9 collective-permute-start.12
  194.1 7.7 %collective-permute-start.14 = (bf16[16,3584]{1,0:T(8,128)(2,1)S(1)}, bf16[16,3584]{1,0:T(8,128)(2,1)S(1)}, u32[]{:S(2)}, u32[]{:S(2)}) collective-permute-start(bf16[16,3584]{1,0:T(8,128)(2,1)S(1)} %get-tuple-element.25), channel_id=1, source_target_pairs={{32,4},{33,5},{34,6},{35,7},{36,0},{37,1},{38,2},{39,3},{40,12},{4... | collective-permute-start | bytes 344072 | tf_op jit(solution)/shard_map/backward_home/ppermute | solution.py:56
  201.8 1.2 collective-permute-done.10
  203.0 4.6 %collective-permute-start.13 = (bf16[16,3584]{1,0:T(8,128)(2,1)S(1)}, bf16[16,3584]{1,0:T(8,128)(2,1)S(1)}, u32[]{:S(2)}, u32[]{:S(2)}) collective-permute-start(bf16[16,3584]{1,0:T(8,128)(2,1)S(1)} %get-tuple-element.26), channel_id=1, source_target_pairs={{32,2},{33,7},{34,4},{35,1},{36,6},{37,3},{38,0},{39,5},{40,10},{4... | collective-permute-start | bytes 344072 | tf_op jit(solution)/shard_map/backward_home/ppermute | solution.py:56
  207.6 2.3 %collective-permute-start.11 = (f32[16,3584]{1,0:T(8,128)S(1)}, f32[16,3584]{1,0:T(8,128)S(1)}, u32[]{:S(2)}, u32[]{:S(2)}) collective-permute-start(f32[16,3584]{1,0:T(8,128)S(1)} %slice_add_fusion), channel_id=1, source_target_pairs={{32,0},{33,1},{34,2},{35,3},{36,4},{37,5},{38,6},{39,7},{40,8},{41... | collective-permute-start | bytes 688136 | tf_op jit(solution)/shard_map/backward_home/ppermute | solution.py:56
  210.7 4.6 %collective-permute-done.14 = bf16[16,3584]{1,0:T(8,128)(2,1)S(1)} collective-permute-done((bf16[16,3584]{1,0:T(8,128)(2,1)S(1)}, bf16[16,3584]{1,0:T(8,128)(2,1)S(1)}, u32[]{:S(2)}, u32[]{:S(2)}) %collective-permute-start.14) | collective-permute-done | bytes 114720 | tf_op jit(solution)/shard_map/backward_home/ppermute | solution.py:56
  215.3 8.6 %collective-permute-done.13 = bf16[16,3584]{1,0:T(8,128)(2,1)S(1)} collective-permute-done((bf16[16,3584]{1,0:T(8,128)(2,1)S(1)}, bf16[16,3584]{1,0:T(8,128)(2,1)S(1)}, u32[]{:S(2)}, u32[]{:S(2)}) %collective-permute-start.13) | collective-permute-done | bytes 114720 | tf_op jit(solution)/shard_map/backward_home/ppermute | solution.py:56
  223.9 3.0 %collective-permute-done.11 = f32[16,3584]{1,0:T(8,128)S(1)} collective-permute-done((f32[16,3584]{1,0:T(8,128)S(1)}, f32[16,3584]{1,0:T(8,128)S(1)}, u32[]{:S(2)}, u32[]{:S(2)}) %collective-permute-start.11) | collective-permute-done | bytes 229408 | tf_op jit(solution)/shard_map/backward_home/ppermute | solution.py:56
  (90 shorter events, 12.6 us)
Async XLA Ops:
  0.6 31.0 %collective-permute-start.2 = (bf16[3584,256]{1,0:T(8,128)(2,1)}, bf16[3584,256]{1,0:T(8,128)(2,1)S(1)}, u32[]{:S(2)}, u32[]{:S(2)}) collective-permute-start(bf16[3584,256]{1,0:T(8,128)(2,1)} %bitcast.70), channel_id=1, source_target_pairs={{0,1},{1,0},{2,3},{3,2},{4,5},{5,4},{6,7},{7,6},{8,9},{9,8},{10,11... | collective-permute-start | bytes 5505032 | tf_op jit(solution)/shard_map/gather_z/ppermute | solution.py:44
  2.6 29.1 %collective-permute-start.3 = (bf16[128,3584]{1,0:T(8,128)(2,1)}, bf16[128,3584]{1,0:T(8,128)(2,1)S(1)}, u32[]{:S(2)}, u32[]{:S(2)}) collective-permute-start(bf16[128,3584]{1,0:T(8,128)(2,1)} %bitcast.87), channel_id=1, source_target_pairs={{0,1},{1,0},{2,3},{3,2},{4,5},{5,4},{6,7},{7,6},{8,9},{9,8},{10,11... | collective-permute-start | bytes 2752520 | tf_op jit(solution)/shard_map/gather_z/ppermute | solution.py:44
  8.6 12.8 %collective-permute-start.1 = (bf16[16,3712]{1,0:T(8,128)(2,1)S(1)}, bf16[16,3712]{1,0:T(8,128)(2,1)S(1)}, u32[]{:S(2)}, u32[]{:S(2)}) collective-permute-start(bf16[16,3712]{1,0:T(8,128)(2,1)S(1)} %pad_maximum_fusion.5), channel_id=1, source_target_pairs={{0,6},{1,3},{2,0},{3,5},{4,2},{5,7},{6,4},{7,1},{8,14},{9,11},{10,... | collective-permute-start | bytes 356360 | tf_op jit(solution)/shard_map/gather_z/ppermute | solution.py:40
  18.7 13.0 %collective-permute-start = (bf16[16,3712]{1,0:T(8,128)(2,1)S(1)}, bf16[16,3712]{1,0:T(8,128)(2,1)S(1)}, u32[]{:S(2)}, u32[]{:S(2)}) collective-permute-start(bf16[16,3712]{1,0:T(8,128)(2,1)S(1)} %pad_maximum_fusion.5), channel_id=1, source_target_pairs={{0,2},{1,7},{2,4},{3,1},{4,6},{5,3},{6,0},{7,5},{8,10},{9,15},{10,... | collective-permute-start | bytes 356360 | tf_op jit(solution)/shard_map/gather_z/ppermute | solution.py:40
  21.4 26.7 %copy-start.8 = (bf16[16,3712]{1,0:T(8,128)(2,1)}, bf16[16,3712]{1,0:T(8,128)(2,1)S(1)}, u32[]{:S(2)}) copy-start(bf16[16,3712]{1,0:T(8,128)(2,1)S(1)} %collective-permute-done.1) | copy-start | bytes 356356
  31.6 16.5 %copy-start.5 = (bf16[16,3712]{1,0:T(8,128)(2,1)}, bf16[16,3712]{1,0:T(8,128)(2,1)S(1)}, u32[]{:S(2)}) copy-start(bf16[16,3712]{1,0:T(8,128)(2,1)S(1)} %collective-permute-done) | copy-start | bytes 356356
  31.6 1.0 copy-start.16
  31.6 16.5 %copy-start.2 = (bf16[3584,256]{1,0:T(8,128)(2,1)}, bf16[3584,256]{1,0:T(8,128)(2,1)S(1)}, u32[]{:S(2)}) copy-start(bf16[3584,256]{1,0:T(8,128)(2,1)S(1)} %collective-permute-done.2) | copy-start | bytes 5505028
  34.3 34.3 %collective-permute-start.4 = (bf16[16,10880]{1,0:T(8,128)(2,1)}, bf16[16,10880]{1,0:T(8,128)(2,1)S(1)}, u32[]{:S(2)}, u32[]{:S(2)}) collective-permute-start(bf16[16,10880]{1,0:T(8,128)(2,1)} %pad_maximum_fusion.3), channel_id=1, source_target_pairs={{0,2},{1,7},{2,4},{3,1},{4,6},{5,3},{6,0},{7,5},{8,10},{9,15},{10,... | collective-permute-start | bytes 1044488 | tf_op jit(solution)/shard_map/gather_z/ppermute | solution.py:40
  39.6 29.0 %collective-permute-start.5 = (bf16[16,7168]{1,0:T(8,128)(2,1)}, bf16[16,7168]{1,0:T(8,128)(2,1)}, u32[]{:S(2)}, u32[]{:S(2)}) collective-permute-start(bf16[16,7168]{1,0:T(8,128)(2,1)} %pad_maximum_fusion.4), channel_id=1, source_target_pairs={{0,6},{1,3},{2,0},{3,5},{4,2},{5,7},{6,4},{7,1},{8,14},{9,11},{10,... | collective-permute-start | bytes 688136 | tf_op jit(solution)/shard_map/gather_z/ppermute | solution.py:40
  45.8 27.3 %copy-start.12 = (s32[64]{0:T(128)}, s32[64]{0:T(128)S(1)}, u32[]{:S(2)}) copy-start(s32[64]{0:T(128)S(1)} %and_select_fusion.3) | copy-start | bytes 772
  48.2 25.7 %slice-start = ((bf16[16,3712]{1,0:T(8,128)(2,1)}), bf16[16,3584]{1,0:T(8,128)(2,1)S(1)}, s32[]{:S(2)}) async-start(bf16[16,3712]{1,0:T(8,128)(2,1)} %copy-done.5), calls=%async_computation.4 | async-start | bytes 229376 | tf_op jit(solution)/shard_map/gather_x/slice | solution.py:197
  48.2 25.7 %copy-start.6 = (bf16[1,16,3584]{2,1,0:T(8,128)(2,1)S(1)}, bf16[1,16,3584]{2,1,0:T(8,128)(2,1)}, u32[]{:S(2)}) copy-start(bf16[1,16,3584]{2,1,0:T(8,128)(2,1)} %param.9) | copy-start | bytes 344068
  48.2 25.7 %slice-start.1 = ((bf16[16,3712]{1,0:T(8,128)(2,1)}), bf16[16,3584]{1,0:T(8,128)(2,1)S(1)}, s32[]{:S(2)}) async-start(bf16[16,3712]{1,0:T(8,128)(2,1)} %copy-done.8), calls=%async_computation.5 | async-start | bytes 229376 | tf_op jit(solution)/shard_map/gather_x/slice | solution.py:197
  71.6 0.6 copy-start.11
  76.4 18.9 %copy-start.7 = (bf16[1,16,3584]{2,1,0:T(8,128)(2,1)S(1)}, bf16[1,16,3584]{2,1,0:T(8,128)(2,1)}, u32[]{:S(2)}) copy-start(bf16[1,16,3584]{2,1,0:T(8,128)(2,1)} %param.11) | copy-start | bytes 344068
  76.4 18.9 %copy-start.9 = (bf16[1,16,3584]{2,1,0:T(8,128)(2,1)S(1)}, bf16[1,16,3584]{2,1,0:T(8,128)(2,1)}, u32[]{:S(2)}) copy-start(bf16[1,16,3584]{2,1,0:T(8,128)(2,1)} %param.10) | copy-start | bytes 344068
  76.4 18.9 %all-to-all-start = ((bf16[4,48,3584]{2,1,0:T(8,128)(2,1)}), bf16[4,48,3584]{2,1,0:T(8,128)(2,1)S(1)}, u32[]{:S(2)}, u32[]{:S(2)}) async-start(bf16[4,48,3584]{2,1,0:T(8,128)(2,1)} %bitcast.10), calls=%async_computation | async-start | bytes 2752512 | tf_op jit(solution)/shard_map/gather_x/all_to_all | solution.py:31
  81.4 13.9 %collective-permute-start.6 = (bf16[16,7168]{1,0:T(8,128)(2,1)S(1)}, bf16[16,7168]{1,0:T(8,128)(2,1)S(1)}, u32[]{:S(2)}, u32[]{:S(2)}) collective-permute-start(bf16[16,7168]{1,0:T(8,128)(2,1)S(1)} %slice.86), channel_id=1, source_target_pairs={{0,2},{1,7},{2,4},{3,1},{4,6},{5,3},{6,0},{7,5},{8,10},{9,15},{10,... | collective-permute-start | bytes 688136 | tf_op jit(solution)/shard_map/gather_x/ppermute | solution.py:40
  98.6 5.0 %copy-start.10 = (bf16[16,128]{0,1:T(8,128)(2,1)S(1)}, bf16[16,128]{0,1:T(8,128)(2,1)}, u32[]{:S(2)}) copy-start(bf16[16,128]{0,1:T(8,128)(2,1)} %slice.100) | copy-start | bytes 12292
  98.6 5.8 %copy-start = (bf16[1,3584,256]{2,1,0:T(8,128)(2,1)S(1)}, bf16[1,3584,256]{2,1,0:T(8,128)(2,1)}, u32[]{:S(2)}) copy-start(bf16[1,3584,256]{2,1,0:T(8,128)(2,1)} %param.12) | copy-start | bytes 5505028
  98.6 26.1 %all-to-all-start.1 = ((bf16[4,48,7168]{2,1,0:T(8,128)(2,1)}), bf16[4,48,7168]{2,1,0:T(8,128)(2,1)}, u32[]{:S(2)}, u32[]{:S(2)}) async-start(bf16[4,48,7168]{2,1,0:T(8,128)(2,1)} %bitcast.72), calls=%async_computation.1 | async-start | bytes 5505024 | tf_op jit(solution)/shard_map/gather_x/all_to_all | solution.py:31
  104.4 1.5 copy-start.3
  105.9 1.2 copy-start.14
  105.9 1.5 copy-start.17
  129.1 5.1 %copy-start.15 = (bf16[1,128,3584]{2,1,0:T(8,128)(2,1)S(1)}, bf16[1,128,3584]{2,1,0:T(8,128)(2,1)}, u32[]{:S(2)}) copy-start(bf16[1,128,3584]{2,1,0:T(8,128)(2,1)} %param.13) | copy-start | bytes 2752516
  129.1 22.8 %all-to-all-start.2 = ((bf16[4,48,3584]{2,1,0:T(8,128)(2,1)}), bf16[4,48,3584]{2,1,0:T(8,128)(2,1)S(1)}, u32[]{:S(2)}, u32[]{:S(2)}) async-start(bf16[4,48,3584]{2,1,0:T(8,128)(2,1)} %bitcast.15), calls=%async_computation.2 | async-start | bytes 2752512 | tf_op jit(solution)/shard_map/forward_experts/all_to_all | solution.py:31
  134.2 2.6 %copy-start.1 = (bf16[1,3584,256]{2,1,0:T(8,128)(2,1)S(1)}, bf16[1,3584,256]{2,1,0:T(8,128)(2,1)}, u32[]{:S(2)}) copy-start(bf16[1,3584,256]{2,1,0:T(8,128)(2,1)} %param.12) | copy-start | bytes 5505028
  136.8 1.5 copy-start.4
  140.2 16.7 %copy-start.13 = (s32[64]{0:T(128)S(1)}, s32[64]{0:T(128)}, u32[]{:S(2)}) copy-start(s32[64]{0:T(128)} %copy-done.12) | copy-start | bytes 772
  151.9 38.7 %all-to-all-start.3 = ((bf16[4,48,3584]{2,1,0:T(8,128)(2,1)}), bf16[4,48,3584]{2,1,0:T(8,128)(2,1)S(1)}, u32[]{:S(2)}, u32[]{:S(2)}) async-start(bf16[4,48,3584]{2,1,0:T(8,128)(2,1)} %bitcast.71), calls=%async_computation.3 | async-start | bytes 2752512 | tf_op jit(solution)/shard_map/backward_experts/all_to_all | solution.py:31
  158.4 35.7 %collective-permute-start.8 = (bf16[16,3584]{1,0:T(8,128)(2,1)S(1)}, bf16[16,3584]{1,0:T(8,128)(2,1)S(1)}, u32[]{:S(2)}, u32[]{:S(2)}) collective-permute-start(bf16[16,3584]{1,0:T(8,128)(2,1)S(1)} %get-tuple-element.27), channel_id=1, source_target_pairs={{0,38},{1,35},{2,32},{3,37},{4,34},{5,39},{6,36},{7,33},{8,46},{9,... | collective-permute-start | bytes 344072 | tf_op jit(solution)/shard_map/forward_home/ppermute | solution.py:56
  173.9 29.1 %collective-permute-start.10 = (bf16[16,3584]{1,0:T(8,128)(2,1)S(1)}, bf16[16,3584]{1,0:T(8,128)(2,1)S(1)}, u32[]{:S(2)}, u32[]{:S(2)}) collective-permute-start(bf16[16,3584]{1,0:T(8,128)(2,1)S(1)} %get-tuple-element.28), channel_id=1, source_target_pairs={{0,36},{1,37},{2,38},{3,39},{4,32},{5,33},{6,34},{7,35},{8,44},{9,... | collective-permute-start | bytes 344072 | tf_op jit(solution)/shard_map/forward_home/ppermute | solution.py:56
  177.9 29.7 %collective-permute-start.9 = (bf16[16,3584]{1,0:T(8,128)(2,1)S(1)}, bf16[16,3584]{1,0:T(8,128)(2,1)S(1)}, u32[]{:S(2)}, u32[]{:S(2)}) collective-permute-start(bf16[16,3584]{1,0:T(8,128)(2,1)S(1)} %get-tuple-element.29), channel_id=1, source_target_pairs={{0,34},{1,39},{2,36},{3,33},{4,38},{5,35},{6,32},{7,37},{8,42},{9,... | collective-permute-start | bytes 344072 | tf_op jit(solution)/shard_map/forward_home/ppermute | solution.py:56
  186.7 23.3 %collective-permute-start.7 = (f32[16,3584]{1,0:T(8,128)S(1)}, f32[16,3584]{1,0:T(8,128)S(1)}, u32[]{:S(2)}, u32[]{:S(2)}) collective-permute-start(f32[16,3584]{1,0:T(8,128)S(1)} %slice_add_fusion.1), channel_id=1, source_target_pairs={{0,32},{1,33},{2,34},{3,35},{4,36},{5,37},{6,38},{7,39},{8,40},{9,... | collective-permute-start | bytes 688136 | tf_op jit(solution)/shard_map/forward_home/ppermute | solution.py:56
  192.1 18.5 %collective-permute-start.12 = (bf16[16,3584]{1,0:T(8,128)(2,1)S(1)}, bf16[16,3584]{1,0:T(8,128)(2,1)S(1)}, u32[]{:S(2)}, u32[]{:S(2)}) collective-permute-start(bf16[16,3584]{1,0:T(8,128)(2,1)S(1)} %get-tuple-element.24), channel_id=1, source_target_pairs={{32,6},{33,3},{34,0},{35,5},{36,2},{37,7},{38,4},{39,1},{40,14},{4... | collective-permute-start | bytes 344072 | tf_op jit(solution)/shard_map/backward_home/ppermute | solution.py:56
  194.1 21.2 %collective-permute-start.14 = (bf16[16,3584]{1,0:T(8,128)(2,1)S(1)}, bf16[16,3584]{1,0:T(8,128)(2,1)S(1)}, u32[]{:S(2)}, u32[]{:S(2)}) collective-permute-start(bf16[16,3584]{1,0:T(8,128)(2,1)S(1)} %get-tuple-element.25), channel_id=1, source_target_pairs={{32,4},{33,5},{34,6},{35,7},{36,0},{37,1},{38,2},{39,3},{40,12},{4... | collective-permute-start | bytes 344072 | tf_op jit(solution)/shard_map/backward_home/ppermute | solution.py:56
  203.0 20.9 %collective-permute-start.13 = (bf16[16,3584]{1,0:T(8,128)(2,1)S(1)}, bf16[16,3584]{1,0:T(8,128)(2,1)S(1)}, u32[]{:S(2)}, u32[]{:S(2)}) collective-permute-start(bf16[16,3584]{1,0:T(8,128)(2,1)S(1)} %get-tuple-element.26), channel_id=1, source_target_pairs={{32,2},{33,7},{34,4},{35,1},{36,6},{37,3},{38,0},{39,5},{40,10},{4... | collective-permute-start | bytes 344072 | tf_op jit(solution)/shard_map/backward_home/ppermute | solution.py:56
  207.6 19.3 %collective-permute-start.11 = (f32[16,3584]{1,0:T(8,128)S(1)}, f32[16,3584]{1,0:T(8,128)S(1)}, u32[]{:S(2)}, u32[]{:S(2)}) collective-permute-start(f32[16,3584]{1,0:T(8,128)S(1)} %slice_add_fusion), channel_id=1, source_target_pairs={{32,0},{33,1},{34,2},{35,3},{36,4},{37,5},{38,6},{39,7},{40,8},{41... | collective-permute-start | bytes 688136 | tf_op jit(solution)/shard_map/backward_home/ppermute | solution.py:56

commit v4 on v3

--- a/solution.py
+++ b/solution.py
@@ -9,6 +9,7 @@
 LANES = 128
 CAP = 12
 OWNERS = (0, -1, 1, -2)
+REACH = (1, -1, 2)
 
 
 def expert_index(x, z, core):
@@ -24,19 +25,17 @@
     ]
 
 
-def across_x(blocks):
-    groups = [
-        [expert_index(x, z, c) for x in range(EXPERTS)] for z in range(Z) for c in range(CORES)
-    ]
-    return lax.all_to_all(blocks, "expert", 0, 0, axis_index_groups=groups, tiled=True)
-
-
 def turn(core):
     return 1 - 2 * core
 
 
 def along_z(block, distance):
     route = expert_route(lambda x, z, c: (x, (z + distance * turn(c)) % Z, c))
+    return lax.ppermute(block, "expert", route)
+
+
+def along_x(block, distance):
+    route = expert_route(lambda x, z, c: ((x + distance * turn(c)) % EXPERTS, z, c))
     return lax.ppermute(block, "expert", route)
 
 
@@ -93,12 +92,18 @@
     return first + second + third, slots
 
 
-def placement(slots, rows):
-    place = jnp.arange(EXPERTS * Z * CAP, dtype=jnp.int32)
+def column_of(table, index):
+    hot = jnp.arange(table.shape[1], dtype=jnp.int32) == index
+    return jnp.sum(jnp.where(hot[None, :], table, 0.0), axis=1, keepdims=True)
+
+
+def placement(slots, expert, rows):
+    slot = column_of(slots, expert)
     block = jnp.arange(slots.shape[0], dtype=jnp.int32) // rows
-    expert, source, slot = place // (Z * CAP), place // CAP % Z, place % CAP
-    wanted = jnp.repeat(slots, Z * CAP, axis=1)
-    return (block[:, None] == source[None, :]) & (wanted == slot.astype(jnp.float32)[None, :])
+    place = jnp.arange(Z * CAP, dtype=jnp.int32)
+    wanted = (place % CAP).astype(jnp.float32)
+    found = (block[:, None] == place[None, :] // CAP) & (slot == wanted[None, :])
+    return found.astype(jnp.bfloat16)
 
 
 def dot(a, b):
@@ -111,7 +116,7 @@
 
 def pack(places, block):
     packed = lax.dot_general(
-        places.astype(jnp.bfloat16),
+        places,
         block,
         (((0,), (0,)), ((), ())),
         preferred_element_type=jnp.float32,
@@ -125,7 +130,7 @@
         both = dot(rows, gate_up)
         gate_val, up_val = jnp.split(both, 2, axis=1)
         hidden.append((jax.nn.silu(gate_val) * up_val).astype(jnp.bfloat16))
-    return dot(jnp.concatenate(hidden, axis=1), down).astype(jnp.bfloat16)
+    return dot(jnp.concatenate(hidden, axis=1), down)
 
 
 def backward_rows(rows, grads, gate_ups, down):
@@ -140,12 +145,14 @@
         grad = jnp.concatenate([gate_grad, up_grad], axis=1).astype(jnp.bfloat16)
         term = dot_t(grad, gate_up)
         total = term if total is None else total + term
-    return total.astype(jnp.bfloat16)
-
-
-def gated_sum(parts, places, shares):
-    weights = jnp.where(places, jnp.repeat(shares, Z * CAP, axis=1), 0.0)
-    return sum(dot(weight, parts) for weight in three_parts(weights))
+    return total
+
+
+def gated_sum(own, parts, places, shares, experts):
+    total = column_of(shares, experts[0]) * own
+    for part, place, expert in zip(parts, places, experts[1:]):
+        total = total + column_of(shares, expert) * dot(place, part)
+    return total
 
 
 def send_home(mixture, residual, step):
@@ -174,7 +181,12 @@
 ):
     tokens, saved, upstream = forward_input[0], backward_input[0], backward_grad[0]
     rows, model = tokens.shape
+    core = lax.axis_index("expert") % CORES
+    me = lax.axis_index("expert") // (Z * CORES)
+    experts = [(me + EXPERTS + d * (1 - 2 * core)) % EXPERTS for d in (0,) + REACH]
+
     with jax.named_scope("gather_z"):
+        near, far = along_z(tokens, 1), along_z(tokens, -1)
         hots = [expert_hot(forward_routes[0]), expert_hot(backward_routes[0])]
         shares = [
             expert_shares(hots[0], forward_gates[0]),
@@ -182,38 +194,46 @@
         ]
         slots = [expert_slots(hot) for hot in hots]
         side = side_columns(jnp.concatenate(shares, axis=1), jnp.concatenate(slots, axis=1))
-        mine = jnp.concatenate([tokens, side], axis=1)
-        near, far = along_z(mine, 1), along_z(mine, -1)
-        gate_up, down = gate_up_weight[0], down_weight[0]
-        gate_up_2, down_2 = other_core(gate_up), other_core(down)
-        near, far, gate_up_2, down_2 = together(near, far, gate_up_2, down_2)
+        sides = [side] + [along_z(side, d) for d in (1, -1, 2)]
+        near, far, *sides = together(near, far, *sides)
+        shares, slots = side_values(jnp.concatenate(sides, axis=0))
+        places = [placement(slots[:, :EXPERTS], e, rows) for e in experts[1:]]
+        back_places = [placement(slots[:, EXPERTS:], e, rows) for e in experts[1:]]
         back_mine = jnp.concatenate([saved, upstream], axis=1)
         both = along_z(jnp.concatenate([near, back_mine], axis=1), 1)
-        both, back_far = together(both, along_z(back_mine, -1))
-        opposite, back_near = both[:, : mine.shape[1]], both[:, mine.shape[1] :]
-        parts = [mine, near, far, opposite]
+        back_far = along_z(back_mine, -1)
+    with jax.named_scope("swap_weights"):
+        gate_up, down, near = together(gate_up_weight[0], down_weight[0], near)
+        gate_up_2, down_2 = other_core(gate_up), other_core(down)
+        both, back_far, gate_up_2, down_2 = together(both, back_far, gate_up_2, down_2)
         gate_ups, down = [gate_up, gate_up_2], jnp.concatenate([down, down_2], axis=0)
-    with jax.named_scope("gather_x"):
-        block = jnp.concatenate([part[:, :model] for part in parts], axis=0)
-        shares, slots = side_values(jnp.concatenate([part[:, model:] for part in parts], axis=0))
-        places = placement(slots[:, :EXPERTS], rows)
-        back_places = placement(slots[:, EXPERTS:], rows)
-        token_rows = across_x(pack(places, block))
-        token_rows, back_opposite = together(token_rows, along_z(back_near, 1))
+    with jax.named_scope("gather_x_forward"):
+        opposite, back_near = both[:, :model], both[:, model:]
+        block = jnp.concatenate([tokens, near, far, opposite], axis=0)
+        parts = [along_x(pack(place, block), d) for place, d in zip(places, REACH)]
+        *parts, back_opposite = together(*parts, along_z(back_near, 1))
+    with jax.named_scope("gather_x_backward"):
         back_block = jnp.concatenate([back_mine, back_near, back_far, back_opposite], axis=0)
-        back_rows = across_x(pack(back_places, back_block))
+        back_parts = [pack(place, back_block) for place in back_places]
+        *parts, back_1, back_2, back_3 = together(*parts, *back_parts)
+        back_parts = [along_x(part, d) for part, d in zip((back_1, back_2, back_3), REACH)]
     with jax.named_scope("forward_experts"):
-        outs = forward_rows(token_rows, gate_ups, down)
-        outs, back_rows = together(outs, back_rows)
-        outs = across_x(outs)
+        own = forward_rows(block, gate_ups, down)
+        outs = [forward_rows(part, gate_ups, down).astype(jnp.bfloat16) for part in parts]
+        *outs, back_parts[0] = together(*outs, back_parts[0])
+        outs = [along_x(out, -d) for out, d in zip(outs, REACH)]
     with jax.named_scope("backward_experts"):
-        back_outs = backward_rows(back_rows[:, :model], back_rows[:, model:], gate_ups, down)
-        back_outs = across_x(back_outs)
+        back_own = backward_rows(back_block[:, :model], back_block[:, model:], gate_ups, down)
+        back_outs = [
+            backward_rows(part[:, :model], part[:, model:], gate_ups, down).astype(jnp.bfloat16)
+            for part in back_parts
+        ]
+        back_outs = [along_x(out, -d) for out, d in zip(back_outs, REACH)]
     with jax.named_scope("forward_home"):
-        mixture = gated_sum(outs, places, shares[:, :EXPERTS])
+        mixture = gated_sum(own, outs, places, shares[:, :EXPERTS], experts)
         forward_next = send_home(mixture, tokens, 1)
     with jax.named_scope("backward_home"):
-        mixture = gated_sum(back_outs, back_places, shares[:, EXPERTS:])
+        mixture = gated_sum(back_own, back_outs, back_places, shares[:, EXPERTS:], experts)
         backward_next = send_home(mixture, upstream, -1)
     return (forward_next[None], backward_next[None])
 

time: 229 us -> 223 us (0.974)
  the two profiles are of different devices: /device:TPU:98 before, /device:TPU:24 now
where the time goes in v4:
time: 223 us; the launch traced here: 219 us
  starting transfers between devices  151 us (68%)
  waiting for transfers between devices  38.8 us (17%)
  matrix products  20.9 us (9%)
  other arithmetic  6.39 us (3%)
    ppermute x8, starting transfers between devices, to_section(): return lax.ppermute(block, ('pipe', 'expert'), route)  51.6 us
    ppermute x8, starting transfers between devices, along_z(): return lax.ppermute(block, 'expert', route)  50.5 us
    ppermute x12, starting transfers between devices, along_x(): return lax.ppermute(block, 'expert', route)  44.6 us
    ppermute x12, waiting for transfers between devices, along_x(): return lax.ppermute(block, 'expert', route)  18 us
    ppermute x8, waiting for transfers between devices, along_z(): return lax.ppermute(block, 'expert', route)  12.4 us
    dot_general x26, matrix products, dot(): return jnp.dot(a, b, preferred_element_type=jnp.float32)  10.6 us
    ppermute x8, waiting for transfers between devices, to_section(): return lax.ppermute(block, ('pipe', 'expert'), route)  8.44 us
    dot_general x12, matrix products, dot_t(): lax.dot_general(a, b, (((1,), (1,)), ((), ())), preferred_element_type=jn...  7.84 us
  transfers between devices with their start and end apart: 30, of which 8 were waited for; matrix products, arithmetic and copies ran while one was open for 8% of the time, Pallas kernels for 0%

profile of v4, /device:TPU:24, one launch (start us, length us, event | category | flops | bytes accessed | tf_op | source)
XLA Modules:
  0.0 219.4 jit_solution(9820666655875235477)
XLA Ops:
  0.6 0.8 fusion.159
  1.4 0.7 fusion.158
  2.5 0.7 select_reduce_fusion
  3.4 15.7 %collective-permute-start.4 = (bf16[16,128]{0,1:T(8,128)(2,1)S(1)}, bf16[16,128]{0,1:T(8,128)(2,1)S(1)}, u32[]{:S(2)}, u32[]{:S(2)}) collective-permute-start(bf16[16,128]{0,1:T(8,128)(2,1)S(1)} %pad.4), channel_id=1, source_target_pairs={{0,4},{1,5},{2,6},{3,7},{4,0},{5,1},{6,2},{7,3},{8,12},{9,13},{10,... | collective-permute-start | bytes 12296 | tf_op jit(solution)/shard_map/gather_z/ppermute | solution.py:34
  19.1 1.9 collective-permute-start.3
  21.0 7.8 %collective-permute-start.2 = (bf16[16,128]{0,1:T(8,128)(2,1)S(1)}, bf16[16,128]{0,1:T(8,128)(2,1)S(1)}, u32[]{:S(2)}, u32[]{:S(2)}) collective-permute-start(bf16[16,128]{0,1:T(8,128)(2,1)S(1)} %pad.4), channel_id=1, source_target_pairs={{0,2},{1,7},{2,4},{3,1},{4,6},{5,3},{6,0},{7,5},{8,10},{9,15},{10,... | collective-permute-start | bytes 12296 | tf_op jit(solution)/shard_map/gather_z/ppermute | solution.py:34
  28.9 1.9 collective-permute-start.1
  30.8 7.8 %collective-permute-start = (bf16[16,3584]{1,0:T(8,128)(2,1)}, bf16[16,3584]{1,0:T(8,128)(2,1)S(1)}, u32[]{:S(2)}, u32[]{:S(2)}) collective-permute-start(bf16[16,3584]{1,0:T(8,128)(2,1)} %bitcast.84), channel_id=1, source_target_pairs={{0,2},{1,7},{2,4},{3,1},{4,6},{5,3},{6,0},{7,5},{8,10},{9,15},{10,... | collective-permute-start | bytes 344072 | tf_op jit(solution)/shard_map/gather_z/ppermute | solution.py:34
  38.8 1.0 pad_maximum_fusion.3
  39.8 2.1 collective-permute-start.6
  41.9 5.9 %collective-permute-done.1 = bf16[16,3584]{1,0:T(8,128)(2,1)S(1)} collective-permute-done((bf16[16,3584]{1,0:T(8,128)(2,1)}, bf16[16,3584]{1,0:T(8,128)(2,1)S(1)}, u32[]{:S(2)}, u32[]{:S(2)}) %collective-permute-start.1) | collective-permute-done | bytes 114720 | tf_op jit(solution)/shard_map/gather_z/ppermute | solution.py:34
  47.8 2.3 %collective-permute-start.7 = (bf16[3584,256]{1,0:T(8,128)(2,1)}, bf16[3584,256]{1,0:T(8,128)(2,1)S(1)}, u32[]{:S(2)}, u32[]{:S(2)}) collective-permute-start(bf16[3584,256]{1,0:T(8,128)(2,1)} %bitcast.62), channel_id=1, source_target_pairs={{0,1},{1,0},{2,3},{3,2},{4,5},{5,4},{6,7},{7,6},{8,9},{9,8},{10,11... | collective-permute-start | bytes 5505032 | tf_op jit(solution)/shard_map/swap_weights/ppermute | solution.py:43
  50.1 1.0 pad_maximum_fusion.2
  51.1 7.4 %collective-permute-start.5 = (bf16[16,10752]{1,0:T(8,128)(2,1)S(1)}, bf16[16,10752]{1,0:T(8,128)(2,1)S(1)}, u32[]{:S(2)}, u32[]{:S(2)}) collective-permute-start(bf16[16,10752]{1,0:T(8,128)(2,1)S(1)} %pad_maximum_fusion.2), channel_id=1, source_target_pairs={{0,2},{1,7},{2,4},{3,1},{4,6},{5,3},{6,0},{7,5},{8,10},{9,15},{10,... | collective-permute-start | bytes 1032200 | tf_op jit(solution)/shard_map/gather_z/ppermute | solution.py:34
  58.5 1.9 collective-permute-start.8
  60.8 6.5 %collective-permute-done.5 = bf16[16,10752]{1,0:T(8,128)(2,1)S(1)} collective-permute-done((bf16[16,10752]{1,0:T(8,128)(2,1)S(1)}, bf16[16,10752]{1,0:T(8,128)(2,1)S(1)}, u32[]{:S(2)}, u32[]{:S(2)}) %collective-permute-start.5) | collective-permute-done | bytes 344096 | tf_op jit(solution)/shard_map/gather_z/ppermute | solution.py:34
  68.3 5.9 %collective-permute-start.12 = (bf16[16,7168]{1,0:T(8,128)(2,1)S(1)}, bf16[16,7168]{1,0:T(8,128)(2,1)S(1)}, u32[]{:S(2)}, u32[]{:S(2)}) collective-permute-start(bf16[16,7168]{1,0:T(8,128)(2,1)S(1)} %slice.85), channel_id=1, source_target_pairs={{0,2},{1,7},{2,4},{3,1},{4,6},{5,3},{6,0},{7,5},{8,10},{9,15},{10,... | collective-permute-start | bytes 688136 | tf_op jit(solution)/shard_map/gather_x_forward/ppermute | solution.py:34
  75.2 4.9 %collective-permute-start.11 = (bf16[48,3584]{1,0:T(8,128)(2,1)S(1)}, bf16[48,3584]{1,0:T(8,128)(2,1)S(1)}, u32[]{:S(2)}, u32[]{:S(2)}) collective-permute-start(bf16[48,3584]{1,0:T(8,128)(2,1)S(1)} %convolution_convert_fusion.6), channel_id=1, source_target_pairs={{0,16},{1,17},{2,18},{3,19},{4,20},{5,21},{6,22},{7,23},{8,24},{9,... | collective-permute-start | bytes 1032200 | tf_op jit(solution)/shard_map/gather_x_forward/ppermute | solution.py:39
  80.2 3.0 %collective-permute-start.10 = (bf16[48,3584]{1,0:T(8,128)(2,1)S(1)}, bf16[48,3584]{1,0:T(8,128)(2,1)S(1)}, u32[]{:S(2)}, u32[]{:S(2)}) collective-permute-start(bf16[48,3584]{1,0:T(8,128)(2,1)S(1)} %convolution_convert_fusion.7), channel_id=1, source_target_pairs={{0,24},{1,9},{2,26},{3,11},{4,28},{5,13},{6,30},{7,15},{8,0},{9,17... | collective-permute-start | bytes 1032200 | tf_op jit(solution)/shard_map/gather_x_forward/ppermute | solution.py:39
  83.2 2.8 %collective-permute-start.9 = (bf16[48,3584]{1,0:T(8,128)(2,1)S(1)}, bf16[48,3584]{1,0:T(8,128)(2,1)S(1)}, u32[]{:S(2)}, u32[]{:S(2)}) collective-permute-start(bf16[48,3584]{1,0:T(8,128)(2,1)S(1)} %convolution_convert_fusion.8), channel_id=1, source_target_pairs={{0,8},{1,25},{2,10},{3,27},{4,12},{5,29},{6,14},{7,31},{8,16},{9,1... | collective-permute-start | bytes 1032200 | tf_op jit(solution)/shard_map/gather_x_forward/ppermute | solution.py:39
  86.2 1.4 collective-permute-done.11
  87.6 7.5 %collective-permute-done.10 = bf16[48,3584]{1,0:T(8,128)(2,1)S(1)} collective-permute-done((bf16[48,3584]{1,0:T(8,128)(2,1)S(1)}, bf16[48,3584]{1,0:T(8,128)(2,1)S(1)}, u32[]{:S(2)}, u32[]{:S(2)}) %collective-permute-start.10) | collective-permute-done | bytes 344096 | tf_op jit(solution)/shard_map/gather_x_forward/ppermute | solution.py:39
  95.1 1.9 collective-permute-done.9
  101.9 0.7 fusion.10
  102.7 2.9 %collective-permute-start.13 = (bf16[48,7168]{1,0:T(8,128)(2,1)S(1)}, bf16[48,7168]{1,0:T(8,128)(2,1)S(1)}, u32[]{:S(2)}, u32[]{:S(2)}) collective-permute-start(bf16[48,7168]{1,0:T(8,128)(2,1)S(1)} %convolution_convert_fusion.2), channel_id=1, source_target_pairs={{0,8},{1,25},{2,10},{3,27},{4,12},{5,29},{6,14},{7,31},{8,16},{9,1... | collective-permute-start | bytes 2064392 | tf_op jit(solution)/shard_map/gather_x_backward/ppermute | solution.py:39
  105.6 4.2 %collective-permute-start.22 = (bf16[48,7168]{1,0:T(8,128)(2,1)S(1)}, bf16[48,7168]{1,0:T(8,128)(2,1)S(1)}, u32[]{:S(2)}, u32[]{:S(2)}) collective-permute-start(bf16[48,7168]{1,0:T(8,128)(2,1)S(1)} %convolution_convert_fusion.1), channel_id=1, source_target_pairs={{0,24},{1,9},{2,26},{3,11},{4,28},{5,13},{6,30},{7,15},{8,0},{9,17... | collective-permute-start | bytes 2064392 | tf_op jit(solution)/shard_map/gather_x_backward/ppermute | solution.py:39
  109.8 3.6 %collective-permute-start.24 = (bf16[48,7168]{1,0:T(8,128)(2,1)S(1)}, bf16[48,7168]{1,0:T(8,128)(2,1)S(1)}, u32[]{:S(2)}, u32[]{:S(2)}) collective-permute-start(bf16[48,7168]{1,0:T(8,128)(2,1)S(1)} %convolution_convert_fusion), channel_id=1, source_target_pairs={{0,16},{1,17},{2,18},{3,19},{4,20},{5,21},{6,22},{7,23},{8,24},{9,... | collective-permute-start | bytes 2064392 | tf_op jit(solution)/shard_map/gather_x_backward/ppermute | solution.py:39
  114.8 0.7 fusion.47
  115.5 5.4 %collective-permute-done.13 = bf16[48,7168]{1,0:T(8,128)(2,1)S(1)} collective-permute-done((bf16[48,7168]{1,0:T(8,128)(2,1)S(1)}, bf16[48,7168]{1,0:T(8,128)(2,1)S(1)}, u32[]{:S(2)}, u32[]{:S(2)}) %collective-permute-start.13) | collective-permute-done | bytes 688160 | tf_op jit(solution)/shard_map/gather_x_backward/ppermute | solution.py:39
  122.5 2.6 %collective-permute-start.14 = (bf16[48,3584]{1,0:T(8,128)(2,1)S(1)}, bf16[48,3584]{1,0:T(8,128)(2,1)S(1)}, u32[]{:S(2)}, u32[]{:S(2)}) collective-permute-start(bf16[48,3584]{1,0:T(8,128)(2,1)S(1)} %convolution_convert_fusion.5), channel_id=1, source_target_pairs={{0,24},{1,9},{2,26},{3,11},{4,28},{5,13},{6,30},{7,15},{8,0},{9,17... | collective-permute-start | bytes 1032200 | tf_op jit(solution)/shard_map/forward_experts/ppermute | solution.py:39
  125.1 3.9 %collective-permute-start.15 = (bf16[48,3584]{1,0:T(8,128)(2,1)S(1)}, bf16[48,3584]{1,0:T(8,128)(2,1)S(1)}, u32[]{:S(2)}, u32[]{:S(2)}) collective-permute-start(bf16[48,3584]{1,0:T(8,128)(2,1)S(1)} %convolution_convert_fusion.4), channel_id=1, source_target_pairs={{0,8},{1,25},{2,10},{3,27},{4,12},{5,29},{6,14},{7,31},{8,16},{9,1... | collective-permute-start | bytes 1032200 | tf_op jit(solution)/shard_map/forward_experts/ppermute | solution.py:39
  129.0 6.9 %collective-permute-start.16 = (bf16[48,3584]{1,0:T(8,128)(2,1)S(1)}, bf16[48,3584]{1,0:T(8,128)(2,1)S(1)}, u32[]{:S(2)}, u32[]{:S(2)}) collective-permute-start(bf16[48,3584]{1,0:T(8,128)(2,1)S(1)} %convolution_convert_fusion.3), channel_id=1, source_target_pairs={{0,16},{1,17},{2,18},{3,19},{4,20},{5,21},{6,22},{7,23},{8,24},{9,... | collective-permute-start | bytes 1032200 | tf_op jit(solution)/shard_map/forward_experts/ppermute | solution.py:39
  137.3 3.5 %collective-permute-start.21 = (bf16[48,3584]{1,0:T(8,128)(2,1)S(1)}, bf16[48,3584]{1,0:T(8,128)(2,1)S(1)}, u32[]{:S(2)}, u32[]{:S(2)}) collective-permute-start(bf16[48,3584]{1,0:T(8,128)(2,1)S(1)} %fusion.7), channel_id=1, source_target_pairs={{0,24},{1,9},{2,26},{3,11},{4,28},{5,13},{6,30},{7,15},{8,0},{9,17... | collective-permute-start | bytes 1032200 | tf_op jit(solution)/shard_map/backward_experts/ppermute | solution.py:39
  143.7 2.5 %collective-permute-start.23 = (bf16[48,3584]{1,0:T(8,128)(2,1)S(1)}, bf16[48,3584]{1,0:T(8,128)(2,1)S(1)}, u32[]{:S(2)}, u32[]{:S(2)}) collective-permute-start(bf16[48,3584]{1,0:T(8,128)(2,1)S(1)} %fusion.8), channel_id=1, source_target_pairs={{0,8},{1,25},{2,10},{3,27},{4,12},{5,29},{6,14},{7,31},{8,16},{9,1... | collective-permute-start | bytes 1032200 | tf_op jit(solution)/shard_map/backward_experts/ppermute | solution.py:39
  149.1 1.7 collective-permute-done.16
  150.7 3.7 %collective-permute-start.25 = (bf16[48,3584]{1,0:T(8,128)(2,1)S(1)}, bf16[48,3584]{1,0:T(8,128)(2,1)S(1)}, u32[]{:S(2)}, u32[]{:S(2)}) collective-permute-start(bf16[48,3584]{1,0:T(8,128)(2,1)S(1)} %fusion.9), channel_id=1, source_target_pairs={{0,16},{1,17},{2,18},{3,19},{4,20},{5,21},{6,22},{7,23},{8,24},{9,... | collective-permute-start | bytes 1032200 | tf_op jit(solution)/shard_map/backward_experts/ppermute | solution.py:39
  156.0 6.8 %collective-permute-start.18 = (bf16[16,3584]{1,0:T(8,128)(2,1)S(1)}, bf16[16,3584]{1,0:T(8,128)(2,1)S(1)}, u32[]{:S(2)}, u32[]{:S(2)}) collective-permute-start(bf16[16,3584]{1,0:T(8,128)(2,1)S(1)} %get-tuple-element.88), channel_id=1, source_target_pairs={{0,38},{1,35},{2,32},{3,37},{4,34},{5,39},{6,36},{7,33},{8,46},{9,... | collective-permute-start | bytes 344072 | tf_op jit(solution)/shard_map/forward_home/ppermute | solution.py:55
  162.8 10.3 %collective-permute-start.20 = (bf16[16,3584]{1,0:T(8,128)(2,1)S(1)}, bf16[16,3584]{1,0:T(8,128)(2,1)S(1)}, u32[]{:S(2)}, u32[]{:S(2)}) collective-permute-start(bf16[16,3584]{1,0:T(8,128)(2,1)S(1)} %get-tuple-element.89), channel_id=1, source_target_pairs={{0,36},{1,37},{2,38},{3,39},{4,32},{5,33},{6,34},{7,35},{8,44},{9,... | collective-permute-start | bytes 344072 | tf_op jit(solution)/shard_map/forward_home/ppermute | solution.py:55
  173.1 2.9 %collective-permute-start.19 = (bf16[16,3584]{1,0:T(8,128)(2,1)S(1)}, bf16[16,3584]{1,0:T(8,128)(2,1)S(1)}, u32[]{:S(2)}, u32[]{:S(2)}) collective-permute-start(bf16[16,3584]{1,0:T(8,128)(2,1)S(1)} %get-tuple-element.90), channel_id=1, source_target_pairs={{0,34},{1,39},{2,36},{3,33},{4,38},{5,35},{6,32},{7,37},{8,42},{9,... | collective-permute-start | bytes 344072 | tf_op jit(solution)/shard_map/forward_home/ppermute | solution.py:55
  176.4 10.1 %collective-permute-start.17 = (f32[16,3584]{1,0:T(8,128)S(1)}, f32[16,3584]{1,0:T(8,128)S(1)}, u32[]{:S(2)}, u32[]{:S(2)}) collective-permute-start(f32[16,3584]{1,0:T(8,128)S(1)} %slice_add_fusion.1), channel_id=1, source_target_pairs={{0,32},{1,33},{2,34},{3,35},{4,36},{5,37},{6,38},{7,39},{8,40},{9,... | collective-permute-start | bytes 688136 | tf_op jit(solution)/shard_map/forward_home/ppermute | solution.py:55
  187.2 0.7 fusion.184
  187.9 8.7 %collective-permute-start.27 = (bf16[16,3584]{1,0:T(8,128)(2,1)S(1)}, bf16[16,3584]{1,0:T(8,128)(2,1)S(1)}, u32[]{:S(2)}, u32[]{:S(2)}) collective-permute-start(bf16[16,3584]{1,0:T(8,128)(2,1)S(1)} %get-tuple-element.85), channel_id=1, source_target_pairs={{32,6},{33,3},{34,0},{35,5},{36,2},{37,7},{38,4},{39,1},{40,14},{4... | collective-permute-start | bytes 344072 | tf_op jit(solution)/shard_map/backward_home/ppermute | solution.py:55
  196.7 1.9 collective-permute-start.29
  198.7 7.8 %collective-permute-start.28 = (bf16[16,3584]{1,0:T(8,128)(2,1)S(1)}, bf16[16,3584]{1,0:T(8,128)(2,1)S(1)}, u32[]{:S(2)}, u32[]{:S(2)}) collective-permute-start(bf16[16,3584]{1,0:T(8,128)(2,1)S(1)} %get-tuple-element.87), channel_id=1, source_target_pairs={{32,2},{33,7},{34,4},{35,1},{36,6},{37,3},{38,0},{39,5},{40,10},{4... | collective-permute-start | bytes 344072 | tf_op jit(solution)/shard_map/backward_home/ppermute | solution.py:55
  206.5 3.0 %collective-permute-start.26 = (f32[16,3584]{1,0:T(8,128)S(1)}, f32[16,3584]{1,0:T(8,128)S(1)}, u32[]{:S(2)}, u32[]{:S(2)}) collective-permute-start(f32[16,3584]{1,0:T(8,128)S(1)} %slice_add_fusion), channel_id=1, source_target_pairs={{32,0},{33,1},{34,2},{35,3},{36,4},{37,5},{38,6},{39,7},{40,8},{41... | collective-permute-start | bytes 688136 | tf_op jit(solution)/shard_map/backward_home/ppermute | solution.py:55
  209.5 0.7 fusion.34
  210.2 8.4 %collective-permute-done.29 = bf16[16,3584]{1,0:T(8,128)(2,1)S(1)} collective-permute-done((bf16[16,3584]{1,0:T(8,128)(2,1)S(1)}, bf16[16,3584]{1,0:T(8,128)(2,1)S(1)}, u32[]{:S(2)}, u32[]{:S(2)}) %collective-permute-start.29) | collective-permute-done | bytes 114720 | tf_op jit(solution)/shard_map/backward_home/ppermute | solution.py:55
  218.7 0.7 fusion.35
  (114 shorter events, 20.3 us)
Async XLA Ops:
  0.6 59.9 %copy-start.3 = (bf16[1,128,3584]{2,1,0:T(8,128)(2,1)S(1)}, bf16[1,128,3584]{2,1,0:T(8,128)(2,1)}, u32[]{:S(2)}) copy-start(bf16[1,128,3584]{2,1,0:T(8,128)(2,1)} %param.13) | copy-start | bytes 2752516
  3.4 36.4 %collective-permute-start.4 = (bf16[16,128]{0,1:T(8,128)(2,1)S(1)}, bf16[16,128]{0,1:T(8,128)(2,1)S(1)}, u32[]{:S(2)}, u32[]{:S(2)}) collective-permute-start(bf16[16,128]{0,1:T(8,128)(2,1)S(1)} %pad.4), channel_id=1, source_target_pairs={{0,4},{1,5},{2,6},{3,7},{4,0},{5,1},{6,2},{7,3},{8,12},{9,13},{10,... | collective-permute-start | bytes 12296 | tf_op jit(solution)/shard_map/gather_z/ppermute | solution.py:34
  19.1 22.8 %collective-permute-start.3 = (bf16[16,128]{0,1:T(8,128)(2,1)S(1)}, bf16[16,128]{0,1:T(8,128)(2,1)S(1)}, u32[]{:S(2)}, u32[]{:S(2)}) collective-permute-start(bf16[16,128]{0,1:T(8,128)(2,1)S(1)} %pad.4), channel_id=1, source_target_pairs={{0,6},{1,3},{2,0},{3,5},{4,2},{5,7},{6,4},{7,1},{8,14},{9,11},{10,... | collective-permute-start | bytes 12296 | tf_op jit(solution)/shard_map/gather_z/ppermute | solution.py:34
  21.0 20.9 %collective-permute-start.2 = (bf16[16,128]{0,1:T(8,128)(2,1)S(1)}, bf16[16,128]{0,1:T(8,128)(2,1)S(1)}, u32[]{:S(2)}, u32[]{:S(2)}) collective-permute-start(bf16[16,128]{0,1:T(8,128)(2,1)S(1)} %pad.4), channel_id=1, source_target_pairs={{0,2},{1,7},{2,4},{3,1},{4,6},{5,3},{6,0},{7,5},{8,10},{9,15},{10,... | collective-permute-start | bytes 12296 | tf_op jit(solution)/shard_map/gather_z/ppermute | solution.py:34
  28.9 18.9 %collective-permute-start.1 = (bf16[16,3584]{1,0:T(8,128)(2,1)}, bf16[16,3584]{1,0:T(8,128)(2,1)S(1)}, u32[]{:S(2)}, u32[]{:S(2)}) collective-permute-start(bf16[16,3584]{1,0:T(8,128)(2,1)} %bitcast.83), channel_id=1, source_target_pairs={{0,6},{1,3},{2,0},{3,5},{4,2},{5,7},{6,4},{7,1},{8,14},{9,11},{10,... | collective-permute-start | bytes 344072 | tf_op jit(solution)/shard_map/gather_z/ppermute | solution.py:34
  30.8 17.0 %collective-permute-start = (bf16[16,3584]{1,0:T(8,128)(2,1)}, bf16[16,3584]{1,0:T(8,128)(2,1)S(1)}, u32[]{:S(2)}, u32[]{:S(2)}) collective-permute-start(bf16[16,3584]{1,0:T(8,128)(2,1)} %bitcast.84), channel_id=1, source_target_pairs={{0,2},{1,7},{2,4},{3,1},{4,6},{5,3},{6,0},{7,5},{8,10},{9,15},{10,... | collective-permute-start | bytes 344072 | tf_op jit(solution)/shard_map/gather_z/ppermute | solution.py:34
  39.8 27.6 %copy-start = (bf16[1,3584,256]{2,1,0:T(8,128)(2,1)S(1)}, bf16[1,3584,256]{2,1,0:T(8,128)(2,1)}, u32[]{:S(2)}) copy-start(bf16[1,3584,256]{2,1,0:T(8,128)(2,1)} %param.12) | copy-start | bytes 5505028
  39.8 27.6 %copy-start.4 = (bf16[1,16,3584]{2,1,0:T(8,128)(2,1)S(1)}, bf16[1,16,3584]{2,1,0:T(8,128)(2,1)}, u32[]{:S(2)}) copy-start(bf16[1,16,3584]{2,1,0:T(8,128)(2,1)} %param.9) | copy-start | bytes 344068
  39.8 21.0 %collective-permute-start.6 = (bf16[16,7168]{1,0:T(8,128)(2,1)S(1)}, bf16[16,7168]{1,0:T(8,128)(2,1)S(1)}, u32[]{:S(2)}, u32[]{:S(2)}) collective-permute-start(bf16[16,7168]{1,0:T(8,128)(2,1)S(1)} %pad_maximum_fusion.3), channel_id=1, source_target_pairs={{0,6},{1,3},{2,0},{3,5},{4,2},{5,7},{6,4},{7,1},{8,14},{9,11},{10,... | collective-permute-start | bytes 688136 | tf_op jit(solution)/shard_map/gather_z/ppermute | solution.py:34
  47.8 19.5 %collective-permute-start.7 = (bf16[3584,256]{1,0:T(8,128)(2,1)}, bf16[3584,256]{1,0:T(8,128)(2,1)S(1)}, u32[]{:S(2)}, u32[]{:S(2)}) collective-permute-start(bf16[3584,256]{1,0:T(8,128)(2,1)} %bitcast.62), channel_id=1, source_target_pairs={{0,1},{1,0},{2,3},{3,2},{4,5},{5,4},{6,7},{7,6},{8,9},{9,8},{10,11... | collective-permute-start | bytes 5505032 | tf_op jit(solution)/shard_map/swap_weights/ppermute | solution.py:43
  51.1 16.2 %collective-permute-start.5 = (bf16[16,10752]{1,0:T(8,128)(2,1)S(1)}, bf16[16,10752]{1,0:T(8,128)(2,1)S(1)}, u32[]{:S(2)}, u32[]{:S(2)}) collective-permute-start(bf16[16,10752]{1,0:T(8,128)(2,1)S(1)} %pad_maximum_fusion.2), channel_id=1, source_target_pairs={{0,2},{1,7},{2,4},{3,1},{4,6},{5,3},{6,0},{7,5},{8,10},{9,15},{10,... | collective-permute-start | bytes 1032200 | tf_op jit(solution)/shard_map/gather_z/ppermute | solution.py:34
  58.5 8.8 %collective-permute-start.8 = (bf16[128,3584]{1,0:T(8,128)(2,1)}, bf16[128,3584]{1,0:T(8,128)(2,1)S(1)}, u32[]{:S(2)}, u32[]{:S(2)}) collective-permute-start(bf16[128,3584]{1,0:T(8,128)(2,1)} %bitcast.81), channel_id=1, source_target_pairs={{0,1},{1,0},{2,3},{3,2},{4,5},{5,4},{6,7},{7,6},{8,9},{9,8},{10,11... | collective-permute-start | bytes 2752520 | tf_op jit(solution)/shard_map/swap_weights/ppermute | solution.py:43
  68.3 17.9 %collective-permute-start.12 = (bf16[16,7168]{1,0:T(8,128)(2,1)S(1)}, bf16[16,7168]{1,0:T(8,128)(2,1)S(1)}, u32[]{:S(2)}, u32[]{:S(2)}) collective-permute-start(bf16[16,7168]{1,0:T(8,128)(2,1)S(1)} %slice.85), channel_id=1, source_target_pairs={{0,2},{1,7},{2,4},{3,1},{4,6},{5,3},{6,0},{7,5},{8,10},{9,15},{10,... | collective-permute-start | bytes 688136 | tf_op jit(solution)/shard_map/gather_x_forward/ppermute | solution.py:34
  74.8 22.2 %copy-start.1 = (bf16[1,16,3584]{2,1,0:T(8,128)(2,1)S(1)}, bf16[1,16,3584]{2,1,0:T(8,128)(2,1)}, u32[]{:S(2)}) copy-start(bf16[1,16,3584]{2,1,0:T(8,128)(2,1)} %param.11) | copy-start | bytes 344068
  74.9 22.2 %copy-start.2 = (bf16[1,16,3584]{2,1,0:T(8,128)(2,1)S(1)}, bf16[1,16,3584]{2,1,0:T(8,128)(2,1)}, u32[]{:S(2)}) copy-start(bf16[1,16,3584]{2,1,0:T(8,128)(2,1)} %param.10) | copy-start | bytes 344068
  75.2 12.4 %collective-permute-start.11 = (bf16[48,3584]{1,0:T(8,128)(2,1)S(1)}, bf16[48,3584]{1,0:T(8,128)(2,1)S(1)}, u32[]{:S(2)}, u32[]{:S(2)}) collective-permute-start(bf16[48,3584]{1,0:T(8,128)(2,1)S(1)} %convolution_convert_fusion.6), channel_id=1, source_target_pairs={{0,16},{1,17},{2,18},{3,19},{4,20},{5,21},{6,22},{7,23},{8,24},{9,... | collective-permute-start | bytes 1032200 | tf_op jit(solution)/shard_map/gather_x_forward/ppermute | solution.py:39
  80.2 14.9 %collective-permute-start.10 = (bf16[48,3584]{1,0:T(8,128)(2,1)S(1)}, bf16[48,3584]{1,0:T(8,128)(2,1)S(1)}, u32[]{:S(2)}, u32[]{:S(2)}) collective-permute-start(bf16[48,3584]{1,0:T(8,128)(2,1)S(1)} %convolution_convert_fusion.7), channel_id=1, source_target_pairs={{0,24},{1,9},{2,26},{3,11},{4,28},{5,13},{6,30},{7,15},{8,0},{9,17... | collective-permute-start | bytes 1032200 | tf_op jit(solution)/shard_map/gather_x_forward/ppermute | solution.py:39
  83.2 13.8 %collective-permute-start.9 = (bf16[48,3584]{1,0:T(8,128)(2,1)S(1)}, bf16[48,3584]{1,0:T(8,128)(2,1)S(1)}, u32[]{:S(2)}, u32[]{:S(2)}) collective-permute-start(bf16[48,3584]{1,0:T(8,128)(2,1)S(1)} %convolution_convert_fusion.8), channel_id=1, source_target_pairs={{0,8},{1,25},{2,10},{3,27},{4,12},{5,29},{6,14},{7,31},{8,16},{9,1... | collective-permute-start | bytes 1032200 | tf_op jit(solution)/shard_map/gather_x_forward/ppermute | solution.py:39
  102.7 18.2 %collective-permute-start.13 = (bf16[48,7168]{1,0:T(8,128)(2,1)S(1)}, bf16[48,7168]{1,0:T(8,128)(2,1)S(1)}, u32[]{:S(2)}, u32[]{:S(2)}) collective-permute-start(bf16[48,7168]{1,0:T(8,128)(2,1)S(1)} %convolution_convert_fusion.2), channel_id=1, source_target_pairs={{0,8},{1,25},{2,10},{3,27},{4,12},{5,29},{6,14},{7,31},{8,16},{9,1... | collective-permute-start | bytes 2064392 | tf_op jit(solution)/shard_map/gather_x_backward/ppermute | solution.py:39
  105.6 31.6 %collective-permute-start.22 = (bf16[48,7168]{1,0:T(8,128)(2,1)S(1)}, bf16[48,7168]{1,0:T(8,128)(2,1)S(1)}, u32[]{:S(2)}, u32[]{:S(2)}) collective-permute-start(bf16[48,7168]{1,0:T(8,128)(2,1)S(1)} %convolution_convert_fusion.1), channel_id=1, source_target_pairs={{0,24},{1,9},{2,26},{3,11},{4,28},{5,13},{6,30},{7,15},{8,0},{9,17... | collective-permute-start | bytes 2064392 | tf_op jit(solution)/shard_map/gather_x_backward/ppermute | solution.py:39
  109.8 33.9 %collective-permute-start.24 = (bf16[48,7168]{1,0:T(8,128)(2,1)S(1)}, bf16[48,7168]{1,0:T(8,128)(2,1)S(1)}, u32[]{:S(2)}, u32[]{:S(2)}) collective-permute-start(bf16[48,7168]{1,0:T(8,128)(2,1)S(1)} %convolution_convert_fusion), channel_id=1, source_target_pairs={{0,16},{1,17},{2,18},{3,19},{4,20},{5,21},{6,22},{7,23},{8,24},{9,... | collective-permute-start | bytes 2064392 | tf_op jit(solution)/shard_map/gather_x_backward/ppermute | solution.py:39
  122.5 32.7 %collective-permute-start.14 = (bf16[48,3584]{1,0:T(8,128)(2,1)S(1)}, bf16[48,3584]{1,0:T(8,128)(2,1)S(1)}, u32[]{:S(2)}, u32[]{:S(2)}) collective-permute-start(bf16[48,3584]{1,0:T(8,128)(2,1)S(1)} %convolution_convert_fusion.5), channel_id=1, source_target_pairs={{0,24},{1,9},{2,26},{3,11},{4,28},{5,13},{6,30},{7,15},{8,0},{9,17... | collective-permute-start | bytes 1032200 | tf_op jit(solution)/shard_map/forward_experts/ppermute | solution.py:39
  125.1 29.7 %collective-permute-start.15 = (bf16[48,3584]{1,0:T(8,128)(2,1)S(1)}, bf16[48,3584]{1,0:T(8,128)(2,1)S(1)}, u32[]{:S(2)}, u32[]{:S(2)}) collective-permute-start(bf16[48,3584]{1,0:T(8,128)(2,1)S(1)} %convolution_convert_fusion.4), channel_id=1, source_target_pairs={{0,8},{1,25},{2,10},{3,27},{4,12},{5,29},{6,14},{7,31},{8,16},{9,1... | collective-permute-start | bytes 1032200 | tf_op jit(solution)/shard_map/forward_experts/ppermute | solution.py:39
  129.0 21.8 %collective-permute-start.16 = (bf16[48,3584]{1,0:T(8,128)(2,1)S(1)}, bf16[48,3584]{1,0:T(8,128)(2,1)S(1)}, u32[]{:S(2)}, u32[]{:S(2)}) collective-permute-start(bf16[48,3584]{1,0:T(8,128)(2,1)S(1)} %convolution_convert_fusion.3), channel_id=1, source_target_pairs={{0,16},{1,17},{2,18},{3,19},{4,20},{5,21},{6,22},{7,23},{8,24},{9,... | collective-permute-start | bytes 1032200 | tf_op jit(solution)/shard_map/forward_experts/ppermute | solution.py:39
  137.3 35.8 %collective-permute-start.21 = (bf16[48,3584]{1,0:T(8,128)(2,1)S(1)}, bf16[48,3584]{1,0:T(8,128)(2,1)S(1)}, u32[]{:S(2)}, u32[]{:S(2)}) collective-permute-start(bf16[48,3584]{1,0:T(8,128)(2,1)S(1)} %fusion.7), channel_id=1, source_target_pairs={{0,24},{1,9},{2,26},{3,11},{4,28},{5,13},{6,30},{7,15},{8,0},{9,17... | collective-permute-start | bytes 1032200 | tf_op jit(solution)/shard_map/backward_experts/ppermute | solution.py:39
  143.7 32.7 %collective-permute-start.23 = (bf16[48,3584]{1,0:T(8,128)(2,1)S(1)}, bf16[48,3584]{1,0:T(8,128)(2,1)S(1)}, u32[]{:S(2)}, u32[]{:S(2)}) collective-permute-start(bf16[48,3584]{1,0:T(8,128)(2,1)S(1)} %fusion.8), channel_id=1, source_target_pairs={{0,8},{1,25},{2,10},{3,27},{4,12},{5,29},{6,14},{7,31},{8,16},{9,1... | collective-permute-start | bytes 1032200 | tf_op jit(solution)/shard_map/backward_experts/ppermute | solution.py:39
  150.7 36.1 %collective-permute-start.25 = (bf16[48,3584]{1,0:T(8,128)(2,1)S(1)}, bf16[48,3584]{1,0:T(8,128)(2,1)S(1)}, u32[]{:S(2)}, u32[]{:S(2)}) collective-permute-start(bf16[48,3584]{1,0:T(8,128)(2,1)S(1)} %fusion.9), channel_id=1, source_target_pairs={{0,16},{1,17},{2,18},{3,19},{4,20},{5,21},{6,22},{7,23},{8,24},{9,... | collective-permute-start | bytes 1032200 | tf_op jit(solution)/shard_map/backward_experts/ppermute | solution.py:39
  156.0 40.7 %collective-permute-start.18 = (bf16[16,3584]{1,0:T(8,128)(2,1)S(1)}, bf16[16,3584]{1,0:T(8,128)(2,1)S(1)}, u32[]{:S(2)}, u32[]{:S(2)}) collective-permute-start(bf16[16,3584]{1,0:T(8,128)(2,1)S(1)} %get-tuple-element.88), channel_id=1, source_target_pairs={{0,38},{1,35},{2,32},{3,37},{4,34},{5,39},{6,36},{7,33},{8,46},{9,... | collective-permute-start | bytes 344072 | tf_op jit(solution)/shard_map/forward_home/ppermute | solution.py:55
  162.8 35.8 %collective-permute-start.20 = (bf16[16,3584]{1,0:T(8,128)(2,1)S(1)}, bf16[16,3584]{1,0:T(8,128)(2,1)S(1)}, u32[]{:S(2)}, u32[]{:S(2)}) collective-permute-start(bf16[16,3584]{1,0:T(8,128)(2,1)S(1)} %get-tuple-element.89), channel_id=1, source_target_pairs={{0,36},{1,37},{2,38},{3,39},{4,32},{5,33},{6,34},{7,35},{8,44},{9,... | collective-permute-start | bytes 344072 | tf_op jit(solution)/shard_map/forward_home/ppermute | solution.py:55
  173.1 33.4 %collective-permute-start.19 = (bf16[16,3584]{1,0:T(8,128)(2,1)S(1)}, bf16[16,3584]{1,0:T(8,128)(2,1)S(1)}, u32[]{:S(2)}, u32[]{:S(2)}) collective-permute-start(bf16[16,3584]{1,0:T(8,128)(2,1)S(1)} %get-tuple-element.90), channel_id=1, source_target_pairs={{0,34},{1,39},{2,36},{3,33},{4,38},{5,35},{6,32},{7,37},{8,42},{9,... | collective-permute-start | bytes 344072 | tf_op jit(solution)/shard_map/forward_home/ppermute | solution.py:55
  176.4 33.1 %collective-permute-start.17 = (f32[16,3584]{1,0:T(8,128)S(1)}, f32[16,3584]{1,0:T(8,128)S(1)}, u32[]{:S(2)}, u32[]{:S(2)}) collective-permute-start(f32[16,3584]{1,0:T(8,128)S(1)} %slice_add_fusion.1), channel_id=1, source_target_pairs={{0,32},{1,33},{2,34},{3,35},{4,36},{5,37},{6,38},{7,39},{8,40},{9,... | collective-permute-start | bytes 688136 | tf_op jit(solution)/shard_map/forward_home/ppermute | solution.py:55
  187.9 22.3 %collective-permute-start.27 = (bf16[16,3584]{1,0:T(8,128)(2,1)S(1)}, bf16[16,3584]{1,0:T(8,128)(2,1)S(1)}, u32[]{:S(2)}, u32[]{:S(2)}) collective-permute-start(bf16[16,3584]{1,0:T(8,128)(2,1)S(1)} %get-tuple-element.85), channel_id=1, source_target_pairs={{32,6},{33,3},{34,0},{35,5},{36,2},{37,7},{38,4},{39,1},{40,14},{4... | collective-permute-start | bytes 344072 | tf_op jit(solution)/shard_map/backward_home/ppermute | solution.py:55
  196.7 21.9 %collective-permute-start.29 = (bf16[16,3584]{1,0:T(8,128)(2,1)S(1)}, bf16[16,3584]{1,0:T(8,128)(2,1)S(1)}, u32[]{:S(2)}, u32[]{:S(2)}) collective-permute-start(bf16[16,3584]{1,0:T(8,128)(2,1)S(1)} %get-tuple-element.86), channel_id=1, source_target_pairs={{32,4},{33,5},{34,6},{35,7},{36,0},{37,1},{38,2},{39,3},{40,12},{4... | collective-permute-start | bytes 344072 | tf_op jit(solution)/shard_map/backward_home/ppermute | solution.py:55
  198.7 20.0 %collective-permute-start.28 = (bf16[16,3584]{1,0:T(8,128)(2,1)S(1)}, bf16[16,3584]{1,0:T(8,128)(2,1)S(1)}, u32[]{:S(2)}, u32[]{:S(2)}) collective-permute-start(bf16[16,3584]{1,0:T(8,128)(2,1)S(1)} %get-tuple-element.87), channel_id=1, source_target_pairs={{32,2},{33,7},{34,4},{35,1},{36,6},{37,3},{38,0},{39,5},{40,10},{4... | collective-permute-start | bytes 344072 | tf_op jit(solution)/shard_map/backward_home/ppermute | solution.py:55
  206.5 12.2 %collective-permute-start.26 = (f32[16,3584]{1,0:T(8,128)S(1)}, f32[16,3584]{1,0:T(8,128)S(1)}, u32[]{:S(2)}, u32[]{:S(2)}) collective-permute-start(f32[16,3584]{1,0:T(8,128)S(1)} %slice_add_fusion), channel_id=1, source_target_pairs={{32,0},{33,1},{34,2},{35,3},{36,4},{37,5},{38,6},{39,7},{40,8},{41... | collective-permute-start | bytes 688136 | tf_op jit(solution)/shard_map/backward_home/ppermute | solution.py:55

commit v5 on v3

v5 whole, which is shorter than its diff:
```python
import jax
import jax.numpy as jnp
from jax import lax
from jax.sharding import PartitionSpec as P

EXPERTS = 4
Z = 4
CORES = 2
LANES = 128


def expert_index(x, z, core):
    return (x * Z + z) * CORES + core


def expert_route(move):
    return [
        (expert_index(x, z, c), expert_index(*move(x, z, c)))
        for x in range(EXPERTS)
        for z in range(Z)
        for c in range(CORES)
    ]


def turn(core):
    return 1 - 2 * core


def gather_z(block):
    groups = [
        [expert_index(x, z, c) for z in range(Z)] for x in range(EXPERTS) for c in range(CORES)
    ]
    blocks = jnp.broadcast_to(block[None], (Z,) + block.shape)
    blocks = lax.all_to_all(blocks, "expert", 0, 0, axis_index_groups=groups, tiled=True)
    return blocks.reshape(Z * block.shape[0], block.shape[1])


def along_x(block, distance):
    route = expert_route(lambda x, z, c: ((x + distance * turn(c)) % EXPERTS, z, c))
    return lax.ppermute(block, "expert", route)


def other_core(block):
    return lax.ppermute(block, "expert", expert_route(lambda x, z, c: (x, z, 1 - c)))


def to_section(block, step, distance):
    sections = lax.axis_size("pipe")
    width = EXPERTS * Z * CORES
    route = [
        (p * width + source, (p + step) * width + target)
        for p in range(sections)
        if 0 <= p + step < sections
        for source, target in expert_route(lambda x, z, c: (x, (z + distance * turn(c)) % Z, c))
    ]
    return lax.ppermute(block, ("pipe", "expert"), route)


def together(*values):
    return lax.optimization_barrier(values)


def expert_hot(routes):
    return routes[:, :, None] == jnp.arange(EXPERTS, dtype=jnp.int32)


def expert_shares(hot, gates):
    return jnp.sum(jnp.where(hot, gates[:, :, None], 0.0), axis=1)


def three_parts(values):
    first = lax.reduce_precision(values, 8, 7)
    second = lax.reduce_precision(values - first, 8, 7)
    return [part.astype(jnp.bfloat16) for part in (first, second, values - first - second)]


def side_columns(shares):
    parts = jnp.concatenate(three_parts(shares), axis=1)
    return jnp.pad(parts, ((0, 0), (0, LANES - parts.shape[1])))


def side_values(columns):
    width = 2 * EXPERTS
    first, second, third = jnp.split(columns[:, : 3 * width].astype(jnp.float32), 3, axis=1)
    return first + second + third


def column_of(table, index):
    hot = jnp.arange(table.shape[1], dtype=jnp.int32) == index
    return jnp.sum(jnp.where(hot[None, :], table, 0.0), axis=1, keepdims=True)


def dot(a, b):
    return jnp.dot(a, b, preferred_element_type=jnp.float32)


def dot_t(a, b):
    return lax.dot_general(a, b, (((1,), (1,)), ((), ())), preferred_element_type=jnp.float32)


def forward_rows(rows, gate_up, down):
    gate_val, up_val = jnp.split(dot(rows, gate_up), 2, axis=1)
    hidden = (jax.nn.silu(gate_val) * up_val).astype(jnp.bfloat16)
    return dot(hidden, down)


def backward_rows(rows, grads, gate_up, down):
    hidden_grad = dot_t(grads, down)
    gate_val, up_val = jnp.split(dot(rows, gate_up), 2, axis=1)
    sig = jax.nn.sigmoid(gate_val)
    gate_grad = hidden_grad * up_val * sig * (1.0 + gate_val * (1.0 - sig))
    up_grad = hidden_grad * gate_val * sig
    grad = jnp.concatenate([gate_grad, up_grad], axis=1).astype(jnp.bfloat16)
    return dot_t(grad, gate_up)


def send_home(mixture, residual, step, place, turned):
    rows = residual.shape[0]
    total = 0.0
    for distance in (0, 1, -1, 2):
        owner = (place + Z + distance * turned) % Z
        block = lax.dynamic_slice_in_dim(mixture, owner * rows, rows, axis=0)
        if distance == 0:
            part = to_section(block + residual.astype(jnp.float32), step, 0)
        else:
            part = to_section(block.astype(jnp.bfloat16), step, distance)
        total = total + part.astype(jnp.float32)
    return total.astype(jnp.bfloat16)


def on_device(
    forward_input,
    backward_input,
    backward_grad,
    gate_up_weight,
    down_weight,
    forward_routes,
    backward_routes,
    forward_gates,
    backward_gates,
):
    tokens, saved, upstream = forward_input[0], backward_input[0], backward_grad[0]
    rows, model = tokens.shape
    index = lax.axis_index("expert")
    turned = 1 - 2 * (index % CORES)
    place = index // CORES % Z
    me = index // (Z * CORES)
    experts = [(me + EXPERTS + d * turned) % EXPERTS for d in (0, -1, 1, -2)]

    with jax.named_scope("gather_weights"):
        gate_up, down = gate_up_weight[0], down_weight[0]
        near = [along_x(gate_up, 1), along_x(gate_up, -1), along_x(down, 1), along_x(down, -1)]
    with jax.named_scope("gather_rows"):
        shares = [
            expert_shares(expert_hot(forward_routes[0]), forward_gates[0]),
            expert_shares(expert_hot(backward_routes[0]), backward_gates[0]),
        ]
        side = side_columns(jnp.concatenate(shares, axis=1))
        mine = gather_z(jnp.concatenate([tokens, saved, upstream, side], axis=1))
        mine, *near = together(mine, *near)
        gate_ups = [gate_up, near[0], near[1], along_x(near[0], 1)]
        downs = [down, near[2], near[3], along_x(near[2], 1)]
        both = [mine, other_core(mine)]
        cuts = (0, model, 2 * model, 3 * model, 3 * model + LANES)
        token_rows, saved_rows, upstream_rows, sides = [
            jnp.concatenate([part[:, low:high] for part in both], axis=0)
            for low, high in zip(cuts, cuts[1:])
        ]
        shares = side_values(sides)
    with jax.named_scope("experts"):
        forward_sum = backward_sum = 0.0
        for expert, gate_up, down in zip(experts, gate_ups, downs):
            out = forward_rows(token_rows, gate_up, down)
            forward_sum = forward_sum + column_of(shares[:, :EXPERTS], expert) * out
            out = backward_rows(saved_rows, upstream_rows, gate_up, down)
            backward_sum = backward_sum + column_of(shares[:, EXPERTS:], expert) * out
    half = Z * rows
    with jax.named_scope("forward_home"):
        other = other_core(forward_sum[half:].astype(jnp.bfloat16)).astype(jnp.float32)
        mixture = forward_sum[:half] + other
        forward_next = send_home(mixture, tokens, 1, place, turned)
    with jax.named_scope("backward_home"):
        other = other_core(backward_sum[half:].astype(jnp.bfloat16)).astype(jnp.float32)
        mixture = backward_sum[:half] + other
        backward_next = send_home(mixture, upstream, -1, place, turned)
    return (forward_next[None], backward_next[None])


def solution(mesh):
    by_token = P("pipe", "expert", None)
    return jax.shard_map(
        on_device,
        mesh=mesh,
        in_specs=(by_token,) * 3 + (P("pipe", None, "expert"),) + (by_token,) * 5,
        out_specs=(by_token, by_token),
        check_vma=False,
    )
```

time: 229 us -> 194 us (0.85)
  the two profiles are of different devices: /device:TPU:98 before, /device:TPU:105 now
where the time goes in v5:
time: 194 us; the launch traced here: 193 us
  waiting for transfers between devices  87.2 us (45%)
  starting transfers between devices  78.9 us (41%)
  matrix products  13.9 us (7%)
  local copies, waits for them, and re-layouts  7.98 us (4%)
  other arithmetic  3.8 us (2%)
    ppermute x6, waiting for transfers between devices, along_x(): return lax.ppermute(block, 'expert', route)  63.8 us
    ppermute x8, starting transfers between devices, to_section(): return lax.ppermute(block, ('pipe', 'expert'), route)  36.7 us
    ppermute x8, waiting for transfers between devices, to_section(): return lax.ppermute(block, ('pipe', 'expert'), route)  23.4 us
    ppermute x6, starting transfers between devices, along_x(): return lax.ppermute(block, 'expert', route)  19.8 us
    all_to_all x1, starting transfers between devices, gather_z(): lax.all_to_all(blocks, 'expert', 0, 0, axis_index_groups=groups, tiled=True)  12.1 us
    ppermute x3, starting transfers between devices, other_core(): lax.ppermute(block, 'expert', expert_route(lambda x, z, c: (x, z, 1 - c)))  10.3 us
    dot_general x12, matrix products, dot(): return jnp.dot(a, b, preferred_element_type=jnp.float32)  7.84 us
    dot_general x8, matrix products, dot_t(): lax.dot_general(a, b, (((1,), (1,)), ((), ())), preferred_element_type=jn...  6.1 us
  transfers between devices with their start and end apart: 18, of which 7 were waited for; matrix products, arithmetic and copies ran while one was open for 9% of the time, Pallas kernels for 0%

profile of v5, /device:TPU:105, one launch (start us, length us, event | category | flops | bytes accessed | tf_op | source)
XLA Modules:
  0.0 193.2 jit_solution(17728214815665822270)
XLA Ops:
  0.6 0.7 select_reduce_fusion.8
  1.5 1.0 fusion.7
  2.5 1.2 broadcast_in_dim.104
  3.7 12.1 %all-to-all-start = ((bf16[4,16,10880]{2,1,0:T(8,128)(2,1)}), bf16[4,16,10880]{2,1,0:T(8,128)(2,1)S(1)}, u32[]{:S(2)}, u32[]{:S(2)}) async-start(bf16[4,16,10880]{2,1,0:T(8,128)(2,1)} %broadcast_in_dim.104), calls=%async_computation | async-start | bytes 2785280 | tf_op jit(solution)/shard_map/gather_rows/all_to_all | solution.py:34
  15.8 3.1 %collective-permute-start.1 = (bf16[3584,256]{1,0:T(8,128)(2,1)S(1)}, bf16[3584,256]{1,0:T(8,128)(2,1)S(1)}, u32[]{:S(2)}, u32[]{:S(2)}) collective-permute-start(bf16[3584,256]{1,0:T(8,128)(2,1)S(1)} %bitcast.46), channel_id=1, source_target_pairs={{0,24},{1,9},{2,26},{3,11},{4,28},{5,13},{6,30},{7,15},{8,0},{9,17... | collective-permute-start | bytes 5505032 | tf_op jit(solution)/shard_map/gather_weights/ppermute | solution.py:40
  19.0 3.4 %collective-permute-start = (bf16[3584,256]{1,0:T(8,128)(2,1)S(1)}, bf16[3584,256]{1,0:T(8,128)(2,1)}, u32[]{:S(2)}, u32[]{:S(2)}) collective-permute-start(bf16[3584,256]{1,0:T(8,128)(2,1)S(1)} %bitcast.47), channel_id=1, source_target_pairs={{0,8},{1,25},{2,10},{3,27},{4,12},{5,29},{6,14},{7,31},{8,16},{9,1... | collective-permute-start | bytes 5505032 | tf_op jit(solution)/shard_map/gather_weights/ppermute | solution.py:40
  22.3 1.9 collective-permute-start.3
  24.3 4.6 %collective-permute-start.2 = (bf16[128,3584]{1,0:T(8,128)(2,1)}, bf16[128,3584]{1,0:T(8,128)(2,1)S(1)}, u32[]{:S(2)}, u32[]{:S(2)}) collective-permute-start(bf16[128,3584]{1,0:T(8,128)(2,1)} %bitcast.49), channel_id=1, source_target_pairs={{0,8},{1,25},{2,10},{3,27},{4,12},{5,29},{6,14},{7,31},{8,16},{9,1... | collective-permute-start | bytes 2752520 | tf_op jit(solution)/shard_map/gather_weights/ppermute | solution.py:40
  28.9 45.6 %collective-permute-done.3 = bf16[128,3584]{1,0:T(8,128)(2,1)S(1)} collective-permute-done((bf16[128,3584]{1,0:T(8,128)(2,1)}, bf16[128,3584]{1,0:T(8,128)(2,1)S(1)}, u32[]{:S(2)}, u32[]{:S(2)}) %collective-permute-start.3) | collective-permute-done | bytes 917536 | tf_op jit(solution)/shard_map/gather_weights/ppermute | solution.py:40
  74.5 6.7 %collective-permute-done.2 = bf16[128,3584]{1,0:T(8,128)(2,1)S(1)} collective-permute-done((bf16[128,3584]{1,0:T(8,128)(2,1)}, bf16[128,3584]{1,0:T(8,128)(2,1)S(1)}, u32[]{:S(2)}, u32[]{:S(2)}) %collective-permute-start.2) | collective-permute-done | bytes 917536 | tf_op jit(solution)/shard_map/gather_weights/ppermute | solution.py:40
  81.2 0.9 copy-done.3
  82.2 1.2 copy-done.1
  83.4 4.7 %collective-permute-start.4 = (bf16[64,10880]{1,0:T(8,128)(2,1)S(1)}, bf16[64,10880]{1,0:T(8,128)(2,1)}, u32[]{:S(2)}, u32[]{:S(2)}) collective-permute-start(bf16[64,10880]{1,0:T(8,128)(2,1)S(1)} %bitcast.43), channel_id=1, source_target_pairs={{0,1},{1,0},{2,3},{3,2},{4,5},{5,4},{6,7},{7,6},{8,9},{9,8},{10,11... | collective-permute-start | bytes 4177928 | tf_op jit(solution)/shard_map/gather_rows/ppermute | solution.py:44
  88.4 4.4 %collective-permute-start.6 = (bf16[128,3584]{1,0:T(8,128)(2,1)}, bf16[128,3584]{1,0:T(8,128)(2,1)S(1)}, u32[]{:S(2)}, u32[]{:S(2)}) collective-permute-start(bf16[128,3584]{1,0:T(8,128)(2,1)} %copy-done.3), channel_id=1, source_target_pairs={{0,8},{1,25},{2,10},{3,27},{4,12},{5,29},{6,14},{7,31},{8,16},{9,1... | collective-permute-start | bytes 2752520 | tf_op jit(solution)/shard_map/gather_rows/ppermute | solution.py:40
  92.7 2.5 %collective-permute-start.5 = (bf16[3584,256]{1,0:T(8,128)(2,1)}, bf16[3584,256]{1,0:T(8,128)(2,1)S(1)}, u32[]{:S(2)}, u32[]{:S(2)}) collective-permute-start(bf16[3584,256]{1,0:T(8,128)(2,1)} %collective-permute-done), channel_id=1, source_target_pairs={{0,8},{1,25},{2,10},{3,27},{4,12},{5,29},{6,14},{7,31},{8,16},{9,1... | collective-permute-start | bytes 5505032 | tf_op jit(solution)/shard_map/gather_rows/ppermute | solution.py:40
  95.3 1.4 fusion.74
  96.7 1.9 fusion.66
  98.6 0.4 fusion.56
  99.1 1.9 fusion.72
  101.0 0.4 fusion.58
  101.4 0.8 slice.68
  102.5 0.4 fusion.71
  104.3 0.8 copy-done.4
  105.5 0.7 convolution_multiply_fusion.3
  106.2 0.4 fusion.18
  106.6 0.8 copy-done.6
  107.8 2.3 %fusion.2 = f32[128,3584]{1,0:T(8,128)S(1)} fusion(f32[128,3584]{1,0:T(8,128)S(1)} %convolution_multiply_fusion.3, bf16[3584,256]{1,0:T(8,128)(2,1)} %collective-permute-done, f32[128]{0:T(128)S(1)} %get-tuple-element.21, bf16[128,128]{1,0:T(8,128)(2,1)S(1)} %get-tuple-element.43, bf16[128,128]{1,0:T(8,128)(2,1)S(1)} %get-tuple-element.42), kind=kOutput, calls=%fused_computation.5 | convolution fusion | flops 235929600 | bytes 5571072 | tf_op jit(solution)/shard_map/experts/dot_general | solution.py:98
  110.0 0.4 fusion.65
  110.9 0.7 fusion.1
  111.6 11.4 %collective-permute-done.5 = bf16[3584,256]{1,0:T(8,128)(2,1)S(1)} collective-permute-done((bf16[3584,256]{1,0:T(8,128)(2,1)}, bf16[3584,256]{1,0:T(8,128)(2,1)S(1)}, u32[]{:S(2)}, u32[]{:S(2)}) %collective-permute-start.5) | collective-permute-done | bytes 1835040 | tf_op jit(solution)/shard_map/gather_rows/ppermute | solution.py:40
  123.0 0.4 fusion.70
  123.9 3.6 %collective-permute-start.7 = (bf16[64,3584]{1,0:T(8,128)(2,1)S(1)}, bf16[64,3584]{1,0:T(8,128)(2,1)S(1)}, u32[]{:S(2)}, u32[]{:S(2)}) collective-permute-start(bf16[64,3584]{1,0:T(8,128)(2,1)S(1)} %slice.91), channel_id=1, source_target_pairs={{0,1},{1,0},{2,3},{3,2},{4,5},{5,4},{6,7},{7,6},{8,9},{9,8},{10,11... | collective-permute-start | bytes 1376264 | tf_op jit(solution)/shard_map/forward_home/ppermute | solution.py:44
  127.5 0.4 fusion.64
  128.4 0.7 fusion
  129.2 1.9 %collective-permute-start.12 = (bf16[64,3584]{1,0:T(8,128)(2,1)S(1)}, bf16[64,3584]{1,0:T(8,128)(2,1)S(1)}, u32[]{:S(2)}, u32[]{:S(2)}) collective-permute-start(bf16[64,3584]{1,0:T(8,128)(2,1)S(1)} %slice.90), channel_id=1, source_target_pairs={{0,1},{1,0},{2,3},{3,2},{4,5},{5,4},{6,7},{7,6},{8,9},{9,8},{10,11... | collective-permute-start | bytes 1376264 | tf_op jit(solution)/shard_map/backward_home/ppermute | solution.py:44
  131.3 7.8 %collective-permute-start.9 = (bf16[16,3584]{1,0:T(8,128)(2,1)S(1)}, bf16[16,3584]{1,0:T(8,128)(2,1)S(1)}, u32[]{:S(2)}, u32[]{:S(2)}) collective-permute-start(bf16[16,3584]{1,0:T(8,128)(2,1)S(1)} %get-tuple-element.35), channel_id=1, source_target_pairs={{0,34},{1,39},{2,36},{3,33},{4,38},{5,35},{6,32},{7,37},{8,42},{9,... | collective-permute-start | bytes 344072 | tf_op jit(solution)/shard_map/forward_home/ppermute | solution.py:56
  139.1 4.0 %collective-permute-start.11 = (bf16[16,3584]{1,0:T(8,128)(2,1)S(1)}, bf16[16,3584]{1,0:T(8,128)(2,1)S(1)}, u32[]{:S(2)}, u32[]{:S(2)}) collective-permute-start(bf16[16,3584]{1,0:T(8,128)(2,1)S(1)} %get-tuple-element.36), channel_id=1, source_target_pairs={{0,36},{1,37},{2,38},{3,39},{4,32},{5,33},{6,34},{7,35},{8,44},{9,... | collective-permute-start | bytes 344072 | tf_op jit(solution)/shard_map/forward_home/ppermute | solution.py:56
  143.1 6.4 %collective-permute-start.10 = (bf16[16,3584]{1,0:T(8,128)(2,1)S(1)}, bf16[16,3584]{1,0:T(8,128)(2,1)S(1)}, u32[]{:S(2)}, u32[]{:S(2)}) collective-permute-start(bf16[16,3584]{1,0:T(8,128)(2,1)S(1)} %get-tuple-element.37), channel_id=1, source_target_pairs={{0,38},{1,35},{2,32},{3,37},{4,34},{5,39},{6,36},{7,33},{8,46},{9,... | collective-permute-start | bytes 344072 | tf_op jit(solution)/shard_map/forward_home/ppermute | solution.py:56
  149.6 5.3 %collective-permute-start.8 = (f32[16,3584]{1,0:T(8,128)S(1)}, f32[16,3584]{1,0:T(8,128)S(1)}, u32[]{:S(2)}, u32[]{:S(2)}) collective-permute-start(f32[16,3584]{1,0:T(8,128)S(1)} %convert_add_fusion.1), channel_id=1, source_target_pairs={{0,32},{1,33},{2,34},{3,35},{4,36},{5,37},{6,38},{7,39},{8,40},{9,... | collective-permute-start | bytes 688136 | tf_op jit(solution)/shard_map/forward_home/ppermute | solution.py:56
  155.1 1.9 collective-permute-start.14
  157.1 7.4 %collective-permute-start.16 = (bf16[16,3584]{1,0:T(8,128)(2,1)S(1)}, bf16[16,3584]{1,0:T(8,128)(2,1)S(1)}, u32[]{:S(2)}, u32[]{:S(2)}) collective-permute-start(bf16[16,3584]{1,0:T(8,128)(2,1)S(1)} %get-tuple-element.33), channel_id=1, source_target_pairs={{32,4},{33,5},{34,6},{35,7},{36,0},{37,1},{38,2},{39,3},{40,12},{4... | collective-permute-start | bytes 344072 | tf_op jit(solution)/shard_map/backward_home/ppermute | solution.py:56
  164.5 5.4 %collective-permute-done.11 = bf16[16,3584]{1,0:T(8,128)(2,1)S(1)} collective-permute-done((bf16[16,3584]{1,0:T(8,128)(2,1)S(1)}, bf16[16,3584]{1,0:T(8,128)(2,1)S(1)}, u32[]{:S(2)}, u32[]{:S(2)}) %collective-permute-start.11) | collective-permute-done | bytes 114720 | tf_op jit(solution)/shard_map/forward_home/ppermute | solution.py:56
  169.9 1.9 collective-permute-start.15
  171.8 1.9 collective-permute-start.13
  173.7 0.7 fusion.8
  174.4 4.2 %collective-permute-done.14 = bf16[16,3584]{1,0:T(8,128)(2,1)S(1)} collective-permute-done((bf16[16,3584]{1,0:T(8,128)(2,1)S(1)}, bf16[16,3584]{1,0:T(8,128)(2,1)S(1)}, u32[]{:S(2)}, u32[]{:S(2)}) %collective-permute-start.14) | collective-permute-done | bytes 114720 | tf_op jit(solution)/shard_map/backward_home/ppermute | solution.py:56
  178.6 13.5 %collective-permute-done.15 = bf16[16,3584]{1,0:T(8,128)(2,1)S(1)} collective-permute-done((bf16[16,3584]{1,0:T(8,128)(2,1)S(1)}, bf16[16,3584]{1,0:T(8,128)(2,1)S(1)}, u32[]{:S(2)}, u32[]{:S(2)}) %collective-permute-start.15) | collective-permute-done | bytes 114720 | tf_op jit(solution)/shard_map/backward_home/ppermute | solution.py:56
  192.5 0.7 fusion.9
  (53 shorter events, 4.6 us)
Async XLA Ops:
  2.5 13.3 %copy-start = (bf16[1,3584,256]{2,1,0:T(8,128)(2,1)S(1)}, bf16[1,3584,256]{2,1,0:T(8,128)(2,1)}, u32[]{:S(2)}) copy-start(bf16[1,3584,256]{2,1,0:T(8,128)(2,1)} %param.12) | copy-start | bytes 5505028
  3.7 79.7 %all-to-all-start = ((bf16[4,16,10880]{2,1,0:T(8,128)(2,1)}), bf16[4,16,10880]{2,1,0:T(8,128)(2,1)S(1)}, u32[]{:S(2)}, u32[]{:S(2)}) async-start(bf16[4,16,10880]{2,1,0:T(8,128)(2,1)} %broadcast_in_dim.104), calls=%async_computation | async-start | bytes 2785280 | tf_op jit(solution)/shard_map/gather_rows/all_to_all | solution.py:34
  15.8 65.4 %collective-permute-start.1 = (bf16[3584,256]{1,0:T(8,128)(2,1)S(1)}, bf16[3584,256]{1,0:T(8,128)(2,1)S(1)}, u32[]{:S(2)}, u32[]{:S(2)}) collective-permute-start(bf16[3584,256]{1,0:T(8,128)(2,1)S(1)} %bitcast.46), channel_id=1, source_target_pairs={{0,24},{1,9},{2,26},{3,11},{4,28},{5,13},{6,30},{7,15},{8,0},{9,17... | collective-permute-start | bytes 5505032 | tf_op jit(solution)/shard_map/gather_weights/ppermute | solution.py:40
  19.0 64.5 %collective-permute-start = (bf16[3584,256]{1,0:T(8,128)(2,1)S(1)}, bf16[3584,256]{1,0:T(8,128)(2,1)}, u32[]{:S(2)}, u32[]{:S(2)}) collective-permute-start(bf16[3584,256]{1,0:T(8,128)(2,1)S(1)} %bitcast.47), channel_id=1, source_target_pairs={{0,8},{1,25},{2,10},{3,27},{4,12},{5,29},{6,14},{7,31},{8,16},{9,1... | collective-permute-start | bytes 5505032 | tf_op jit(solution)/shard_map/gather_weights/ppermute | solution.py:40
  22.3 52.1 %collective-permute-start.3 = (bf16[128,3584]{1,0:T(8,128)(2,1)}, bf16[128,3584]{1,0:T(8,128)(2,1)S(1)}, u32[]{:S(2)}, u32[]{:S(2)}) collective-permute-start(bf16[128,3584]{1,0:T(8,128)(2,1)} %bitcast.48), channel_id=1, source_target_pairs={{0,24},{1,9},{2,26},{3,11},{4,28},{5,13},{6,30},{7,15},{8,0},{9,17... | collective-permute-start | bytes 2752520 | tf_op jit(solution)/shard_map/gather_weights/ppermute | solution.py:40
  24.3 56.9 %collective-permute-start.2 = (bf16[128,3584]{1,0:T(8,128)(2,1)}, bf16[128,3584]{1,0:T(8,128)(2,1)S(1)}, u32[]{:S(2)}, u32[]{:S(2)}) collective-permute-start(bf16[128,3584]{1,0:T(8,128)(2,1)} %bitcast.49), channel_id=1, source_target_pairs={{0,8},{1,25},{2,10},{3,27},{4,12},{5,29},{6,14},{7,31},{8,16},{9,1... | collective-permute-start | bytes 2752520 | tf_op jit(solution)/shard_map/gather_weights/ppermute | solution.py:40
  74.5 6.8 %copy-start.5 = (bf16[128,3584]{1,0:T(8,128)(2,1)}, bf16[128,3584]{1,0:T(8,128)(2,1)S(1)}, u32[]{:S(2)}) copy-start(bf16[128,3584]{1,0:T(8,128)(2,1)S(1)} %collective-permute-done.3) | copy-start | bytes 2752516
  81.2 1.0 copy-start.3
  82.2 1.2 copy-start.1
  83.4 11.9 %collective-permute-start.4 = (bf16[64,10880]{1,0:T(8,128)(2,1)S(1)}, bf16[64,10880]{1,0:T(8,128)(2,1)}, u32[]{:S(2)}, u32[]{:S(2)}) collective-permute-start(bf16[64,10880]{1,0:T(8,128)(2,1)S(1)} %bitcast.43), channel_id=1, source_target_pairs={{0,1},{1,0},{2,3},{3,2},{4,5},{5,4},{6,7},{7,6},{8,9},{9,8},{10,11... | collective-permute-start | bytes 4177928 | tf_op jit(solution)/shard_map/gather_rows/ppermute | solution.py:44
  88.4 35.1 %collective-permute-start.6 = (bf16[128,3584]{1,0:T(8,128)(2,1)}, bf16[128,3584]{1,0:T(8,128)(2,1)S(1)}, u32[]{:S(2)}, u32[]{:S(2)}) collective-permute-start(bf16[128,3584]{1,0:T(8,128)(2,1)} %copy-done.3), channel_id=1, source_target_pairs={{0,8},{1,25},{2,10},{3,27},{4,12},{5,29},{6,14},{7,31},{8,16},{9,1... | collective-permute-start | bytes 2752520 | tf_op jit(solution)/shard_map/gather_rows/ppermute | solution.py:40
  92.7 30.3 %collective-permute-start.5 = (bf16[3584,256]{1,0:T(8,128)(2,1)}, bf16[3584,256]{1,0:T(8,128)(2,1)S(1)}, u32[]{:S(2)}, u32[]{:S(2)}) collective-permute-start(bf16[3584,256]{1,0:T(8,128)(2,1)} %collective-permute-done), channel_id=1, source_target_pairs={{0,8},{1,25},{2,10},{3,27},{4,12},{5,29},{6,14},{7,31},{8,16},{9,1... | collective-permute-start | bytes 5505032 | tf_op jit(solution)/shard_map/gather_rows/ppermute | solution.py:40
  101.0 1.5 copy-start.2
  102.3 1.2 copy-start.7
  103.9 1.2 copy-start.4
  106.2 1.2 copy-start.6
  123.9 7.2 %collective-permute-start.7 = (bf16[64,3584]{1,0:T(8,128)(2,1)S(1)}, bf16[64,3584]{1,0:T(8,128)(2,1)S(1)}, u32[]{:S(2)}, u32[]{:S(2)}) collective-permute-start(bf16[64,3584]{1,0:T(8,128)(2,1)S(1)} %slice.91), channel_id=1, source_target_pairs={{0,1},{1,0},{2,3},{3,2},{4,5},{5,4},{6,7},{7,6},{8,9},{9,8},{10,11... | collective-permute-start | bytes 1376264 | tf_op jit(solution)/shard_map/forward_home/ppermute | solution.py:44
  129.1 20.4 %copy-start.8 = (bf16[1,16,3584]{2,1,0:T(8,128)(2,1)S(1)}, bf16[1,16,3584]{2,1,0:T(8,128)(2,1)}, u32[]{:S(2)}) copy-start(bf16[1,16,3584]{2,1,0:T(8,128)(2,1)} %param.9) | copy-start | bytes 344068
  129.2 25.7 %collective-permute-start.12 = (bf16[64,3584]{1,0:T(8,128)(2,1)S(1)}, bf16[64,3584]{1,0:T(8,128)(2,1)S(1)}, u32[]{:S(2)}, u32[]{:S(2)}) collective-permute-start(bf16[64,3584]{1,0:T(8,128)(2,1)S(1)} %slice.90), channel_id=1, source_target_pairs={{0,1},{1,0},{2,3},{3,2},{4,5},{5,4},{6,7},{7,6},{8,9},{9,8},{10,11... | collective-permute-start | bytes 1376264 | tf_op jit(solution)/shard_map/backward_home/ppermute | solution.py:44
  131.2 23.8 %copy-start.9 = (bf16[1,16,3584]{2,1,0:T(8,128)(2,1)S(1)}, bf16[1,16,3584]{2,1,0:T(8,128)(2,1)}, u32[]{:S(2)}) copy-start(bf16[1,16,3584]{2,1,0:T(8,128)(2,1)} %param.11) | copy-start | bytes 344068
  131.3 25.7 %collective-permute-start.9 = (bf16[16,3584]{1,0:T(8,128)(2,1)S(1)}, bf16[16,3584]{1,0:T(8,128)(2,1)S(1)}, u32[]{:S(2)}, u32[]{:S(2)}) collective-permute-start(bf16[16,3584]{1,0:T(8,128)(2,1)S(1)} %get-tuple-element.35), channel_id=1, source_target_pairs={{0,34},{1,39},{2,36},{3,33},{4,38},{5,35},{6,32},{7,37},{8,42},{9,... | collective-permute-start | bytes 344072 | tf_op jit(solution)/shard_map/forward_home/ppermute | solution.py:56
  139.1 30.8 %collective-permute-start.11 = (bf16[16,3584]{1,0:T(8,128)(2,1)S(1)}, bf16[16,3584]{1,0:T(8,128)(2,1)S(1)}, u32[]{:S(2)}, u32[]{:S(2)}) collective-permute-start(bf16[16,3584]{1,0:T(8,128)(2,1)S(1)} %get-tuple-element.36), channel_id=1, source_target_pairs={{0,36},{1,37},{2,38},{3,39},{4,32},{5,33},{6,34},{7,35},{8,44},{9,... | collective-permute-start | bytes 344072 | tf_op jit(solution)/shard_map/forward_home/ppermute | solution.py:56
  143.1 28.6 %collective-permute-start.10 = (bf16[16,3584]{1,0:T(8,128)(2,1)S(1)}, bf16[16,3584]{1,0:T(8,128)(2,1)S(1)}, u32[]{:S(2)}, u32[]{:S(2)}) collective-permute-start(bf16[16,3584]{1,0:T(8,128)(2,1)S(1)} %get-tuple-element.37), channel_id=1, source_target_pairs={{0,38},{1,35},{2,32},{3,37},{4,34},{5,39},{6,36},{7,33},{8,46},{9,... | collective-permute-start | bytes 344072 | tf_op jit(solution)/shard_map/forward_home/ppermute | solution.py:56
  149.6 24.2 %collective-permute-start.8 = (f32[16,3584]{1,0:T(8,128)S(1)}, f32[16,3584]{1,0:T(8,128)S(1)}, u32[]{:S(2)}, u32[]{:S(2)}) collective-permute-start(f32[16,3584]{1,0:T(8,128)S(1)} %convert_add_fusion.1), channel_id=1, source_target_pairs={{0,32},{1,33},{2,34},{3,35},{4,36},{5,37},{6,38},{7,39},{8,40},{9,... | collective-permute-start | bytes 688136 | tf_op jit(solution)/shard_map/forward_home/ppermute | solution.py:56
  155.1 23.5 %collective-permute-start.14 = (bf16[16,3584]{1,0:T(8,128)(2,1)S(1)}, bf16[16,3584]{1,0:T(8,128)(2,1)S(1)}, u32[]{:S(2)}, u32[]{:S(2)}) collective-permute-start(bf16[16,3584]{1,0:T(8,128)(2,1)S(1)} %get-tuple-element.32), channel_id=1, source_target_pairs={{32,2},{33,7},{34,4},{35,1},{36,6},{37,3},{38,0},{39,5},{40,10},{4... | collective-permute-start | bytes 344072 | tf_op jit(solution)/shard_map/backward_home/ppermute | solution.py:56
  157.1 21.6 %collective-permute-start.16 = (bf16[16,3584]{1,0:T(8,128)(2,1)S(1)}, bf16[16,3584]{1,0:T(8,128)(2,1)S(1)}, u32[]{:S(2)}, u32[]{:S(2)}) collective-permute-start(bf16[16,3584]{1,0:T(8,128)(2,1)S(1)} %get-tuple-element.33), channel_id=1, source_target_pairs={{32,4},{33,5},{34,6},{35,7},{36,0},{37,1},{38,2},{39,3},{40,12},{4... | collective-permute-start | bytes 344072 | tf_op jit(solution)/shard_map/backward_home/ppermute | solution.py:56
  169.9 22.3 %collective-permute-start.15 = (bf16[16,3584]{1,0:T(8,128)(2,1)S(1)}, bf16[16,3584]{1,0:T(8,128)(2,1)S(1)}, u32[]{:S(2)}, u32[]{:S(2)}) collective-permute-start(bf16[16,3584]{1,0:T(8,128)(2,1)S(1)} %get-tuple-element.34), channel_id=1, source_target_pairs={{32,6},{33,3},{34,0},{35,5},{36,2},{37,7},{38,4},{39,1},{40,14},{4... | collective-permute-start | bytes 344072 | tf_op jit(solution)/shard_map/backward_home/ppermute | solution.py:56
  171.8 20.7 %collective-permute-start.13 = (f32[16,3584]{1,0:T(8,128)S(1)}, f32[16,3584]{1,0:T(8,128)S(1)}, u32[]{:S(2)}, u32[]{:S(2)}) collective-permute-start(f32[16,3584]{1,0:T(8,128)S(1)} %convert_add_fusion), channel_id=1, source_target_pairs={{32,0},{33,1},{34,2},{35,3},{36,4},{37,5},{38,6},{39,7},{40,8},{41... | collective-permute-start | bytes 688136 | tf_op jit(solution)/shard_map/backward_home/ppermute | solution.py:56

commit v6 on v5

--- a/solution.py
+++ b/solution.py
@@ -26,13 +26,9 @@
     return 1 - 2 * core
 
 
-def gather_z(block):
-    groups = [
-        [expert_index(x, z, c) for z in range(Z)] for x in range(EXPERTS) for c in range(CORES)
-    ]
-    blocks = jnp.broadcast_to(block[None], (Z,) + block.shape)
-    blocks = lax.all_to_all(blocks, "expert", 0, 0, axis_index_groups=groups, tiled=True)
-    return blocks.reshape(Z * block.shape[0], block.shape[1])
+def along_z(block, distance):
+    route = expert_route(lambda x, z, c: (x, (z + distance * turn(c)) % Z, c))
+    return lax.ppermute(block, "expert", route)
 
 
 def along_x(block, distance):
@@ -101,11 +97,11 @@
 def forward_rows(rows, gate_up, down):
     gate_val, up_val = jnp.split(dot(rows, gate_up), 2, axis=1)
     hidden = (jax.nn.silu(gate_val) * up_val).astype(jnp.bfloat16)
-    return dot(hidden, down)
+    return dot_t(hidden, down)
 
 
 def backward_rows(rows, grads, gate_up, down):
-    hidden_grad = dot_t(grads, down)
+    hidden_grad = dot(grads, down)
     gate_val, up_val = jnp.split(dot(rows, gate_up), 2, axis=1)
     sig = jax.nn.sigmoid(gate_val)
     gate_grad = hidden_grad * up_val * sig * (1.0 + gate_val * (1.0 - sig))
@@ -114,17 +110,12 @@
     return dot_t(grad, gate_up)
 
 
-def send_home(mixture, residual, step, place, turned):
-    rows = residual.shape[0]
-    total = 0.0
-    for distance in (0, 1, -1, 2):
-        owner = (place + Z + distance * turned) % Z
-        block = lax.dynamic_slice_in_dim(mixture, owner * rows, rows, axis=0)
-        if distance == 0:
-            part = to_section(block + residual.astype(jnp.float32), step, 0)
-        else:
-            part = to_section(block.astype(jnp.bfloat16), step, distance)
-        total = total + part.astype(jnp.float32)
+def send_home(mixture, residual, passed, step):
+    own, near, far = jnp.split(mixture, Z, axis=0)[:3]
+    near = near + passed.astype(jnp.float32)
+    total = to_section(own + residual.astype(jnp.float32), step, 0)
+    total = total + to_section(far.astype(jnp.bfloat16), step, 1).astype(jnp.float32)
+    total = total + to_section(near.astype(jnp.bfloat16), step, -1).astype(jnp.float32)
     return total.astype(jnp.bfloat16)
 
 
@@ -143,23 +134,25 @@
     rows, model = tokens.shape
     index = lax.axis_index("expert")
     turned = 1 - 2 * (index % CORES)
-    place = index // CORES % Z
     me = index // (Z * CORES)
     experts = [(me + EXPERTS + d * turned) % EXPERTS for d in (0, -1, 1, -2)]
 
     with jax.named_scope("gather_weights"):
-        gate_up, down = gate_up_weight[0], down_weight[0]
-        near = [along_x(gate_up, 1), along_x(gate_up, -1), along_x(down, 1), along_x(down, -1)]
+        weights = jnp.concatenate([gate_up_weight[0], down_weight[0].T], axis=1)
+        near, far = along_x(weights, 1), along_x(weights, -1)
     with jax.named_scope("gather_rows"):
         shares = [
             expert_shares(expert_hot(forward_routes[0]), forward_gates[0]),
             expert_shares(expert_hot(backward_routes[0]), backward_gates[0]),
         ]
         side = side_columns(jnp.concatenate(shares, axis=1))
-        mine = gather_z(jnp.concatenate([tokens, saved, upstream, side], axis=1))
-        mine, *near = together(mine, *near)
-        gate_ups = [gate_up, near[0], near[1], along_x(near[0], 1)]
-        downs = [down, near[2], near[3], along_x(near[2], 1)]
+        mine = jnp.concatenate([tokens, saved, upstream, side], axis=1)
+        below, above = along_z(mine, 1), along_z(mine, -1)
+        opposite = along_z(below, 1)
+    with jax.named_scope("gather_opposite"):
+        near, far, below, above, opposite = together(near, far, below, above, opposite)
+        weights = [weights, near, far, along_x(near, 1)]
+        mine = jnp.concatenate([mine, below, above, opposite], axis=0)
         both = [mine, other_core(mine)]
         cuts = (0, model, 2 * model, 3 * model, 3 * model + LANES)
         token_rows, saved_rows, upstream_rows, sides = [
@@ -169,20 +162,25 @@
         shares = side_values(sides)
     with jax.named_scope("experts"):
         forward_sum = backward_sum = 0.0
-        for expert, gate_up, down in zip(experts, gate_ups, downs):
+        width = gate_up_weight.shape[2]
+        for expert, weight in zip(experts, weights):
+            gate_up, down = weight[:, :width], weight[:, width:]
             out = forward_rows(token_rows, gate_up, down)
             forward_sum = forward_sum + column_of(shares[:, :EXPERTS], expert) * out
             out = backward_rows(saved_rows, upstream_rows, gate_up, down)
             backward_sum = backward_sum + column_of(shares[:, EXPERTS:], expert) * out
     half = Z * rows
-    with jax.named_scope("forward_home"):
-        other = other_core(forward_sum[half:].astype(jnp.bfloat16)).astype(jnp.float32)
-        mixture = forward_sum[:half] + other
-        forward_next = send_home(mixture, tokens, 1, place, turned)
-    with jax.named_scope("backward_home"):
-        other = other_core(backward_sum[half:].astype(jnp.bfloat16)).astype(jnp.float32)
-        mixture = backward_sum[:half] + other
-        backward_next = send_home(mixture, upstream, -1, place, turned)
+    with jax.named_scope("cores"):
+        others = [
+            other_core(total[half:].astype(jnp.bfloat16)) for total in (forward_sum, backward_sum)
+        ]
+        mixture = forward_sum[:half] + others[0].astype(jnp.float32)
+        back_mixture = backward_sum[:half] + others[1].astype(jnp.float32)
+    with jax.named_scope("home"):
+        passed = [total[half - rows :] for total in (mixture, back_mixture)]
+        passed = along_z(jnp.concatenate(passed, axis=1).astype(jnp.bfloat16), -1)
+        forward_next = send_home(mixture, tokens, passed[:, :model], 1)
+        backward_next = send_home(back_mixture, upstream, passed[:, model:], -1)
     return (forward_next[None], backward_next[None])
 
 

time: 194 us -> 181 us (0.933)
  the two profiles are of different devices: /device:TPU:105 before, /device:TPU:24 now
where the time goes in v6:
time: 181 us; the launch traced here: 179 us
  starting transfers between devices  99.3 us (55%)
  waiting for transfers between devices  45.6 us (25%)
  matrix products  23.3 us (13%)
  other arithmetic  4.96 us (3%)
  local copies, waits for them, and re-layouts  4.24 us (2%)
    ppermute x4, starting transfers between devices, along_z(): return lax.ppermute(block, 'expert', route)  52.3 us
    ppermute x6, starting transfers between devices, to_section(): return lax.ppermute(block, ('pipe', 'expert'), route)  31.5 us
    ppermute x4, waiting for transfers between devices, along_z(): return lax.ppermute(block, 'expert', route)  24 us
    dot_general x12, matrix products, dot(): return jnp.dot(a, b, preferred_element_type=jnp.float32)  13.3 us
    ppermute x3, waiting for transfers between devices, along_x(): return lax.ppermute(block, 'expert', route)  10.1 us
    dot_general x8, matrix products, dot_t(): lax.dot_general(a, b, (((1,), (1,)), ((), ())), preferred_element_type=jn...  9.96 us
    ppermute x6, waiting for transfers between devices, to_section(): return lax.ppermute(block, ('pipe', 'expert'), route)  9.88 us
    ppermute x3, starting transfers between devices, along_x(): return lax.ppermute(block, 'expert', route)  9.24 us
  transfers between devices with their start and end apart: 16, of which 9 were waited for; matrix products, arithmetic and copies ran while one was open for 15% of the time, Pallas kernels for 0%

profile of v6, /device:TPU:24, one launch (start us, length us, event | category | flops | bytes accessed | tf_op | source)
XLA Modules:
  0.0 178.7 jit_solution(9841772962312258263)
XLA Ops:
  0.6 1.7 copy.36
  2.5 1.8 %pad_maximum_fusion = bf16[3584,384]{1,0:T(8,128)(2,1)} fusion(bf16[3584,128]{1,0:T(8,128)(2,1)S(1)} %copy.36, bf16[3584,256]{1,0:T(8,128)(2,1)S(1)} %bitcast.29), kind=kLoop, calls=%fused_computation.14 | loop fusion | flops 5505024 | bytes 5505024 | tf_op jit(solution)/shard_map/gather_weights/concatenate | solution.py:141
  4.3 4.7 %collective-permute-start.1 = (bf16[3584,384]{1,0:T(8,128)(2,1)}, bf16[3584,384]{1,0:T(8,128)(2,1)}, u32[]{:S(2)}, u32[]{:S(2)}) collective-permute-start(bf16[3584,384]{1,0:T(8,128)(2,1)} %pad_maximum_fusion), channel_id=1, source_target_pairs={{0,24},{1,9},{2,26},{3,11},{4,28},{5,13},{6,30},{7,15},{8,0},{9,17... | collective-permute-start | bytes 8257544 | tf_op jit(solution)/shard_map/gather_weights/ppermute | solution.py:36
  8.9 1.9 %collective-permute-start = (bf16[3584,384]{1,0:T(8,128)(2,1)}, bf16[3584,384]{1,0:T(8,128)(2,1)}, u32[]{:S(2)}, u32[]{:S(2)}) collective-permute-start(bf16[3584,384]{1,0:T(8,128)(2,1)} %pad_maximum_fusion), channel_id=1, source_target_pairs={{0,8},{1,25},{2,10},{3,27},{4,12},{5,29},{6,14},{7,31},{8,16},{9,1... | collective-permute-start | bytes 8257544 | tf_op jit(solution)/shard_map/gather_weights/ppermute | solution.py:36
  11.1 9.1 %collective-permute-start.2 = (bf16[16,10880]{1,0:T(8,128)(2,1)S(1)}, bf16[16,10880]{1,0:T(8,128)(2,1)S(1)}, u32[]{:S(2)}, u32[]{:S(2)}) collective-permute-start(bf16[16,10880]{1,0:T(8,128)(2,1)S(1)} %pad_maximum_fusion.5), channel_id=1, source_target_pairs={{0,2},{1,7},{2,4},{3,1},{4,6},{5,3},{6,0},{7,5},{8,10},{9,15},{10,... | collective-permute-start | bytes 1044488 | tf_op jit(solution)/shard_map/gather_rows/ppermute | solution.py:31
  20.2 5.6 %collective-permute-start.3 = (bf16[16,10880]{1,0:T(8,128)(2,1)S(1)}, bf16[16,10880]{1,0:T(8,128)(2,1)S(1)}, u32[]{:S(2)}, u32[]{:S(2)}) collective-permute-start(bf16[16,10880]{1,0:T(8,128)(2,1)S(1)} %pad_maximum_fusion.5), channel_id=1, source_target_pairs={{0,6},{1,3},{2,0},{3,5},{4,2},{5,7},{6,4},{7,1},{8,14},{9,11},{10,... | collective-permute-start | bytes 1044488 | tf_op jit(solution)/shard_map/gather_rows/ppermute | solution.py:31
  25.8 3.6 %collective-permute-done.2 = bf16[16,10880]{1,0:T(8,128)(2,1)S(1)} collective-permute-done((bf16[16,10880]{1,0:T(8,128)(2,1)S(1)}, bf16[16,10880]{1,0:T(8,128)(2,1)S(1)}, u32[]{:S(2)}, u32[]{:S(2)}) %collective-permute-start.2) | collective-permute-done | bytes 348192 | tf_op jit(solution)/shard_map/gather_rows/ppermute | solution.py:31
  29.4 30.4 %collective-permute-start.4 = (bf16[16,10880]{1,0:T(8,128)(2,1)S(1)}, bf16[16,10880]{1,0:T(8,128)(2,1)S(1)}, u32[]{:S(2)}, u32[]{:S(2)}) collective-permute-start(bf16[16,10880]{1,0:T(8,128)(2,1)S(1)} %collective-permute-done.2), channel_id=1, source_target_pairs={{0,2},{1,7},{2,4},{3,1},{4,6},{5,3},{6,0},{7,5},{8,10},{9,15},{10,... | collective-permute-start | bytes 1044488 | tf_op jit(solution)/shard_map/gather_rows/ppermute | solution.py:31
  59.8 14.8 %collective-permute-done.4 = bf16[16,10880]{1,0:T(8,128)(2,1)S(1)} collective-permute-done((bf16[16,10880]{1,0:T(8,128)(2,1)S(1)}, bf16[16,10880]{1,0:T(8,128)(2,1)S(1)}, u32[]{:S(2)}, u32[]{:S(2)}) %collective-permute-start.4) | collective-permute-done | bytes 348192 | tf_op jit(solution)/shard_map/gather_rows/ppermute | solution.py:31
  74.7 1.0 pad_maximum_fusion.1
  75.7 1.9 %collective-permute-start.5 = (bf16[64,10880]{1,0:T(8,128)(2,1)S(1)}, bf16[64,10880]{1,0:T(8,128)(2,1)}, u32[]{:S(2)}, u32[]{:S(2)}) collective-permute-start(bf16[64,10880]{1,0:T(8,128)(2,1)S(1)} %pad_maximum_fusion.1), channel_id=1, source_target_pairs={{0,1},{1,0},{2,3},{3,2},{4,5},{5,4},{6,7},{7,6},{8,9},{9,8},{10,11... | collective-permute-start | bytes 4177928 | tf_op jit(solution)/shard_map/gather_opposite/ppermute | solution.py:40
  77.7 2.7 %collective-permute-start.6 = (bf16[3584,384]{1,0:T(8,128)(2,1)}, bf16[3584,384]{1,0:T(8,128)(2,1)S(1)}, u32[]{:S(2)}, u32[]{:S(2)}) collective-permute-start(bf16[3584,384]{1,0:T(8,128)(2,1)} %collective-permute-done), channel_id=1, source_target_pairs={{0,8},{1,25},{2,10},{3,27},{4,12},{5,29},{6,14},{7,31},{8,16},{9,1... | collective-permute-start | bytes 8257544 | tf_op jit(solution)/shard_map/gather_opposite/ppermute | solution.py:36
  80.8 1.4 fusion.91
  82.2 1.9 %fusion.17 = f32[128,256]{1,0:T(8,128)S(1)} fusion(bf16[3584,384]{1,0:T(8,128)(2,1)} %collective-permute-done, bf16[64,3584]{1,0:T(8,128)(2,1)S(1)} %get-tuple-element.33, bf16[64,3584]{1,0:T(8,128)(2,1)S(1)} %get-tuple-element.30), kind=kOutput, calls=%fused_computation.26 | convolution fusion | flops 236716032 | bytes 2883584 | tf_op jit(solution)/shard_map/experts/dot_general | solution.py:90
  84.1 0.4 fusion.80
  84.6 1.9 %fusion.12 = f32[128,256]{1,0:T(8,128)S(1)} fusion(bf16[3584,384]{1,0:T(8,128)(2,1)} %collective-permute-done.1, bf16[64,3584]{1,0:T(8,128)(2,1)S(1)} %get-tuple-element.33, bf16[64,3584]{1,0:T(8,128)(2,1)S(1)} %get-tuple-element.30), kind=kOutput, calls=%fused_computation.21 | convolution fusion | flops 236716032 | bytes 2883584 | tf_op jit(solution)/shard_map/experts/dot_general | solution.py:90
  86.5 1.6 fusion.45
  88.1 1.7 fusion.42
  89.8 0.4 fusion.48
  90.2 0.7 slice.111
  90.9 1.9 %fusion.19 = f32[128,256]{1,0:T(8,128)S(1)} fusion(bf16[3584,384]{1,0:T(8,128)(2,1)} %collective-permute-done, bf16[64,3584]{1,0:T(8,128)(2,1)S(1)} %get-tuple-element.35, bf16[64,3584]{1,0:T(8,128)(2,1)S(1)} %get-tuple-element.32), kind=kOutput, calls=%fused_computation.28 | convolution fusion | flops 236716032 | bytes 2883584 | tf_op jit(solution)/shard_map/experts/dot_general | solution.py:90
  93.2 1.9 %fusion.14 = f32[128,256]{1,0:T(8,128)S(1)} fusion(bf16[3584,384]{1,0:T(8,128)(2,1)} %collective-permute-done.1, bf16[64,3584]{1,0:T(8,128)(2,1)S(1)} %get-tuple-element.35, bf16[64,3584]{1,0:T(8,128)(2,1)S(1)} %get-tuple-element.32), kind=kOutput, calls=%fused_computation.23 | convolution fusion | flops 236716032 | bytes 2883584 | tf_op jit(solution)/shard_map/experts/dot_general | solution.py:90
  95.1 0.4 fusion.82
  95.9 0.7 convolution_multiply_fusion.3
  96.7 1.6 fusion.5
  98.3 1.6 fusion.4
  99.9 2.3 %fusion.2 = f32[128,3584]{1,0:T(8,128)S(1)} fusion(f32[128,3584]{1,0:T(8,128)S(1)} %convolution_multiply_fusion.3, bf16[3584,384]{1,0:T(8,128)(2,1)} %collective-permute-done, f32[128]{0:T(128)S(1)} %get-tuple-element.21, bf16[128,128]{1,0:T(8,128)(2,1)S(1)} %get-tuple-element.49, bf16[128,128]{1,0:T(8,128)(2,1)S(1)} %get-tuple-element.48), kind=kOutput, calls=%fused_computation.5 | convolution fusion | flops 235929600 | bytes 5571072 | tf_op jit(solution)/shard_map/experts/dot_general | solution.py:94
  102.1 2.3 %fusion.1 = f32[128,3584]{1,0:T(8,128)S(1)} fusion(f32[128,3584]{1,0:T(8,128)S(1)} %fusion.2, bf16[3584,384]{1,0:T(8,128)(2,1)} %collective-permute-done.1, f32[128]{0:T(128)S(1)} %get-tuple-element.23, bf16[128,128]{1,0:T(8,128)(2,1)S(1)} %get-tuple-element.47, bf16[128,128]{1,0:T(8,128)(2,1)S(1)} %get-tuple-element.46), kind=kOutput, calls=%fused_computation.3 | convolution fusion | flops 235929600 | bytes 5571072 | tf_op jit(solution)/shard_map/experts/dot_general | solution.py:94
  104.4 10.1 %collective-permute-done.6 = bf16[3584,384]{1,0:T(8,128)(2,1)S(1)} collective-permute-done((bf16[3584,384]{1,0:T(8,128)(2,1)}, bf16[3584,384]{1,0:T(8,128)(2,1)S(1)}, u32[]{:S(2)}, u32[]{:S(2)}) %collective-permute-start.6) | collective-permute-done | bytes 2752544 | tf_op jit(solution)/shard_map/gather_opposite/ppermute | solution.py:36
  114.5 0.4 fusion.9
  115.4 1.9 %collective-permute-start.7 = (bf16[64,3584]{1,0:T(8,128)(2,1)S(1)}, bf16[64,3584]{1,0:T(8,128)(2,1)S(1)}, u32[]{:S(2)}, u32[]{:S(2)}) collective-permute-start(bf16[64,3584]{1,0:T(8,128)(2,1)S(1)} %slice.175), channel_id=1, source_target_pairs={{0,1},{1,0},{2,3},{3,2},{4,5},{5,4},{6,7},{7,6},{8,9},{9,8},{10,11... | collective-permute-start | bytes 1376264 | tf_op jit(solution)/shard_map/cores/ppermute | solution.py:40
  117.3 0.4 fusion.7
  118.1 0.7 fusion
  118.9 2.4 %collective-permute-start.10 = (bf16[64,3584]{1,0:T(8,128)(2,1)S(1)}, bf16[64,3584]{1,0:T(8,128)(2,1)S(1)}, u32[]{:S(2)}, u32[]{:S(2)}) collective-permute-start(bf16[64,3584]{1,0:T(8,128)(2,1)S(1)} %slice.174), channel_id=1, source_target_pairs={{0,1},{1,0},{2,3},{3,2},{4,5},{5,4},{6,7},{7,6},{8,9},{9,8},{10,11... | collective-permute-start | bytes 1376264 | tf_op jit(solution)/shard_map/cores/ppermute | solution.py:40
  121.5 1.3 collective-permute-done.10
  122.9 7.2 %collective-permute-start.11 = (bf16[16,7168]{1,0:T(8,128)(2,1)S(1)}, bf16[16,7168]{1,0:T(8,128)(2,1)S(1)}, u32[]{:S(2)}, u32[]{:S(2)}) collective-permute-start(bf16[16,7168]{1,0:T(8,128)(2,1)S(1)} %pad_maximum_fusion.6), channel_id=1, source_target_pairs={{0,6},{1,3},{2,0},{3,5},{4,2},{5,7},{6,4},{7,1},{8,14},{9,11},{10,... | collective-permute-start | bytes 688136 | tf_op jit(solution)/shard_map/home/ppermute | solution.py:31
  130.2 1.9 %collective-permute-start.9 = (bf16[16,3584]{1,0:T(8,128)(2,1)S(1)}, bf16[16,3584]{1,0:T(8,128)(2,1)S(1)}, u32[]{:S(2)}, u32[]{:S(2)}) collective-permute-start(bf16[16,3584]{1,0:T(8,128)(2,1)S(1)} %get-tuple-element.42), channel_id=1, source_target_pairs={{0,34},{1,39},{2,36},{3,33},{4,38},{5,35},{6,32},{7,37},{8,42},{9,... | collective-permute-start | bytes 344072 | tf_op jit(solution)/shard_map/home/ppermute | solution.py:52
  132.1 9.8 %collective-permute-start.14 = (bf16[16,3584]{1,0:T(8,128)(2,1)S(1)}, bf16[16,3584]{1,0:T(8,128)(2,1)S(1)}, u32[]{:S(2)}, u32[]{:S(2)}) collective-permute-start(bf16[16,3584]{1,0:T(8,128)(2,1)S(1)} %get-tuple-element.40), channel_id=1, source_target_pairs={{32,2},{33,7},{34,4},{35,1},{36,6},{37,3},{38,0},{39,5},{40,10},{4... | collective-permute-start | bytes 344072 | tf_op jit(solution)/shard_map/home/ppermute | solution.py:52
  141.9 5.6 %collective-permute-done.11 = bf16[16,7168]{1,0:T(8,128)(2,1)S(1)} collective-permute-done((bf16[16,7168]{1,0:T(8,128)(2,1)S(1)}, bf16[16,7168]{1,0:T(8,128)(2,1)S(1)}, u32[]{:S(2)}, u32[]{:S(2)}) %collective-permute-start.11) | collective-permute-done | bytes 229408 | tf_op jit(solution)/shard_map/home/ppermute | solution.py:31
  147.6 1.9 %collective-permute-start.15 = (bf16[16,3584]{1,0:T(8,128)(2,1)S(1)}, bf16[16,3584]{1,0:T(8,128)(2,1)S(1)}, u32[]{:S(2)}, u32[]{:S(2)}) collective-permute-start(bf16[16,3584]{1,0:T(8,128)(2,1)S(1)} %get-tuple-element.37), channel_id=1, source_target_pairs={{32,6},{33,3},{34,0},{35,5},{36,2},{37,7},{38,4},{39,1},{40,14},{4... | collective-permute-start | bytes 344072 | tf_op jit(solution)/shard_map/home/ppermute | solution.py:52
  149.5 10.7 %collective-permute-start.13 = (f32[16,3584]{1,0:T(8,128)S(1)}, f32[16,3584]{1,0:T(8,128)S(1)}, u32[]{:S(2)}, u32[]{:S(2)}) collective-permute-start(f32[16,3584]{1,0:T(8,128)S(1)} %get-tuple-element.36), channel_id=1, source_target_pairs={{32,0},{33,1},{34,2},{35,3},{36,4},{37,5},{38,6},{39,7},{40,8},{41... | collective-permute-start | bytes 688136 | tf_op jit(solution)/shard_map/home/ppermute | solution.py:52
  160.2 3.2 %collective-permute-start.12 = (bf16[16,3584]{1,0:T(8,128)(2,1)S(1)}, bf16[16,3584]{1,0:T(8,128)(2,1)S(1)}, u32[]{:S(2)}, u32[]{:S(2)}) collective-permute-start(bf16[16,3584]{1,0:T(8,128)(2,1)S(1)} %get-tuple-element.39), channel_id=1, source_target_pairs={{0,38},{1,35},{2,32},{3,37},{4,34},{5,39},{6,36},{7,33},{8,46},{9,... | collective-permute-start | bytes 344072 | tf_op jit(solution)/shard_map/home/ppermute | solution.py:52
  163.5 3.9 %collective-permute-start.8 = (f32[16,3584]{1,0:T(8,128)S(1)}, f32[16,3584]{1,0:T(8,128)S(1)}, u32[]{:S(2)}, u32[]{:S(2)}) collective-permute-start(f32[16,3584]{1,0:T(8,128)S(1)} %get-tuple-element.38), channel_id=1, source_target_pairs={{0,32},{1,33},{2,34},{3,35},{4,36},{5,37},{6,38},{7,39},{8,40},{9,... | collective-permute-start | bytes 688136 | tf_op jit(solution)/shard_map/home/ppermute | solution.py:52
  167.4 1.5 collective-permute-done.13
  169.0 0.7 fusion.36
  169.7 7.0 %collective-permute-done.12 = bf16[16,3584]{1,0:T(8,128)(2,1)S(1)} collective-permute-done((bf16[16,3584]{1,0:T(8,128)(2,1)S(1)}, bf16[16,3584]{1,0:T(8,128)(2,1)S(1)}, u32[]{:S(2)}, u32[]{:S(2)}) %collective-permute-start.12) | collective-permute-done | bytes 114720 | tf_op jit(solution)/shard_map/home/ppermute | solution.py:52
  176.7 1.3 collective-permute-done.8
  178.0 0.7 fusion.35
  (51 shorter events, 2.8 us)
Async XLA Ops:
  0.6 1.8 copy-start
  2.4 8.5 %copy-start.5 = (f32[1,16,2]{1,2,0:T(2,128)S(1)}, f32[1,16,2]{1,2,0:T(2,128)}, u32[]{:S(2)}) copy-start(f32[1,16,2]{1,2,0:T(2,128)} %param.17) | copy-start | bytes 388
  2.4 8.5 %copy-start.6 = (s32[1,16,2]{1,2,0:T(2,128)S(1)}, s32[1,16,2]{1,2,0:T(2,128)}, u32[]{:S(2)}) copy-start(s32[1,16,2]{1,2,0:T(2,128)} %param.15) | copy-start | bytes 388
  2.4 8.5 %copy-start.7 = (f32[1,16,2]{1,2,0:T(2,128)S(1)}, f32[1,16,2]{1,2,0:T(2,128)}, u32[]{:S(2)}) copy-start(f32[1,16,2]{1,2,0:T(2,128)} %param.16) | copy-start | bytes 388
  2.4 8.5 %copy-start.8 = (s32[1,16,2]{1,2,0:T(2,128)S(1)}, s32[1,16,2]{1,2,0:T(2,128)}, u32[]{:S(2)}) copy-start(s32[1,16,2]{1,2,0:T(2,128)} %param.14) | copy-start | bytes 388
  2.4 8.6 %copy-start.2 = (bf16[1,16,3584]{2,1,0:T(8,128)(2,1)S(1)}, bf16[1,16,3584]{2,1,0:T(8,128)(2,1)}, u32[]{:S(2)}) copy-start(bf16[1,16,3584]{2,1,0:T(8,128)(2,1)} %param.11) | copy-start | bytes 344068
  2.4 8.6 %copy-start.3 = (bf16[1,16,3584]{2,1,0:T(8,128)(2,1)S(1)}, bf16[1,16,3584]{2,1,0:T(8,128)(2,1)}, u32[]{:S(2)}) copy-start(bf16[1,16,3584]{2,1,0:T(8,128)(2,1)} %param.9) | copy-start | bytes 344068
  2.4 8.6 %copy-start.4 = (bf16[1,16,3584]{2,1,0:T(8,128)(2,1)S(1)}, bf16[1,16,3584]{2,1,0:T(8,128)(2,1)}, u32[]{:S(2)}) copy-start(bf16[1,16,3584]{2,1,0:T(8,128)(2,1)} %param.10) | copy-start | bytes 344068
  4.3 70.4 %collective-permute-start.1 = (bf16[3584,384]{1,0:T(8,128)(2,1)}, bf16[3584,384]{1,0:T(8,128)(2,1)}, u32[]{:S(2)}, u32[]{:S(2)}) collective-permute-start(bf16[3584,384]{1,0:T(8,128)(2,1)} %pad_maximum_fusion), channel_id=1, source_target_pairs={{0,24},{1,9},{2,26},{3,11},{4,28},{5,13},{6,30},{7,15},{8,0},{9,17... | collective-permute-start | bytes 8257544 | tf_op jit(solution)/shard_map/gather_weights/ppermute | solution.py:36
  8.9 65.7 %collective-permute-start = (bf16[3584,384]{1,0:T(8,128)(2,1)}, bf16[3584,384]{1,0:T(8,128)(2,1)}, u32[]{:S(2)}, u32[]{:S(2)}) collective-permute-start(bf16[3584,384]{1,0:T(8,128)(2,1)} %pad_maximum_fusion), channel_id=1, source_target_pairs={{0,8},{1,25},{2,10},{3,27},{4,12},{5,29},{6,14},{7,31},{8,16},{9,1... | collective-permute-start | bytes 8257544 | tf_op jit(solution)/shard_map/gather_weights/ppermute | solution.py:36
  11.1 18.3 %collective-permute-start.2 = (bf16[16,10880]{1,0:T(8,128)(2,1)S(1)}, bf16[16,10880]{1,0:T(8,128)(2,1)S(1)}, u32[]{:S(2)}, u32[]{:S(2)}) collective-permute-start(bf16[16,10880]{1,0:T(8,128)(2,1)S(1)} %pad_maximum_fusion.5), channel_id=1, source_target_pairs={{0,2},{1,7},{2,4},{3,1},{4,6},{5,3},{6,0},{7,5},{8,10},{9,15},{10,... | collective-permute-start | bytes 1044488 | tf_op jit(solution)/shard_map/gather_rows/ppermute | solution.py:31
  20.2 39.6 %collective-permute-start.3 = (bf16[16,10880]{1,0:T(8,128)(2,1)S(1)}, bf16[16,10880]{1,0:T(8,128)(2,1)S(1)}, u32[]{:S(2)}, u32[]{:S(2)}) collective-permute-start(bf16[16,10880]{1,0:T(8,128)(2,1)S(1)} %pad_maximum_fusion.5), channel_id=1, source_target_pairs={{0,6},{1,3},{2,0},{3,5},{4,2},{5,7},{6,4},{7,1},{8,14},{9,11},{10,... | collective-permute-start | bytes 1044488 | tf_op jit(solution)/shard_map/gather_rows/ppermute | solution.py:31
  29.4 45.3 %collective-permute-start.4 = (bf16[16,10880]{1,0:T(8,128)(2,1)S(1)}, bf16[16,10880]{1,0:T(8,128)(2,1)S(1)}, u32[]{:S(2)}, u32[]{:S(2)}) collective-permute-start(bf16[16,10880]{1,0:T(8,128)(2,1)S(1)} %collective-permute-done.2), channel_id=1, source_target_pairs={{0,2},{1,7},{2,4},{3,1},{4,6},{5,3},{6,0},{7,5},{8,10},{9,15},{10,... | collective-permute-start | bytes 1044488 | tf_op jit(solution)/shard_map/gather_rows/ppermute | solution.py:31
  75.7 5.2 %collective-permute-start.5 = (bf16[64,10880]{1,0:T(8,128)(2,1)S(1)}, bf16[64,10880]{1,0:T(8,128)(2,1)}, u32[]{:S(2)}, u32[]{:S(2)}) collective-permute-start(bf16[64,10880]{1,0:T(8,128)(2,1)S(1)} %pad_maximum_fusion.1), channel_id=1, source_target_pairs={{0,1},{1,0},{2,3},{3,2},{4,5},{5,4},{6,7},{7,6},{8,9},{9,8},{10,11... | collective-permute-start | bytes 4177928 | tf_op jit(solution)/shard_map/gather_opposite/ppermute | solution.py:40
  77.7 36.8 %collective-permute-start.6 = (bf16[3584,384]{1,0:T(8,128)(2,1)}, bf16[3584,384]{1,0:T(8,128)(2,1)S(1)}, u32[]{:S(2)}, u32[]{:S(2)}) collective-permute-start(bf16[3584,384]{1,0:T(8,128)(2,1)} %collective-permute-done), channel_id=1, source_target_pairs={{0,8},{1,25},{2,10},{3,27},{4,12},{5,29},{6,14},{7,31},{8,16},{9,1... | collective-permute-start | bytes 8257544 | tf_op jit(solution)/shard_map/gather_opposite/ppermute | solution.py:36
  88.1 1.7 copy-start.1
  115.4 6.0 %collective-permute-start.7 = (bf16[64,3584]{1,0:T(8,128)(2,1)S(1)}, bf16[64,3584]{1,0:T(8,128)(2,1)S(1)}, u32[]{:S(2)}, u32[]{:S(2)}) collective-permute-start(bf16[64,3584]{1,0:T(8,128)(2,1)S(1)} %slice.175), channel_id=1, source_target_pairs={{0,1},{1,0},{2,3},{3,2},{4,5},{5,4},{6,7},{7,6},{8,9},{9,8},{10,11... | collective-permute-start | bytes 1376264 | tf_op jit(solution)/shard_map/cores/ppermute | solution.py:40
  118.9 3.8 %collective-permute-start.10 = (bf16[64,3584]{1,0:T(8,128)(2,1)S(1)}, bf16[64,3584]{1,0:T(8,128)(2,1)S(1)}, u32[]{:S(2)}, u32[]{:S(2)}) collective-permute-start(bf16[64,3584]{1,0:T(8,128)(2,1)S(1)} %slice.174), channel_id=1, source_target_pairs={{0,1},{1,0},{2,3},{3,2},{4,5},{5,4},{6,7},{7,6},{8,9},{9,8},{10,11... | collective-permute-start | bytes 1376264 | tf_op jit(solution)/shard_map/cores/ppermute | solution.py:40
  122.9 24.6 %collective-permute-start.11 = (bf16[16,7168]{1,0:T(8,128)(2,1)S(1)}, bf16[16,7168]{1,0:T(8,128)(2,1)S(1)}, u32[]{:S(2)}, u32[]{:S(2)}) collective-permute-start(bf16[16,7168]{1,0:T(8,128)(2,1)S(1)} %pad_maximum_fusion.6), channel_id=1, source_target_pairs={{0,6},{1,3},{2,0},{3,5},{4,2},{5,7},{6,4},{7,1},{8,14},{9,11},{10,... | collective-permute-start | bytes 688136 | tf_op jit(solution)/shard_map/home/ppermute | solution.py:31
  130.2 39.5 %collective-permute-start.9 = (bf16[16,3584]{1,0:T(8,128)(2,1)S(1)}, bf16[16,3584]{1,0:T(8,128)(2,1)S(1)}, u32[]{:S(2)}, u32[]{:S(2)}) collective-permute-start(bf16[16,3584]{1,0:T(8,128)(2,1)S(1)} %get-tuple-element.42), channel_id=1, source_target_pairs={{0,34},{1,39},{2,36},{3,33},{4,38},{5,35},{6,32},{7,37},{8,42},{9,... | collective-permute-start | bytes 344072 | tf_op jit(solution)/shard_map/home/ppermute | solution.py:52
  132.1 31.4 %collective-permute-start.14 = (bf16[16,3584]{1,0:T(8,128)(2,1)S(1)}, bf16[16,3584]{1,0:T(8,128)(2,1)S(1)}, u32[]{:S(2)}, u32[]{:S(2)}) collective-permute-start(bf16[16,3584]{1,0:T(8,128)(2,1)S(1)} %get-tuple-element.40), channel_id=1, source_target_pairs={{32,2},{33,7},{34,4},{35,1},{36,6},{37,3},{38,0},{39,5},{40,10},{4... | collective-permute-start | bytes 344072 | tf_op jit(solution)/shard_map/home/ppermute | solution.py:52
  147.6 19.9 %collective-permute-start.15 = (bf16[16,3584]{1,0:T(8,128)(2,1)S(1)}, bf16[16,3584]{1,0:T(8,128)(2,1)S(1)}, u32[]{:S(2)}, u32[]{:S(2)}) collective-permute-start(bf16[16,3584]{1,0:T(8,128)(2,1)S(1)} %get-tuple-element.37), channel_id=1, source_target_pairs={{32,6},{33,3},{34,0},{35,5},{36,2},{37,7},{38,4},{39,1},{40,14},{4... | collective-permute-start | bytes 344072 | tf_op jit(solution)/shard_map/home/ppermute | solution.py:52
  149.5 19.5 %collective-permute-start.13 = (f32[16,3584]{1,0:T(8,128)S(1)}, f32[16,3584]{1,0:T(8,128)S(1)}, u32[]{:S(2)}, u32[]{:S(2)}) collective-permute-start(f32[16,3584]{1,0:T(8,128)S(1)} %get-tuple-element.36), channel_id=1, source_target_pairs={{32,0},{33,1},{34,2},{35,3},{36,4},{37,5},{38,6},{39,7},{40,8},{41... | collective-permute-start | bytes 688136 | tf_op jit(solution)/shard_map/home/ppermute | solution.py:52
  160.2 16.5 %collective-permute-start.12 = (bf16[16,3584]{1,0:T(8,128)(2,1)S(1)}, bf16[16,3584]{1,0:T(8,128)(2,1)S(1)}, u32[]{:S(2)}, u32[]{:S(2)}) collective-permute-start(bf16[16,3584]{1,0:T(8,128)(2,1)S(1)} %get-tuple-element.39), channel_id=1, source_target_pairs={{0,38},{1,35},{2,32},{3,37},{4,34},{5,39},{6,36},{7,33},{8,46},{9,... | collective-permute-start | bytes 344072 | tf_op jit(solution)/shard_map/home/ppermute | solution.py:52
  163.5 14.5 %collective-permute-start.8 = (f32[16,3584]{1,0:T(8,128)S(1)}, f32[16,3584]{1,0:T(8,128)S(1)}, u32[]{:S(2)}, u32[]{:S(2)}) collective-permute-start(f32[16,3584]{1,0:T(8,128)S(1)} %get-tuple-element.38), channel_id=1, source_target_pairs={{0,32},{1,33},{2,34},{3,35},{4,36},{5,37},{6,38},{7,39},{8,40},{9,... | collective-permute-start | bytes 688136 | tf_op jit(solution)/shard_map/home/ppermute | solution.py:52

commit v7 on v6

--- a/solution.py
+++ b/solution.py
@@ -97,11 +97,11 @@
 def forward_rows(rows, gate_up, down):
     gate_val, up_val = jnp.split(dot(rows, gate_up), 2, axis=1)
     hidden = (jax.nn.silu(gate_val) * up_val).astype(jnp.bfloat16)
-    return dot_t(hidden, down)
+    return dot(hidden, down)
 
 
 def backward_rows(rows, grads, gate_up, down):
-    hidden_grad = dot(grads, down)
+    hidden_grad = dot_t(grads, down)
     gate_val, up_val = jnp.split(dot(rows, gate_up), 2, axis=1)
     sig = jax.nn.sigmoid(gate_val)
     gate_grad = hidden_grad * up_val * sig * (1.0 + gate_val * (1.0 - sig))
@@ -138,8 +138,8 @@
     experts = [(me + EXPERTS + d * turned) % EXPERTS for d in (0, -1, 1, -2)]
 
     with jax.named_scope("gather_weights"):
-        weights = jnp.concatenate([gate_up_weight[0], down_weight[0].T], axis=1)
-        near, far = along_x(weights, 1), along_x(weights, -1)
+        gate_up, down = gate_up_weight[0], down_weight[0]
+        near = [along_x(gate_up, 1), along_x(gate_up, -1), along_x(down, 1), along_x(down, -1)]
     with jax.named_scope("gather_rows"):
         shares = [
             expert_shares(expert_hot(forward_routes[0]), forward_gates[0]),
@@ -148,11 +148,12 @@
         side = side_columns(jnp.concatenate(shares, axis=1))
         mine = jnp.concatenate([tokens, saved, upstream, side], axis=1)
         below, above = along_z(mine, 1), along_z(mine, -1)
-        opposite = along_z(below, 1)
+        opposite = along_z(mine, 2)
     with jax.named_scope("gather_opposite"):
-        near, far, below, above, opposite = together(near, far, below, above, opposite)
-        weights = [weights, near, far, along_x(near, 1)]
         mine = jnp.concatenate([mine, below, above, opposite], axis=0)
+        mine, *near = together(mine, *near)
+        gate_ups = [gate_up, near[0], near[1], along_x(near[0], 1)]
+        downs = [down, near[2], near[3], along_x(near[2], 1)]
         both = [mine, other_core(mine)]
         cuts = (0, model, 2 * model, 3 * model, 3 * model + LANES)
         token_rows, saved_rows, upstream_rows, sides = [
@@ -162,9 +163,7 @@
         shares = side_values(sides)
     with jax.named_scope("experts"):
         forward_sum = backward_sum = 0.0
-        width = gate_up_weight.shape[2]
-        for expert, weight in zip(experts, weights):
-            gate_up, down = weight[:, :width], weight[:, width:]
+        for expert, gate_up, down in zip(experts, gate_ups, downs):
             out = forward_rows(token_rows, gate_up, down)
             forward_sum = forward_sum + column_of(shares[:, :EXPERTS], expert) * out
             out = backward_rows(saved_rows, upstream_rows, gate_up, down)

time: 181 us -> 207 us (1.14)
  waiting for transfers between devices: 45.6 us -> 100 us
  starting transfers between devices: 99.3 us -> 77.6 us
  matrix products: 23.3 us -> 14 us
    ppermute x4, waiting for transfers between devices: 24 us -> 60.7 us  [along_z(): return lax.ppermute(block, 'expert', route)]
    ppermute x3 -> x6, waiting for transfers between devices: 10.1 us -> 29.1 us  [along_x(): return lax.ppermute(block, 'expert', route)]
    ppermute x4, starting transfers between devices: 52.3 us -> 33.9 us  [along_z(): return lax.ppermute(block, 'expert', route)]
    ppermute x6, starting transfers between devices: 31.5 us -> 18.9 us  [to_section(): return lax.ppermute(block, ('pipe', 'expert'), route)]
    ppermute x3 -> x6, starting transfers between devices: 9.24 us -> 18.6 us  [along_x(): return lax.ppermute(block, 'expert', route)]
    dot_general x12, matrix products: 13.3 us -> 7.93 us  [dot(): return jnp.dot(a, b, preferred_element_type=jnp.float32)]
    dot_general x8, matrix products: 9.96 us -> 6.08 us  [dot_t(): lax.dot_general(a, b, (((1,), (1,)), ((), ())), preferred_element_type=jn...]
    unnamed x19 -> x17, local copies, waits for them, and re-layouts: 0.19 us -> 3.66 us
  transfers between devices with their start and end apart: 16 -> 19, of which waited for: 9 -> 8; matrix products, arithmetic and copies ran while one was open for 15% -> 10% of each run, Pallas kernels for 0% -> 0%
where the time goes in v7:
time: 207 us; the launch traced here: 204 us
  waiting for transfers between devices  100 us (48%)
  starting transfers between devices  77.6 us (37%)
  matrix products  14 us (7%)
  local copies, waits for them, and re-layouts  6.01 us (3%)
  other arithmetic  5.01 us (2%)
    ppermute x4, waiting for transfers between devices, along_z(): return lax.ppermute(block, 'expert', route)  60.7 us
    ppermute x4, starting transfers between devices, along_z(): return lax.ppermute(block, 'expert', route)  33.9 us
    ppermute x6, waiting for transfers between devices, along_x(): return lax.ppermute(block, 'expert', route)  29.1 us
    ppermute x6, starting transfers between devices, to_section(): return lax.ppermute(block, ('pipe', 'expert'), route)  18.9 us
    ppermute x6, starting transfers between devices, along_x(): return lax.ppermute(block, 'expert', route)  18.6 us
    ppermute x6, waiting for transfers between devices, to_section(): return lax.ppermute(block, ('pipe', 'expert'), route)  9.03 us
    dot_general x12, matrix products, dot(): return jnp.dot(a, b, preferred_element_type=jnp.float32)  7.93 us
    ppermute x3, starting transfers between devices, other_core(): lax.ppermute(block, 'expert', expert_route(lambda x, z, c: (x, z, 1 - c)))  6.24 us
  transfers between devices with their start and end apart: 19, of which 8 were waited for; matrix products, arithmetic and copies ran while one was open for 10% of the time, Pallas kernels for 0%

profile of v7, /device:TPU:24, one launch (start us, length us, event | category | flops | bytes accessed | tf_op | source)
XLA Modules:
  0.0 204.0 jit_solution(17075385966828996589)
XLA Ops:
  0.6 4.7 %collective-permute-start.4 = (bf16[3584,256]{1,0:T(8,128)(2,1)}, bf16[3584,256]{1,0:T(8,128)(2,1)}, u32[]{:S(2)}, u32[]{:S(2)}) collective-permute-start(bf16[3584,256]{1,0:T(8,128)(2,1)} %bitcast.42), channel_id=1, source_target_pairs={{0,24},{1,9},{2,26},{3,11},{4,28},{5,13},{6,30},{7,15},{8,0},{9,17... | collective-permute-start | bytes 5505032 | tf_op jit(solution)/shard_map/gather_weights/ppermute | solution.py:36
  5.3 1.9 collective-permute-start.3
  7.2 0.7 select_reduce_fusion.8
  8.1 1.0 pad_maximum_fusion.4
  9.1 15.7 %collective-permute-start.2 = (bf16[16,10880]{1,0:T(8,128)(2,1)S(1)}, bf16[16,10880]{1,0:T(8,128)(2,1)S(1)}, u32[]{:S(2)}, u32[]{:S(2)}) collective-permute-start(bf16[16,10880]{1,0:T(8,128)(2,1)S(1)} %pad_maximum_fusion.4), channel_id=1, source_target_pairs={{0,4},{1,5},{2,6},{3,7},{4,0},{5,1},{6,2},{7,3},{8,12},{9,13},{10,... | collective-permute-start | bytes 1044488 | tf_op jit(solution)/shard_map/gather_rows/ppermute | solution.py:31
  24.9 1.9 collective-permute-start.1
  26.8 7.8 %collective-permute-start = (bf16[16,10880]{1,0:T(8,128)(2,1)S(1)}, bf16[16,10880]{1,0:T(8,128)(2,1)S(1)}, u32[]{:S(2)}, u32[]{:S(2)}) collective-permute-start(bf16[16,10880]{1,0:T(8,128)(2,1)S(1)} %pad_maximum_fusion.4), channel_id=1, source_target_pairs={{0,2},{1,7},{2,4},{3,1},{4,6},{5,3},{6,0},{7,5},{8,10},{9,15},{10,... | collective-permute-start | bytes 1044488 | tf_op jit(solution)/shard_map/gather_rows/ppermute | solution.py:31
  34.6 8.8 %collective-permute-done.2 = bf16[16,10880]{1,0:T(8,128)(2,1)S(1)} collective-permute-done((bf16[16,10880]{1,0:T(8,128)(2,1)S(1)}, bf16[16,10880]{1,0:T(8,128)(2,1)S(1)}, u32[]{:S(2)}, u32[]{:S(2)}) %collective-permute-start.2) | collective-permute-done | bytes 348192 | tf_op jit(solution)/shard_map/gather_rows/ppermute | solution.py:31
  43.4 6.2 %collective-permute-start.6 = (bf16[128,3584]{1,0:T(8,128)(2,1)}, bf16[128,3584]{1,0:T(8,128)(2,1)S(1)}, u32[]{:S(2)}, u32[]{:S(2)}) collective-permute-start(bf16[128,3584]{1,0:T(8,128)(2,1)} %bitcast.48), channel_id=1, source_target_pairs={{0,24},{1,9},{2,26},{3,11},{4,28},{5,13},{6,30},{7,15},{8,0},{9,17... | collective-permute-start | bytes 2752520 | tf_op jit(solution)/shard_map/gather_weights/ppermute | solution.py:36
  49.7 36.0 %collective-permute-done.1 = bf16[16,10880]{1,0:T(8,128)(2,1)S(1)} collective-permute-done((bf16[16,10880]{1,0:T(8,128)(2,1)S(1)}, bf16[16,10880]{1,0:T(8,128)(2,1)S(1)}, u32[]{:S(2)}, u32[]{:S(2)}) %collective-permute-start.1) | collective-permute-done | bytes 348192 | tf_op jit(solution)/shard_map/gather_rows/ppermute | solution.py:31
  85.7 1.9 collective-permute-start.5
  87.7 1.1 pad_maximum_fusion
  88.8 13.6 %collective-permute-done.5 = bf16[128,3584]{1,0:T(8,128)(2,1)S(1)} collective-permute-done((bf16[128,3584]{1,0:T(8,128)(2,1)}, bf16[128,3584]{1,0:T(8,128)(2,1)S(1)}, u32[]{:S(2)}, u32[]{:S(2)}) %collective-permute-start.5) | collective-permute-done | bytes 917536 | tf_op jit(solution)/shard_map/gather_weights/ppermute | solution.py:36
  102.4 0.9 copy-done.3
  103.4 1.9 collective-permute-start.7
  105.4 1.9 collective-permute-start.9
  107.4 1.9 collective-permute-start.8
  109.4 1.4 fusion.76
  110.8 0.4 fusion.66
  111.2 1.1 copy-done
  112.7 0.4 fusion.72
  113.1 0.4 fusion.58
  113.6 0.7 slice.86
  114.4 2.0 fusion.71
  117.5 0.8 copy-done.4
  118.7 0.7 convolution_multiply_fusion.3
  119.8 0.8 copy-done.6
  121.0 0.8 fusion.2
  121.7 1.9 fusion.65
  124.1 2.3 %fusion.1 = f32[128,3584]{1,0:T(8,128)S(1)} fusion(f32[128,3584]{1,0:T(8,128)S(1)} %fusion.2, bf16[3584,256]{1,0:T(8,128)(2,1)} %collective-permute-done.4, f32[128]{0:T(128)S(1)} %get-tuple-element.23, bf16[128,128]{1,0:T(8,128)(2,1)S(1)} %get-tuple-element.47, bf16[128,128]{1,0:T(8,128)(2,1)S(1)} %get-tuple-element.46), kind=kOutput, calls=%fused_computation.3 | convolution fusion | flops 235929600 | bytes 5571072 | tf_op jit(solution)/shard_map/experts/dot_general | solution.py:94
  126.3 15.5 %collective-permute-done.8 = bf16[3584,256]{1,0:T(8,128)(2,1)S(1)} collective-permute-done((bf16[3584,256]{1,0:T(8,128)(2,1)S(1)}, bf16[3584,256]{1,0:T(8,128)(2,1)S(1)}, u32[]{:S(2)}, u32[]{:S(2)}) %collective-permute-start.8) | collective-permute-done | bytes 1835040 | tf_op jit(solution)/shard_map/gather_opposite/ppermute | solution.py:36
  141.8 0.4 fusion.70
  142.7 1.9 collective-permute-start.10
  144.6 0.4 fusion.64
  145.5 0.7 fusion
  146.2 2.4 %collective-permute-start.13 = (bf16[64,3584]{1,0:T(8,128)(2,1)S(1)}, bf16[64,3584]{1,0:T(8,128)(2,1)S(1)}, u32[]{:S(2)}, u32[]{:S(2)}) collective-permute-start(bf16[64,3584]{1,0:T(8,128)(2,1)S(1)} %slice.114), channel_id=1, source_target_pairs={{0,1},{1,0},{2,3},{3,2},{4,5},{5,4},{6,7},{7,6},{8,9},{9,8},{10,11... | collective-permute-start | bytes 1376264 | tf_op jit(solution)/shard_map/cores/ppermute | solution.py:40
  148.9 1.2 collective-permute-done.13
  150.3 8.4 %collective-permute-start.14 = (bf16[16,7168]{1,0:T(8,128)(2,1)S(1)}, bf16[16,7168]{1,0:T(8,128)(2,1)S(1)}, u32[]{:S(2)}, u32[]{:S(2)}) collective-permute-start(bf16[16,7168]{1,0:T(8,128)(2,1)S(1)} %pad_maximum_fusion.5), channel_id=1, source_target_pairs={{0,6},{1,3},{2,0},{3,5},{4,2},{5,7},{6,4},{7,1},{8,14},{9,11},{10,... | collective-permute-start | bytes 688136 | tf_op jit(solution)/shard_map/home/ppermute | solution.py:31
  158.7 1.9 collective-permute-start.12
  160.6 1.9 collective-permute-start.17
  162.6 15.8 %collective-permute-done.14 = bf16[16,7168]{1,0:T(8,128)(2,1)S(1)} collective-permute-done((bf16[16,7168]{1,0:T(8,128)(2,1)S(1)}, bf16[16,7168]{1,0:T(8,128)(2,1)S(1)}, u32[]{:S(2)}, u32[]{:S(2)}) %collective-permute-start.14) | collective-permute-done | bytes 229408 | tf_op jit(solution)/shard_map/home/ppermute | solution.py:31
  178.4 1.9 collective-permute-start.18
  180.4 7.1 %collective-permute-start.16 = (f32[16,3584]{1,0:T(8,128)S(1)}, f32[16,3584]{1,0:T(8,128)S(1)}, u32[]{:S(2)}, u32[]{:S(2)}) collective-permute-start(f32[16,3584]{1,0:T(8,128)S(1)} %get-tuple-element.36), channel_id=1, source_target_pairs={{32,0},{33,1},{34,2},{35,3},{36,4},{37,5},{38,6},{39,7},{40,8},{41... | collective-permute-start | bytes 688136 | tf_op jit(solution)/shard_map/home/ppermute | solution.py:52
  187.5 2.6 %collective-permute-start.15 = (bf16[16,3584]{1,0:T(8,128)(2,1)S(1)}, bf16[16,3584]{1,0:T(8,128)(2,1)S(1)}, u32[]{:S(2)}, u32[]{:S(2)}) collective-permute-start(bf16[16,3584]{1,0:T(8,128)(2,1)S(1)} %get-tuple-element.39), channel_id=1, source_target_pairs={{0,38},{1,35},{2,32},{3,37},{4,34},{5,39},{6,36},{7,33},{8,46},{9,... | collective-permute-start | bytes 344072 | tf_op jit(solution)/shard_map/home/ppermute | solution.py:52
  190.1 3.5 %collective-permute-start.11 = (f32[16,3584]{1,0:T(8,128)S(1)}, f32[16,3584]{1,0:T(8,128)S(1)}, u32[]{:S(2)}, u32[]{:S(2)}) collective-permute-start(f32[16,3584]{1,0:T(8,128)S(1)} %get-tuple-element.38), channel_id=1, source_target_pairs={{0,32},{1,33},{2,34},{3,35},{4,36},{5,37},{6,38},{7,39},{8,40},{9,... | collective-permute-start | bytes 688136 | tf_op jit(solution)/shard_map/home/ppermute | solution.py:52
  193.9 0.7 fusion.9
  194.6 8.7 %collective-permute-done.15 = bf16[16,3584]{1,0:T(8,128)(2,1)S(1)} collective-permute-done((bf16[16,3584]{1,0:T(8,128)(2,1)S(1)}, bf16[16,3584]{1,0:T(8,128)(2,1)S(1)}, u32[]{:S(2)}, u32[]{:S(2)}) %collective-permute-start.15) | collective-permute-done | bytes 114720 | tf_op jit(solution)/shard_map/home/ppermute | solution.py:52
  203.3 0.7 fusion.8
  (53 shorter events, 5.1 us)
Async XLA Ops:
  0.6 101.8 %collective-permute-start.4 = (bf16[3584,256]{1,0:T(8,128)(2,1)}, bf16[3584,256]{1,0:T(8,128)(2,1)}, u32[]{:S(2)}, u32[]{:S(2)}) collective-permute-start(bf16[3584,256]{1,0:T(8,128)(2,1)} %bitcast.42), channel_id=1, source_target_pairs={{0,24},{1,9},{2,26},{3,11},{4,28},{5,13},{6,30},{7,15},{8,0},{9,17... | collective-permute-start | bytes 5505032 | tf_op jit(solution)/shard_map/gather_weights/ppermute | solution.py:36
  5.3 97.1 %collective-permute-start.3 = (bf16[3584,256]{1,0:T(8,128)(2,1)}, bf16[3584,256]{1,0:T(8,128)(2,1)S(1)}, u32[]{:S(2)}, u32[]{:S(2)}) collective-permute-start(bf16[3584,256]{1,0:T(8,128)(2,1)} %bitcast.43), channel_id=1, source_target_pairs={{0,8},{1,25},{2,10},{3,27},{4,12},{5,29},{6,14},{7,31},{8,16},{9,1... | collective-permute-start | bytes 5505032 | tf_op jit(solution)/shard_map/gather_weights/ppermute | solution.py:36
  9.1 34.3 %collective-permute-start.2 = (bf16[16,10880]{1,0:T(8,128)(2,1)S(1)}, bf16[16,10880]{1,0:T(8,128)(2,1)S(1)}, u32[]{:S(2)}, u32[]{:S(2)}) collective-permute-start(bf16[16,10880]{1,0:T(8,128)(2,1)S(1)} %pad_maximum_fusion.4), channel_id=1, source_target_pairs={{0,4},{1,5},{2,6},{3,7},{4,0},{5,1},{6,2},{7,3},{8,12},{9,13},{10,... | collective-permute-start | bytes 1044488 | tf_op jit(solution)/shard_map/gather_rows/ppermute | solution.py:31
  24.9 60.9 %collective-permute-start.1 = (bf16[16,10880]{1,0:T(8,128)(2,1)S(1)}, bf16[16,10880]{1,0:T(8,128)(2,1)S(1)}, u32[]{:S(2)}, u32[]{:S(2)}) collective-permute-start(bf16[16,10880]{1,0:T(8,128)(2,1)S(1)} %pad_maximum_fusion.4), channel_id=1, source_target_pairs={{0,6},{1,3},{2,0},{3,5},{4,2},{5,7},{6,4},{7,1},{8,14},{9,11},{10,... | collective-permute-start | bytes 1044488 | tf_op jit(solution)/shard_map/gather_rows/ppermute | solution.py:31
  26.8 60.9 %collective-permute-start = (bf16[16,10880]{1,0:T(8,128)(2,1)S(1)}, bf16[16,10880]{1,0:T(8,128)(2,1)S(1)}, u32[]{:S(2)}, u32[]{:S(2)}) collective-permute-start(bf16[16,10880]{1,0:T(8,128)(2,1)S(1)} %pad_maximum_fusion.4), channel_id=1, source_target_pairs={{0,2},{1,7},{2,4},{3,1},{4,6},{5,3},{6,0},{7,5},{8,10},{9,15},{10,... | collective-permute-start | bytes 1044488 | tf_op jit(solution)/shard_map/gather_rows/ppermute | solution.py:31
  43.4 45.3 %collective-permute-start.6 = (bf16[128,3584]{1,0:T(8,128)(2,1)}, bf16[128,3584]{1,0:T(8,128)(2,1)S(1)}, u32[]{:S(2)}, u32[]{:S(2)}) collective-permute-start(bf16[128,3584]{1,0:T(8,128)(2,1)} %bitcast.48), channel_id=1, source_target_pairs={{0,24},{1,9},{2,26},{3,11},{4,28},{5,13},{6,30},{7,15},{8,0},{9,17... | collective-permute-start | bytes 2752520 | tf_op jit(solution)/shard_map/gather_weights/ppermute | solution.py:36
  85.7 16.7 %collective-permute-start.5 = (bf16[128,3584]{1,0:T(8,128)(2,1)}, bf16[128,3584]{1,0:T(8,128)(2,1)S(1)}, u32[]{:S(2)}, u32[]{:S(2)}) collective-permute-start(bf16[128,3584]{1,0:T(8,128)(2,1)} %bitcast.49), channel_id=1, source_target_pairs={{0,8},{1,25},{2,10},{3,27},{4,12},{5,29},{6,14},{7,31},{8,16},{9,1... | collective-permute-start | bytes 2752520 | tf_op jit(solution)/shard_map/gather_weights/ppermute | solution.py:36
  88.8 16.5 %copy-start.5 = (bf16[128,3584]{1,0:T(8,128)(2,1)}, bf16[128,3584]{1,0:T(8,128)(2,1)S(1)}, u32[]{:S(2)}) copy-start(bf16[128,3584]{1,0:T(8,128)(2,1)S(1)} %collective-permute-done.6) | copy-start | bytes 2752516
  102.4 1.0 copy-start.3
  103.4 6.0 %collective-permute-start.7 = (bf16[64,10880]{1,0:T(8,128)(2,1)S(1)}, bf16[64,10880]{1,0:T(8,128)(2,1)}, u32[]{:S(2)}, u32[]{:S(2)}) collective-permute-start(bf16[64,10880]{1,0:T(8,128)(2,1)S(1)} %pad_maximum_fusion), channel_id=1, source_target_pairs={{0,1},{1,0},{2,3},{3,2},{4,5},{5,4},{6,7},{7,6},{8,9},{9,8},{10,11... | collective-permute-start | bytes 4177928 | tf_op jit(solution)/shard_map/gather_opposite/ppermute | solution.py:40
  105.4 36.8 %collective-permute-start.9 = (bf16[128,3584]{1,0:T(8,128)(2,1)}, bf16[128,3584]{1,0:T(8,128)(2,1)S(1)}, u32[]{:S(2)}, u32[]{:S(2)}) collective-permute-start(bf16[128,3584]{1,0:T(8,128)(2,1)} %copy-done.3), channel_id=1, source_target_pairs={{0,8},{1,25},{2,10},{3,27},{4,12},{5,29},{6,14},{7,31},{8,16},{9,1... | collective-permute-start | bytes 2752520 | tf_op jit(solution)/shard_map/gather_opposite/ppermute | solution.py:36
  107.4 34.4 %collective-permute-start.8 = (bf16[3584,256]{1,0:T(8,128)(2,1)S(1)}, bf16[3584,256]{1,0:T(8,128)(2,1)S(1)}, u32[]{:S(2)}, u32[]{:S(2)}) collective-permute-start(bf16[3584,256]{1,0:T(8,128)(2,1)S(1)} %collective-permute-done.3), channel_id=1, source_target_pairs={{0,8},{1,25},{2,10},{3,27},{4,12},{5,29},{6,14},{7,31},{8,16},{9,1... | collective-permute-start | bytes 5505032 | tf_op jit(solution)/shard_map/gather_opposite/ppermute | solution.py:36
  110.8 1.5 copy-start
  114.3 2.4 %copy-start.7 = (bf16[1,128,3584]{2,1,0:T(8,128)(2,1)S(1)}, bf16[1,128,3584]{2,1,0:T(8,128)(2,1)}, u32[]{:S(2)}) copy-start(bf16[1,128,3584]{2,1,0:T(8,128)(2,1)} %param.13) | copy-start | bytes 2752516
  117.1 1.2 copy-start.4
  119.4 1.2 copy-start.6
  142.7 6.0 %collective-permute-start.10 = (bf16[64,3584]{1,0:T(8,128)(2,1)S(1)}, bf16[64,3584]{1,0:T(8,128)(2,1)S(1)}, u32[]{:S(2)}, u32[]{:S(2)}) collective-permute-start(bf16[64,3584]{1,0:T(8,128)(2,1)S(1)} %slice.115), channel_id=1, source_target_pairs={{0,1},{1,0},{2,3},{3,2},{4,5},{5,4},{6,7},{7,6},{8,9},{9,8},{10,11... | collective-permute-start | bytes 1376264 | tf_op jit(solution)/shard_map/cores/ppermute | solution.py:40
  146.2 3.8 %collective-permute-start.13 = (bf16[64,3584]{1,0:T(8,128)(2,1)S(1)}, bf16[64,3584]{1,0:T(8,128)(2,1)S(1)}, u32[]{:S(2)}, u32[]{:S(2)}) collective-permute-start(bf16[64,3584]{1,0:T(8,128)(2,1)S(1)} %slice.114), channel_id=1, source_target_pairs={{0,1},{1,0},{2,3},{3,2},{4,5},{5,4},{6,7},{7,6},{8,9},{9,8},{10,11... | collective-permute-start | bytes 1376264 | tf_op jit(solution)/shard_map/cores/ppermute | solution.py:40
  148.8 29.6 %copy-start.1 = (bf16[1,16,3584]{2,1,0:T(8,128)(2,1)S(1)}, bf16[1,16,3584]{2,1,0:T(8,128)(2,1)}, u32[]{:S(2)}) copy-start(bf16[1,16,3584]{2,1,0:T(8,128)(2,1)} %param.11) | copy-start | bytes 344068
  148.8 38.6 %copy-start.2 = (bf16[1,16,3584]{2,1,0:T(8,128)(2,1)S(1)}, bf16[1,16,3584]{2,1,0:T(8,128)(2,1)}, u32[]{:S(2)}) copy-start(bf16[1,16,3584]{2,1,0:T(8,128)(2,1)} %param.9) | copy-start | bytes 344068
  150.3 28.1 %collective-permute-start.14 = (bf16[16,7168]{1,0:T(8,128)(2,1)S(1)}, bf16[16,7168]{1,0:T(8,128)(2,1)S(1)}, u32[]{:S(2)}, u32[]{:S(2)}) collective-permute-start(bf16[16,7168]{1,0:T(8,128)(2,1)S(1)} %pad_maximum_fusion.5), channel_id=1, source_target_pairs={{0,6},{1,3},{2,0},{3,5},{4,2},{5,7},{6,4},{7,1},{8,14},{9,11},{10,... | collective-permute-start | bytes 688136 | tf_op jit(solution)/shard_map/home/ppermute | solution.py:31
  158.7 35.9 %collective-permute-start.12 = (bf16[16,3584]{1,0:T(8,128)(2,1)S(1)}, bf16[16,3584]{1,0:T(8,128)(2,1)S(1)}, u32[]{:S(2)}, u32[]{:S(2)}) collective-permute-start(bf16[16,3584]{1,0:T(8,128)(2,1)S(1)} %get-tuple-element.42), channel_id=1, source_target_pairs={{0,34},{1,39},{2,36},{3,33},{4,38},{5,35},{6,32},{7,37},{8,42},{9,... | collective-permute-start | bytes 344072 | tf_op jit(solution)/shard_map/home/ppermute | solution.py:52
  160.6 29.5 %collective-permute-start.17 = (bf16[16,3584]{1,0:T(8,128)(2,1)S(1)}, bf16[16,3584]{1,0:T(8,128)(2,1)S(1)}, u32[]{:S(2)}, u32[]{:S(2)}) collective-permute-start(bf16[16,3584]{1,0:T(8,128)(2,1)S(1)} %get-tuple-element.40), channel_id=1, source_target_pairs={{32,2},{33,7},{34,4},{35,1},{36,6},{37,3},{38,0},{39,5},{40,10},{4... | collective-permute-start | bytes 344072 | tf_op jit(solution)/shard_map/home/ppermute | solution.py:52
  178.4 15.2 %collective-permute-start.18 = (bf16[16,3584]{1,0:T(8,128)(2,1)S(1)}, bf16[16,3584]{1,0:T(8,128)(2,1)S(1)}, u32[]{:S(2)}, u32[]{:S(2)}) collective-permute-start(bf16[16,3584]{1,0:T(8,128)(2,1)S(1)} %get-tuple-element.37), channel_id=1, source_target_pairs={{32,6},{33,3},{34,0},{35,5},{36,2},{37,7},{38,4},{39,1},{40,14},{4... | collective-permute-start | bytes 344072 | tf_op jit(solution)/shard_map/home/ppermute | solution.py:52
  180.4 13.5 %collective-permute-start.16 = (f32[16,3584]{1,0:T(8,128)S(1)}, f32[16,3584]{1,0:T(8,128)S(1)}, u32[]{:S(2)}, u32[]{:S(2)}) collective-permute-start(f32[16,3584]{1,0:T(8,128)S(1)} %get-tuple-element.36), channel_id=1, source_target_pairs={{32,0},{33,1},{34,2},{35,3},{36,4},{37,5},{38,6},{39,7},{40,8},{41... | collective-permute-start | bytes 688136 | tf_op jit(solution)/shard_map/home/ppermute | solution.py:52
  187.5 15.8 %collective-permute-start.15 = (bf16[16,3584]{1,0:T(8,128)(2,1)S(1)}, bf16[16,3584]{1,0:T(8,128)(2,1)S(1)}, u32[]{:S(2)}, u32[]{:S(2)}) collective-permute-start(bf16[16,3584]{1,0:T(8,128)(2,1)S(1)} %get-tuple-element.39), channel_id=1, source_target_pairs={{0,38},{1,35},{2,32},{3,37},{4,34},{5,39},{6,36},{7,33},{8,46},{9,... | collective-permute-start | bytes 344072 | tf_op jit(solution)/shard_map/home/ppermute | solution.py:52
  190.1 13.2 %collective-permute-start.11 = (f32[16,3584]{1,0:T(8,128)S(1)}, f32[16,3584]{1,0:T(8,128)S(1)}, u32[]{:S(2)}, u32[]{:S(2)}) collective-permute-start(f32[16,3584]{1,0:T(8,128)S(1)} %get-tuple-element.38), channel_id=1, source_target_pairs={{0,32},{1,33},{2,34},{3,35},{4,36},{5,37},{6,38},{7,39},{8,40},{9,... | collective-permute-start | bytes 688136 | tf_op jit(solution)/shard_map/home/ppermute | solution.py:52

commit v8 on v6

v8 whole, which is shorter than its diff:
```python
import jax
import jax.numpy as jnp
from jax import lax
from jax.sharding import PartitionSpec as P

EXPERTS = 4
Z = 4
CORES = 2
LANES = 128
CAP = 12


def expert_index(x, z, core):
    return (x * Z + z) * CORES + core


def expert_route(move):
    return [
        (expert_index(x, z, c), expert_index(*move(x, z, c)))
        for x in range(EXPERTS)
        for z in range(Z)
        for c in range(CORES)
    ]


def turn(core):
    return 1 - 2 * core


def along_z(block, distance):
    route = expert_route(lambda x, z, c: (x, (z + distance * turn(c)) % Z, c))
    return lax.ppermute(block, "expert", route)


def along_x(block, distance):
    route = expert_route(lambda x, z, c: ((x + distance * turn(c)) % EXPERTS, z, c))
    return lax.ppermute(block, "expert", route)


def other_core(block):
    return lax.ppermute(block, "expert", expert_route(lambda x, z, c: (x, z, 1 - c)))


def to_section(block, step, distance):
    sections = lax.axis_size("pipe")
    width = EXPERTS * Z * CORES
    route = [
        (p * width + source, (p + step) * width + target)
        for p in range(sections)
        if 0 <= p + step < sections
        for source, target in expert_route(lambda x, z, c: (x, (z + distance * turn(c)) % Z, c))
    ]
    return lax.ppermute(block, ("pipe", "expert"), route)


def together(*values):
    return lax.optimization_barrier(values)


def expert_hot(routes):
    return routes[:, :, None] == jnp.arange(EXPERTS, dtype=jnp.int32)


def expert_shares(hot, gates):
    return jnp.sum(jnp.where(hot, gates[:, :, None], 0.0), axis=1)


def expert_slots(hot):
    named = jnp.any(hot, axis=1)
    count = named.astype(jnp.int32)
    earlier = jnp.cumsum(count, axis=0) - count
    return jnp.where(named, earlier, -1).astype(jnp.float32)


def three_parts(values):
    first = lax.reduce_precision(values, 8, 7)
    second = lax.reduce_precision(values - first, 8, 7)
    return [part.astype(jnp.bfloat16) for part in (first, second, values - first - second)]


def side_columns(shares, slots):
    parts = jnp.concatenate(three_parts(shares) + [slots.astype(jnp.bfloat16)], axis=1)
    return jnp.pad(parts, ((0, 0), (0, LANES - parts.shape[1])))


def side_values(columns):
    width = 2 * EXPERTS
    parts = columns[:, : 4 * width].astype(jnp.float32)
    first, second, third, slots = jnp.split(parts, 4, axis=1)
    return first + second + third, slots


def column_of(table, index):
    hot = jnp.arange(table.shape[1], dtype=jnp.int32) == index
    return jnp.sum(jnp.where(hot[None, :], table, 0.0), axis=1, keepdims=True)


def placement(slots, expert, rows):
    slot = column_of(slots, expert)
    block = jnp.arange(slots.shape[0], dtype=jnp.int32) // rows
    place = jnp.arange(Z * CAP, dtype=jnp.int32)
    wanted = (place % CAP).astype(jnp.float32)
    found = (block[:, None] == place[None, :] // CAP) & (slot == wanted[None, :])
    return found.astype(jnp.bfloat16)


def dot(a, b):
    return jnp.dot(a, b, preferred_element_type=jnp.float32)


def dot_t(a, b):
    return lax.dot_general(a, b, (((1,), (1,)), ((), ())), preferred_element_type=jnp.float32)


def pack(places, block):
    packed = lax.dot_general(
        places,
        block,
        (((0,), (0,)), ((), ())),
        preferred_element_type=jnp.float32,
    )
    return packed.astype(jnp.bfloat16)


def forward_rows(rows, weight):
    width = 2 * weight.shape[1] // 3
    gate_val, up_val = jnp.split(dot(rows, weight[:, :width]), 2, axis=1)
    hidden = (jax.nn.silu(gate_val) * up_val).astype(jnp.bfloat16)
    return dot_t(hidden, weight[:, width:])


def backward_rows(rows, grads, weight):
    width = 2 * weight.shape[1] // 3
    hidden_grad = dot(grads, weight[:, width:])
    gate_val, up_val = jnp.split(dot(rows, weight[:, :width]), 2, axis=1)
    sig = jax.nn.sigmoid(gate_val)
    gate_grad = hidden_grad * up_val * sig * (1.0 + gate_val * (1.0 - sig))
    up_grad = hidden_grad * gate_val * sig
    grad = jnp.concatenate([gate_grad, up_grad], axis=1).astype(jnp.bfloat16)
    return dot_t(grad, weight[:, :width])


def pass_on(mixture):
    return along_z(jnp.split(mixture, Z, axis=0)[3].astype(jnp.bfloat16), -1)


def send_home(mixture, residual, passed, step):
    own, near, far = jnp.split(mixture, Z, axis=0)[:3]
    near = near + passed.astype(jnp.float32)
    total = to_section(own + residual.astype(jnp.float32), step, 0)
    total = total + to_section(far.astype(jnp.bfloat16), step, 1).astype(jnp.float32)
    total = total + to_section(near.astype(jnp.bfloat16), step, -1).astype(jnp.float32)
    return total.astype(jnp.bfloat16)


def on_device(
    forward_input,
    backward_input,
    backward_grad,
    gate_up_weight,
    down_weight,
    forward_routes,
    backward_routes,
    forward_gates,
    backward_gates,
):
    tokens, saved, upstream = forward_input[0], backward_input[0], backward_grad[0]
    rows, model = tokens.shape
    index = lax.axis_index("expert")
    turned = 1 - 2 * (index % CORES)
    me = index // (Z * CORES)
    experts = [(me + EXPERTS + d * turned) % EXPERTS for d in (0, -1, 1)]
    opposite = (me + 2) % EXPERTS
    half = Z * rows

    with jax.named_scope("gather_weights"):
        weights = jnp.concatenate([gate_up_weight[0], down_weight[0].T], axis=1)
        near, far = along_x(weights, 1), along_x(weights, -1)
        twin = other_core(weights)
    with jax.named_scope("forward_z"):
        hots = [expert_hot(forward_routes[0]), expert_hot(backward_routes[0])]
        shares = [
            expert_shares(hots[0], forward_gates[0]),
            expert_shares(hots[1], backward_gates[0]),
        ]
        slots = [expert_slots(hot) for hot in hots]
        side = side_columns(jnp.concatenate(shares, axis=1), jnp.concatenate(slots, axis=1))
        mine = jnp.concatenate([tokens, side], axis=1)
        below, above = along_z(mine, 1), along_z(mine, -1)
        back_mine = jnp.concatenate([saved, upstream], axis=1)
        below, above, twin, back_mine = together(below, above, twin, back_mine)
        mine = jnp.concatenate([mine, below, above, along_z(below, 1)], axis=0)
    with jax.named_scope("backward_z"):
        below, above = along_z(back_mine, 1), along_z(back_mine, -1)
        back_mine = jnp.concatenate([back_mine, below, above, along_z(below, 1)], axis=0)
    with jax.named_scope("forward_opposite"):
        block = mine[:, :model]
        shares, slots = side_values(mine[:, model:])
        place = placement(slots[:, :EXPERTS], opposite, rows)
        back_place = placement(slots[:, EXPERTS:], opposite, rows)
        visitors = along_x(pack(place, block), 2)
        mine, visitors = together(mine, visitors)
        out = sum(forward_rows(visitors, weight) for weight in (weights, twin))
        returned = along_x(out.astype(jnp.bfloat16), 2)
        near, far, returned = together(near, far, returned)
    with jax.named_scope("backward_opposite"):
        back_visitors = along_x(pack(back_place, back_mine), 2)
    with jax.named_scope("forward_experts"):
        other = other_core(mine)
        token_rows = jnp.concatenate([block, other[:, :model]], axis=0)
        other_shares, _ = side_values(other[:, model:])
        both_shares = jnp.concatenate([shares, other_shares], axis=0)
        total = 0.0
        for expert, weight in zip(experts, (weights, near, far)):
            share = column_of(both_shares[:, :EXPERTS], expert)
            total = total + share * forward_rows(token_rows, weight)
        swapped = other_core(total[half:].astype(jnp.bfloat16)).astype(jnp.float32)
        share = column_of(shares[:, :EXPERTS], opposite)
        mixture = total[:half] + swapped + share * dot(place, returned)
        forward_mixture, passed = mixture, pass_on(mixture)
    with jax.named_scope("backward_visitors"):
        out = sum(
            backward_rows(back_visitors[:, :model], back_visitors[:, model:], weight)
            for weight in (weights, twin)
        )
        back_returned = along_x(out.astype(jnp.bfloat16), 2)
    with jax.named_scope("backward_experts"):
        back_rows = jnp.concatenate([back_mine, other_core(back_mine)], axis=0)
        last, back_returned, passed = together(far, back_returned, passed)
        total = 0.0
        for expert, weight in zip(experts, (weights, near, last)):
            share = column_of(both_shares[:, EXPERTS:], expert)
            out = backward_rows(back_rows[:, :model], back_rows[:, model:], weight)
            total = total + share * out
        swapped = other_core(total[half:].astype(jnp.bfloat16)).astype(jnp.float32)
        share = column_of(shares[:, EXPERTS:], opposite)
        mixture = total[:half] + swapped + share * dot(back_place, back_returned)
    with jax.named_scope("forward_home"):
        forward_next = send_home(forward_mixture, tokens, passed, 1)
    with jax.named_scope("backward_home"):
        backward_next = send_home(mixture, upstream, pass_on(mixture), -1)
    return (forward_next[None], backward_next[None])


def solution(mesh):
    by_token = P("pipe", "expert", None)
    return jax.shard_map(
        on_device,
        mesh=mesh,
        in_specs=(by_token,) * 3 + (P("pipe", None, "expert"),) + (by_token,) * 5,
        out_specs=(by_token, by_token),
        check_vma=False,
    )
```

time: 181 us -> 224 us (1.24)
  the two profiles are of different devices: /device:TPU:24 before, /device:TPU:16 now
where the time goes in v8:
time: 224 us; the launch traced here: 223 us
  starting transfers between devices  115 us (51%)
  waiting for transfers between devices  49.3 us (22%)
  matrix products  40.2 us (18%)
  local copies, waits for them, and re-layouts  11.7 us (5%)
  other arithmetic  4.85 us (2%)
    ppermute x8, starting transfers between devices, along_z(): return lax.ppermute(block, 'expert', route)  53.3 us
    ppermute x6, starting transfers between devices, to_section(): return lax.ppermute(block, ('pipe', 'expert'), route)  26.6 us
    ppermute x6, starting transfers between devices, along_x(): return lax.ppermute(block, 'expert', route)  23.5 us
    dot_general x17, matrix products, dot(): return jnp.dot(a, b, preferred_element_type=jnp.float32)  22.8 us
    ppermute x6, waiting for transfers between devices, along_x(): return lax.ppermute(block, 'expert', route)  20.5 us
    ppermute x6, waiting for transfers between devices, to_section(): return lax.ppermute(block, ('pipe', 'expert'), route)  15.3 us
    dot_general x10, matrix products, dot_t(): lax.dot_general(a, b, (((1,), (1,)), ((), ())), preferred_element_type=jn...  14.5 us
    ppermute x8, waiting for transfers between devices, along_z(): return lax.ppermute(block, 'expert', route)  13.4 us
  transfers between devices with their start and end apart: 25, of which 7 were waited for; matrix products, arithmetic and copies ran while one was open for 20% of the time, Pallas kernels for 0%

profile of v8, /device:TPU:16, one launch (start us, length us, event | category | flops | bytes accessed | tf_op | source)
XLA Modules:
  0.0 222.7 jit_solution(4522147975488017202)
XLA Ops:
  0.6 1.7 copy.55
  2.5 1.9 pad_maximum_fusion
  4.3 1.9 collective-permute-start.2
  6.9 9.1 %collective-permute-start = (bf16[16,3712]{1,0:T(8,128)(2,1)S(1)}, bf16[16,3712]{1,0:T(8,128)(2,1)S(1)}, u32[]{:S(2)}, u32[]{:S(2)}) collective-permute-start(bf16[16,3712]{1,0:T(8,128)(2,1)S(1)} %pad_maximum_fusion.7), channel_id=1, source_target_pairs={{0,2},{1,7},{2,4},{3,1},{4,6},{5,3},{6,0},{7,5},{8,10},{9,15},{10,... | collective-permute-start | bytes 356360 | tf_op jit(solution)/shard_map/forward_z/ppermute | solution.py:32
  16.1 5.6 %collective-permute-start.1 = (bf16[16,3712]{1,0:T(8,128)(2,1)S(1)}, bf16[16,3712]{1,0:T(8,128)(2,1)S(1)}, u32[]{:S(2)}, u32[]{:S(2)}) collective-permute-start(bf16[16,3712]{1,0:T(8,128)(2,1)S(1)} %pad_maximum_fusion.7), channel_id=1, source_target_pairs={{0,6},{1,3},{2,0},{3,5},{4,2},{5,7},{6,4},{7,1},{8,14},{9,11},{10,... | collective-permute-start | bytes 356360 | tf_op jit(solution)/shard_map/forward_z/ppermute | solution.py:32
  21.6 3.4 %collective-permute-start.6 = (bf16[3584,384]{1,0:T(8,128)(2,1)}, bf16[3584,384]{1,0:T(8,128)(2,1)}, u32[]{:S(2)}, u32[]{:S(2)}) collective-permute-start(bf16[3584,384]{1,0:T(8,128)(2,1)} %pad_maximum_fusion), channel_id=1, source_target_pairs={{0,8},{1,25},{2,10},{3,27},{4,12},{5,29},{6,14},{7,31},{8,16},{9,1... | collective-permute-start | bytes 8257544 | tf_op jit(solution)/shard_map/gather_weights/ppermute | solution.py:37
  25.0 3.7 %collective-permute-start.7 = (bf16[3584,384]{1,0:T(8,128)(2,1)}, bf16[3584,384]{1,0:T(8,128)(2,1)}, u32[]{:S(2)}, u32[]{:S(2)}) collective-permute-start(bf16[3584,384]{1,0:T(8,128)(2,1)} %pad_maximum_fusion), channel_id=1, source_target_pairs={{0,24},{1,9},{2,26},{3,11},{4,28},{5,13},{6,30},{7,15},{8,0},{9,17... | collective-permute-start | bytes 8257544 | tf_op jit(solution)/shard_map/gather_weights/ppermute | solution.py:37
  29.5 2.2 %collective-permute-done.1 = bf16[16,3712]{1,0:T(8,128)(2,1)S(1)} collective-permute-done((bf16[16,3712]{1,0:T(8,128)(2,1)S(1)}, bf16[16,3712]{1,0:T(8,128)(2,1)S(1)}, u32[]{:S(2)}, u32[]{:S(2)}) %collective-permute-start.1) | collective-permute-done | bytes 118816 | tf_op jit(solution)/shard_map/forward_z/ppermute | solution.py:32
  31.8 7.7 %collective-permute-start.3 = (bf16[16,3712]{1,0:T(8,128)(2,1)S(1)}, bf16[16,3712]{1,0:T(8,128)(2,1)S(1)}, u32[]{:S(2)}, u32[]{:S(2)}) collective-permute-start(bf16[16,3712]{1,0:T(8,128)(2,1)S(1)} %collective-permute-done), channel_id=1, source_target_pairs={{0,2},{1,7},{2,4},{3,1},{4,6},{5,3},{6,0},{7,5},{8,10},{9,15},{10,... | collective-permute-start | bytes 356360 | tf_op jit(solution)/shard_map/forward_z/ppermute | solution.py:32
  39.5 1.8 constant_dynamic-update-slice_fusion.8
  41.3 4.6 %collective-permute-start.12 = (bf16[16,7168]{1,0:T(8,128)(2,1)}, bf16[16,7168]{1,0:T(8,128)(2,1)}, u32[]{:S(2)}, u32[]{:S(2)}) collective-permute-start(bf16[16,7168]{1,0:T(8,128)(2,1)} %pad_maximum_fusion.6), channel_id=1, source_target_pairs={{0,2},{1,7},{2,4},{3,1},{4,6},{5,3},{6,0},{7,5},{8,10},{9,15},{10,... | collective-permute-start | bytes 688136 | tf_op jit(solution)/shard_map/backward_z/ppermute | solution.py:32
  45.9 5.1 %collective-permute-start.13 = (bf16[16,7168]{1,0:T(8,128)(2,1)}, bf16[16,7168]{1,0:T(8,128)(2,1)}, u32[]{:S(2)}, u32[]{:S(2)}) collective-permute-start(bf16[16,7168]{1,0:T(8,128)(2,1)} %pad_maximum_fusion.6), channel_id=1, source_target_pairs={{0,6},{1,3},{2,0},{3,5},{4,2},{5,7},{6,4},{7,1},{8,14},{9,11},{10,... | collective-permute-start | bytes 688136 | tf_op jit(solution)/shard_map/backward_z/ppermute | solution.py:32
  52.7 5.1 %collective-permute-start.4 = (bf16[48,3584]{1,0:T(8,128)(2,1)S(1)}, bf16[48,3584]{1,0:T(8,128)(2,1)S(1)}, u32[]{:S(2)}, u32[]{:S(2)}) collective-permute-start(bf16[48,3584]{1,0:T(8,128)(2,1)S(1)} %convolution_convert_fusion.1), channel_id=1, source_target_pairs={{0,16},{1,17},{2,18},{3,19},{4,20},{5,21},{6,22},{7,23},{8,24},{9,... | collective-permute-start | bytes 1032200 | tf_op jit(solution)/shard_map/forward_opposite/ppermute | solution.py:37
  57.7 7.3 %collective-permute-done.12 = bf16[16,7168]{1,0:T(8,128)(2,1)} collective-permute-done((bf16[16,7168]{1,0:T(8,128)(2,1)}, bf16[16,7168]{1,0:T(8,128)(2,1)}, u32[]{:S(2)}, u32[]{:S(2)}) %collective-permute-start.12) | collective-permute-done | bytes 229408 | tf_op jit(solution)/shard_map/backward_z/ppermute | solution.py:32
  65.1 8.4 %collective-permute-start.14 = (bf16[16,7168]{1,0:T(8,128)(2,1)}, bf16[16,7168]{1,0:T(8,128)(2,1)S(1)}, u32[]{:S(2)}, u32[]{:S(2)}) collective-permute-start(bf16[16,7168]{1,0:T(8,128)(2,1)} %collective-permute-done.12), channel_id=1, source_target_pairs={{0,2},{1,7},{2,4},{3,1},{4,6},{5,3},{6,0},{7,5},{8,10},{9,15},{10,... | collective-permute-start | bytes 688136 | tf_op jit(solution)/shard_map/backward_z/ppermute | solution.py:32
  73.5 1.7 constant_dynamic-update-slice_fusion.7
  75.2 1.8 constant_dynamic-update-slice_fusion.6
  77.0 17.0 %collective-permute-done.4 = bf16[48,3584]{1,0:T(8,128)(2,1)S(1)} collective-permute-done((bf16[48,3584]{1,0:T(8,128)(2,1)S(1)}, bf16[48,3584]{1,0:T(8,128)(2,1)S(1)}, u32[]{:S(2)}, u32[]{:S(2)}) %collective-permute-start.4) | collective-permute-done | bytes 344096 | tf_op jit(solution)/shard_map/forward_opposite/ppermute | solution.py:37
  94.8 1.9 fusion.19
  98.3 2.1 collective-permute-start.8
  100.5 4.0 %collective-permute-start.5 = (bf16[64,3712]{1,0:T(8,128)(2,1)S(1)}, bf16[64,3712]{1,0:T(8,128)(2,1)S(1)}, u32[]{:S(2)}, u32[]{:S(2)}) collective-permute-start(bf16[64,3712]{1,0:T(8,128)(2,1)S(1)} %pad_maximum_fusion.2), channel_id=1, source_target_pairs={{0,1},{1,0},{2,3},{3,2},{4,5},{5,4},{6,7},{7,6},{8,9},{9,8},{10,11... | collective-permute-start | bytes 1425416 | tf_op jit(solution)/shard_map/forward_experts/ppermute | solution.py:41
  105.3 1.9 collective-permute-start.19
  107.2 2.5 %convolution_convert_fusion = bf16[48,7168]{1,0:T(8,128)(2,1)} fusion(bf16[64,7168]{1,0:T(8,128)(2,1)} %get-tuple-element.51, f32[48]{0:T(128)S(1)} %get-tuple-element.80, s32[48]{0:T(128)S(1)} %get-tuple-element.79, f32[64]{0:T(128)S(1)} %get-tuple-element.41, s32[64]{0:T(128)S(1)} %and_select_fusion.2), kind=kOutput, calls=%fused_computation | convolution fusion | flops 44393472 | bytes 1606528 | tf_op jit(solution)/shard_map/backward_opposite/dot_general | solution.py:116
  109.7 4.6 %collective-permute-start.15 = (bf16[48,7168]{1,0:T(8,128)(2,1)}, bf16[48,7168]{1,0:T(8,128)(2,1)}, u32[]{:S(2)}, u32[]{:S(2)}) collective-permute-start(bf16[48,7168]{1,0:T(8,128)(2,1)} %convolution_convert_fusion), channel_id=1, source_target_pairs={{0,16},{1,17},{2,18},{3,19},{4,20},{5,21},{6,22},{7,23},{8,24},{9,... | collective-permute-start | bytes 2064392 | tf_op jit(solution)/shard_map/backward_opposite/ppermute | solution.py:37
  116.2 2.5 %fusion.6 = f32[128,256]{1,0:T(8,128)} fusion(bf16[3584,384]{1,0:T(8,128)(2,1)} %collective-permute-done.7, bf16[64,3584]{1,0:T(8,128)(2,1)S(1)} %slice.133, bf16[64,3584]{1,0:T(8,128)(2,1)S(1)} %copy-done.4), kind=kOutput, calls=%fused_computation.19 | convolution fusion | flops 236716032 | bytes 2883584 | tf_op jit(solution)/shard_map/forward_experts/dot_general | solution.py:108
  120.4 1.9 fusion.14
  122.3 1.6 fusion.3
  125.6 2.1 collective-permute-start.9
  127.7 3.5 %collective-permute-done.15 = bf16[48,7168]{1,0:T(8,128)(2,1)} collective-permute-done((bf16[48,7168]{1,0:T(8,128)(2,1)}, bf16[48,7168]{1,0:T(8,128)(2,1)}, u32[]{:S(2)}, u32[]{:S(2)}) %collective-permute-start.15) | collective-permute-done | bytes 688160 | tf_op jit(solution)/shard_map/backward_opposite/ppermute | solution.py:37
  131.2 2.0 fusion.17
  138.3 2.3 %fusion.4 = bf16[48,3584]{1,0:T(8,128)(2,1)S(1)} fusion(f32[48,3584]{1,0:T(8,128)S(1)} %fusion.95, bf16[3584,384]{1,0:T(8,128)(2,1)} %collective-permute-done.2, bf16[48,128]{1,0:T(8,128)(2,1)S(1)} %get-tuple-element.65, bf16[48,128]{1,0:T(8,128)(2,1)S(1)} %get-tuple-element.64), kind=kOutput, calls=%fused_computation.15 | convolution fusion | flops 88473600 | bytes 2891776 | tf_op jit(solution)/shard_map/backward_visitors/dot_general | solution.py:112
  140.6 4.6 %collective-permute-start.16 = (bf16[48,3584]{1,0:T(8,128)(2,1)S(1)}, bf16[48,3584]{1,0:T(8,128)(2,1)S(1)}, u32[]{:S(2)}, u32[]{:S(2)}) collective-permute-start(bf16[48,3584]{1,0:T(8,128)(2,1)S(1)} %fusion.4), channel_id=1, source_target_pairs={{0,16},{1,17},{2,18},{3,19},{4,20},{5,21},{6,22},{7,23},{8,24},{9,... | collective-permute-start | bytes 1032200 | tf_op jit(solution)/shard_map/backward_visitors/ppermute | solution.py:37
  146.5 1.9 fusion.12
  152.2 7.8 %collective-permute-start.17 = (bf16[16,3584]{1,0:T(8,128)(2,1)S(1)}, bf16[16,3584]{1,0:T(8,128)(2,1)S(1)}, u32[]{:S(2)}, u32[]{:S(2)}) collective-permute-start(bf16[16,3584]{1,0:T(8,128)(2,1)S(1)} %get-tuple-element.49), channel_id=1, source_target_pairs={{0,6},{1,3},{2,0},{3,5},{4,2},{5,7},{6,4},{7,1},{8,14},{9,11},{10,... | collective-permute-start | bytes 344072 | tf_op jit(solution)/shard_map/forward_experts/ppermute | solution.py:32
  160.1 2.3 %fusion.1 = f32[128,3584]{1,0:T(8,128)S(1)} fusion(f32[128,3584]{1,0:T(8,128)S(1)} %convolution_multiply_fusion.2, bf16[3584,384]{1,0:T(8,128)(2,1)} %collective-permute-done.6, f32[128]{0:T(128)S(1)} %get-tuple-element.37, bf16[128,128]{1,0:T(8,128)(2,1)S(1)} %get-tuple-element.61, bf16[128,128]{1,0:T(8,128)(2,1)S(1)} %get-tuple-element.60), kind=kOutput, calls=%fused_computation.4 | convolution fusion | flops 235929600 | bytes 5571072 | tf_op jit(solution)/shard_map/backward_experts/dot_general | solution.py:112
  162.4 3.9 %collective-permute-done.17 = bf16[16,3584]{1,0:T(8,128)(2,1)S(1)} collective-permute-done((bf16[16,3584]{1,0:T(8,128)(2,1)S(1)}, bf16[16,3584]{1,0:T(8,128)(2,1)S(1)}, u32[]{:S(2)}, u32[]{:S(2)}) %collective-permute-start.17) | collective-permute-done | bytes 114720 | tf_op jit(solution)/shard_map/forward_experts/ppermute | solution.py:32
  166.2 1.9 fusion.9
  169.7 2.3 %fusion = f32[128,3584]{1,0:T(8,128)S(1)} fusion(f32[128,3584]{1,0:T(8,128)S(1)} %fusion.1, bf16[3584,384]{1,0:T(8,128)(2,1)} %collective-permute-done.7, f32[128]{0:T(128)S(1)} %get-tuple-element.30, bf16[128,128]{1,0:T(8,128)(2,1)S(1)} %get-tuple-element.59, bf16[128,128]{1,0:T(8,128)(2,1)S(1)} %get-tuple-element.58), kind=kOutput, calls=%fused_computation.2 | convolution fusion | flops 235929600 | bytes 5571072 | tf_op jit(solution)/shard_map/backward_experts/dot_general | solution.py:112
  172.1 1.9 collective-permute-start.20
  174.0 5.1 %collective-permute-start.11 = (bf16[16,3584]{1,0:T(8,128)(2,1)S(1)}, bf16[16,3584]{1,0:T(8,128)(2,1)S(1)}, u32[]{:S(2)}, u32[]{:S(2)}) collective-permute-start(bf16[16,3584]{1,0:T(8,128)(2,1)S(1)} %get-tuple-element.48), channel_id=1, source_target_pairs={{0,34},{1,39},{2,36},{3,33},{4,38},{5,35},{6,32},{7,37},{8,42},{9,... | collective-permute-start | bytes 344072 | tf_op jit(solution)/shard_map/forward_home/ppermute | solution.py:53
  179.5 4.9 %collective-permute-start.23 = (bf16[16,3584]{1,0:T(8,128)(2,1)S(1)}, bf16[16,3584]{1,0:T(8,128)(2,1)S(1)}, u32[]{:S(2)}, u32[]{:S(2)}) collective-permute-start(bf16[16,3584]{1,0:T(8,128)(2,1)S(1)} %get-tuple-element.47), channel_id=1, source_target_pairs={{0,6},{1,3},{2,0},{3,5},{4,2},{5,7},{6,4},{7,1},{8,14},{9,11},{10,... | collective-permute-start | bytes 344072 | tf_op jit(solution)/shard_map/backward_home/ppermute | solution.py:32
  184.5 2.6 %collective-permute-start.10 = (f32[16,3584]{1,0:T(8,128)S(1)}, f32[16,3584]{1,0:T(8,128)S(1)}, u32[]{:S(2)}, u32[]{:S(2)}) collective-permute-start(f32[16,3584]{1,0:T(8,128)S(1)} %get-tuple-element.44), channel_id=1, source_target_pairs={{0,32},{1,33},{2,34},{3,35},{4,36},{5,37},{6,38},{7,39},{8,40},{9,... | collective-permute-start | bytes 688136 | tf_op jit(solution)/shard_map/forward_home/ppermute | solution.py:53
  187.1 6.6 %collective-permute-start.18 = (bf16[16,3584]{1,0:T(8,128)(2,1)S(1)}, bf16[16,3584]{1,0:T(8,128)(2,1)S(1)}, u32[]{:S(2)}, u32[]{:S(2)}) collective-permute-start(bf16[16,3584]{1,0:T(8,128)(2,1)S(1)} %get-tuple-element.45), channel_id=1, source_target_pairs={{0,38},{1,35},{2,32},{3,37},{4,34},{5,39},{6,36},{7,33},{8,46},{9,... | collective-permute-start | bytes 344072 | tf_op jit(solution)/shard_map/forward_home/ppermute | solution.py:53
  193.7 6.8 %collective-permute-start.22 = (bf16[16,3584]{1,0:T(8,128)(2,1)S(1)}, bf16[16,3584]{1,0:T(8,128)(2,1)S(1)}, u32[]{:S(2)}, u32[]{:S(2)}) collective-permute-start(bf16[16,3584]{1,0:T(8,128)(2,1)S(1)} %get-tuple-element.46), channel_id=1, source_target_pairs={{32,2},{33,7},{34,4},{35,1},{36,6},{37,3},{38,0},{39,5},{40,10},{4... | collective-permute-start | bytes 344072 | tf_op jit(solution)/shard_map/backward_home/ppermute | solution.py:53
  200.6 2.3 %collective-permute-start.21 = (f32[16,3584]{1,0:T(8,128)S(1)}, f32[16,3584]{1,0:T(8,128)S(1)}, u32[]{:S(2)}, u32[]{:S(2)}) collective-permute-start(f32[16,3584]{1,0:T(8,128)S(1)} %get-tuple-element.42), channel_id=1, source_target_pairs={{32,0},{33,1},{34,2},{35,3},{36,4},{37,5},{38,6},{39,7},{40,8},{41... | collective-permute-start | bytes 688136 | tf_op jit(solution)/shard_map/backward_home/ppermute | solution.py:53
  202.8 3.3 %collective-permute-start.24 = (bf16[16,3584]{1,0:T(8,128)(2,1)S(1)}, bf16[16,3584]{1,0:T(8,128)(2,1)S(1)}, u32[]{:S(2)}, u32[]{:S(2)}) collective-permute-start(bf16[16,3584]{1,0:T(8,128)(2,1)S(1)} %get-tuple-element.43), channel_id=1, source_target_pairs={{32,6},{33,3},{34,0},{35,5},{36,2},{37,7},{38,4},{39,1},{40,14},{4... | collective-permute-start | bytes 344072 | tf_op jit(solution)/shard_map/backward_home/ppermute | solution.py:53
  206.1 2.1 collective-permute-done.18
  208.9 13.1 %collective-permute-done.24 = bf16[16,3584]{1,0:T(8,128)(2,1)S(1)} collective-permute-done((bf16[16,3584]{1,0:T(8,128)(2,1)S(1)}, bf16[16,3584]{1,0:T(8,128)(2,1)S(1)}, u32[]{:S(2)}, u32[]{:S(2)}) %collective-permute-start.24) | collective-permute-done | bytes 114720 | tf_op jit(solution)/shard_map/backward_home/ppermute | solution.py:53
  (115 shorter events, 24.8 us)
Async XLA Ops:
  0.6 1.8 copy-start
  2.4 3.8 %copy-start.16 = (s32[1,16,2]{1,2,0:T(2,128)S(1)}, s32[1,16,2]{1,2,0:T(2,128)}, u32[]{:S(2)}) copy-start(s32[1,16,2]{1,2,0:T(2,128)} %param.14) | copy-start | bytes 388
  2.4 4.1 %copy-start.14 = (s32[1,16,2]{1,2,0:T(2,128)S(1)}, s32[1,16,2]{1,2,0:T(2,128)}, u32[]{:S(2)}) copy-start(s32[1,16,2]{1,2,0:T(2,128)} %param.15) | copy-start | bytes 388
  2.4 4.3 %copy-start.13 = (f32[1,16,2]{1,2,0:T(2,128)S(1)}, f32[1,16,2]{1,2,0:T(2,128)}, u32[]{:S(2)}) copy-start(f32[1,16,2]{1,2,0:T(2,128)} %param.17) | copy-start | bytes 388
  2.4 4.3 %copy-start.15 = (f32[1,16,2]{1,2,0:T(2,128)S(1)}, f32[1,16,2]{1,2,0:T(2,128)}, u32[]{:S(2)}) copy-start(f32[1,16,2]{1,2,0:T(2,128)} %param.16) | copy-start | bytes 388
  2.4 4.5 %copy-start.2 = (bf16[1,16,3584]{2,1,0:T(8,128)(2,1)S(1)}, bf16[1,16,3584]{2,1,0:T(8,128)(2,1)}, u32[]{:S(2)}) copy-start(bf16[1,16,3584]{2,1,0:T(8,128)(2,1)} %param.9) | copy-start | bytes 344068
  2.4 26.3 %copy-start.8 = (bf16[1,16,3584]{2,1,0:T(8,128)(2,1)S(1)}, bf16[1,16,3584]{2,1,0:T(8,128)(2,1)}, u32[]{:S(2)}) copy-start(bf16[1,16,3584]{2,1,0:T(8,128)(2,1)} %param.11) | copy-start | bytes 344068
  2.4 26.3 %copy-start.11 = (bf16[1,16,3584]{2,1,0:T(8,128)(2,1)S(1)}, bf16[1,16,3584]{2,1,0:T(8,128)(2,1)}, u32[]{:S(2)}) copy-start(bf16[1,16,3584]{2,1,0:T(8,128)(2,1)} %param.10) | copy-start | bytes 344068
  4.3 27.5 %collective-permute-start.2 = (bf16[3584,384]{1,0:T(8,128)(2,1)}, bf16[3584,384]{1,0:T(8,128)(2,1)}, u32[]{:S(2)}, u32[]{:S(2)}) collective-permute-start(bf16[3584,384]{1,0:T(8,128)(2,1)} %pad_maximum_fusion), channel_id=1, source_target_pairs={{0,1},{1,0},{2,3},{3,2},{4,5},{5,4},{6,7},{7,6},{8,9},{9,8},{10,11... | collective-permute-start | bytes 8257544 | tf_op jit(solution)/shard_map/gather_weights/ppermute | solution.py:41
  6.9 22.6 %collective-permute-start = (bf16[16,3712]{1,0:T(8,128)(2,1)S(1)}, bf16[16,3712]{1,0:T(8,128)(2,1)S(1)}, u32[]{:S(2)}, u32[]{:S(2)}) collective-permute-start(bf16[16,3712]{1,0:T(8,128)(2,1)S(1)} %pad_maximum_fusion.7), channel_id=1, source_target_pairs={{0,2},{1,7},{2,4},{3,1},{4,6},{5,3},{6,0},{7,5},{8,10},{9,15},{10,... | collective-permute-start | bytes 356360 | tf_op jit(solution)/shard_map/forward_z/ppermute | solution.py:32
  16.1 15.7 %collective-permute-start.1 = (bf16[16,3712]{1,0:T(8,128)(2,1)S(1)}, bf16[16,3712]{1,0:T(8,128)(2,1)S(1)}, u32[]{:S(2)}, u32[]{:S(2)}) collective-permute-start(bf16[16,3712]{1,0:T(8,128)(2,1)S(1)} %pad_maximum_fusion.7), channel_id=1, source_target_pairs={{0,6},{1,3},{2,0},{3,5},{4,2},{5,7},{6,4},{7,1},{8,14},{9,11},{10,... | collective-permute-start | bytes 356360 | tf_op jit(solution)/shard_map/forward_z/ppermute | solution.py:32
  21.6 88.1 %collective-permute-start.6 = (bf16[3584,384]{1,0:T(8,128)(2,1)}, bf16[3584,384]{1,0:T(8,128)(2,1)}, u32[]{:S(2)}, u32[]{:S(2)}) collective-permute-start(bf16[3584,384]{1,0:T(8,128)(2,1)} %pad_maximum_fusion), channel_id=1, source_target_pairs={{0,8},{1,25},{2,10},{3,27},{4,12},{5,29},{6,14},{7,31},{8,16},{9,1... | collective-permute-start | bytes 8257544 | tf_op jit(solution)/shard_map/gather_weights/ppermute | solution.py:37
  25.0 89.3 %collective-permute-start.7 = (bf16[3584,384]{1,0:T(8,128)(2,1)}, bf16[3584,384]{1,0:T(8,128)(2,1)}, u32[]{:S(2)}, u32[]{:S(2)}) collective-permute-start(bf16[3584,384]{1,0:T(8,128)(2,1)} %pad_maximum_fusion), channel_id=1, source_target_pairs={{0,24},{1,9},{2,26},{3,11},{4,28},{5,13},{6,30},{7,15},{8,0},{9,17... | collective-permute-start | bytes 8257544 | tf_op jit(solution)/shard_map/gather_weights/ppermute | solution.py:37
  31.8 19.2 %collective-permute-start.3 = (bf16[16,3712]{1,0:T(8,128)(2,1)S(1)}, bf16[16,3712]{1,0:T(8,128)(2,1)S(1)}, u32[]{:S(2)}, u32[]{:S(2)}) collective-permute-start(bf16[16,3712]{1,0:T(8,128)(2,1)S(1)} %collective-permute-done), channel_id=1, source_target_pairs={{0,2},{1,7},{2,4},{3,1},{4,6},{5,3},{6,0},{7,5},{8,10},{9,15},{10,... | collective-permute-start | bytes 356360 | tf_op jit(solution)/shard_map/forward_z/ppermute | solution.py:32
  41.3 23.8 %collective-permute-start.12 = (bf16[16,7168]{1,0:T(8,128)(2,1)}, bf16[16,7168]{1,0:T(8,128)(2,1)}, u32[]{:S(2)}, u32[]{:S(2)}) collective-permute-start(bf16[16,7168]{1,0:T(8,128)(2,1)} %pad_maximum_fusion.6), channel_id=1, source_target_pairs={{0,2},{1,7},{2,4},{3,1},{4,6},{5,3},{6,0},{7,5},{8,10},{9,15},{10,... | collective-permute-start | bytes 688136 | tf_op jit(solution)/shard_map/backward_z/ppermute | solution.py:32
  45.9 29.4 %collective-permute-start.13 = (bf16[16,7168]{1,0:T(8,128)(2,1)}, bf16[16,7168]{1,0:T(8,128)(2,1)}, u32[]{:S(2)}, u32[]{:S(2)}) collective-permute-start(bf16[16,7168]{1,0:T(8,128)(2,1)} %pad_maximum_fusion.6), channel_id=1, source_target_pairs={{0,6},{1,3},{2,0},{3,5},{4,2},{5,7},{6,4},{7,1},{8,14},{9,11},{10,... | collective-permute-start | bytes 688136 | tf_op jit(solution)/shard_map/backward_z/ppermute | solution.py:32
  52.7 41.8 %copy-start.1 = (bf16[1,128,3584]{2,1,0:T(8,128)(2,1)S(1)}, bf16[1,128,3584]{2,1,0:T(8,128)(2,1)}, u32[]{:S(2)}) copy-start(bf16[1,128,3584]{2,1,0:T(8,128)(2,1)} %param.13) | copy-start | bytes 2752516
  52.7 41.4 %collective-permute-start.4 = (bf16[48,3584]{1,0:T(8,128)(2,1)S(1)}, bf16[48,3584]{1,0:T(8,128)(2,1)S(1)}, u32[]{:S(2)}, u32[]{:S(2)}) collective-permute-start(bf16[48,3584]{1,0:T(8,128)(2,1)S(1)} %convolution_convert_fusion.1), channel_id=1, source_target_pairs={{0,16},{1,17},{2,18},{3,19},{4,20},{5,21},{6,22},{7,23},{8,24},{9,... | collective-permute-start | bytes 1032200 | tf_op jit(solution)/shard_map/forward_opposite/ppermute | solution.py:37
  65.1 39.4 %collective-permute-start.14 = (bf16[16,7168]{1,0:T(8,128)(2,1)}, bf16[16,7168]{1,0:T(8,128)(2,1)S(1)}, u32[]{:S(2)}, u32[]{:S(2)}) collective-permute-start(bf16[16,7168]{1,0:T(8,128)(2,1)} %collective-permute-done.12), channel_id=1, source_target_pairs={{0,2},{1,7},{2,4},{3,1},{4,6},{5,3},{6,0},{7,5},{8,10},{9,15},{10,... | collective-permute-start | bytes 688136 | tf_op jit(solution)/shard_map/backward_z/ppermute | solution.py:32
  98.3 16.8 %copy-start.4 = (bf16[64,3584]{1,0:T(8,128)(2,1)S(1)}, bf16[64,3584]{1,0:T(8,128)(2,1)}, u32[]{:S(2)}) copy-start(bf16[64,3584]{1,0:T(8,128)(2,1)} %slice.131) | copy-start | bytes 1376260
  98.3 16.0 %collective-permute-start.8 = (bf16[48,3584]{1,0:T(8,128)(2,1)S(1)}, bf16[48,3584]{1,0:T(8,128)(2,1)S(1)}, u32[]{:S(2)}, u32[]{:S(2)}) collective-permute-start(bf16[48,3584]{1,0:T(8,128)(2,1)S(1)} %fusion.5), channel_id=1, source_target_pairs={{0,16},{1,17},{2,18},{3,19},{4,20},{5,21},{6,22},{7,23},{8,24},{9,... | collective-permute-start | bytes 1032200 | tf_op jit(solution)/shard_map/forward_opposite/ppermute | solution.py:37
  100.5 13.9 %collective-permute-start.5 = (bf16[64,3712]{1,0:T(8,128)(2,1)S(1)}, bf16[64,3712]{1,0:T(8,128)(2,1)S(1)}, u32[]{:S(2)}, u32[]{:S(2)}) collective-permute-start(bf16[64,3712]{1,0:T(8,128)(2,1)S(1)} %pad_maximum_fusion.2), channel_id=1, source_target_pairs={{0,1},{1,0},{2,3},{3,2},{4,5},{5,4},{6,7},{7,6},{8,9},{9,8},{10,11... | collective-permute-start | bytes 1425416 | tf_op jit(solution)/shard_map/forward_experts/ppermute | solution.py:41
  105.3 40.0 %collective-permute-start.19 = (bf16[64,7168]{1,0:T(8,128)(2,1)}, bf16[64,7168]{1,0:T(8,128)(2,1)}, u32[]{:S(2)}, u32[]{:S(2)}) collective-permute-start(bf16[64,7168]{1,0:T(8,128)(2,1)} %get-tuple-element.51), channel_id=1, source_target_pairs={{0,1},{1,0},{2,3},{3,2},{4,5},{5,4},{6,7},{7,6},{8,9},{9,8},{10,11... | collective-permute-start | bytes 2752520 | tf_op jit(solution)/shard_map/backward_experts/ppermute | solution.py:41
  109.7 21.5 %collective-permute-start.15 = (bf16[48,7168]{1,0:T(8,128)(2,1)}, bf16[48,7168]{1,0:T(8,128)(2,1)}, u32[]{:S(2)}, u32[]{:S(2)}) collective-permute-start(bf16[48,7168]{1,0:T(8,128)(2,1)} %convolution_convert_fusion), channel_id=1, source_target_pairs={{0,16},{1,17},{2,18},{3,19},{4,20},{5,21},{6,22},{7,23},{8,24},{9,... | collective-permute-start | bytes 2064392 | tf_op jit(solution)/shard_map/backward_opposite/ppermute | solution.py:37
  114.3 0.8 copy-start.9
  115.1 3.6 %copy-start.6 = (bf16[64,3584]{1,0:T(8,128)(2,1)}, bf16[64,3584]{1,0:T(8,128)(2,1)S(1)}, u32[]{:S(2)}) copy-start(bf16[64,3584]{1,0:T(8,128)(2,1)S(1)} %slice.133) | copy-start | bytes 1376260
  118.8 1.6 copy-start.5
  118.9 1.5 copy-start.7
  122.3 1.6 copy-start.12
  125.6 26.1 %collective-permute-start.9 = (bf16[64,3584]{1,0:T(8,128)(2,1)S(1)}, bf16[64,3584]{1,0:T(8,128)(2,1)S(1)}, u32[]{:S(2)}, u32[]{:S(2)}) collective-permute-start(bf16[64,3584]{1,0:T(8,128)(2,1)S(1)} %slice.226), channel_id=1, source_target_pairs={{0,1},{1,0},{2,3},{3,2},{4,5},{5,4},{6,7},{7,6},{8,9},{9,8},{10,11... | collective-permute-start | bytes 1376264 | tf_op jit(solution)/shard_map/forward_experts/ppermute | solution.py:41
  138.3 7.0 %copy-start.3 = (bf16[128,7168]{1,0:T(8,128)(2,1)S(1)}, bf16[128,7168]{1,0:T(8,128)(2,1)}, u32[]{:S(2)}) copy-start(bf16[128,7168]{1,0:T(8,128)(2,1)} %get-tuple-element.50) | copy-start | bytes 5505028
  140.6 21.7 %collective-permute-start.16 = (bf16[48,3584]{1,0:T(8,128)(2,1)S(1)}, bf16[48,3584]{1,0:T(8,128)(2,1)S(1)}, u32[]{:S(2)}, u32[]{:S(2)}) collective-permute-start(bf16[48,3584]{1,0:T(8,128)(2,1)S(1)} %fusion.4), channel_id=1, source_target_pairs={{0,16},{1,17},{2,18},{3,19},{4,20},{5,21},{6,22},{7,23},{8,24},{9,... | collective-permute-start | bytes 1032200 | tf_op jit(solution)/shard_map/backward_visitors/ppermute | solution.py:37
  150.9 1.0 copy-start.10
  152.2 14.0 %collective-permute-start.17 = (bf16[16,3584]{1,0:T(8,128)(2,1)S(1)}, bf16[16,3584]{1,0:T(8,128)(2,1)S(1)}, u32[]{:S(2)}, u32[]{:S(2)}) collective-permute-start(bf16[16,3584]{1,0:T(8,128)(2,1)S(1)} %get-tuple-element.49), channel_id=1, source_target_pairs={{0,6},{1,3},{2,0},{3,5},{4,2},{5,7},{6,4},{7,1},{8,14},{9,11},{10,... | collective-permute-start | bytes 344072 | tf_op jit(solution)/shard_map/forward_experts/ppermute | solution.py:32
  172.1 7.0 %collective-permute-start.20 = (bf16[64,3584]{1,0:T(8,128)(2,1)S(1)}, bf16[64,3584]{1,0:T(8,128)(2,1)S(1)}, u32[]{:S(2)}, u32[]{:S(2)}) collective-permute-start(bf16[64,3584]{1,0:T(8,128)(2,1)S(1)} %slice.225), channel_id=1, source_target_pairs={{0,1},{1,0},{2,3},{3,2},{4,5},{5,4},{6,7},{7,6},{8,9},{9,8},{10,11... | collective-permute-start | bytes 1376264 | tf_op jit(solution)/shard_map/backward_experts/ppermute | solution.py:41
  174.0 28.8 %collective-permute-start.11 = (bf16[16,3584]{1,0:T(8,128)(2,1)S(1)}, bf16[16,3584]{1,0:T(8,128)(2,1)S(1)}, u32[]{:S(2)}, u32[]{:S(2)}) collective-permute-start(bf16[16,3584]{1,0:T(8,128)(2,1)S(1)} %get-tuple-element.48), channel_id=1, source_target_pairs={{0,34},{1,39},{2,36},{3,33},{4,38},{5,35},{6,32},{7,37},{8,42},{9,... | collective-permute-start | bytes 344072 | tf_op jit(solution)/shard_map/forward_home/ppermute | solution.py:53
  179.5 21.0 %collective-permute-start.23 = (bf16[16,3584]{1,0:T(8,128)(2,1)S(1)}, bf16[16,3584]{1,0:T(8,128)(2,1)S(1)}, u32[]{:S(2)}, u32[]{:S(2)}) collective-permute-start(bf16[16,3584]{1,0:T(8,128)(2,1)S(1)} %get-tuple-element.47), channel_id=1, source_target_pairs={{0,6},{1,3},{2,0},{3,5},{4,2},{5,7},{6,4},{7,1},{8,14},{9,11},{10,... | collective-permute-start | bytes 344072 | tf_op jit(solution)/shard_map/backward_home/ppermute | solution.py:32
  184.5 23.7 %collective-permute-start.10 = (f32[16,3584]{1,0:T(8,128)S(1)}, f32[16,3584]{1,0:T(8,128)S(1)}, u32[]{:S(2)}, u32[]{:S(2)}) collective-permute-start(f32[16,3584]{1,0:T(8,128)S(1)} %get-tuple-element.44), channel_id=1, source_target_pairs={{0,32},{1,33},{2,34},{3,35},{4,36},{5,37},{6,38},{7,39},{8,40},{9,... | collective-permute-start | bytes 688136 | tf_op jit(solution)/shard_map/forward_home/ppermute | solution.py:53
  187.1 21.1 %collective-permute-start.18 = (bf16[16,3584]{1,0:T(8,128)(2,1)S(1)}, bf16[16,3584]{1,0:T(8,128)(2,1)S(1)}, u32[]{:S(2)}, u32[]{:S(2)}) collective-permute-start(bf16[16,3584]{1,0:T(8,128)(2,1)S(1)} %get-tuple-element.45), channel_id=1, source_target_pairs={{0,38},{1,35},{2,32},{3,37},{4,34},{5,39},{6,36},{7,33},{8,46},{9,... | collective-permute-start | bytes 344072 | tf_op jit(solution)/shard_map/forward_home/ppermute | solution.py:53
  193.7 15.2 %collective-permute-start.22 = (bf16[16,3584]{1,0:T(8,128)(2,1)S(1)}, bf16[16,3584]{1,0:T(8,128)(2,1)S(1)}, u32[]{:S(2)}, u32[]{:S(2)}) collective-permute-start(bf16[16,3584]{1,0:T(8,128)(2,1)S(1)} %get-tuple-element.46), channel_id=1, source_target_pairs={{32,2},{33,7},{34,4},{35,1},{36,6},{37,3},{38,0},{39,5},{40,10},{4... | collective-permute-start | bytes 344072 | tf_op jit(solution)/shard_map/backward_home/ppermute | solution.py:53
  200.6 21.5 %collective-permute-start.21 = (f32[16,3584]{1,0:T(8,128)S(1)}, f32[16,3584]{1,0:T(8,128)S(1)}, u32[]{:S(2)}, u32[]{:S(2)}) collective-permute-start(f32[16,3584]{1,0:T(8,128)S(1)} %get-tuple-element.42), channel_id=1, source_target_pairs={{32,0},{33,1},{34,2},{35,3},{36,4},{37,5},{38,6},{39,7},{40,8},{41... | collective-permute-start | bytes 688136 | tf_op jit(solution)/shard_map/backward_home/ppermute | solution.py:53
  202.8 19.2 %collective-permute-start.24 = (bf16[16,3584]{1,0:T(8,128)(2,1)S(1)}, bf16[16,3584]{1,0:T(8,128)(2,1)S(1)}, u32[]{:S(2)}, u32[]{:S(2)}) collective-permute-start(bf16[16,3584]{1,0:T(8,128)(2,1)S(1)} %get-tuple-element.43), channel_id=1, source_target_pairs={{32,6},{33,3},{34,0},{35,5},{36,2},{37,7},{38,4},{39,1},{40,14},{4... | collective-permute-start | bytes 344072 | tf_op jit(solution)/shard_map/backward_home/ppermute | solution.py:53

commit v9 on v6

--- a/solution.py
+++ b/solution.py
@@ -40,16 +40,10 @@
     return lax.ppermute(block, "expert", expert_route(lambda x, z, c: (x, z, 1 - c)))
 
 
-def to_section(block, step, distance):
+def to_section(block, step):
     sections = lax.axis_size("pipe")
-    width = EXPERTS * Z * CORES
-    route = [
-        (p * width + source, (p + step) * width + target)
-        for p in range(sections)
-        if 0 <= p + step < sections
-        for source, target in expert_route(lambda x, z, c: (x, (z + distance * turn(c)) % Z, c))
-    ]
-    return lax.ppermute(block, ("pipe", "expert"), route)
+    route = [(p, p + step) for p in range(sections) if 0 <= p + step < sections]
+    return lax.ppermute(block, "pipe", route)
 
 
 def together(*values):
@@ -110,15 +104,6 @@
     return dot_t(grad, gate_up)
 
 
-def send_home(mixture, residual, passed, step):
-    own, near, far = jnp.split(mixture, Z, axis=0)[:3]
-    near = near + passed.astype(jnp.float32)
-    total = to_section(own + residual.astype(jnp.float32), step, 0)
-    total = total + to_section(far.astype(jnp.bfloat16), step, 1).astype(jnp.float32)
-    total = total + to_section(near.astype(jnp.bfloat16), step, -1).astype(jnp.float32)
-    return total.astype(jnp.bfloat16)
-
-
 def on_device(
     forward_input,
     backward_input,
@@ -171,16 +156,20 @@
             backward_sum = backward_sum + column_of(shares[:, EXPERTS:], expert) * out
     half = Z * rows
     with jax.named_scope("cores"):
-        others = [
-            other_core(total[half:].astype(jnp.bfloat16)) for total in (forward_sum, backward_sum)
-        ]
-        mixture = forward_sum[:half] + others[0].astype(jnp.float32)
-        back_mixture = backward_sum[:half] + others[1].astype(jnp.float32)
+        total = jnp.concatenate([forward_sum, backward_sum], axis=1)
+        other = other_core(total[half:].astype(jnp.bfloat16))
+        total = total[:half] + other.astype(jnp.float32)
     with jax.named_scope("home"):
-        passed = [total[half - rows :] for total in (mixture, back_mixture)]
-        passed = along_z(jnp.concatenate(passed, axis=1).astype(jnp.bfloat16), -1)
-        forward_next = send_home(mixture, tokens, passed[:, :model], 1)
-        backward_next = send_home(back_mixture, upstream, passed[:, model:], -1)
+        own, near, far, passed = jnp.split(total, Z, axis=0)
+        passed = along_z(passed.astype(jnp.bfloat16), -1)
+        far = along_z(far.astype(jnp.bfloat16), 1)
+        near = along_z((near + passed.astype(jnp.float32)).astype(jnp.bfloat16), -1)
+        residual = jnp.concatenate([tokens, upstream], axis=1).astype(jnp.float32)
+        total = own + residual + far.astype(jnp.float32) + near.astype(jnp.float32)
+        total = total.astype(jnp.bfloat16)
+    with jax.named_scope("sections"):
+        forward_next = to_section(total[:, :model], 1)
+        backward_next = to_section(total[:, model:], -1)
     return (forward_next[None], backward_next[None])
 
 

time: 181 us -> 179 us (0.989)
  starting transfers between devices: 99.3 us -> 81.7 us
  waiting for transfers between devices: 45.6 us -> 62 us
    ppermute x6 -> x2, starting transfers between devices: 31.5 us -> 5.84 us  [to_section(): return lax.ppermute(block, 'pipe', route)]
    ppermute x4 -> x6, waiting for transfers between devices: 24 us -> 42.4 us  [along_z(): return lax.ppermute(block, 'expert', route)]
    ppermute x4 -> x6, starting transfers between devices: 52.3 us -> 62.7 us  [along_z(): return lax.ppermute(block, 'expert', route)]
    ppermute x6 -> x2, waiting for transfers between devices: 9.88 us -> 6.64 us  [to_section(): return lax.ppermute(block, 'pipe', route)]
    ppermute x3 -> x2, starting transfers between devices: 6.24 us -> 3.84 us  [other_core(): lax.ppermute(block, 'expert', expert_route(lambda x, z, c: (x, z, 1 - c)))]
  transfers between devices with their start and end apart: 16 -> 13, of which waited for: 9 -> 9; matrix products, arithmetic and copies ran while one was open for 15% -> 13% of each run, Pallas kernels for 0% -> 0%
where the time goes in v9:
time: 179 us; the launch traced here: 177 us
  starting transfers between devices  81.7 us (46%)
  waiting for transfers between devices  62 us (35%)
  matrix products  23.3 us (13%)
  local copies, waits for them, and re-layouts  5.44 us (3%)
  other arithmetic  3.75 us (2%)
    ppermute x6, starting transfers between devices, along_z(): return lax.ppermute(block, 'expert', route)  62.7 us
    ppermute x6, waiting for transfers between devices, along_z(): return lax.ppermute(block, 'expert', route)  42.4 us
    dot_general x12, matrix products, dot(): return jnp.dot(a, b, preferred_element_type=jnp.float32)  13.3 us
    ppermute x3, waiting for transfers between devices, along_x(): return lax.ppermute(block, 'expert', route)  10.1 us
    dot_general x8, matrix products, dot_t(): lax.dot_general(a, b, (((1,), (1,)), ((), ())), preferred_element_type=jn...  9.94 us
    ppermute x3, starting transfers between devices, along_x(): return lax.ppermute(block, 'expert', route)  9.24 us
    ppermute x2, waiting for transfers between devices, to_section(): return lax.ppermute(block, 'pipe', route)  6.64 us
    ppermute x2, starting transfers between devices, to_section(): return lax.ppermute(block, 'pipe', route)  5.84 us
  transfers between devices with their start and end apart: 13, of which 9 were waited for; matrix products, arithmetic and copies ran while one was open for 13% of the time, Pallas kernels for 0%

profile of v9, /device:TPU:24, one launch (start us, length us, event | category | flops | bytes accessed | tf_op | source)
XLA Modules:
  0.0 177.3 jit_solution(5371247295636324372)
XLA Ops:
  0.6 1.7 copy.36
  2.5 1.8 %pad_maximum_fusion = bf16[3584,384]{1,0:T(8,128)(2,1)} fusion(bf16[3584,128]{1,0:T(8,128)(2,1)S(1)} %copy.36, bf16[3584,256]{1,0:T(8,128)(2,1)S(1)} %bitcast.25), kind=kLoop, calls=%fused_computation.16 | loop fusion | flops 5505024 | bytes 5505024 | tf_op jit(solution)/shard_map/gather_weights/concatenate | solution.py:126
  4.3 4.7 %collective-permute-start.1 = (bf16[3584,384]{1,0:T(8,128)(2,1)}, bf16[3584,384]{1,0:T(8,128)(2,1)}, u32[]{:S(2)}, u32[]{:S(2)}) collective-permute-start(bf16[3584,384]{1,0:T(8,128)(2,1)} %pad_maximum_fusion), channel_id=1, source_target_pairs={{0,24},{1,9},{2,26},{3,11},{4,28},{5,13},{6,30},{7,15},{8,0},{9,17... | collective-permute-start | bytes 8257544 | tf_op jit(solution)/shard_map/gather_weights/ppermute | solution.py:36
  8.9 1.9 %collective-permute-start = (bf16[3584,384]{1,0:T(8,128)(2,1)}, bf16[3584,384]{1,0:T(8,128)(2,1)}, u32[]{:S(2)}, u32[]{:S(2)}) collective-permute-start(bf16[3584,384]{1,0:T(8,128)(2,1)} %pad_maximum_fusion), channel_id=1, source_target_pairs={{0,8},{1,25},{2,10},{3,27},{4,12},{5,29},{6,14},{7,31},{8,16},{9,1... | collective-permute-start | bytes 8257544 | tf_op jit(solution)/shard_map/gather_weights/ppermute | solution.py:36
  11.1 9.1 %collective-permute-start.2 = (bf16[16,10880]{1,0:T(8,128)(2,1)S(1)}, bf16[16,10880]{1,0:T(8,128)(2,1)S(1)}, u32[]{:S(2)}, u32[]{:S(2)}) collective-permute-start(bf16[16,10880]{1,0:T(8,128)(2,1)S(1)} %pad_maximum_fusion.6), channel_id=1, source_target_pairs={{0,2},{1,7},{2,4},{3,1},{4,6},{5,3},{6,0},{7,5},{8,10},{9,15},{10,... | collective-permute-start | bytes 1044488 | tf_op jit(solution)/shard_map/gather_rows/ppermute | solution.py:31
  20.2 5.6 %collective-permute-start.3 = (bf16[16,10880]{1,0:T(8,128)(2,1)S(1)}, bf16[16,10880]{1,0:T(8,128)(2,1)S(1)}, u32[]{:S(2)}, u32[]{:S(2)}) collective-permute-start(bf16[16,10880]{1,0:T(8,128)(2,1)S(1)} %pad_maximum_fusion.6), channel_id=1, source_target_pairs={{0,6},{1,3},{2,0},{3,5},{4,2},{5,7},{6,4},{7,1},{8,14},{9,11},{10,... | collective-permute-start | bytes 1044488 | tf_op jit(solution)/shard_map/gather_rows/ppermute | solution.py:31
  25.8 3.6 %collective-permute-done.2 = bf16[16,10880]{1,0:T(8,128)(2,1)S(1)} collective-permute-done((bf16[16,10880]{1,0:T(8,128)(2,1)S(1)}, bf16[16,10880]{1,0:T(8,128)(2,1)S(1)}, u32[]{:S(2)}, u32[]{:S(2)}) %collective-permute-start.2) | collective-permute-done | bytes 348192 | tf_op jit(solution)/shard_map/gather_rows/ppermute | solution.py:31
  29.4 30.4 %collective-permute-start.4 = (bf16[16,10880]{1,0:T(8,128)(2,1)S(1)}, bf16[16,10880]{1,0:T(8,128)(2,1)S(1)}, u32[]{:S(2)}, u32[]{:S(2)}) collective-permute-start(bf16[16,10880]{1,0:T(8,128)(2,1)S(1)} %collective-permute-done.2), channel_id=1, source_target_pairs={{0,2},{1,7},{2,4},{3,1},{4,6},{5,3},{6,0},{7,5},{8,10},{9,15},{10,... | collective-permute-start | bytes 1044488 | tf_op jit(solution)/shard_map/gather_rows/ppermute | solution.py:31
  59.9 14.8 %collective-permute-done.4 = bf16[16,10880]{1,0:T(8,128)(2,1)S(1)} collective-permute-done((bf16[16,10880]{1,0:T(8,128)(2,1)S(1)}, bf16[16,10880]{1,0:T(8,128)(2,1)S(1)}, u32[]{:S(2)}, u32[]{:S(2)}) %collective-permute-start.4) | collective-permute-done | bytes 348192 | tf_op jit(solution)/shard_map/gather_rows/ppermute | solution.py:31
  74.7 1.0 pad_maximum_fusion.2
  75.7 1.9 %collective-permute-start.5 = (bf16[64,10880]{1,0:T(8,128)(2,1)S(1)}, bf16[64,10880]{1,0:T(8,128)(2,1)}, u32[]{:S(2)}, u32[]{:S(2)}) collective-permute-start(bf16[64,10880]{1,0:T(8,128)(2,1)S(1)} %pad_maximum_fusion.2), channel_id=1, source_target_pairs={{0,1},{1,0},{2,3},{3,2},{4,5},{5,4},{6,7},{7,6},{8,9},{9,8},{10,11... | collective-permute-start | bytes 4177928 | tf_op jit(solution)/shard_map/gather_opposite/ppermute | solution.py:40
  77.7 2.7 %collective-permute-start.6 = (bf16[3584,384]{1,0:T(8,128)(2,1)}, bf16[3584,384]{1,0:T(8,128)(2,1)S(1)}, u32[]{:S(2)}, u32[]{:S(2)}) collective-permute-start(bf16[3584,384]{1,0:T(8,128)(2,1)} %collective-permute-done), channel_id=1, source_target_pairs={{0,8},{1,25},{2,10},{3,27},{4,12},{5,29},{6,14},{7,31},{8,16},{9,1... | collective-permute-start | bytes 8257544 | tf_op jit(solution)/shard_map/gather_opposite/ppermute | solution.py:36
  80.8 1.4 fusion.94
  82.2 1.9 %fusion.20 = f32[128,256]{1,0:T(8,128)S(1)} fusion(bf16[3584,384]{1,0:T(8,128)(2,1)} %collective-permute-done, bf16[64,3584]{1,0:T(8,128)(2,1)S(1)} %get-tuple-element.32, bf16[64,3584]{1,0:T(8,128)(2,1)S(1)} %get-tuple-element.29), kind=kOutput, calls=%fused_computation.32 | convolution fusion | flops 236716032 | bytes 2883584 | tf_op jit(solution)/shard_map/experts/dot_general | solution.py:84
  84.2 0.4 fusion.83
  84.6 1.9 %fusion.15 = f32[128,256]{1,0:T(8,128)S(1)} fusion(bf16[3584,384]{1,0:T(8,128)(2,1)} %collective-permute-done.1, bf16[64,3584]{1,0:T(8,128)(2,1)S(1)} %get-tuple-element.32, bf16[64,3584]{1,0:T(8,128)(2,1)S(1)} %get-tuple-element.29), kind=kOutput, calls=%fused_computation.27 | convolution fusion | flops 236716032 | bytes 2883584 | tf_op jit(solution)/shard_map/experts/dot_general | solution.py:84
  86.5 1.6 fusion.48
  88.1 1.7 fusion.45
  89.8 0.4 fusion.51
  90.2 0.7 slice.92
  90.9 1.9 %fusion.22 = f32[128,256]{1,0:T(8,128)S(1)} fusion(bf16[3584,384]{1,0:T(8,128)(2,1)} %collective-permute-done, bf16[64,3584]{1,0:T(8,128)(2,1)S(1)} %get-tuple-element.31, bf16[64,3584]{1,0:T(8,128)(2,1)S(1)} %get-tuple-element.28), kind=kOutput, calls=%fused_computation.34 | convolution fusion | flops 236716032 | bytes 2883584 | tf_op jit(solution)/shard_map/experts/dot_general | solution.py:84
  93.2 1.9 %fusion.17 = f32[128,256]{1,0:T(8,128)S(1)} fusion(bf16[3584,384]{1,0:T(8,128)(2,1)} %collective-permute-done.1, bf16[64,3584]{1,0:T(8,128)(2,1)S(1)} %get-tuple-element.31, bf16[64,3584]{1,0:T(8,128)(2,1)S(1)} %get-tuple-element.28), kind=kOutput, calls=%fused_computation.29 | convolution fusion | flops 236716032 | bytes 2883584 | tf_op jit(solution)/shard_map/experts/dot_general | solution.py:84
  95.1 0.4 fusion.85
  95.5 0.4 convolution_multiply_fusion.7
  95.9 0.7 convolution_multiply_fusion.3
  96.7 1.6 fusion.5
  98.3 1.6 fusion.4
  99.9 2.3 %fusion.2 = f32[128,3584]{1,0:T(8,128)S(1)} fusion(f32[128,3584]{1,0:T(8,128)S(1)} %convolution_multiply_fusion.3, bf16[3584,384]{1,0:T(8,128)(2,1)} %collective-permute-done, f32[128]{0:T(128)S(1)} %get-tuple-element.21, bf16[128,128]{1,0:T(8,128)(2,1)S(1)} %get-tuple-element.43, bf16[128,128]{1,0:T(8,128)(2,1)S(1)} %get-tuple-element.42), kind=kOutput, calls=%fused_computation.5 | convolution fusion | flops 235929600 | bytes 5571072 | tf_op jit(solution)/shard_map/experts/dot_general | solution.py:88
  102.1 2.3 %fusion.1 = f32[128,3584]{1,0:T(8,128)S(1)} fusion(f32[128,3584]{1,0:T(8,128)S(1)} %fusion.2, bf16[3584,384]{1,0:T(8,128)(2,1)} %collective-permute-done.1, f32[128]{0:T(128)S(1)} %get-tuple-element.23, bf16[128,128]{1,0:T(8,128)(2,1)S(1)} %get-tuple-element.41, bf16[128,128]{1,0:T(8,128)(2,1)S(1)} %get-tuple-element.40), kind=kOutput, calls=%fused_computation.3 | convolution fusion | flops 235929600 | bytes 5571072 | tf_op jit(solution)/shard_map/experts/dot_general | solution.py:88
  104.4 10.1 %collective-permute-done.6 = bf16[3584,384]{1,0:T(8,128)(2,1)S(1)} collective-permute-done((bf16[3584,384]{1,0:T(8,128)(2,1)}, bf16[3584,384]{1,0:T(8,128)(2,1)S(1)}, u32[]{:S(2)}, u32[]{:S(2)}) %collective-permute-start.6) | collective-permute-done | bytes 2752544 | tf_op jit(solution)/shard_map/gather_opposite/ppermute | solution.py:36
  114.5 0.4 fusion.10
  114.9 0.4 fusion.12
  115.3 0.4 fusion.42
  115.7 0.4 fusion.3
  116.2 0.7 fusion
  117.0 1.9 %collective-permute-start.7 = (bf16[64,7168]{1,0:T(8,128)(2,1)S(1)}, bf16[64,7168]{1,0:T(8,128)(2,1)S(1)}, u32[]{:S(2)}, u32[]{:S(2)}) collective-permute-start(bf16[64,7168]{1,0:T(8,128)(2,1)S(1)} %fusion.8), channel_id=1, source_target_pairs={{0,1},{1,0},{2,3},{3,2},{4,5},{5,4},{6,7},{7,6},{8,9},{9,8},{10,11... | collective-permute-start | bytes 2752520 | tf_op jit(solution)/shard_map/cores/ppermute | solution.py:40
  118.9 2.4 %collective-permute-done.7 = bf16[64,7168]{1,0:T(8,128)(2,1)S(1)} collective-permute-done((bf16[64,7168]{1,0:T(8,128)(2,1)S(1)}, bf16[64,7168]{1,0:T(8,128)(2,1)S(1)}, u32[]{:S(2)}, u32[]{:S(2)}) %collective-permute-start.7) | collective-permute-done | bytes 917536 | tf_op jit(solution)/shard_map/cores/ppermute | solution.py:40
  121.7 7.2 %collective-permute-start.9 = (bf16[16,7168]{1,0:T(8,128)(2,1)S(1)}, bf16[16,7168]{1,0:T(8,128)(2,1)S(1)}, u32[]{:S(2)}, u32[]{:S(2)}) collective-permute-start(bf16[16,7168]{1,0:T(8,128)(2,1)S(1)} %get-tuple-element.35), channel_id=1, source_target_pairs={{0,6},{1,3},{2,0},{3,5},{4,2},{5,7},{6,4},{7,1},{8,14},{9,11},{10,... | collective-permute-start | bytes 688136 | tf_op jit(solution)/shard_map/home/ppermute | solution.py:31
  128.9 3.0 %collective-permute-start.8 = (bf16[16,7168]{1,0:T(8,128)(2,1)S(1)}, bf16[16,7168]{1,0:T(8,128)(2,1)S(1)}, u32[]{:S(2)}, u32[]{:S(2)}) collective-permute-start(bf16[16,7168]{1,0:T(8,128)(2,1)S(1)} %get-tuple-element.34), channel_id=1, source_target_pairs={{0,2},{1,7},{2,4},{3,1},{4,6},{5,3},{6,0},{7,5},{8,10},{9,15},{10,... | collective-permute-start | bytes 688136 | tf_op jit(solution)/shard_map/home/ppermute | solution.py:31
  131.9 15.7 %collective-permute-done.9 = bf16[16,7168]{1,0:T(8,128)(2,1)S(1)} collective-permute-done((bf16[16,7168]{1,0:T(8,128)(2,1)S(1)}, bf16[16,7168]{1,0:T(8,128)(2,1)S(1)}, u32[]{:S(2)}, u32[]{:S(2)}) %collective-permute-start.9) | collective-permute-done | bytes 229408 | tf_op jit(solution)/shard_map/home/ppermute | solution.py:31
  147.6 7.4 %collective-permute-start.10 = (bf16[16,7168]{1,0:T(8,128)(2,1)S(1)}, bf16[16,7168]{1,0:T(8,128)(2,1)S(1)}, u32[]{:S(2)}, u32[]{:S(2)}) collective-permute-start(bf16[16,7168]{1,0:T(8,128)(2,1)S(1)} %fusion.36), channel_id=1, source_target_pairs={{0,6},{1,3},{2,0},{3,5},{4,2},{5,7},{6,4},{7,1},{8,14},{9,11},{10,... | collective-permute-start | bytes 688136 | tf_op jit(solution)/shard_map/home/ppermute | solution.py:31
  155.0 8.3 %collective-permute-done.10 = bf16[16,7168]{1,0:T(8,128)(2,1)S(1)} collective-permute-done((bf16[16,7168]{1,0:T(8,128)(2,1)S(1)}, bf16[16,7168]{1,0:T(8,128)(2,1)S(1)}, u32[]{:S(2)}, u32[]{:S(2)}) %collective-permute-start.10) | collective-permute-done | bytes 229408 | tf_op jit(solution)/shard_map/home/ppermute | solution.py:31
  163.5 1.9 %collective-permute-start.12 = (bf16[16,3584]{1,0:T(8,128)(2,1)S(1)}, bf16[16,3584]{1,0:T(8,128)(2,1)S(1)}, u32[]{:S(2)}, u32[]{:S(2)}) collective-permute-start(bf16[16,3584]{1,0:T(8,128)(2,1)S(1)} %get-tuple-element.36), channel_id=1, source_target_pairs={{32,0},{64,32},{96,64},{128,96},{160,128},{192,160},{224,192},{256... | collective-permute-start | bytes 344072 | tf_op jit(solution)/shard_map/sections/ppermute | solution.py:46
  165.4 3.9 %collective-permute-start.11 = (bf16[16,3584]{1,0:T(8,128)(2,1)S(1)}, bf16[16,3584]{1,0:T(8,128)(2,1)S(1)}, u32[]{:S(2)}, u32[]{:S(2)}) collective-permute-start(bf16[16,3584]{1,0:T(8,128)(2,1)S(1)} %get-tuple-element.37), channel_id=1, source_target_pairs={{0,32},{32,64},{64,96},{96,128},{128,160},{160,192},{192,224},{224... | collective-permute-start | bytes 344072 | tf_op jit(solution)/shard_map/sections/ppermute | solution.py:46
  169.4 0.8 collective-permute-done.12
  170.2 5.8 %collective-permute-done.11 = bf16[16,3584]{1,0:T(8,128)(2,1)S(1)} collective-permute-done((bf16[16,3584]{1,0:T(8,128)(2,1)S(1)}, bf16[16,3584]{1,0:T(8,128)(2,1)S(1)}, u32[]{:S(2)}, u32[]{:S(2)}) %collective-permute-start.11) | collective-permute-done | bytes 114720 | tf_op jit(solution)/shard_map/sections/ppermute | solution.py:46
  176.0 0.6 copy.52
  176.6 0.6 copy.53
  (42 shorter events, 1.6 us)
Async XLA Ops:
  0.6 1.8 %copy-start = (bf16[1,3584,256]{2,1,0:T(8,128)(2,1)S(1)}, bf16[1,3584,256]{2,1,0:T(8,128)(2,1)}, u32[]{:S(2)}) copy-start(bf16[1,3584,256]{2,1,0:T(8,128)(2,1)} %param.12) | copy-start | bytes 5505028
  2.4 8.5 %copy-start.5 = (f32[1,16,2]{1,2,0:T(2,128)S(1)}, f32[1,16,2]{1,2,0:T(2,128)}, u32[]{:S(2)}) copy-start(f32[1,16,2]{1,2,0:T(2,128)} %param.17) | copy-start | bytes 388
  2.4 8.5 %copy-start.6 = (s32[1,16,2]{1,2,0:T(2,128)S(1)}, s32[1,16,2]{1,2,0:T(2,128)}, u32[]{:S(2)}) copy-start(s32[1,16,2]{1,2,0:T(2,128)} %param.15) | copy-start | bytes 388
  2.4 8.5 %copy-start.7 = (f32[1,16,2]{1,2,0:T(2,128)S(1)}, f32[1,16,2]{1,2,0:T(2,128)}, u32[]{:S(2)}) copy-start(f32[1,16,2]{1,2,0:T(2,128)} %param.16) | copy-start | bytes 388
  2.4 8.5 %copy-start.8 = (s32[1,16,2]{1,2,0:T(2,128)S(1)}, s32[1,16,2]{1,2,0:T(2,128)}, u32[]{:S(2)}) copy-start(s32[1,16,2]{1,2,0:T(2,128)} %param.14) | copy-start | bytes 388
  2.4 8.6 %copy-start.2 = (bf16[1,16,3584]{2,1,0:T(8,128)(2,1)S(1)}, bf16[1,16,3584]{2,1,0:T(8,128)(2,1)}, u32[]{:S(2)}) copy-start(bf16[1,16,3584]{2,1,0:T(8,128)(2,1)} %param.11) | copy-start | bytes 344068
  2.4 8.6 %copy-start.3 = (bf16[1,16,3584]{2,1,0:T(8,128)(2,1)S(1)}, bf16[1,16,3584]{2,1,0:T(8,128)(2,1)}, u32[]{:S(2)}) copy-start(bf16[1,16,3584]{2,1,0:T(8,128)(2,1)} %param.9) | copy-start | bytes 344068
  2.4 8.6 %copy-start.4 = (bf16[1,16,3584]{2,1,0:T(8,128)(2,1)S(1)}, bf16[1,16,3584]{2,1,0:T(8,128)(2,1)}, u32[]{:S(2)}) copy-start(bf16[1,16,3584]{2,1,0:T(8,128)(2,1)} %param.10) | copy-start | bytes 344068
  4.3 70.4 %collective-permute-start.1 = (bf16[3584,384]{1,0:T(8,128)(2,1)}, bf16[3584,384]{1,0:T(8,128)(2,1)}, u32[]{:S(2)}, u32[]{:S(2)}) collective-permute-start(bf16[3584,384]{1,0:T(8,128)(2,1)} %pad_maximum_fusion), channel_id=1, source_target_pairs={{0,24},{1,9},{2,26},{3,11},{4,28},{5,13},{6,30},{7,15},{8,0},{9,17... | collective-permute-start | bytes 8257544 | tf_op jit(solution)/shard_map/gather_weights/ppermute | solution.py:36
  8.9 65.7 %collective-permute-start = (bf16[3584,384]{1,0:T(8,128)(2,1)}, bf16[3584,384]{1,0:T(8,128)(2,1)}, u32[]{:S(2)}, u32[]{:S(2)}) collective-permute-start(bf16[3584,384]{1,0:T(8,128)(2,1)} %pad_maximum_fusion), channel_id=1, source_target_pairs={{0,8},{1,25},{2,10},{3,27},{4,12},{5,29},{6,14},{7,31},{8,16},{9,1... | collective-permute-start | bytes 8257544 | tf_op jit(solution)/shard_map/gather_weights/ppermute | solution.py:36
  11.1 18.3 %collective-permute-start.2 = (bf16[16,10880]{1,0:T(8,128)(2,1)S(1)}, bf16[16,10880]{1,0:T(8,128)(2,1)S(1)}, u32[]{:S(2)}, u32[]{:S(2)}) collective-permute-start(bf16[16,10880]{1,0:T(8,128)(2,1)S(1)} %pad_maximum_fusion.6), channel_id=1, source_target_pairs={{0,2},{1,7},{2,4},{3,1},{4,6},{5,3},{6,0},{7,5},{8,10},{9,15},{10,... | collective-permute-start | bytes 1044488 | tf_op jit(solution)/shard_map/gather_rows/ppermute | solution.py:31
  20.2 39.6 %collective-permute-start.3 = (bf16[16,10880]{1,0:T(8,128)(2,1)S(1)}, bf16[16,10880]{1,0:T(8,128)(2,1)S(1)}, u32[]{:S(2)}, u32[]{:S(2)}) collective-permute-start(bf16[16,10880]{1,0:T(8,128)(2,1)S(1)} %pad_maximum_fusion.6), channel_id=1, source_target_pairs={{0,6},{1,3},{2,0},{3,5},{4,2},{5,7},{6,4},{7,1},{8,14},{9,11},{10,... | collective-permute-start | bytes 1044488 | tf_op jit(solution)/shard_map/gather_rows/ppermute | solution.py:31
  29.4 45.3 %collective-permute-start.4 = (bf16[16,10880]{1,0:T(8,128)(2,1)S(1)}, bf16[16,10880]{1,0:T(8,128)(2,1)S(1)}, u32[]{:S(2)}, u32[]{:S(2)}) collective-permute-start(bf16[16,10880]{1,0:T(8,128)(2,1)S(1)} %collective-permute-done.2), channel_id=1, source_target_pairs={{0,2},{1,7},{2,4},{3,1},{4,6},{5,3},{6,0},{7,5},{8,10},{9,15},{10,... | collective-permute-start | bytes 1044488 | tf_op jit(solution)/shard_map/gather_rows/ppermute | solution.py:31
  75.7 5.2 %collective-permute-start.5 = (bf16[64,10880]{1,0:T(8,128)(2,1)S(1)}, bf16[64,10880]{1,0:T(8,128)(2,1)}, u32[]{:S(2)}, u32[]{:S(2)}) collective-permute-start(bf16[64,10880]{1,0:T(8,128)(2,1)S(1)} %pad_maximum_fusion.2), channel_id=1, source_target_pairs={{0,1},{1,0},{2,3},{3,2},{4,5},{5,4},{6,7},{7,6},{8,9},{9,8},{10,11... | collective-permute-start | bytes 4177928 | tf_op jit(solution)/shard_map/gather_opposite/ppermute | solution.py:40
  77.7 36.8 %collective-permute-start.6 = (bf16[3584,384]{1,0:T(8,128)(2,1)}, bf16[3584,384]{1,0:T(8,128)(2,1)S(1)}, u32[]{:S(2)}, u32[]{:S(2)}) collective-permute-start(bf16[3584,384]{1,0:T(8,128)(2,1)} %collective-permute-done), channel_id=1, source_target_pairs={{0,8},{1,25},{2,10},{3,27},{4,12},{5,29},{6,14},{7,31},{8,16},{9,1... | collective-permute-start | bytes 8257544 | tf_op jit(solution)/shard_map/gather_opposite/ppermute | solution.py:36
  88.1 1.7 copy-start.1
  117.0 4.4 %collective-permute-start.7 = (bf16[64,7168]{1,0:T(8,128)(2,1)S(1)}, bf16[64,7168]{1,0:T(8,128)(2,1)S(1)}, u32[]{:S(2)}, u32[]{:S(2)}) collective-permute-start(bf16[64,7168]{1,0:T(8,128)(2,1)S(1)} %fusion.8), channel_id=1, source_target_pairs={{0,1},{1,0},{2,3},{3,2},{4,5},{5,4},{6,7},{7,6},{8,9},{9,8},{10,11... | collective-permute-start | bytes 2752520 | tf_op jit(solution)/shard_map/cores/ppermute | solution.py:40
  121.7 25.9 %collective-permute-start.9 = (bf16[16,7168]{1,0:T(8,128)(2,1)S(1)}, bf16[16,7168]{1,0:T(8,128)(2,1)S(1)}, u32[]{:S(2)}, u32[]{:S(2)}) collective-permute-start(bf16[16,7168]{1,0:T(8,128)(2,1)S(1)} %get-tuple-element.35), channel_id=1, source_target_pairs={{0,6},{1,3},{2,0},{3,5},{4,2},{5,7},{6,4},{7,1},{8,14},{9,11},{10,... | collective-permute-start | bytes 688136 | tf_op jit(solution)/shard_map/home/ppermute | solution.py:31
  128.9 26.1 %collective-permute-start.8 = (bf16[16,7168]{1,0:T(8,128)(2,1)S(1)}, bf16[16,7168]{1,0:T(8,128)(2,1)S(1)}, u32[]{:S(2)}, u32[]{:S(2)}) collective-permute-start(bf16[16,7168]{1,0:T(8,128)(2,1)S(1)} %get-tuple-element.34), channel_id=1, source_target_pairs={{0,2},{1,7},{2,4},{3,1},{4,6},{5,3},{6,0},{7,5},{8,10},{9,15},{10,... | collective-permute-start | bytes 688136 | tf_op jit(solution)/shard_map/home/ppermute | solution.py:31
  147.6 15.8 %collective-permute-start.10 = (bf16[16,7168]{1,0:T(8,128)(2,1)S(1)}, bf16[16,7168]{1,0:T(8,128)(2,1)S(1)}, u32[]{:S(2)}, u32[]{:S(2)}) collective-permute-start(bf16[16,7168]{1,0:T(8,128)(2,1)S(1)} %fusion.36), channel_id=1, source_target_pairs={{0,6},{1,3},{2,0},{3,5},{4,2},{5,7},{6,4},{7,1},{8,14},{9,11},{10,... | collective-permute-start | bytes 688136 | tf_op jit(solution)/shard_map/home/ppermute | solution.py:31
  163.5 6.7 %collective-permute-start.12 = (bf16[16,3584]{1,0:T(8,128)(2,1)S(1)}, bf16[16,3584]{1,0:T(8,128)(2,1)S(1)}, u32[]{:S(2)}, u32[]{:S(2)}) collective-permute-start(bf16[16,3584]{1,0:T(8,128)(2,1)S(1)} %get-tuple-element.36), channel_id=1, source_target_pairs={{32,0},{64,32},{96,64},{128,96},{160,128},{192,160},{224,192},{256... | collective-permute-start | bytes 344072 | tf_op jit(solution)/shard_map/sections/ppermute | solution.py:46
  165.4 10.6 %collective-permute-start.11 = (bf16[16,3584]{1,0:T(8,128)(2,1)S(1)}, bf16[16,3584]{1,0:T(8,128)(2,1)S(1)}, u32[]{:S(2)}, u32[]{:S(2)}) collective-permute-start(bf16[16,3584]{1,0:T(8,128)(2,1)S(1)} %get-tuple-element.37), channel_id=1, source_target_pairs={{0,32},{32,64},{64,96},{96,128},{128,160},{160,192},{192,224},{224... | collective-permute-start | bytes 344072 | tf_op jit(solution)/shard_map/sections/ppermute | solution.py:46

commit v10 on v9

--- a/solution.py
+++ b/solution.py
@@ -1,12 +1,16 @@
 import jax
 import jax.numpy as jnp
 from jax import lax
+from jax.experimental import pallas as pl
+from jax.experimental.pallas import tpu as pltpu
 from jax.sharding import PartitionSpec as P
 
 EXPERTS = 4
 Z = 4
 CORES = 2
 LANES = 128
+CHUNK = 512
+ROOM = 40 * 1024 * 1024
 
 
 def expert_index(x, z, core):
@@ -69,15 +73,11 @@
     return jnp.pad(parts, ((0, 0), (0, LANES - parts.shape[1])))
 
 
-def side_values(columns):
-    width = 2 * EXPERTS
-    first, second, third = jnp.split(columns[:, : 3 * width].astype(jnp.float32), 3, axis=1)
-    return first + second + third
-
-
-def column_of(table, index):
-    hot = jnp.arange(table.shape[1], dtype=jnp.int32) == index
-    return jnp.sum(jnp.where(hot[None, :], table, 0.0), axis=1, keepdims=True)
+def share_picks(experts):
+    lane = jnp.arange(LANES, dtype=jnp.int32)
+    wanted = jnp.stack(experts + [EXPERTS + e for e in experts])
+    picks = (lane[:, None] % (2 * EXPERTS) == wanted[None, :]) & (lane[:, None] < 6 * EXPERTS)
+    return jnp.pad(picks.astype(jnp.bfloat16), ((0, 0), (0, LANES - wanted.shape[0])))
 
 
 def dot(a, b):
@@ -88,20 +88,73 @@
     return lax.dot_general(a, b, (((1,), (1,)), ((), ())), preferred_element_type=jnp.float32)
 
 
-def forward_rows(rows, gate_up, down):
-    gate_val, up_val = jnp.split(dot(rows, gate_up), 2, axis=1)
-    hidden = (jax.nn.silu(gate_val) * up_val).astype(jnp.bfloat16)
-    return dot_t(hidden, down)
-
-
-def backward_rows(rows, grads, gate_up, down):
-    hidden_grad = dot(grads, down)
-    gate_val, up_val = jnp.split(dot(rows, gate_up), 2, axis=1)
+def fill_rows(mine, other, rows):
+    half, model = mine.shape[0], rows[0].shape[1]
+    for k, target in enumerate(rows):
+        target[:half, :] = mine[:, k * model : (k + 1) * model]
+        target[half:, :] = other[:, k * model : (k + 1) * model]
+
+
+def pick_shares(mine, other, picks, model):
+    sides = [part[:, 3 * model :] for part in (mine, other)]
+    return jnp.concatenate([dot(side, picks[...]) for side in sides], axis=0)
+
+
+def one_expert(rows, weight, share, back_share):
+    token, saved, upstream = rows
+    half = weight.shape[1] // 3
+    both = dot(token[...], weight[:, : 2 * half])
+    gate_val, up_val = both[:, :half], both[:, half:]
+    hidden = (gate_val * jax.nn.sigmoid(gate_val) * up_val).astype(jnp.bfloat16)
+    hidden_grad = dot(upstream[...], weight[:, 2 * half :])
+    both = dot(saved[...], weight[:, : 2 * half])
+    gate_val, up_val = both[:, :half], both[:, half:]
     sig = jax.nn.sigmoid(gate_val)
     gate_grad = hidden_grad * up_val * sig * (1.0 + gate_val * (1.0 - sig))
     up_grad = hidden_grad * gate_val * sig
     grad = jnp.concatenate([gate_grad, up_grad], axis=1).astype(jnp.bfloat16)
-    return dot_t(grad, gate_up)
+    for low in range(0, token.shape[1], CHUNK):
+        cut = slice(low, low + CHUNK)
+        out = share * dot_t(hidden, weight[cut, 2 * half :])
+        yield cut, out, back_share * dot_t(grad, weight[cut, : 2 * half])
+
+
+def first_kernel(mine, other, picks, *refs):
+    weights, (total, back_total), rows = refs[:3], refs[3:5], refs[5:]
+    fill_rows(mine, other, rows)
+    shares = pick_shares(mine, other, picks, rows[0].shape[1])
+    for k, weight in enumerate(weights):
+        share, back_share = shares[:, k : k + 1], shares[:, 3 + k : 4 + k]
+        for cut, out, back_out in one_expert(rows, weight, share, back_share):
+            if k > 0:
+                out, back_out = out + total[:, cut], back_out + back_total[:, cut]
+            total[:, cut], back_total[:, cut] = out, back_out
+
+
+def last_kernel(mine, other, picks, weight, total, back_total, keep, give, *rows):
+    fill_rows(mine, other, rows)
+    half, model = mine.shape[0], rows[0].shape[1]
+    shares = pick_shares(mine, other, picks, model)
+    for cut, out, back_out in one_expert(rows, weight, shares[:, :1], shares[:, 1:2]):
+        back_cut = slice(model + cut.start, model + cut.stop)
+        out, back_out = out + total[:, cut], back_out + back_total[:, cut]
+        keep[:, cut], keep[:, back_cut] = out[:half], back_out[:half]
+        give[:, cut] = out[half:].astype(jnp.bfloat16)
+        give[:, back_cut] = back_out[half:].astype(jnp.bfloat16)
+
+
+def run_kernel(kernel, operands, outs, model):
+    whole = pl.BlockSpec(memory_space=pltpu.VMEM)
+    both = 2 * operands[0].shape[0]
+    return pl.pallas_call(
+        kernel,
+        out_shape=outs,
+        in_specs=[whole] * len(operands),
+        out_specs=tuple(whole for _ in outs),
+        scratch_shapes=[pltpu.VMEM((both, model), jnp.bfloat16) for _ in range(3)],
+        compiler_params=pltpu.CompilerParams(vmem_limit_bytes=ROOM),
+        cost_estimate=pl.CostEstimate(flops=1000, bytes_accessed=1000, transcendentals=0),
+    )(*operands)
 
 
 def on_device(
@@ -138,27 +191,21 @@
         near, far, below, above, opposite = together(near, far, below, above, opposite)
         weights = [weights, near, far, along_x(near, 1)]
         mine = jnp.concatenate([mine, below, above, opposite], axis=0)
-        both = [mine, other_core(mine)]
-        cuts = (0, model, 2 * model, 3 * model, 3 * model + LANES)
-        token_rows, saved_rows, upstream_rows, sides = [
-            jnp.concatenate([part[:, low:high] for part in both], axis=0)
-            for low, high in zip(cuts, cuts[1:])
-        ]
-        shares = side_values(sides)
+        other = other_core(mine)
+    half = Z * rows
     with jax.named_scope("experts"):
-        forward_sum = backward_sum = 0.0
-        width = gate_up_weight.shape[2]
-        for expert, weight in zip(experts, weights):
-            gate_up, down = weight[:, :width], weight[:, width:]
-            out = forward_rows(token_rows, gate_up, down)
-            forward_sum = forward_sum + column_of(shares[:, :EXPERTS], expert) * out
-            out = backward_rows(saved_rows, upstream_rows, gate_up, down)
-            backward_sum = backward_sum + column_of(shares[:, EXPERTS:], expert) * out
-    half = Z * rows
+        outs = (jax.ShapeDtypeStruct((2 * half, model), jnp.float32),) * 2
+        operands = (mine, other, share_picks(experts[:3]), *weights[:3])
+        sums = run_kernel(first_kernel, operands, outs, model)
+    with jax.named_scope("last_expert"):
+        outs = (
+            jax.ShapeDtypeStruct((half, 2 * model), jnp.float32),
+            jax.ShapeDtypeStruct((half, 2 * model), jnp.bfloat16),
+        )
+        operands = (mine, other, share_picks(experts[3:]), weights[3], *sums)
+        keep, give = run_kernel(last_kernel, operands, outs, model)
     with jax.named_scope("cores"):
-        total = jnp.concatenate([forward_sum, backward_sum], axis=1)
-        other = other_core(total[half:].astype(jnp.bfloat16))
-        total = total[:half] + other.astype(jnp.float32)
+        total = keep + other_core(give).astype(jnp.float32)
     with jax.named_scope("home"):
         own, near, far, passed = jnp.split(total, Z, axis=0)
         passed = along_z(passed.astype(jnp.bfloat16), -1)

time: 179 us -> 177 us (0.989)
  matrix products: 23.3 us -> 0 us
  Pallas kernels: 0 us -> 11.8 us
  waiting for transfers between devices: 62 us -> 67.2 us
  starting transfers between devices: 81.7 us -> 84.7 us
  local copies, waits for them, and re-layouts: 5.44 us -> 7.24 us
    dot_general x20 -> x0, matrix products: 23.3 us -> none  [the longest x12 13.3 us: dot(): return jnp.dot(a, b, preferred_element_type=jnp.float32)]
    pallas_call x0 -> x2, Pallas kernels: none -> 11.8 us  [run_kernel(): pl.pallas_call(kernel, out_shape=outs, in_specs=[whole] * len(operands),...]
    ppermute x3, waiting for transfers between devices: 10.1 us -> 19.4 us  [along_x(): return lax.ppermute(block, 'expert', route)]
    unnamed x21, local copies, waits for them, and re-layouts: 1.49 us -> 6.93 us
    ppermute x2, waiting for transfers between devices: 6.64 us -> 2.35 us  [to_section(): return lax.ppermute(block, 'pipe', route)]
    ppermute x2, starting transfers between devices: 5.84 us -> 8.54 us  [to_section(): return lax.ppermute(block, 'pipe', route)]
    ppermute x2, waiting for transfers between devices: 2.78 us -> 5.05 us  [other_core(): lax.ppermute(block, 'expert', expert_route(lambda x, z, c: (x, z, 1 - c)))]
    slice x4 -> x0, local copies, waits for them, and re-layouts: 2.21 us -> none  [on_device(): part[:, low:high]]
  transfers between devices with their start and end apart: 13 -> 13, of which waited for: 9 -> 10; matrix products, arithmetic and copies ran while one was open for 13% -> 1% of each run, Pallas kernels for 0% -> 5%
where the time goes in v10:
time: 177 us; the launch traced here: 175 us
  starting transfers between devices  84.7 us (48%)
  waiting for transfers between devices  67.2 us (38%)
  Pallas kernels  11.8 us (7%)
  local copies, waits for them, and re-layouts  7.24 us (4%)
  other arithmetic  3.15 us (2%)
    ppermute x6, starting transfers between devices, along_z(): return lax.ppermute(block, 'expert', route)  63 us
    ppermute x6, waiting for transfers between devices, along_z(): return lax.ppermute(block, 'expert', route)  40.4 us
    ppermute x3, waiting for transfers between devices, along_x(): return lax.ppermute(block, 'expert', route)  19.4 us
    pallas_call x2, Pallas kernels, run_kernel(): pl.pallas_call(kernel, out_shape=outs, in_specs=[whole] * len(operands),...  11.8 us
    ppermute x3, starting transfers between devices, along_x(): return lax.ppermute(block, 'expert', route)  9.24 us
    ppermute x2, starting transfers between devices, to_section(): return lax.ppermute(block, 'pipe', route)  8.54 us
    unnamed x21, local copies, waits for them, and re-layouts  6.93 us
    ppermute x2, waiting for transfers between devices, other_core(): lax.ppermute(block, 'expert', expert_route(lambda x, z, c: (x, z, 1 - c)))  5.05 us
  transfers between devices with their start and end apart: 13, of which 10 were waited for; matrix products, arithmetic and copies ran while one was open for 1% of the time, Pallas kernels for 5%

profile of v10, /device:TPU:24, one launch (start us, length us, event | category | flops | bytes accessed | tf_op | source)
XLA Modules:
  0.0 175.1 jit_solution(11213519173199755040)
XLA Ops:
  0.6 2.2 %copy.21 = bf16[1,128,3584]{1,2,0:T(8,128)(2,1)} copy(bf16[1,128,3584]{2,1,0:T(8,128)(2,1)} %param.13) | data formatting | bytes 1835008 | tf_op args[4]
  2.9 0.0 copy-start.2
  2.9 0.0 copy-start.3
  2.9 0.0 copy-start.4
  2.9 2.1 %pad_maximum_fusion.refs_0_ = bf16[3584,384]{1,0:T(8,128)(2,1)S(1)} fusion(bf16[3584,128]{1,0:T(8,128)(2,1)} %bitcast.21, bf16[3584,256]{1,0:T(8,128)(2,1)} %bitcast.22), kind=kLoop, calls=%fused_computation | loop fusion | flops 5505024 | bytes 5505024 | tf_op jit(solution)/shard_map/gather_weights/concatenate | solution.py:179
  5.1 3.4 %collective-permute-start = (bf16[3584,384]{1,0:T(8,128)(2,1)S(1)}, bf16[3584,384]{1,0:T(8,128)(2,1)}, u32[]{:S(2)}, u32[]{:S(2)}) collective-permute-start(bf16[3584,384]{1,0:T(8,128)(2,1)S(1)} %pad_maximum_fusion.refs_0_), channel_id=1, source_target_pairs={{0,8},{1,25},{2,10},{3,27},{4,12},{5,29},{6,14},{7,31},{8,16},{9,1... | collective-permute-start | bytes 8257544 | tf_op jit(solution)/shard_map/gather_weights/ppermute | solution.py:40
  8.5 3.7 %collective-permute-start.1 = (bf16[3584,384]{1,0:T(8,128)(2,1)S(1)}, bf16[3584,384]{1,0:T(8,128)(2,1)}, u32[]{:S(2)}, u32[]{:S(2)}) collective-permute-start(bf16[3584,384]{1,0:T(8,128)(2,1)S(1)} %pad_maximum_fusion.refs_0_), channel_id=1, source_target_pairs={{0,24},{1,9},{2,26},{3,11},{4,28},{5,13},{6,30},{7,15},{8,0},{9,17... | collective-permute-start | bytes 8257544 | tf_op jit(solution)/shard_map/gather_weights/ppermute | solution.py:40
  12.1 1.6 copy-done
  13.8 0.1 copy.19
  13.9 0.1 copy.20
  14.0 0.1 reduce-precision_convert_fusion.1
  14.0 0.1 fusion.9
  14.2 9.1 %collective-permute-start.2 = (bf16[16,10880]{1,0:T(8,128)(2,1)S(1)}, bf16[16,10880]{1,0:T(8,128)(2,1)S(1)}, u32[]{:S(2)}, u32[]{:S(2)}) collective-permute-start(bf16[16,10880]{1,0:T(8,128)(2,1)S(1)} %pad_maximum_fusion.2), channel_id=1, source_target_pairs={{0,2},{1,7},{2,4},{3,1},{4,6},{5,3},{6,0},{7,5},{8,10},{9,15},{10,... | collective-permute-start | bytes 1044488 | tf_op jit(solution)/shard_map/gather_rows/ppermute | solution.py:35
  23.3 5.6 %collective-permute-start.3 = (bf16[16,10880]{1,0:T(8,128)(2,1)S(1)}, bf16[16,10880]{1,0:T(8,128)(2,1)S(1)}, u32[]{:S(2)}, u32[]{:S(2)}) collective-permute-start(bf16[16,10880]{1,0:T(8,128)(2,1)S(1)} %pad_maximum_fusion.2), channel_id=1, source_target_pairs={{0,6},{1,3},{2,0},{3,5},{4,2},{5,7},{6,4},{7,1},{8,14},{9,11},{10,... | collective-permute-start | bytes 1044488 | tf_op jit(solution)/shard_map/gather_rows/ppermute | solution.py:35
  28.8 3.6 %collective-permute-done.2 = bf16[16,10880]{1,0:T(8,128)(2,1)S(1)} collective-permute-done((bf16[16,10880]{1,0:T(8,128)(2,1)S(1)}, bf16[16,10880]{1,0:T(8,128)(2,1)S(1)}, u32[]{:S(2)}, u32[]{:S(2)}) %collective-permute-start.2) | collective-permute-done | bytes 348192 | tf_op jit(solution)/shard_map/gather_rows/ppermute | solution.py:35
  32.5 30.7 %collective-permute-start.4 = (bf16[16,10880]{1,0:T(8,128)(2,1)S(1)}, bf16[16,10880]{1,0:T(8,128)(2,1)S(1)}, u32[]{:S(2)}, u32[]{:S(2)}) collective-permute-start(bf16[16,10880]{1,0:T(8,128)(2,1)S(1)} %collective-permute-done.2), channel_id=1, source_target_pairs={{0,2},{1,7},{2,4},{3,1},{4,6},{5,3},{6,0},{7,5},{8,10},{9,15},{10,... | collective-permute-start | bytes 1044488 | tf_op jit(solution)/shard_map/gather_rows/ppermute | solution.py:35
  63.2 5.1 %collective-permute-done.3 = bf16[16,10880]{1,0:T(8,128)(2,1)S(1)} collective-permute-done((bf16[16,10880]{1,0:T(8,128)(2,1)S(1)}, bf16[16,10880]{1,0:T(8,128)(2,1)S(1)}, u32[]{:S(2)}, u32[]{:S(2)}) %collective-permute-start.3) | collective-permute-done | bytes 348192 | tf_op jit(solution)/shard_map/gather_rows/ppermute | solution.py:35
  68.3 9.5 %collective-permute-done.4 = bf16[16,10880]{1,0:T(8,128)(2,1)S(1)} collective-permute-done((bf16[16,10880]{1,0:T(8,128)(2,1)S(1)}, bf16[16,10880]{1,0:T(8,128)(2,1)S(1)}, u32[]{:S(2)}, u32[]{:S(2)}) %collective-permute-start.4) | collective-permute-done | bytes 348192 | tf_op jit(solution)/shard_map/gather_rows/ppermute | solution.py:35
  77.7 0.0 collective-permute-done.refs_1_
  77.7 0.0 collective-permute-done.1.refs_2_
  77.7 2.2 %collective-permute-start.6 = (bf16[3584,384]{1,0:T(8,128)(2,1)}, bf16[3584,384]{1,0:T(8,128)(2,1)}, u32[]{:S(2)}, u32[]{:S(2)}) collective-permute-start(bf16[3584,384]{1,0:T(8,128)(2,1)} %collective-permute-done.refs_1_), channel_id=1, source_target_pairs={{0,8},{1,25},{2,10},{3,27},{4,12},{5,29},{6,14},{7,31},{8,16},{9,1... | collective-permute-start | bytes 8257544 | tf_op jit(solution)/shard_map/gather_opposite/ppermute | solution.py:40
  79.9 0.1 pad_maximum_fusion.1.mine
  80.0 1.9 %collective-permute-start.5 = (bf16[64,10880]{1,0:T(8,128)(2,1)S(1)}, bf16[64,10880]{1,0:T(8,128)(2,1)S(1)}, u32[]{:S(2)}, u32[]{:S(2)}) collective-permute-start(bf16[64,10880]{1,0:T(8,128)(2,1)S(1)} %pad_maximum_fusion.1.mine), channel_id=1, source_target_pairs={{0,1},{1,0},{2,3},{3,2},{4,5},{5,4},{6,7},{7,6},{8,9},{9,8},{10,11... | collective-permute-start | bytes 4177928 | tf_op jit(solution)/shard_map/gather_opposite/ppermute | solution.py:44
  82.1 0.1 stack.39
  82.2 0.1 pad_add_fusion
  82.2 0.1 compare_and_fusion
  82.4 0.1 compare_and_fusion.1
  82.5 2.6 %collective-permute-done.5.other = bf16[64,10880]{1,0:T(8,128)(2,1)S(1)} collective-permute-done((bf16[64,10880]{1,0:T(8,128)(2,1)S(1)}, bf16[64,10880]{1,0:T(8,128)(2,1)S(1)}, u32[]{:S(2)}, u32[]{:S(2)}) %collective-permute-start.5) | collective-permute-done | bytes 1392672 | tf_op jit(solution)/shard_map/gather_opposite/ppermute | solution.py:44
  85.1 1.8 %copy-done.1 = bf16[3584,384]{1,0:T(8,128)(2,1)S(1)} copy-done((bf16[3584,384]{1,0:T(8,128)(2,1)S(1)}, bf16[3584,384]{1,0:T(8,128)(2,1)}, u32[]{:S(2)}) %copy-start.1) | copy-done | bytes 2752536
  86.9 7.9 %experts.1 = (f32[128,3584]{1,0:T(8,128)S(1)}, f32[128,3584]{1,0:T(8,128)S(1)}) custom-call(bf16[64,10880]{1,0:T(8,128)(2,1)S(1)} %pad_maximum_fusion.1.mine, bf16[64,10880]{1,0:T(8,128)(2,1)S(1)} %collective-permute-done.5.other, bf16[128,128]{1,0:T(8,128)(2,1)S(1)} %pad_convert_fusion.picks, bf16[3584,384]{1,0:T(8,128)(2,1)S(1)} %copy-done.1, ...), custom_call_target="tpu_custom_call" | custom-call | flops 1000 | bytes 1000 | tf_op jit(solution)/shard_map/experts/pallas_call | solution.py:149
  94.8 19.4 %collective-permute-done.6.weight = bf16[3584,384]{1,0:T(8,128)(2,1)} collective-permute-done((bf16[3584,384]{1,0:T(8,128)(2,1)}, bf16[3584,384]{1,0:T(8,128)(2,1)}, u32[]{:S(2)}, u32[]{:S(2)}) %collective-permute-start.6) | collective-permute-done | bytes 2752544 | tf_op jit(solution)/shard_map/gather_opposite/ppermute | solution.py:40
  114.2 3.9 %last_expert.1 = (f32[64,7168]{1,0:T(8,128)S(1)}, bf16[64,7168]{1,0:T(8,128)(2,1)S(1)}) custom-call(bf16[64,10880]{1,0:T(8,128)(2,1)S(1)} %pad_maximum_fusion.1.mine, bf16[64,10880]{1,0:T(8,128)(2,1)S(1)} %collective-permute-done.5.other, bf16[128,128]{1,0:T(8,128)(2,1)S(1)} %pad_convert_fusion.1.picks, bf16[3584,384]{1,0:T(8,128)(2,1)} %collective-permute-done.6.weight, ...), custom_call_target="tpu_custom_call" | custom-call | flops 1000 | bytes 1000 | tf_op jit(solution)/shard_map/last_expert/pallas_call | solution.py:149
  118.1 1.9 %collective-permute-start.7 = (bf16[64,7168]{1,0:T(8,128)(2,1)S(1)}, bf16[64,7168]{1,0:T(8,128)(2,1)S(1)}, u32[]{:S(2)}, u32[]{:S(2)}) collective-permute-start(bf16[64,7168]{1,0:T(8,128)(2,1)S(1)} %get-tuple-element.19), channel_id=1, source_target_pairs={{0,1},{1,0},{2,3},{3,2},{4,5},{5,4},{6,7},{7,6},{8,9},{9,8},{10,11... | collective-permute-start | bytes 2752520 | tf_op jit(solution)/shard_map/cores/ppermute | solution.py:44
  120.1 2.4 %collective-permute-done.7 = bf16[64,7168]{1,0:T(8,128)(2,1)S(1)} collective-permute-done((bf16[64,7168]{1,0:T(8,128)(2,1)S(1)}, bf16[64,7168]{1,0:T(8,128)(2,1)S(1)}, u32[]{:S(2)}, u32[]{:S(2)}) %collective-permute-start.7) | collective-permute-done | bytes 917536 | tf_op jit(solution)/shard_map/cores/ppermute | solution.py:44
  122.5 0.2 fusion.10
  122.8 6.2 %collective-permute-start.9 = (bf16[16,7168]{1,0:T(8,128)(2,1)S(1)}, bf16[16,7168]{1,0:T(8,128)(2,1)S(1)}, u32[]{:S(2)}, u32[]{:S(2)}) collective-permute-start(bf16[16,7168]{1,0:T(8,128)(2,1)S(1)} %get-tuple-element.23), channel_id=1, source_target_pairs={{0,6},{1,3},{2,0},{3,5},{4,2},{5,7},{6,4},{7,1},{8,14},{9,11},{10,... | collective-permute-start | bytes 688136 | tf_op jit(solution)/shard_map/home/ppermute | solution.py:35
  129.0 4.0 %collective-permute-start.8 = (bf16[16,7168]{1,0:T(8,128)(2,1)S(1)}, bf16[16,7168]{1,0:T(8,128)(2,1)S(1)}, u32[]{:S(2)}, u32[]{:S(2)}) collective-permute-start(bf16[16,7168]{1,0:T(8,128)(2,1)S(1)} %get-tuple-element.22), channel_id=1, source_target_pairs={{0,2},{1,7},{2,4},{3,1},{4,6},{5,3},{6,0},{7,5},{8,10},{9,15},{10,... | collective-permute-start | bytes 688136 | tf_op jit(solution)/shard_map/home/ppermute | solution.py:35
  133.0 17.9 %collective-permute-done.9 = bf16[16,7168]{1,0:T(8,128)(2,1)S(1)} collective-permute-done((bf16[16,7168]{1,0:T(8,128)(2,1)S(1)}, bf16[16,7168]{1,0:T(8,128)(2,1)S(1)}, u32[]{:S(2)}, u32[]{:S(2)}) %collective-permute-start.9) | collective-permute-done | bytes 229408 | tf_op jit(solution)/shard_map/home/ppermute | solution.py:35
  150.9 7.4 %collective-permute-start.10 = (bf16[16,7168]{1,0:T(8,128)(2,1)S(1)}, bf16[16,7168]{1,0:T(8,128)(2,1)S(1)}, u32[]{:S(2)}, u32[]{:S(2)}) collective-permute-start(bf16[16,7168]{1,0:T(8,128)(2,1)S(1)} %fusion), channel_id=1, source_target_pairs={{0,6},{1,3},{2,0},{3,5},{4,2},{5,7},{6,4},{7,1},{8,14},{9,11},{10,... | collective-permute-start | bytes 688136 | tf_op jit(solution)/shard_map/home/ppermute | solution.py:35
  158.4 0.0 collective-permute-done.8
  158.4 4.4 %collective-permute-done.10 = bf16[16,7168]{1,0:T(8,128)(2,1)S(1)} collective-permute-done((bf16[16,7168]{1,0:T(8,128)(2,1)S(1)}, bf16[16,7168]{1,0:T(8,128)(2,1)S(1)}, u32[]{:S(2)}, u32[]{:S(2)}) %collective-permute-start.10) | collective-permute-done | bytes 229408 | tf_op jit(solution)/shard_map/home/ppermute | solution.py:35
  162.8 0.1 fusion.3
  162.9 1.9 %collective-permute-start.11 = (bf16[16,3584]{1,0:T(8,128)(2,1)S(1)}, bf16[16,3584]{1,0:T(8,128)(2,1)S(1)}, u32[]{:S(2)}, u32[]{:S(2)}) collective-permute-start(bf16[16,3584]{1,0:T(8,128)(2,1)S(1)} %get-tuple-element.25), channel_id=1, source_target_pairs={{0,32},{32,64},{64,96},{96,128},{128,160},{160,192},{192,224},{224... | collective-permute-start | bytes 344072 | tf_op jit(solution)/shard_map/sections/ppermute | solution.py:50
  164.8 6.6 %collective-permute-start.12 = (bf16[16,3584]{1,0:T(8,128)(2,1)S(1)}, bf16[16,3584]{1,0:T(8,128)(2,1)S(1)}, u32[]{:S(2)}, u32[]{:S(2)}) collective-permute-start(bf16[16,3584]{1,0:T(8,128)(2,1)S(1)} %get-tuple-element.24), channel_id=1, source_target_pairs={{32,0},{64,32},{96,64},{128,96},{160,128},{192,160},{224,192},{256... | collective-permute-start | bytes 344072 | tf_op jit(solution)/shard_map/sections/ppermute | solution.py:50
  171.5 2.0 %collective-permute-done.11 = bf16[16,3584]{1,0:T(8,128)(2,1)S(1)} collective-permute-done((bf16[16,3584]{1,0:T(8,128)(2,1)S(1)}, bf16[16,3584]{1,0:T(8,128)(2,1)S(1)}, u32[]{:S(2)}, u32[]{:S(2)}) %collective-permute-start.11) | collective-permute-done | bytes 114720 | tf_op jit(solution)/shard_map/sections/ppermute | solution.py:50
  173.4 0.4 collective-permute-done.12
  173.8 0.6 copy.26
  174.4 0.6 copy.27
  (23 shorter events, 0.2 us)
Async XLA Ops:
  2.9 10.9 %copy-start.5 = (f32[1,16,2]{1,2,0:T(2,128)S(1)}, f32[1,16,2]{1,2,0:T(2,128)}, u32[]{:S(2)}) copy-start(f32[1,16,2]{1,2,0:T(2,128)} %param.16) | copy-start | bytes 388
  2.9 10.9 %copy-start.6 = (s32[1,16,2]{1,2,0:T(2,128)S(1)}, s32[1,16,2]{1,2,0:T(2,128)}, u32[]{:S(2)}) copy-start(s32[1,16,2]{1,2,0:T(2,128)} %param.14) | copy-start | bytes 388
  2.9 11.0 %copy-start.7 = (f32[1,16,2]{1,2,0:T(2,128)S(1)}, f32[1,16,2]{1,2,0:T(2,128)}, u32[]{:S(2)}) copy-start(f32[1,16,2]{1,2,0:T(2,128)} %param.17) | copy-start | bytes 388
  2.9 11.0 %copy-start.8 = (s32[1,16,2]{1,2,0:T(2,128)S(1)}, s32[1,16,2]{1,2,0:T(2,128)}, u32[]{:S(2)}) copy-start(s32[1,16,2]{1,2,0:T(2,128)} %param.15) | copy-start | bytes 388
  2.9 11.2 %copy-start.2 = (bf16[1,16,3584]{2,1,0:T(8,128)(2,1)S(1)}, bf16[1,16,3584]{2,1,0:T(8,128)(2,1)}, u32[]{:S(2)}) copy-start(bf16[1,16,3584]{2,1,0:T(8,128)(2,1)} %param.11) | copy-start | bytes 344068
  2.9 11.2 %copy-start.3 = (bf16[1,16,3584]{2,1,0:T(8,128)(2,1)S(1)}, bf16[1,16,3584]{2,1,0:T(8,128)(2,1)}, u32[]{:S(2)}) copy-start(bf16[1,16,3584]{2,1,0:T(8,128)(2,1)} %param.9) | copy-start | bytes 344068
  2.9 11.2 %copy-start.4 = (bf16[1,16,3584]{2,1,0:T(8,128)(2,1)S(1)}, bf16[1,16,3584]{2,1,0:T(8,128)(2,1)}, u32[]{:S(2)}) copy-start(bf16[1,16,3584]{2,1,0:T(8,128)(2,1)} %param.10) | copy-start | bytes 344068
  5.1 72.7 %collective-permute-start = (bf16[3584,384]{1,0:T(8,128)(2,1)S(1)}, bf16[3584,384]{1,0:T(8,128)(2,1)}, u32[]{:S(2)}, u32[]{:S(2)}) collective-permute-start(bf16[3584,384]{1,0:T(8,128)(2,1)S(1)} %pad_maximum_fusion.refs_0_), channel_id=1, source_target_pairs={{0,8},{1,25},{2,10},{3,27},{4,12},{5,29},{6,14},{7,31},{8,16},{9,1... | collective-permute-start | bytes 8257544 | tf_op jit(solution)/shard_map/gather_weights/ppermute | solution.py:40
  8.5 69.3 %collective-permute-start.1 = (bf16[3584,384]{1,0:T(8,128)(2,1)S(1)}, bf16[3584,384]{1,0:T(8,128)(2,1)}, u32[]{:S(2)}, u32[]{:S(2)}) collective-permute-start(bf16[3584,384]{1,0:T(8,128)(2,1)S(1)} %pad_maximum_fusion.refs_0_), channel_id=1, source_target_pairs={{0,24},{1,9},{2,26},{3,11},{4,28},{5,13},{6,30},{7,15},{8,0},{9,17... | collective-permute-start | bytes 8257544 | tf_op jit(solution)/shard_map/gather_weights/ppermute | solution.py:40
  12.1 1.6 copy-start
  14.2 18.3 %collective-permute-start.2 = (bf16[16,10880]{1,0:T(8,128)(2,1)S(1)}, bf16[16,10880]{1,0:T(8,128)(2,1)S(1)}, u32[]{:S(2)}, u32[]{:S(2)}) collective-permute-start(bf16[16,10880]{1,0:T(8,128)(2,1)S(1)} %pad_maximum_fusion.2), channel_id=1, source_target_pairs={{0,2},{1,7},{2,4},{3,1},{4,6},{5,3},{6,0},{7,5},{8,10},{9,15},{10,... | collective-permute-start | bytes 1044488 | tf_op jit(solution)/shard_map/gather_rows/ppermute | solution.py:35
  23.3 45.0 %collective-permute-start.3 = (bf16[16,10880]{1,0:T(8,128)(2,1)S(1)}, bf16[16,10880]{1,0:T(8,128)(2,1)S(1)}, u32[]{:S(2)}, u32[]{:S(2)}) collective-permute-start(bf16[16,10880]{1,0:T(8,128)(2,1)S(1)} %pad_maximum_fusion.2), channel_id=1, source_target_pairs={{0,6},{1,3},{2,0},{3,5},{4,2},{5,7},{6,4},{7,1},{8,14},{9,11},{10,... | collective-permute-start | bytes 1044488 | tf_op jit(solution)/shard_map/gather_rows/ppermute | solution.py:35
  32.5 45.3 %collective-permute-start.4 = (bf16[16,10880]{1,0:T(8,128)(2,1)S(1)}, bf16[16,10880]{1,0:T(8,128)(2,1)S(1)}, u32[]{:S(2)}, u32[]{:S(2)}) collective-permute-start(bf16[16,10880]{1,0:T(8,128)(2,1)S(1)} %collective-permute-done.2), channel_id=1, source_target_pairs={{0,2},{1,7},{2,4},{3,1},{4,6},{5,3},{6,0},{7,5},{8,10},{9,15},{10,... | collective-permute-start | bytes 1044488 | tf_op jit(solution)/shard_map/gather_rows/ppermute | solution.py:35
  77.7 36.5 %collective-permute-start.6 = (bf16[3584,384]{1,0:T(8,128)(2,1)}, bf16[3584,384]{1,0:T(8,128)(2,1)}, u32[]{:S(2)}, u32[]{:S(2)}) collective-permute-start(bf16[3584,384]{1,0:T(8,128)(2,1)} %collective-permute-done.refs_1_), channel_id=1, source_target_pairs={{0,8},{1,25},{2,10},{3,27},{4,12},{5,29},{6,14},{7,31},{8,16},{9,1... | collective-permute-start | bytes 8257544 | tf_op jit(solution)/shard_map/gather_opposite/ppermute | solution.py:40
  80.0 5.0 %collective-permute-start.5 = (bf16[64,10880]{1,0:T(8,128)(2,1)S(1)}, bf16[64,10880]{1,0:T(8,128)(2,1)S(1)}, u32[]{:S(2)}, u32[]{:S(2)}) collective-permute-start(bf16[64,10880]{1,0:T(8,128)(2,1)S(1)} %pad_maximum_fusion.1.mine), channel_id=1, source_target_pairs={{0,1},{1,0},{2,3},{3,2},{4,5},{5,4},{6,7},{7,6},{8,9},{9,8},{10,11... | collective-permute-start | bytes 4177928 | tf_op jit(solution)/shard_map/gather_opposite/ppermute | solution.py:44
  85.1 1.8 %copy-start.1 = (bf16[3584,384]{1,0:T(8,128)(2,1)S(1)}, bf16[3584,384]{1,0:T(8,128)(2,1)}, u32[]{:S(2)}) copy-start(bf16[3584,384]{1,0:T(8,128)(2,1)} %copy-done) | copy-start | bytes 8257540
  118.1 4.4 %collective-permute-start.7 = (bf16[64,7168]{1,0:T(8,128)(2,1)S(1)}, bf16[64,7168]{1,0:T(8,128)(2,1)S(1)}, u32[]{:S(2)}, u32[]{:S(2)}) collective-permute-start(bf16[64,7168]{1,0:T(8,128)(2,1)S(1)} %get-tuple-element.19), channel_id=1, source_target_pairs={{0,1},{1,0},{2,3},{3,2},{4,5},{5,4},{6,7},{7,6},{8,9},{9,8},{10,11... | collective-permute-start | bytes 2752520 | tf_op jit(solution)/shard_map/cores/ppermute | solution.py:44
  122.8 28.1 %collective-permute-start.9 = (bf16[16,7168]{1,0:T(8,128)(2,1)S(1)}, bf16[16,7168]{1,0:T(8,128)(2,1)S(1)}, u32[]{:S(2)}, u32[]{:S(2)}) collective-permute-start(bf16[16,7168]{1,0:T(8,128)(2,1)S(1)} %get-tuple-element.23), channel_id=1, source_target_pairs={{0,6},{1,3},{2,0},{3,5},{4,2},{5,7},{6,4},{7,1},{8,14},{9,11},{10,... | collective-permute-start | bytes 688136 | tf_op jit(solution)/shard_map/home/ppermute | solution.py:35
  129.0 29.4 %collective-permute-start.8 = (bf16[16,7168]{1,0:T(8,128)(2,1)S(1)}, bf16[16,7168]{1,0:T(8,128)(2,1)S(1)}, u32[]{:S(2)}, u32[]{:S(2)}) collective-permute-start(bf16[16,7168]{1,0:T(8,128)(2,1)S(1)} %get-tuple-element.22), channel_id=1, source_target_pairs={{0,2},{1,7},{2,4},{3,1},{4,6},{5,3},{6,0},{7,5},{8,10},{9,15},{10,... | collective-permute-start | bytes 688136 | tf_op jit(solution)/shard_map/home/ppermute | solution.py:35
  150.9 11.8 %collective-permute-start.10 = (bf16[16,7168]{1,0:T(8,128)(2,1)S(1)}, bf16[16,7168]{1,0:T(8,128)(2,1)S(1)}, u32[]{:S(2)}, u32[]{:S(2)}) collective-permute-start(bf16[16,7168]{1,0:T(8,128)(2,1)S(1)} %fusion), channel_id=1, source_target_pairs={{0,6},{1,3},{2,0},{3,5},{4,2},{5,7},{6,4},{7,1},{8,14},{9,11},{10,... | collective-permute-start | bytes 688136 | tf_op jit(solution)/shard_map/home/ppermute | solution.py:35
  162.9 10.5 %collective-permute-start.11 = (bf16[16,3584]{1,0:T(8,128)(2,1)S(1)}, bf16[16,3584]{1,0:T(8,128)(2,1)S(1)}, u32[]{:S(2)}, u32[]{:S(2)}) collective-permute-start(bf16[16,3584]{1,0:T(8,128)(2,1)S(1)} %get-tuple-element.25), channel_id=1, source_target_pairs={{0,32},{32,64},{64,96},{96,128},{128,160},{160,192},{192,224},{224... | collective-permute-start | bytes 344072 | tf_op jit(solution)/shard_map/sections/ppermute | solution.py:50
  164.8 9.0 %collective-permute-start.12 = (bf16[16,3584]{1,0:T(8,128)(2,1)S(1)}, bf16[16,3584]{1,0:T(8,128)(2,1)S(1)}, u32[]{:S(2)}, u32[]{:S(2)}) collective-permute-start(bf16[16,3584]{1,0:T(8,128)(2,1)S(1)} %get-tuple-element.24), channel_id=1, source_target_pairs={{32,0},{64,32},{96,64},{128,96},{160,128},{192,160},{224,192},{256... | collective-permute-start | bytes 344072 | tf_op jit(solution)/shard_map/sections/ppermute | solution.py:50

commit v11 on v10

--- a/solution.py
+++ b/solution.py
@@ -9,7 +9,8 @@
 Z = 4
 CORES = 2
 LANES = 128
-CHUNK = 512
+CHUNK = 256
+JOIN_PIECES = 4
 ROOM = 40 * 1024 * 1024
 
 
@@ -44,10 +45,16 @@
     return lax.ppermute(block, "expert", expert_route(lambda x, z, c: (x, z, 1 - c)))
 
 
-def to_section(block, step):
+def to_section(block, step, distance):
     sections = lax.axis_size("pipe")
-    route = [(p, p + step) for p in range(sections) if 0 <= p + step < sections]
-    return lax.ppermute(block, "pipe", route)
+    width = EXPERTS * Z * CORES
+    route = [
+        (p * width + source, (p + step) * width + target)
+        for p in range(sections)
+        if 0 <= p + step < sections
+        for source, target in expert_route(lambda x, z, c: (x, (z + distance * turn(c)) % Z, c))
+    ]
+    return lax.ppermute(block, ("pipe", "expert"), route)
 
 
 def together(*values):
@@ -88,6 +95,40 @@
     return lax.dot_general(a, b, (((1,), (1,)), ((), ())), preferred_element_type=jnp.float32)
 
 
+def join_kernel(gate_up, down, joined, done):
+    model, depth = gate_up.shape[0], down.shape[0]
+    piece = model // JOIN_PIECES
+    pairs = [
+        (gate_up.at[pl.ds(k * piece, piece), :], joined.at[pl.ds(k * piece, piece), :])
+        for k in range(JOIN_PIECES)
+    ]
+    pairs += [
+        (down.at[:, pl.ds(k * CHUNK, CHUNK)], joined.at[pl.ds(model + k * depth, depth), :])
+        for k in range(model // CHUNK)
+    ]
+    copies = [
+        pltpu.make_async_copy(source, target, done.at[k])
+        for k, (source, target) in enumerate(pairs)
+    ]
+    for copy in copies:
+        copy.start()
+    for copy in copies:
+        copy.wait()
+
+
+def join_weights(gate_up, down):
+    model, depth = gate_up.shape[0], down.shape[0]
+    anywhere = pl.BlockSpec(memory_space=pl.ANY)
+    rows = model + model // CHUNK * depth
+    return pl.pallas_call(
+        join_kernel,
+        out_shape=jax.ShapeDtypeStruct((rows, CHUNK), gate_up.dtype),
+        in_specs=[anywhere, anywhere],
+        out_specs=anywhere,
+        scratch_shapes=[pltpu.SemaphoreType.DMA((JOIN_PIECES + model // CHUNK,))],
+    )(gate_up, down)
+
+
 def fill_rows(mine, other, rows):
     half, model = mine.shape[0], rows[0].shape[1]
     for k, target in enumerate(rows):
@@ -102,40 +143,40 @@
 
 def one_expert(rows, weight, share, back_share):
     token, saved, upstream = rows
-    half = weight.shape[1] // 3
-    both = dot(token[...], weight[:, : 2 * half])
+    model, half = token.shape[1], CHUNK // 2
+    cuts = [slice(low, low + CHUNK) for low in range(0, model, CHUNK)]
+    downs = [slice(model + k * half, model + (k + 1) * half) for k in range(len(cuts))]
+    gate_up = weight[:model, :]
+    both = dot(token[...], gate_up)
     gate_val, up_val = both[:, :half], both[:, half:]
     hidden = (gate_val * jax.nn.sigmoid(gate_val) * up_val).astype(jnp.bfloat16)
-    hidden_grad = dot(upstream[...], weight[:, 2 * half :])
-    both = dot(saved[...], weight[:, : 2 * half])
+    hidden_grad = sum(dot_t(upstream[:, cut], weight[at, :]) for cut, at in zip(cuts, downs))
+    both = dot(saved[...], gate_up)
     gate_val, up_val = both[:, :half], both[:, half:]
     sig = jax.nn.sigmoid(gate_val)
     gate_grad = hidden_grad * up_val * sig * (1.0 + gate_val * (1.0 - sig))
     up_grad = hidden_grad * gate_val * sig
     grad = jnp.concatenate([gate_grad, up_grad], axis=1).astype(jnp.bfloat16)
-    for low in range(0, token.shape[1], CHUNK):
-        cut = slice(low, low + CHUNK)
-        out = share * dot_t(hidden, weight[cut, 2 * half :])
-        yield cut, out, back_share * dot_t(grad, weight[cut, : 2 * half])
+    for cut, at in zip(cuts, downs):
+        yield cut, share * dot(hidden, weight[at, :]), back_share * dot_t(grad, weight[cut, :])
 
 
 def first_kernel(mine, other, picks, *refs):
-    weights, (total, back_total), rows = refs[:3], refs[3:5], refs[5:]
+    weights, (total, back_total), rows, shares = refs[:3], refs[3:5], refs[5:8], refs[8]
     fill_rows(mine, other, rows)
-    shares = pick_shares(mine, other, picks, rows[0].shape[1])
+    shares[...] = pick_shares(mine, other, picks, rows[0].shape[1])
     for k, weight in enumerate(weights):
-        share, back_share = shares[:, k : k + 1], shares[:, 3 + k : 4 + k]
+        share, back_share = shares[:, k : k + 1], shares[:, EXPERTS + k : EXPERTS + k + 1]
         for cut, out, back_out in one_expert(rows, weight, share, back_share):
             if k > 0:
                 out, back_out = out + total[:, cut], back_out + back_total[:, cut]
             total[:, cut], back_total[:, cut] = out, back_out
 
 
-def last_kernel(mine, other, picks, weight, total, back_total, keep, give, *rows):
-    fill_rows(mine, other, rows)
-    half, model = mine.shape[0], rows[0].shape[1]
-    shares = pick_shares(mine, other, picks, model)
-    for cut, out, back_out in one_expert(rows, weight, shares[:, :1], shares[:, 1:2]):
+def last_kernel(total, back_total, token, saved, upstream, shares, weight, keep, give):
+    half, model = keep.shape[0], token.shape[1]
+    share, back_share = shares[:, EXPERTS - 1 : EXPERTS], shares[:, 2 * EXPERTS - 1 : 2 * EXPERTS]
+    for cut, out, back_out in one_expert((token, saved, upstream), weight, share, back_share):
         back_cut = slice(model + cut.start, model + cut.stop)
         out, back_out = out + total[:, cut], back_out + back_total[:, cut]
         keep[:, cut], keep[:, back_cut] = out[:half], back_out[:half]
@@ -143,15 +184,13 @@
         give[:, back_cut] = back_out[half:].astype(jnp.bfloat16)
 
 
-def run_kernel(kernel, operands, outs, model):
+def run_kernel(kernel, operands, outs):
     whole = pl.BlockSpec(memory_space=pltpu.VMEM)
-    both = 2 * operands[0].shape[0]
     return pl.pallas_call(
         kernel,
         out_shape=outs,
         in_specs=[whole] * len(operands),
         out_specs=tuple(whole for _ in outs),
-        scratch_shapes=[pltpu.VMEM((both, model), jnp.bfloat16) for _ in range(3)],
         compiler_params=pltpu.CompilerParams(vmem_limit_bytes=ROOM),
         cost_estimate=pl.CostEstimate(flops=1000, bytes_accessed=1000, transcendentals=0),
     )(*operands)
@@ -176,7 +215,7 @@
     experts = [(me + EXPERTS + d * turned) % EXPERTS for d in (0, -1, 1, -2)]
 
     with jax.named_scope("gather_weights"):
-        weights = jnp.concatenate([gate_up_weight[0], down_weight[0].T], axis=1)
+        weights = join_weights(gate_up_weight[0], down_weight[0])
         near, far = along_x(weights, 1), along_x(weights, -1)
     with jax.named_scope("gather_rows"):
         shares = [
@@ -194,29 +233,35 @@
         other = other_core(mine)
     half = Z * rows
     with jax.named_scope("experts"):
-        outs = (jax.ShapeDtypeStruct((2 * half, model), jnp.float32),) * 2
-        operands = (mine, other, share_picks(experts[:3]), *weights[:3])
-        sums = run_kernel(first_kernel, operands, outs, model)
+        outs = [jax.ShapeDtypeStruct((2 * half, model), jnp.float32)] * 2
+        outs += [jax.ShapeDtypeStruct((2 * half, model), jnp.bfloat16)] * 3
+        outs += [jax.ShapeDtypeStruct((2 * half, LANES), jnp.float32)]
+        sums = run_kernel(first_kernel, (mine, other, share_picks(experts), *weights[:3]), outs)
+    with jax.named_scope("residual"):
+        tokens, upstream, *sums = together(tokens, upstream, *sums)
+        residuals = to_section(tokens, 1, 0), to_section(upstream, -1, 0)
+        *residuals, last_weight = together(*residuals, weights[3])
     with jax.named_scope("last_expert"):
         outs = (
             jax.ShapeDtypeStruct((half, 2 * model), jnp.float32),
             jax.ShapeDtypeStruct((half, 2 * model), jnp.bfloat16),
         )
-        operands = (mine, other, share_picks(experts[3:]), weights[3], *sums)
-        keep, give = run_kernel(last_kernel, operands, outs, model)
+        keep, give = run_kernel(last_kernel, (*sums, last_weight), outs)
     with jax.named_scope("cores"):
         total = keep + other_core(give).astype(jnp.float32)
     with jax.named_scope("home"):
         own, near, far, passed = jnp.split(total, Z, axis=0)
         passed = along_z(passed.astype(jnp.bfloat16), -1)
-        far = along_z(far.astype(jnp.bfloat16), 1)
-        near = along_z((near + passed.astype(jnp.float32)).astype(jnp.bfloat16), -1)
-        residual = jnp.concatenate([tokens, upstream], axis=1).astype(jnp.float32)
-        total = own + residual + far.astype(jnp.float32) + near.astype(jnp.float32)
-        total = total.astype(jnp.bfloat16)
-    with jax.named_scope("sections"):
-        forward_next = to_section(total[:, :model], 1)
-        backward_next = to_section(total[:, model:], -1)
+        own, far = own.astype(jnp.bfloat16), far.astype(jnp.bfloat16)
+        parts = [to_section(own[:, :model], 1, 0), to_section(own[:, model:], -1, 0)]
+        parts += [to_section(far[:, :model], 1, 1), to_section(far[:, model:], -1, 1)]
+        passed, *parts = together(passed, *parts)
+        near = (near + passed.astype(jnp.float32)).astype(jnp.bfloat16)
+        parts += [to_section(near[:, :model], 1, -1), to_section(near[:, model:], -1, -1)]
+        sides = [[residuals[k]] + parts[k::2] for k in range(2)]
+        forward_next, backward_next = [
+            sum(part.astype(jnp.float32) for part in side).astype(jnp.bfloat16) for side in sides
+        ]
     return (forward_next[None], backward_next[None])
 
 

time: 177 us -> 256 us (1.45)
  Pallas kernels: 11.8 us -> 97.9 us
  starting transfers between devices: 84.7 us -> 104 us
  waiting for transfers between devices: 67.2 us -> 48.3 us
  local copies, waits for them, and re-layouts: 7.24 us -> 0.36 us
    pallas_call x0 -> x1, Pallas kernels: none -> 84.6 us  [join_weights(): pl.pallas_call(join_kernel, out_shape=jax.ShapeDtypeStruct((rows, CHUNK),...]
    ppermute x2 -> x8, starting transfers between devices: 8.54 us -> 39 us  [to_section(): return lax.ppermute(block, ('pipe', 'expert'), route)]
    ppermute x6 -> x4, waiting for transfers between devices: 40.4 us -> 18.4 us  [along_z(): return lax.ppermute(block, 'expert', route)]
    ppermute x2 -> x8, waiting for transfers between devices: 2.35 us -> 16.9 us  [to_section(): return lax.ppermute(block, ('pipe', 'expert'), route)]
    ppermute x3, waiting for transfers between devices: 19.4 us -> 7.35 us  [along_x(): return lax.ppermute(block, 'expert', route)]
    ppermute x6 -> x4, starting transfers between devices: 63 us -> 51.6 us  [along_z(): return lax.ppermute(block, 'expert', route)]
    unnamed x21 -> x16, local copies, waits for them, and re-layouts: 6.93 us -> 0.03 us
  transfers between devices with their start and end apart: 13 -> 17, of which waited for: 10 -> 12; matrix products, arithmetic and copies ran while one was open for 1% -> 1% of each run, Pallas kernels for 5% -> 4%
where the time goes in v11:
time: 256 us; the launch traced here: 255 us
  starting transfers between devices  104 us (41%)
  Pallas kernels  97.9 us (38%)
  waiting for transfers between devices  48.3 us (19%)
  other arithmetic  3.26 us (1%)
    pallas_call x1, Pallas kernels, join_weights(): pl.pallas_call(join_kernel, out_shape=jax.ShapeDtypeStruct((rows, CHUNK),...  84.6 us
    ppermute x4, starting transfers between devices, along_z(): return lax.ppermute(block, 'expert', route)  51.6 us
    ppermute x8, starting transfers between devices, to_section(): return lax.ppermute(block, ('pipe', 'expert'), route)  39 us
    ppermute x4, waiting for transfers between devices, along_z(): return lax.ppermute(block, 'expert', route)  18.4 us
    ppermute x8, waiting for transfers between devices, to_section(): return lax.ppermute(block, ('pipe', 'expert'), route)  16.9 us
    pallas_call x2, Pallas kernels, run_kernel(): pl.pallas_call(kernel, out_shape=outs, in_specs=[whole] * len(operands),...  13.2 us
    ppermute x3, starting transfers between devices, along_x(): return lax.ppermute(block, 'expert', route)  9.25 us
    ppermute x3, waiting for transfers between devices, along_x(): return lax.ppermute(block, 'expert', route)  7.35 us
  transfers between devices with their start and end apart: 17, of which 12 were waited for; matrix products, arithmetic and copies ran while one was open for 1% of the time, Pallas kernels for 4%

profile of v11, /device:TPU:24, one launch (start us, length us, event | category | flops | bytes accessed | tf_op | source)
XLA Modules:
  0.0 254.6 jit_solution(7425056779512631248)
XLA Ops:
  0.7 84.6 %gather_weights.1.refs_0_ = bf16[5376,256]{1,0:T(8,128)(2,1)} custom-call(bf16[3584,256]{1,0:T(8,128)(2,1)} %bitcast.21, bf16[128,3584]{1,0:T(8,128)(2,1)} %bitcast.22), custom_call_target="tpu_custom_call" | custom-call | tf_op jit(solution)/shard_map/gather_weights/pallas_call | solution.py:123
  85.4 4.7 %collective-permute-start.1 = (bf16[5376,256]{1,0:T(8,128)(2,1)}, bf16[5376,256]{1,0:T(8,128)(2,1)}, u32[]{:S(2)}, u32[]{:S(2)}) collective-permute-start(bf16[5376,256]{1,0:T(8,128)(2,1)} %gather_weights.1.refs_0_), channel_id=1, source_target_pairs={{0,24},{1,9},{2,26},{3,11},{4,28},{5,13},{6,30},{7,15},{8,0},{9,17... | collective-permute-start | bytes 8257544 | tf_op jit(solution)/shard_map/gather_weights/ppermute | solution.py:41
  90.0 1.9 collective-permute-start
  92.0 0.1 copy.18
  92.1 0.1 copy.17
  92.2 0.1 reduce-precision_convert_fusion.1
  92.3 0.1 fusion.8
  92.4 9.4 %collective-permute-start.2 = (bf16[16,10880]{1,0:T(8,128)(2,1)S(1)}, bf16[16,10880]{1,0:T(8,128)(2,1)S(1)}, u32[]{:S(2)}, u32[]{:S(2)}) collective-permute-start(bf16[16,10880]{1,0:T(8,128)(2,1)S(1)} %pad_maximum_fusion.1), channel_id=1, source_target_pairs={{0,2},{1,7},{2,4},{3,1},{4,6},{5,3},{6,0},{7,5},{8,10},{9,15},{10,... | collective-permute-start | bytes 1044488 | tf_op jit(solution)/shard_map/gather_rows/ppermute | solution.py:36
  101.8 5.6 %collective-permute-start.3 = (bf16[16,10880]{1,0:T(8,128)(2,1)S(1)}, bf16[16,10880]{1,0:T(8,128)(2,1)S(1)}, u32[]{:S(2)}, u32[]{:S(2)}) collective-permute-start(bf16[16,10880]{1,0:T(8,128)(2,1)S(1)} %pad_maximum_fusion.1), channel_id=1, source_target_pairs={{0,6},{1,3},{2,0},{3,5},{4,2},{5,7},{6,4},{7,1},{8,14},{9,11},{10,... | collective-permute-start | bytes 1044488 | tf_op jit(solution)/shard_map/gather_rows/ppermute | solution.py:36
  107.3 3.6 %collective-permute-done.2 = bf16[16,10880]{1,0:T(8,128)(2,1)S(1)} collective-permute-done((bf16[16,10880]{1,0:T(8,128)(2,1)S(1)}, bf16[16,10880]{1,0:T(8,128)(2,1)S(1)}, u32[]{:S(2)}, u32[]{:S(2)}) %collective-permute-start.2) | collective-permute-done | bytes 348192 | tf_op jit(solution)/shard_map/gather_rows/ppermute | solution.py:36
  111.0 30.4 %collective-permute-start.4 = (bf16[16,10880]{1,0:T(8,128)(2,1)S(1)}, bf16[16,10880]{1,0:T(8,128)(2,1)S(1)}, u32[]{:S(2)}, u32[]{:S(2)}) collective-permute-start(bf16[16,10880]{1,0:T(8,128)(2,1)S(1)} %collective-permute-done.2), channel_id=1, source_target_pairs={{0,2},{1,7},{2,4},{3,1},{4,6},{5,3},{6,0},{7,5},{8,10},{9,15},{10,... | collective-permute-start | bytes 1044488 | tf_op jit(solution)/shard_map/gather_rows/ppermute | solution.py:36
  141.4 0.0 collective-permute-done.3
  141.4 14.8 %collective-permute-done.4 = bf16[16,10880]{1,0:T(8,128)(2,1)S(1)} collective-permute-done((bf16[16,10880]{1,0:T(8,128)(2,1)S(1)}, bf16[16,10880]{1,0:T(8,128)(2,1)S(1)}, u32[]{:S(2)}, u32[]{:S(2)}) %collective-permute-start.4) | collective-permute-done | bytes 348192 | tf_op jit(solution)/shard_map/gather_rows/ppermute | solution.py:36
  156.2 0.0 collective-permute-done.1.refs_2_
  156.2 0.0 collective-permute-done.refs_1_
  156.2 2.7 %collective-permute-start.8 = (bf16[5376,256]{1,0:T(8,128)(2,1)}, bf16[5376,256]{1,0:T(8,128)(2,1)}, u32[]{:S(2)}, u32[]{:S(2)}) collective-permute-start(bf16[5376,256]{1,0:T(8,128)(2,1)} %collective-permute-done.refs_1_), channel_id=1, source_target_pairs={{0,8},{1,25},{2,10},{3,27},{4,12},{5,29},{6,14},{7,31},{8,16},{9,1... | collective-permute-start | bytes 8257544 | tf_op jit(solution)/shard_map/gather_opposite/ppermute | solution.py:41
  158.9 1.2 pad_maximum_fusion.mine
  160.1 1.9 collective-permute-start.5
  162.1 0.1 stack.35
  162.2 0.1 compare_and_fusion
  162.4 3.1 %collective-permute-done.5.other = bf16[64,10880]{1,0:T(8,128)(2,1)} collective-permute-done((bf16[64,10880]{1,0:T(8,128)(2,1)}, bf16[64,10880]{1,0:T(8,128)(2,1)}, u32[]{:S(2)}, u32[]{:S(2)}) %collective-permute-start.5) | collective-permute-done | bytes 1392672 | tf_op jit(solution)/shard_map/gather_opposite/ppermute | solution.py:45
  165.5 9.3 %experts.1 = (f32[128,3584]{1,0:T(8,128)S(1)}, f32[128,3584]{1,0:T(8,128)S(1)}, bf16[128,3584]{1,0:T(8,128)(2,1)S(1)}, bf16[128,3584]{1,0:T(8,128)(2,1)S(1)}, bf...) custom-call(bf16[64,10880]{1,0:T(8,128)(2,1)} %pad_maximum_fusion.mine, ...), custom_call_target="tpu_custom_call" | custom-call | flops 1000 | bytes 1000 | tf_op jit(solution)/shard_map/experts/pallas_call | solution.py:189
  174.8 1.9 collective-permute-start.6
  176.7 6.6 %collective-permute-start.7 = (bf16[16,3584]{1,0:T(8,128)(2,1)S(1)}, bf16[16,3584]{1,0:T(8,128)(2,1)S(1)}, u32[]{:S(2)}, u32[]{:S(2)}) collective-permute-start(bf16[16,3584]{1,0:T(8,128)(2,1)S(1)} %bitcast.30), channel_id=1, source_target_pairs={{32,0},{33,1},{34,2},{35,3},{36,4},{37,5},{38,6},{39,7},{40,8},{41... | collective-permute-start | bytes 344072 | tf_op jit(solution)/shard_map/residual/ppermute | solution.py:57
  183.4 1.8 collective-permute-done.6
  185.2 0.6 collective-permute-done.7
  185.8 7.3 %collective-permute-done.8.weight = bf16[5376,256]{1,0:T(8,128)(2,1)} collective-permute-done((bf16[5376,256]{1,0:T(8,128)(2,1)}, bf16[5376,256]{1,0:T(8,128)(2,1)}, u32[]{:S(2)}, u32[]{:S(2)}) %collective-permute-start.8) | collective-permute-done | bytes 2752544 | tf_op jit(solution)/shard_map/gather_opposite/ppermute | solution.py:41
  193.1 3.9 %last_expert.1 = (f32[64,7168]{1,0:T(8,128)S(1)}, bf16[64,7168]{1,0:T(8,128)(2,1)S(1)}) custom-call(f32[128,3584]{1,0:T(8,128)S(1)} %get-tuple-element.45.total, f32[128,3584]{1,0:T(8,128)S(1)} %get-tuple-element.46.back_total, bf16[128,3584]{1,0:T(8,128)(2,1)S(1)} %get-tuple-element.47.token, bf16[128,3584]{1,0:T(8,128)(2,1)S(1)} %get-tuple-element.48.saved, ...), custom_call_target="tpu_custom_call" | custom-call | flops 1000 | bytes 1000 | tf_op jit(solution)/shard_map/last_expert/pallas_call | solution.py:189
  197.1 1.9 collective-permute-start.9
  199.0 2.4 collective-permute-done.9
  201.4 0.2 fusion.9
  201.7 6.3 %collective-permute-start.10 = (bf16[16,7168]{1,0:T(8,128)(2,1)S(1)}, bf16[16,7168]{1,0:T(8,128)(2,1)S(1)}, u32[]{:S(2)}, u32[]{:S(2)}) collective-permute-start(bf16[16,7168]{1,0:T(8,128)(2,1)S(1)} %split.13), channel_id=1, source_target_pairs={{0,6},{1,3},{2,0},{3,5},{4,2},{5,7},{6,4},{7,1},{8,14},{9,11},{10,... | collective-permute-start | bytes 688136 | tf_op jit(solution)/shard_map/home/ppermute | solution.py:36
  208.0 4.5 %collective-permute-start.14 = (bf16[16,3584]{1,0:T(8,128)(2,1)S(1)}, bf16[16,3584]{1,0:T(8,128)(2,1)S(1)}, u32[]{:S(2)}, u32[]{:S(2)}) collective-permute-start(bf16[16,3584]{1,0:T(8,128)(2,1)S(1)} %get-tuple-element.62), channel_id=1, source_target_pairs={{32,2},{33,7},{34,4},{35,1},{36,6},{37,3},{38,0},{39,5},{40,10},{4... | collective-permute-start | bytes 344072 | tf_op jit(solution)/shard_map/home/ppermute | solution.py:57
  212.6 7.2 %collective-permute-start.13 = (bf16[16,3584]{1,0:T(8,128)(2,1)S(1)}, bf16[16,3584]{1,0:T(8,128)(2,1)S(1)}, u32[]{:S(2)}, u32[]{:S(2)}) collective-permute-start(bf16[16,3584]{1,0:T(8,128)(2,1)S(1)} %get-tuple-element.63), channel_id=1, source_target_pairs={{0,34},{1,39},{2,36},{3,33},{4,38},{5,35},{6,32},{7,37},{8,42},{9,... | collective-permute-start | bytes 344072 | tf_op jit(solution)/shard_map/home/ppermute | solution.py:57
  219.8 2.0 collective-permute-start.12
  221.8 3.9 %collective-permute-start.11 = (bf16[16,3584]{1,0:T(8,128)(2,1)S(1)}, bf16[16,3584]{1,0:T(8,128)(2,1)S(1)}, u32[]{:S(2)}, u32[]{:S(2)}) collective-permute-start(bf16[16,3584]{1,0:T(8,128)(2,1)S(1)} %get-tuple-element.65), channel_id=1, source_target_pairs={{0,32},{1,33},{2,34},{3,35},{4,36},{5,37},{6,38},{7,39},{8,40},{9,... | collective-permute-start | bytes 344072 | tf_op jit(solution)/shard_map/home/ppermute | solution.py:57
  225.7 1.0 collective-permute-done.14
  226.7 2.9 %collective-permute-done.13 = bf16[16,3584]{1,0:T(8,128)(2,1)S(1)} collective-permute-done((bf16[16,3584]{1,0:T(8,128)(2,1)S(1)}, bf16[16,3584]{1,0:T(8,128)(2,1)S(1)}, u32[]{:S(2)}, u32[]{:S(2)}) %collective-permute-start.13) | collective-permute-done | bytes 114720 | tf_op jit(solution)/shard_map/home/ppermute | solution.py:57
  229.6 1.9 collective-permute-done.12
  231.5 1.2 collective-permute-done.11
  232.7 0.0 collective-permute-done.10
  232.7 0.1 fusion
  232.8 6.4 %collective-permute-start.16 = (bf16[16,3584]{1,0:T(8,128)(2,1)S(1)}, bf16[16,3584]{1,0:T(8,128)(2,1)S(1)}, u32[]{:S(2)}, u32[]{:S(2)}) collective-permute-start(bf16[16,3584]{1,0:T(8,128)(2,1)S(1)} %get-tuple-element.66), channel_id=1, source_target_pairs={{32,6},{33,3},{34,0},{35,5},{36,2},{37,7},{38,4},{39,1},{40,14},{4... | collective-permute-start | bytes 344072 | tf_op jit(solution)/shard_map/home/ppermute | solution.py:57
  239.2 6.5 %collective-permute-start.15 = (bf16[16,3584]{1,0:T(8,128)(2,1)S(1)}, bf16[16,3584]{1,0:T(8,128)(2,1)S(1)}, u32[]{:S(2)}, u32[]{:S(2)}) collective-permute-start(bf16[16,3584]{1,0:T(8,128)(2,1)S(1)} %get-tuple-element.67), channel_id=1, source_target_pairs={{0,38},{1,35},{2,32},{3,37},{4,34},{5,39},{6,36},{7,33},{8,46},{9,... | collective-permute-start | bytes 344072 | tf_op jit(solution)/shard_map/home/ppermute | solution.py:57
  245.7 0.0 collective-permute-done.16
  245.7 0.7 fusion.2
  246.4 7.4 %collective-permute-done.15 = bf16[16,3584]{1,0:T(8,128)(2,1)S(1)} collective-permute-done((bf16[16,3584]{1,0:T(8,128)(2,1)S(1)}, bf16[16,3584]{1,0:T(8,128)(2,1)S(1)}, u32[]{:S(2)}, u32[]{:S(2)}) %collective-permute-start.15) | collective-permute-done | bytes 114720 | tf_op jit(solution)/shard_map/home/ppermute | solution.py:57
  253.9 0.7 fusion.1
  (25 shorter events, 0.2 us)
Async XLA Ops:
  0.6 91.3 %copy-start.4 = (f32[1,16,2]{1,2,0:T(2,128)S(1)}, f32[1,16,2]{1,2,0:T(2,128)}, u32[]{:S(2)}) copy-start(f32[1,16,2]{1,2,0:T(2,128)} %param.17) | copy-start | bytes 388
  0.6 91.3 %copy-start.5 = (s32[1,16,2]{1,2,0:T(2,128)S(1)}, s32[1,16,2]{1,2,0:T(2,128)}, u32[]{:S(2)}) copy-start(s32[1,16,2]{1,2,0:T(2,128)} %param.15) | copy-start | bytes 388
  0.7 91.4 %copy-start.6 = (f32[1,16,2]{1,2,0:T(2,128)S(1)}, f32[1,16,2]{1,2,0:T(2,128)}, u32[]{:S(2)}) copy-start(f32[1,16,2]{1,2,0:T(2,128)} %param.16) | copy-start | bytes 388
  0.7 91.4 %copy-start.7 = (s32[1,16,2]{1,2,0:T(2,128)S(1)}, s32[1,16,2]{1,2,0:T(2,128)}, u32[]{:S(2)}) copy-start(s32[1,16,2]{1,2,0:T(2,128)} %param.14) | copy-start | bytes 388
  0.7 91.7 %copy-start.1 = (bf16[1,16,3584]{2,1,0:T(8,128)(2,1)S(1)}, bf16[1,16,3584]{2,1,0:T(8,128)(2,1)}, u32[]{:S(2)}) copy-start(bf16[1,16,3584]{2,1,0:T(8,128)(2,1)} %param.10) | copy-start | bytes 344068
  0.7 91.7 %copy-start.2 = (bf16[1,16,3584]{2,1,0:T(8,128)(2,1)S(1)}, bf16[1,16,3584]{2,1,0:T(8,128)(2,1)}, u32[]{:S(2)}) copy-start(bf16[1,16,3584]{2,1,0:T(8,128)(2,1)} %param.9) | copy-start | bytes 344068
  0.7 91.7 %copy-start.3 = (bf16[1,16,3584]{2,1,0:T(8,128)(2,1)S(1)}, bf16[1,16,3584]{2,1,0:T(8,128)(2,1)}, u32[]{:S(2)}) copy-start(bf16[1,16,3584]{2,1,0:T(8,128)(2,1)} %param.11) | copy-start | bytes 344068
  85.4 70.9 %collective-permute-start.1 = (bf16[5376,256]{1,0:T(8,128)(2,1)}, bf16[5376,256]{1,0:T(8,128)(2,1)}, u32[]{:S(2)}, u32[]{:S(2)}) collective-permute-start(bf16[5376,256]{1,0:T(8,128)(2,1)} %gather_weights.1.refs_0_), channel_id=1, source_target_pairs={{0,24},{1,9},{2,26},{3,11},{4,28},{5,13},{6,30},{7,15},{8,0},{9,17... | collective-permute-start | bytes 8257544 | tf_op jit(solution)/shard_map/gather_weights/ppermute | solution.py:41
  90.0 66.2 %collective-permute-start = (bf16[5376,256]{1,0:T(8,128)(2,1)}, bf16[5376,256]{1,0:T(8,128)(2,1)}, u32[]{:S(2)}, u32[]{:S(2)}) collective-permute-start(bf16[5376,256]{1,0:T(8,128)(2,1)} %gather_weights.1.refs_0_), channel_id=1, source_target_pairs={{0,8},{1,25},{2,10},{3,27},{4,12},{5,29},{6,14},{7,31},{8,16},{9,1... | collective-permute-start | bytes 8257544 | tf_op jit(solution)/shard_map/gather_weights/ppermute | solution.py:41
  92.4 73.1 %copy-start = (bf16[5376,256]{1,0:T(8,128)(2,1)S(1)}, bf16[5376,256]{1,0:T(8,128)(2,1)}, u32[]{:S(2)}) copy-start(bf16[5376,256]{1,0:T(8,128)(2,1)} %gather_weights.1.refs_0_) | copy-start | bytes 8257540
  92.4 18.6 %collective-permute-start.2 = (bf16[16,10880]{1,0:T(8,128)(2,1)S(1)}, bf16[16,10880]{1,0:T(8,128)(2,1)S(1)}, u32[]{:S(2)}, u32[]{:S(2)}) collective-permute-start(bf16[16,10880]{1,0:T(8,128)(2,1)S(1)} %pad_maximum_fusion.1), channel_id=1, source_target_pairs={{0,2},{1,7},{2,4},{3,1},{4,6},{5,3},{6,0},{7,5},{8,10},{9,15},{10,... | collective-permute-start | bytes 1044488 | tf_op jit(solution)/shard_map/gather_rows/ppermute | solution.py:36
  101.8 39.6 %collective-permute-start.3 = (bf16[16,10880]{1,0:T(8,128)(2,1)S(1)}, bf16[16,10880]{1,0:T(8,128)(2,1)S(1)}, u32[]{:S(2)}, u32[]{:S(2)}) collective-permute-start(bf16[16,10880]{1,0:T(8,128)(2,1)S(1)} %pad_maximum_fusion.1), channel_id=1, source_target_pairs={{0,6},{1,3},{2,0},{3,5},{4,2},{5,7},{6,4},{7,1},{8,14},{9,11},{10,... | collective-permute-start | bytes 1044488 | tf_op jit(solution)/shard_map/gather_rows/ppermute | solution.py:36
  111.0 45.3 %collective-permute-start.4 = (bf16[16,10880]{1,0:T(8,128)(2,1)S(1)}, bf16[16,10880]{1,0:T(8,128)(2,1)S(1)}, u32[]{:S(2)}, u32[]{:S(2)}) collective-permute-start(bf16[16,10880]{1,0:T(8,128)(2,1)S(1)} %collective-permute-done.2), channel_id=1, source_target_pairs={{0,2},{1,7},{2,4},{3,1},{4,6},{5,3},{6,0},{7,5},{8,10},{9,15},{10,... | collective-permute-start | bytes 1044488 | tf_op jit(solution)/shard_map/gather_rows/ppermute | solution.py:36
  156.2 36.9 %collective-permute-start.8 = (bf16[5376,256]{1,0:T(8,128)(2,1)}, bf16[5376,256]{1,0:T(8,128)(2,1)}, u32[]{:S(2)}, u32[]{:S(2)}) collective-permute-start(bf16[5376,256]{1,0:T(8,128)(2,1)} %collective-permute-done.refs_1_), channel_id=1, source_target_pairs={{0,8},{1,25},{2,10},{3,27},{4,12},{5,29},{6,14},{7,31},{8,16},{9,1... | collective-permute-start | bytes 8257544 | tf_op jit(solution)/shard_map/gather_opposite/ppermute | solution.py:41
  160.1 5.4 %collective-permute-start.5 = (bf16[64,10880]{1,0:T(8,128)(2,1)}, bf16[64,10880]{1,0:T(8,128)(2,1)}, u32[]{:S(2)}, u32[]{:S(2)}) collective-permute-start(bf16[64,10880]{1,0:T(8,128)(2,1)} %pad_maximum_fusion.mine), channel_id=1, source_target_pairs={{0,1},{1,0},{2,3},{3,2},{4,5},{5,4},{6,7},{7,6},{8,9},{9,8},{10,11... | collective-permute-start | bytes 4177928 | tf_op jit(solution)/shard_map/gather_opposite/ppermute | solution.py:45
  174.8 10.4 %collective-permute-start.6 = (bf16[16,3584]{1,0:T(8,128)(2,1)S(1)}, bf16[16,3584]{1,0:T(8,128)(2,1)S(1)}, u32[]{:S(2)}, u32[]{:S(2)}) collective-permute-start(bf16[16,3584]{1,0:T(8,128)(2,1)S(1)} %bitcast.27), channel_id=1, source_target_pairs={{0,32},{1,33},{2,34},{3,35},{4,36},{5,37},{6,38},{7,39},{8,40},{9,... | collective-permute-start | bytes 344072 | tf_op jit(solution)/shard_map/residual/ppermute | solution.py:57
  176.7 9.0 %collective-permute-start.7 = (bf16[16,3584]{1,0:T(8,128)(2,1)S(1)}, bf16[16,3584]{1,0:T(8,128)(2,1)S(1)}, u32[]{:S(2)}, u32[]{:S(2)}) collective-permute-start(bf16[16,3584]{1,0:T(8,128)(2,1)S(1)} %bitcast.30), channel_id=1, source_target_pairs={{32,0},{33,1},{34,2},{35,3},{36,4},{37,5},{38,6},{39,7},{40,8},{41... | collective-permute-start | bytes 344072 | tf_op jit(solution)/shard_map/residual/ppermute | solution.py:57
  197.1 4.4 %collective-permute-start.9 = (bf16[64,7168]{1,0:T(8,128)(2,1)S(1)}, bf16[64,7168]{1,0:T(8,128)(2,1)S(1)}, u32[]{:S(2)}, u32[]{:S(2)}) collective-permute-start(bf16[64,7168]{1,0:T(8,128)(2,1)S(1)} %get-tuple-element.53), channel_id=1, source_target_pairs={{0,1},{1,0},{2,3},{3,2},{4,5},{5,4},{6,7},{7,6},{8,9},{9,8},{10,11... | collective-permute-start | bytes 2752520 | tf_op jit(solution)/shard_map/cores/ppermute | solution.py:45
  201.7 31.1 %collective-permute-start.10 = (bf16[16,7168]{1,0:T(8,128)(2,1)S(1)}, bf16[16,7168]{1,0:T(8,128)(2,1)S(1)}, u32[]{:S(2)}, u32[]{:S(2)}) collective-permute-start(bf16[16,7168]{1,0:T(8,128)(2,1)S(1)} %split.13), channel_id=1, source_target_pairs={{0,6},{1,3},{2,0},{3,5},{4,2},{5,7},{6,4},{7,1},{8,14},{9,11},{10,... | collective-permute-start | bytes 688136 | tf_op jit(solution)/shard_map/home/ppermute | solution.py:36
  208.0 18.7 %collective-permute-start.14 = (bf16[16,3584]{1,0:T(8,128)(2,1)S(1)}, bf16[16,3584]{1,0:T(8,128)(2,1)S(1)}, u32[]{:S(2)}, u32[]{:S(2)}) collective-permute-start(bf16[16,3584]{1,0:T(8,128)(2,1)S(1)} %get-tuple-element.62), channel_id=1, source_target_pairs={{32,2},{33,7},{34,4},{35,1},{36,6},{37,3},{38,0},{39,5},{40,10},{4... | collective-permute-start | bytes 344072 | tf_op jit(solution)/shard_map/home/ppermute | solution.py:57
  212.6 17.1 %collective-permute-start.13 = (bf16[16,3584]{1,0:T(8,128)(2,1)S(1)}, bf16[16,3584]{1,0:T(8,128)(2,1)S(1)}, u32[]{:S(2)}, u32[]{:S(2)}) collective-permute-start(bf16[16,3584]{1,0:T(8,128)(2,1)S(1)} %get-tuple-element.63), channel_id=1, source_target_pairs={{0,34},{1,39},{2,36},{3,33},{4,38},{5,35},{6,32},{7,37},{8,42},{9,... | collective-permute-start | bytes 344072 | tf_op jit(solution)/shard_map/home/ppermute | solution.py:57
  219.8 11.7 %collective-permute-start.12 = (bf16[16,3584]{1,0:T(8,128)(2,1)S(1)}, bf16[16,3584]{1,0:T(8,128)(2,1)S(1)}, u32[]{:S(2)}, u32[]{:S(2)}) collective-permute-start(bf16[16,3584]{1,0:T(8,128)(2,1)S(1)} %get-tuple-element.64), channel_id=1, source_target_pairs={{32,0},{33,1},{34,2},{35,3},{36,4},{37,5},{38,6},{39,7},{40,8},{41... | collective-permute-start | bytes 344072 | tf_op jit(solution)/shard_map/home/ppermute | solution.py:57
  221.8 11.0 %collective-permute-start.11 = (bf16[16,3584]{1,0:T(8,128)(2,1)S(1)}, bf16[16,3584]{1,0:T(8,128)(2,1)S(1)}, u32[]{:S(2)}, u32[]{:S(2)}) collective-permute-start(bf16[16,3584]{1,0:T(8,128)(2,1)S(1)} %get-tuple-element.65), channel_id=1, source_target_pairs={{0,32},{1,33},{2,34},{3,35},{4,36},{5,37},{6,38},{7,39},{8,40},{9,... | collective-permute-start | bytes 344072 | tf_op jit(solution)/shard_map/home/ppermute | solution.py:57
  232.8 12.9 %collective-permute-start.16 = (bf16[16,3584]{1,0:T(8,128)(2,1)S(1)}, bf16[16,3584]{1,0:T(8,128)(2,1)S(1)}, u32[]{:S(2)}, u32[]{:S(2)}) collective-permute-start(bf16[16,3584]{1,0:T(8,128)(2,1)S(1)} %get-tuple-element.66), channel_id=1, source_target_pairs={{32,6},{33,3},{34,0},{35,5},{36,2},{37,7},{38,4},{39,1},{40,14},{4... | collective-permute-start | bytes 344072 | tf_op jit(solution)/shard_map/home/ppermute | solution.py:57
  239.2 14.6 %collective-permute-start.15 = (bf16[16,3584]{1,0:T(8,128)(2,1)S(1)}, bf16[16,3584]{1,0:T(8,128)(2,1)S(1)}, u32[]{:S(2)}, u32[]{:S(2)}) collective-permute-start(bf16[16,3584]{1,0:T(8,128)(2,1)S(1)} %get-tuple-element.67), channel_id=1, source_target_pairs={{0,38},{1,35},{2,32},{3,37},{4,34},{5,39},{6,36},{7,33},{8,46},{9,... | collective-permute-start | bytes 344072 | tf_op jit(solution)/shard_map/home/ppermute | solution.py:57

commit v12 on v11

--- a/solution.py
+++ b/solution.py
@@ -124,7 +124,7 @@
         join_kernel,
         out_shape=jax.ShapeDtypeStruct((rows, CHUNK), gate_up.dtype),
         in_specs=[anywhere, anywhere],
-        out_specs=anywhere,
+        out_specs=pl.BlockSpec(memory_space=pltpu.VMEM),
         scratch_shapes=[pltpu.SemaphoreType.DMA((JOIN_PIECES + model // CHUNK,))],
     )(gate_up, down)
 

time: 256 us -> 174 us (0.68)
  Pallas kernels: 97.9 us -> 16.7 us
    pallas_call x1, Pallas kernels: 84.6 us -> 3.43 us  [join_weights(): pl.pallas_call(join_kernel, out_shape=jax.ShapeDtypeStruct((rows, CHUNK),...]
  transfers between devices with their start and end apart: 17 -> 17, of which waited for: 12 -> 12; matrix products, arithmetic and copies ran while one was open for 1% -> 1% of each run, Pallas kernels for 4% -> 5%
where the time goes in v12:
time: 174 us; the launch traced here: 173 us
  starting transfers between devices  104 us (60%)
  waiting for transfers between devices  48.4 us (28%)
  Pallas kernels  16.7 us (10%)
  other arithmetic  3.26 us (2%)
    ppermute x4, starting transfers between devices, along_z(): return lax.ppermute(block, 'expert', route)  51.6 us
    ppermute x8, starting transfers between devices, to_section(): return lax.ppermute(block, ('pipe', 'expert'), route)  39 us
    ppermute x4, waiting for transfers between devices, along_z(): return lax.ppermute(block, 'expert', route)  18.4 us
    ppermute x8, waiting for transfers between devices, to_section(): return lax.ppermute(block, ('pipe', 'expert'), route)  17 us
    pallas_call x2, Pallas kernels, run_kernel(): pl.pallas_call(kernel, out_shape=outs, in_specs=[whole] * len(operands),...  13.2 us
    ppermute x3, starting transfers between devices, along_x(): return lax.ppermute(block, 'expert', route)  9.25 us
    ppermute x3, waiting for transfers between devices, along_x(): return lax.ppermute(block, 'expert', route)  7.35 us
    ppermute x2, waiting for transfers between devices, other_core(): lax.ppermute(block, 'expert', expert_route(lambda x, z, c: (x, z, 1 - c)))  5.58 us
  transfers between devices with their start and end apart: 17, of which 12 were waited for; matrix products, arithmetic and copies ran while one was open for 1% of the time, Pallas kernels for 5%

profile of v12, /device:TPU:24, one launch (start us, length us, event | category | flops | bytes accessed | tf_op | source)
XLA Modules:
  0.0 173.4 jit_solution(9003235915453380164)
XLA Ops:
  0.7 3.4 %gather_weights.1.refs_0_ = bf16[5376,256]{1,0:T(8,128)(2,1)} custom-call(bf16[3584,256]{1,0:T(8,128)(2,1)} %bitcast.21, bf16[128,3584]{1,0:T(8,128)(2,1)} %bitcast.22), custom_call_target="tpu_custom_call" | custom-call | tf_op jit(solution)/shard_map/gather_weights/pallas_call | solution.py:123
  4.1 4.7 %collective-permute-start.1 = (bf16[5376,256]{1,0:T(8,128)(2,1)}, bf16[5376,256]{1,0:T(8,128)(2,1)}, u32[]{:S(2)}, u32[]{:S(2)}) collective-permute-start(bf16[5376,256]{1,0:T(8,128)(2,1)} %gather_weights.1.refs_0_), channel_id=1, source_target_pairs={{0,24},{1,9},{2,26},{3,11},{4,28},{5,13},{6,30},{7,15},{8,0},{9,17... | collective-permute-start | bytes 8257544 | tf_op jit(solution)/shard_map/gather_weights/ppermute | solution.py:41
  8.8 1.9 %collective-permute-start = (bf16[5376,256]{1,0:T(8,128)(2,1)}, bf16[5376,256]{1,0:T(8,128)(2,1)}, u32[]{:S(2)}, u32[]{:S(2)}) collective-permute-start(bf16[5376,256]{1,0:T(8,128)(2,1)} %gather_weights.1.refs_0_), channel_id=1, source_target_pairs={{0,8},{1,25},{2,10},{3,27},{4,12},{5,29},{6,14},{7,31},{8,16},{9,1... | collective-permute-start | bytes 8257544 | tf_op jit(solution)/shard_map/gather_weights/ppermute | solution.py:41
  10.8 0.1 copy.18
  10.9 0.1 copy.17
  11.0 0.1 reduce-precision_convert_fusion.1
  11.1 0.1 fusion.8
  11.2 9.4 %collective-permute-start.2 = (bf16[16,10880]{1,0:T(8,128)(2,1)S(1)}, bf16[16,10880]{1,0:T(8,128)(2,1)S(1)}, u32[]{:S(2)}, u32[]{:S(2)}) collective-permute-start(bf16[16,10880]{1,0:T(8,128)(2,1)S(1)} %pad_maximum_fusion.1), channel_id=1, source_target_pairs={{0,2},{1,7},{2,4},{3,1},{4,6},{5,3},{6,0},{7,5},{8,10},{9,15},{10,... | collective-permute-start | bytes 1044488 | tf_op jit(solution)/shard_map/gather_rows/ppermute | solution.py:36
  20.6 5.6 %collective-permute-start.3 = (bf16[16,10880]{1,0:T(8,128)(2,1)S(1)}, bf16[16,10880]{1,0:T(8,128)(2,1)S(1)}, u32[]{:S(2)}, u32[]{:S(2)}) collective-permute-start(bf16[16,10880]{1,0:T(8,128)(2,1)S(1)} %pad_maximum_fusion.1), channel_id=1, source_target_pairs={{0,6},{1,3},{2,0},{3,5},{4,2},{5,7},{6,4},{7,1},{8,14},{9,11},{10,... | collective-permute-start | bytes 1044488 | tf_op jit(solution)/shard_map/gather_rows/ppermute | solution.py:36
  26.1 3.6 %collective-permute-done.2 = bf16[16,10880]{1,0:T(8,128)(2,1)S(1)} collective-permute-done((bf16[16,10880]{1,0:T(8,128)(2,1)S(1)}, bf16[16,10880]{1,0:T(8,128)(2,1)S(1)}, u32[]{:S(2)}, u32[]{:S(2)}) %collective-permute-start.2) | collective-permute-done | bytes 348192 | tf_op jit(solution)/shard_map/gather_rows/ppermute | solution.py:36
  29.8 30.4 %collective-permute-start.4 = (bf16[16,10880]{1,0:T(8,128)(2,1)S(1)}, bf16[16,10880]{1,0:T(8,128)(2,1)S(1)}, u32[]{:S(2)}, u32[]{:S(2)}) collective-permute-start(bf16[16,10880]{1,0:T(8,128)(2,1)S(1)} %collective-permute-done.2), channel_id=1, source_target_pairs={{0,2},{1,7},{2,4},{3,1},{4,6},{5,3},{6,0},{7,5},{8,10},{9,15},{10,... | collective-permute-start | bytes 1044488 | tf_op jit(solution)/shard_map/gather_rows/ppermute | solution.py:36
  60.2 0.0 collective-permute-done.3
  60.2 14.8 %collective-permute-done.4 = bf16[16,10880]{1,0:T(8,128)(2,1)S(1)} collective-permute-done((bf16[16,10880]{1,0:T(8,128)(2,1)S(1)}, bf16[16,10880]{1,0:T(8,128)(2,1)S(1)}, u32[]{:S(2)}, u32[]{:S(2)}) %collective-permute-start.4) | collective-permute-done | bytes 348192 | tf_op jit(solution)/shard_map/gather_rows/ppermute | solution.py:36
  75.0 0.0 collective-permute-done.1.refs_2_
  75.0 0.0 collective-permute-done.refs_1_
  75.0 2.7 %collective-permute-start.8 = (bf16[5376,256]{1,0:T(8,128)(2,1)}, bf16[5376,256]{1,0:T(8,128)(2,1)}, u32[]{:S(2)}, u32[]{:S(2)}) collective-permute-start(bf16[5376,256]{1,0:T(8,128)(2,1)} %collective-permute-done.refs_1_), channel_id=1, source_target_pairs={{0,8},{1,25},{2,10},{3,27},{4,12},{5,29},{6,14},{7,31},{8,16},{9,1... | collective-permute-start | bytes 8257544 | tf_op jit(solution)/shard_map/gather_opposite/ppermute | solution.py:41
  77.7 1.2 pad_maximum_fusion.mine
  78.9 1.9 %collective-permute-start.5 = (bf16[64,10880]{1,0:T(8,128)(2,1)}, bf16[64,10880]{1,0:T(8,128)(2,1)}, u32[]{:S(2)}, u32[]{:S(2)}) collective-permute-start(bf16[64,10880]{1,0:T(8,128)(2,1)} %pad_maximum_fusion.mine), channel_id=1, source_target_pairs={{0,1},{1,0},{2,3},{3,2},{4,5},{5,4},{6,7},{7,6},{8,9},{9,8},{10,11... | collective-permute-start | bytes 4177928 | tf_op jit(solution)/shard_map/gather_opposite/ppermute | solution.py:45
  80.9 0.1 stack.35
  81.0 0.1 compare_and_fusion
  81.1 3.1 %collective-permute-done.5.other = bf16[64,10880]{1,0:T(8,128)(2,1)} collective-permute-done((bf16[64,10880]{1,0:T(8,128)(2,1)}, bf16[64,10880]{1,0:T(8,128)(2,1)}, u32[]{:S(2)}, u32[]{:S(2)}) %collective-permute-start.5) | collective-permute-done | bytes 1392672 | tf_op jit(solution)/shard_map/gather_opposite/ppermute | solution.py:45
  84.3 9.3 %experts.1 = (f32[128,3584]{1,0:T(8,128)S(1)}, f32[128,3584]{1,0:T(8,128)S(1)}, bf16[128,3584]{1,0:T(8,128)(2,1)S(1)}, bf16[128,3584]{1,0:T(8,128)(2,1)S(1)}, bf...) custom-call(bf16[64,10880]{1,0:T(8,128)(2,1)} %pad_maximum_fusion.mine, ...), custom_call_target="tpu_custom_call" | custom-call | flops 1000 | bytes 1000 | tf_op jit(solution)/shard_map/experts/pallas_call | solution.py:189
  93.6 1.9 %collective-permute-start.6 = (bf16[16,3584]{1,0:T(8,128)(2,1)S(1)}, bf16[16,3584]{1,0:T(8,128)(2,1)S(1)}, u32[]{:S(2)}, u32[]{:S(2)}) collective-permute-start(bf16[16,3584]{1,0:T(8,128)(2,1)S(1)} %bitcast.27), channel_id=1, source_target_pairs={{0,32},{1,33},{2,34},{3,35},{4,36},{5,37},{6,38},{7,39},{8,40},{9,... | collective-permute-start | bytes 344072 | tf_op jit(solution)/shard_map/residual/ppermute | solution.py:57
  95.5 6.6 %collective-permute-start.7 = (bf16[16,3584]{1,0:T(8,128)(2,1)S(1)}, bf16[16,3584]{1,0:T(8,128)(2,1)S(1)}, u32[]{:S(2)}, u32[]{:S(2)}) collective-permute-start(bf16[16,3584]{1,0:T(8,128)(2,1)S(1)} %bitcast.30), channel_id=1, source_target_pairs={{32,0},{33,1},{34,2},{35,3},{36,4},{37,5},{38,6},{39,7},{40,8},{41... | collective-permute-start | bytes 344072 | tf_op jit(solution)/shard_map/residual/ppermute | solution.py:57
  102.2 1.8 %collective-permute-done.6 = bf16[16,3584]{1,0:T(8,128)(2,1)S(1)} collective-permute-done((bf16[16,3584]{1,0:T(8,128)(2,1)S(1)}, bf16[16,3584]{1,0:T(8,128)(2,1)S(1)}, u32[]{:S(2)}, u32[]{:S(2)}) %collective-permute-start.6) | collective-permute-done | bytes 114720 | tf_op jit(solution)/shard_map/residual/ppermute | solution.py:57
  104.0 0.6 collective-permute-done.7
  104.6 7.3 %collective-permute-done.8.weight = bf16[5376,256]{1,0:T(8,128)(2,1)} collective-permute-done((bf16[5376,256]{1,0:T(8,128)(2,1)}, bf16[5376,256]{1,0:T(8,128)(2,1)}, u32[]{:S(2)}, u32[]{:S(2)}) %collective-permute-start.8) | collective-permute-done | bytes 2752544 | tf_op jit(solution)/shard_map/gather_opposite/ppermute | solution.py:41
  111.9 3.9 %last_expert.1 = (f32[64,7168]{1,0:T(8,128)S(1)}, bf16[64,7168]{1,0:T(8,128)(2,1)S(1)}) custom-call(f32[128,3584]{1,0:T(8,128)S(1)} %get-tuple-element.45.total, f32[128,3584]{1,0:T(8,128)S(1)} %get-tuple-element.46.back_total, bf16[128,3584]{1,0:T(8,128)(2,1)S(1)} %get-tuple-element.47.token, bf16[128,3584]{1,0:T(8,128)(2,1)S(1)} %get-tuple-element.48.saved, ...), custom_call_target="tpu_custom_call" | custom-call | flops 1000 | bytes 1000 | tf_op jit(solution)/shard_map/last_expert/pallas_call | solution.py:189
  115.8 1.9 %collective-permute-start.9 = (bf16[64,7168]{1,0:T(8,128)(2,1)S(1)}, bf16[64,7168]{1,0:T(8,128)(2,1)S(1)}, u32[]{:S(2)}, u32[]{:S(2)}) collective-permute-start(bf16[64,7168]{1,0:T(8,128)(2,1)S(1)} %get-tuple-element.53), channel_id=1, source_target_pairs={{0,1},{1,0},{2,3},{3,2},{4,5},{5,4},{6,7},{7,6},{8,9},{9,8},{10,11... | collective-permute-start | bytes 2752520 | tf_op jit(solution)/shard_map/cores/ppermute | solution.py:45
  117.8 2.4 %collective-permute-done.9 = bf16[64,7168]{1,0:T(8,128)(2,1)S(1)} collective-permute-done((bf16[64,7168]{1,0:T(8,128)(2,1)S(1)}, bf16[64,7168]{1,0:T(8,128)(2,1)S(1)}, u32[]{:S(2)}, u32[]{:S(2)}) %collective-permute-start.9) | collective-permute-done | bytes 917536 | tf_op jit(solution)/shard_map/cores/ppermute | solution.py:45
  120.2 0.2 fusion.9
  120.5 6.3 %collective-permute-start.10 = (bf16[16,7168]{1,0:T(8,128)(2,1)S(1)}, bf16[16,7168]{1,0:T(8,128)(2,1)S(1)}, u32[]{:S(2)}, u32[]{:S(2)}) collective-permute-start(bf16[16,7168]{1,0:T(8,128)(2,1)S(1)} %split.13), channel_id=1, source_target_pairs={{0,6},{1,3},{2,0},{3,5},{4,2},{5,7},{6,4},{7,1},{8,14},{9,11},{10,... | collective-permute-start | bytes 688136 | tf_op jit(solution)/shard_map/home/ppermute | solution.py:36
  126.8 4.5 %collective-permute-start.14 = (bf16[16,3584]{1,0:T(8,128)(2,1)S(1)}, bf16[16,3584]{1,0:T(8,128)(2,1)S(1)}, u32[]{:S(2)}, u32[]{:S(2)}) collective-permute-start(bf16[16,3584]{1,0:T(8,128)(2,1)S(1)} %get-tuple-element.62), channel_id=1, source_target_pairs={{32,2},{33,7},{34,4},{35,1},{36,6},{37,3},{38,0},{39,5},{40,10},{4... | collective-permute-start | bytes 344072 | tf_op jit(solution)/shard_map/home/ppermute | solution.py:57
  131.4 7.2 %collective-permute-start.13 = (bf16[16,3584]{1,0:T(8,128)(2,1)S(1)}, bf16[16,3584]{1,0:T(8,128)(2,1)S(1)}, u32[]{:S(2)}, u32[]{:S(2)}) collective-permute-start(bf16[16,3584]{1,0:T(8,128)(2,1)S(1)} %get-tuple-element.63), channel_id=1, source_target_pairs={{0,34},{1,39},{2,36},{3,33},{4,38},{5,35},{6,32},{7,37},{8,42},{9,... | collective-permute-start | bytes 344072 | tf_op jit(solution)/shard_map/home/ppermute | solution.py:57
  138.6 2.0 %collective-permute-start.12 = (bf16[16,3584]{1,0:T(8,128)(2,1)S(1)}, bf16[16,3584]{1,0:T(8,128)(2,1)S(1)}, u32[]{:S(2)}, u32[]{:S(2)}) collective-permute-start(bf16[16,3584]{1,0:T(8,128)(2,1)S(1)} %get-tuple-element.64), channel_id=1, source_target_pairs={{32,0},{33,1},{34,2},{35,3},{36,4},{37,5},{38,6},{39,7},{40,8},{41... | collective-permute-start | bytes 344072 | tf_op jit(solution)/shard_map/home/ppermute | solution.py:57
  140.6 3.9 %collective-permute-start.11 = (bf16[16,3584]{1,0:T(8,128)(2,1)S(1)}, bf16[16,3584]{1,0:T(8,128)(2,1)S(1)}, u32[]{:S(2)}, u32[]{:S(2)}) collective-permute-start(bf16[16,3584]{1,0:T(8,128)(2,1)S(1)} %get-tuple-element.65), channel_id=1, source_target_pairs={{0,32},{1,33},{2,34},{3,35},{4,36},{5,37},{6,38},{7,39},{8,40},{9,... | collective-permute-start | bytes 344072 | tf_op jit(solution)/shard_map/home/ppermute | solution.py:57
  144.5 1.0 collective-permute-done.14
  145.5 2.9 %collective-permute-done.13 = bf16[16,3584]{1,0:T(8,128)(2,1)S(1)} collective-permute-done((bf16[16,3584]{1,0:T(8,128)(2,1)S(1)}, bf16[16,3584]{1,0:T(8,128)(2,1)S(1)}, u32[]{:S(2)}, u32[]{:S(2)}) %collective-permute-start.13) | collective-permute-done | bytes 114720 | tf_op jit(solution)/shard_map/home/ppermute | solution.py:57
  148.4 1.9 %collective-permute-done.12 = bf16[16,3584]{1,0:T(8,128)(2,1)S(1)} collective-permute-done((bf16[16,3584]{1,0:T(8,128)(2,1)S(1)}, bf16[16,3584]{1,0:T(8,128)(2,1)S(1)}, u32[]{:S(2)}, u32[]{:S(2)}) %collective-permute-start.12) | collective-permute-done | bytes 114720 | tf_op jit(solution)/shard_map/home/ppermute | solution.py:57
  150.3 1.2 collective-permute-done.11
  151.5 0.0 collective-permute-done.10
  151.5 0.1 fusion
  151.6 6.4 %collective-permute-start.16 = (bf16[16,3584]{1,0:T(8,128)(2,1)S(1)}, bf16[16,3584]{1,0:T(8,128)(2,1)S(1)}, u32[]{:S(2)}, u32[]{:S(2)}) collective-permute-start(bf16[16,3584]{1,0:T(8,128)(2,1)S(1)} %get-tuple-element.66), channel_id=1, source_target_pairs={{32,6},{33,3},{34,0},{35,5},{36,2},{37,7},{38,4},{39,1},{40,14},{4... | collective-permute-start | bytes 344072 | tf_op jit(solution)/shard_map/home/ppermute | solution.py:57
  158.0 6.5 %collective-permute-start.15 = (bf16[16,3584]{1,0:T(8,128)(2,1)S(1)}, bf16[16,3584]{1,0:T(8,128)(2,1)S(1)}, u32[]{:S(2)}, u32[]{:S(2)}) collective-permute-start(bf16[16,3584]{1,0:T(8,128)(2,1)S(1)} %get-tuple-element.67), channel_id=1, source_target_pairs={{0,38},{1,35},{2,32},{3,37},{4,34},{5,39},{6,36},{7,33},{8,46},{9,... | collective-permute-start | bytes 344072 | tf_op jit(solution)/shard_map/home/ppermute | solution.py:57
  164.5 0.0 collective-permute-done.16
  164.5 0.7 fusion.2
  165.2 7.5 %collective-permute-done.15 = bf16[16,3584]{1,0:T(8,128)(2,1)S(1)} collective-permute-done((bf16[16,3584]{1,0:T(8,128)(2,1)S(1)}, bf16[16,3584]{1,0:T(8,128)(2,1)S(1)}, u32[]{:S(2)}, u32[]{:S(2)}) %collective-permute-start.15) | collective-permute-done | bytes 114720 | tf_op jit(solution)/shard_map/home/ppermute | solution.py:57
  172.7 0.7 fusion.1
  (25 shorter events, 0.2 us)
Async XLA Ops:
  0.6 10.1 %copy-start.4 = (f32[1,16,2]{1,2,0:T(2,128)S(1)}, f32[1,16,2]{1,2,0:T(2,128)}, u32[]{:S(2)}) copy-start(f32[1,16,2]{1,2,0:T(2,128)} %param.17) | copy-start | bytes 388
  0.6 10.1 %copy-start.5 = (s32[1,16,2]{1,2,0:T(2,128)S(1)}, s32[1,16,2]{1,2,0:T(2,128)}, u32[]{:S(2)}) copy-start(s32[1,16,2]{1,2,0:T(2,128)} %param.15) | copy-start | bytes 388
  0.7 10.2 %copy-start.6 = (f32[1,16,2]{1,2,0:T(2,128)S(1)}, f32[1,16,2]{1,2,0:T(2,128)}, u32[]{:S(2)}) copy-start(f32[1,16,2]{1,2,0:T(2,128)} %param.16) | copy-start | bytes 388
  0.7 10.2 %copy-start.7 = (s32[1,16,2]{1,2,0:T(2,128)S(1)}, s32[1,16,2]{1,2,0:T(2,128)}, u32[]{:S(2)}) copy-start(s32[1,16,2]{1,2,0:T(2,128)} %param.14) | copy-start | bytes 388
  0.7 10.5 %copy-start.1 = (bf16[1,16,3584]{2,1,0:T(8,128)(2,1)S(1)}, bf16[1,16,3584]{2,1,0:T(8,128)(2,1)}, u32[]{:S(2)}) copy-start(bf16[1,16,3584]{2,1,0:T(8,128)(2,1)} %param.10) | copy-start | bytes 344068
  0.7 10.5 %copy-start.2 = (bf16[1,16,3584]{2,1,0:T(8,128)(2,1)S(1)}, bf16[1,16,3584]{2,1,0:T(8,128)(2,1)}, u32[]{:S(2)}) copy-start(bf16[1,16,3584]{2,1,0:T(8,128)(2,1)} %param.9) | copy-start | bytes 344068
  0.7 10.5 %copy-start.3 = (bf16[1,16,3584]{2,1,0:T(8,128)(2,1)S(1)}, bf16[1,16,3584]{2,1,0:T(8,128)(2,1)}, u32[]{:S(2)}) copy-start(bf16[1,16,3584]{2,1,0:T(8,128)(2,1)} %param.11) | copy-start | bytes 344068
  4.1 70.9 %collective-permute-start.1 = (bf16[5376,256]{1,0:T(8,128)(2,1)}, bf16[5376,256]{1,0:T(8,128)(2,1)}, u32[]{:S(2)}, u32[]{:S(2)}) collective-permute-start(bf16[5376,256]{1,0:T(8,128)(2,1)} %gather_weights.1.refs_0_), channel_id=1, source_target_pairs={{0,24},{1,9},{2,26},{3,11},{4,28},{5,13},{6,30},{7,15},{8,0},{9,17... | collective-permute-start | bytes 8257544 | tf_op jit(solution)/shard_map/gather_weights/ppermute | solution.py:41
  8.8 66.2 %collective-permute-start = (bf16[5376,256]{1,0:T(8,128)(2,1)}, bf16[5376,256]{1,0:T(8,128)(2,1)}, u32[]{:S(2)}, u32[]{:S(2)}) collective-permute-start(bf16[5376,256]{1,0:T(8,128)(2,1)} %gather_weights.1.refs_0_), channel_id=1, source_target_pairs={{0,8},{1,25},{2,10},{3,27},{4,12},{5,29},{6,14},{7,31},{8,16},{9,1... | collective-permute-start | bytes 8257544 | tf_op jit(solution)/shard_map/gather_weights/ppermute | solution.py:41
  11.2 73.1 %copy-start = (bf16[5376,256]{1,0:T(8,128)(2,1)S(1)}, bf16[5376,256]{1,0:T(8,128)(2,1)}, u32[]{:S(2)}) copy-start(bf16[5376,256]{1,0:T(8,128)(2,1)} %gather_weights.1.refs_0_) | copy-start | bytes 8257540
  11.2 18.6 %collective-permute-start.2 = (bf16[16,10880]{1,0:T(8,128)(2,1)S(1)}, bf16[16,10880]{1,0:T(8,128)(2,1)S(1)}, u32[]{:S(2)}, u32[]{:S(2)}) collective-permute-start(bf16[16,10880]{1,0:T(8,128)(2,1)S(1)} %pad_maximum_fusion.1), channel_id=1, source_target_pairs={{0,2},{1,7},{2,4},{3,1},{4,6},{5,3},{6,0},{7,5},{8,10},{9,15},{10,... | collective-permute-start | bytes 1044488 | tf_op jit(solution)/shard_map/gather_rows/ppermute | solution.py:36
  20.6 39.6 %collective-permute-start.3 = (bf16[16,10880]{1,0:T(8,128)(2,1)S(1)}, bf16[16,10880]{1,0:T(8,128)(2,1)S(1)}, u32[]{:S(2)}, u32[]{:S(2)}) collective-permute-start(bf16[16,10880]{1,0:T(8,128)(2,1)S(1)} %pad_maximum_fusion.1), channel_id=1, source_target_pairs={{0,6},{1,3},{2,0},{3,5},{4,2},{5,7},{6,4},{7,1},{8,14},{9,11},{10,... | collective-permute-start | bytes 1044488 | tf_op jit(solution)/shard_map/gather_rows/ppermute | solution.py:36
  29.8 45.3 %collective-permute-start.4 = (bf16[16,10880]{1,0:T(8,128)(2,1)S(1)}, bf16[16,10880]{1,0:T(8,128)(2,1)S(1)}, u32[]{:S(2)}, u32[]{:S(2)}) collective-permute-start(bf16[16,10880]{1,0:T(8,128)(2,1)S(1)} %collective-permute-done.2), channel_id=1, source_target_pairs={{0,2},{1,7},{2,4},{3,1},{4,6},{5,3},{6,0},{7,5},{8,10},{9,15},{10,... | collective-permute-start | bytes 1044488 | tf_op jit(solution)/shard_map/gather_rows/ppermute | solution.py:36
  75.0 36.9 %collective-permute-start.8 = (bf16[5376,256]{1,0:T(8,128)(2,1)}, bf16[5376,256]{1,0:T(8,128)(2,1)}, u32[]{:S(2)}, u32[]{:S(2)}) collective-permute-start(bf16[5376,256]{1,0:T(8,128)(2,1)} %collective-permute-done.refs_1_), channel_id=1, source_target_pairs={{0,8},{1,25},{2,10},{3,27},{4,12},{5,29},{6,14},{7,31},{8,16},{9,1... | collective-permute-start | bytes 8257544 | tf_op jit(solution)/shard_map/gather_opposite/ppermute | solution.py:41
  78.9 5.4 %collective-permute-start.5 = (bf16[64,10880]{1,0:T(8,128)(2,1)}, bf16[64,10880]{1,0:T(8,128)(2,1)}, u32[]{:S(2)}, u32[]{:S(2)}) collective-permute-start(bf16[64,10880]{1,0:T(8,128)(2,1)} %pad_maximum_fusion.mine), channel_id=1, source_target_pairs={{0,1},{1,0},{2,3},{3,2},{4,5},{5,4},{6,7},{7,6},{8,9},{9,8},{10,11... | collective-permute-start | bytes 4177928 | tf_op jit(solution)/shard_map/gather_opposite/ppermute | solution.py:45
  93.6 10.4 %collective-permute-start.6 = (bf16[16,3584]{1,0:T(8,128)(2,1)S(1)}, bf16[16,3584]{1,0:T(8,128)(2,1)S(1)}, u32[]{:S(2)}, u32[]{:S(2)}) collective-permute-start(bf16[16,3584]{1,0:T(8,128)(2,1)S(1)} %bitcast.27), channel_id=1, source_target_pairs={{0,32},{1,33},{2,34},{3,35},{4,36},{5,37},{6,38},{7,39},{8,40},{9,... | collective-permute-start | bytes 344072 | tf_op jit(solution)/shard_map/residual/ppermute | solution.py:57
  95.5 9.0 %collective-permute-start.7 = (bf16[16,3584]{1,0:T(8,128)(2,1)S(1)}, bf16[16,3584]{1,0:T(8,128)(2,1)S(1)}, u32[]{:S(2)}, u32[]{:S(2)}) collective-permute-start(bf16[16,3584]{1,0:T(8,128)(2,1)S(1)} %bitcast.30), channel_id=1, source_target_pairs={{32,0},{33,1},{34,2},{35,3},{36,4},{37,5},{38,6},{39,7},{40,8},{41... | collective-permute-start | bytes 344072 | tf_op jit(solution)/shard_map/residual/ppermute | solution.py:57
  115.8 4.4 %collective-permute-start.9 = (bf16[64,7168]{1,0:T(8,128)(2,1)S(1)}, bf16[64,7168]{1,0:T(8,128)(2,1)S(1)}, u32[]{:S(2)}, u32[]{:S(2)}) collective-permute-start(bf16[64,7168]{1,0:T(8,128)(2,1)S(1)} %get-tuple-element.53), channel_id=1, source_target_pairs={{0,1},{1,0},{2,3},{3,2},{4,5},{5,4},{6,7},{7,6},{8,9},{9,8},{10,11... | collective-permute-start | bytes 2752520 | tf_op jit(solution)/shard_map/cores/ppermute | solution.py:45
  120.5 31.1 %collective-permute-start.10 = (bf16[16,7168]{1,0:T(8,128)(2,1)S(1)}, bf16[16,7168]{1,0:T(8,128)(2,1)S(1)}, u32[]{:S(2)}, u32[]{:S(2)}) collective-permute-start(bf16[16,7168]{1,0:T(8,128)(2,1)S(1)} %split.13), channel_id=1, source_target_pairs={{0,6},{1,3},{2,0},{3,5},{4,2},{5,7},{6,4},{7,1},{8,14},{9,11},{10,... | collective-permute-start | bytes 688136 | tf_op jit(solution)/shard_map/home/ppermute | solution.py:36
  126.8 18.7 %collective-permute-start.14 = (bf16[16,3584]{1,0:T(8,128)(2,1)S(1)}, bf16[16,3584]{1,0:T(8,128)(2,1)S(1)}, u32[]{:S(2)}, u32[]{:S(2)}) collective-permute-start(bf16[16,3584]{1,0:T(8,128)(2,1)S(1)} %get-tuple-element.62), channel_id=1, source_target_pairs={{32,2},{33,7},{34,4},{35,1},{36,6},{37,3},{38,0},{39,5},{40,10},{4... | collective-permute-start | bytes 344072 | tf_op jit(solution)/shard_map/home/ppermute | solution.py:57
  131.4 17.1 %collective-permute-start.13 = (bf16[16,3584]{1,0:T(8,128)(2,1)S(1)}, bf16[16,3584]{1,0:T(8,128)(2,1)S(1)}, u32[]{:S(2)}, u32[]{:S(2)}) collective-permute-start(bf16[16,3584]{1,0:T(8,128)(2,1)S(1)} %get-tuple-element.63), channel_id=1, source_target_pairs={{0,34},{1,39},{2,36},{3,33},{4,38},{5,35},{6,32},{7,37},{8,42},{9,... | collective-permute-start | bytes 344072 | tf_op jit(solution)/shard_map/home/ppermute | solution.py:57
  138.6 11.7 %collective-permute-start.12 = (bf16[16,3584]{1,0:T(8,128)(2,1)S(1)}, bf16[16,3584]{1,0:T(8,128)(2,1)S(1)}, u32[]{:S(2)}, u32[]{:S(2)}) collective-permute-start(bf16[16,3584]{1,0:T(8,128)(2,1)S(1)} %get-tuple-element.64), channel_id=1, source_target_pairs={{32,0},{33,1},{34,2},{35,3},{36,4},{37,5},{38,6},{39,7},{40,8},{41... | collective-permute-start | bytes 344072 | tf_op jit(solution)/shard_map/home/ppermute | solution.py:57
  140.6 11.0 %collective-permute-start.11 = (bf16[16,3584]{1,0:T(8,128)(2,1)S(1)}, bf16[16,3584]{1,0:T(8,128)(2,1)S(1)}, u32[]{:S(2)}, u32[]{:S(2)}) collective-permute-start(bf16[16,3584]{1,0:T(8,128)(2,1)S(1)} %get-tuple-element.65), channel_id=1, source_target_pairs={{0,32},{1,33},{2,34},{3,35},{4,36},{5,37},{6,38},{7,39},{8,40},{9,... | collective-permute-start | bytes 344072 | tf_op jit(solution)/shard_map/home/ppermute | solution.py:57
  151.6 12.9 %collective-permute-start.16 = (bf16[16,3584]{1,0:T(8,128)(2,1)S(1)}, bf16[16,3584]{1,0:T(8,128)(2,1)S(1)}, u32[]{:S(2)}, u32[]{:S(2)}) collective-permute-start(bf16[16,3584]{1,0:T(8,128)(2,1)S(1)} %get-tuple-element.66), channel_id=1, source_target_pairs={{32,6},{33,3},{34,0},{35,5},{36,2},{37,7},{38,4},{39,1},{40,14},{4... | collective-permute-start | bytes 344072 | tf_op jit(solution)/shard_map/home/ppermute | solution.py:57
  158.0 14.7 %collective-permute-start.15 = (bf16[16,3584]{1,0:T(8,128)(2,1)S(1)}, bf16[16,3584]{1,0:T(8,128)(2,1)S(1)}, u32[]{:S(2)}, u32[]{:S(2)}) collective-permute-start(bf16[16,3584]{1,0:T(8,128)(2,1)S(1)} %get-tuple-element.67), channel_id=1, source_target_pairs={{0,38},{1,35},{2,32},{3,37},{4,34},{5,39},{6,36},{7,33},{8,46},{9,... | collective-permute-start | bytes 344072 | tf_op jit(solution)/shard_map/home/ppermute | solution.py:57

commit v13 on v12

--- a/solution.py
+++ b/solution.py
@@ -253,11 +253,11 @@
         own, near, far, passed = jnp.split(total, Z, axis=0)
         passed = along_z(passed.astype(jnp.bfloat16), -1)
         own, far = own.astype(jnp.bfloat16), far.astype(jnp.bfloat16)
-        parts = [to_section(own[:, :model], 1, 0), to_section(own[:, model:], -1, 0)]
-        parts += [to_section(far[:, :model], 1, 1), to_section(far[:, model:], -1, 1)]
+        parts = [to_section(far[:, :model], 1, 1), to_section(far[:, model:], -1, 1)]
         passed, *parts = together(passed, *parts)
         near = (near + passed.astype(jnp.float32)).astype(jnp.bfloat16)
         parts += [to_section(near[:, :model], 1, -1), to_section(near[:, model:], -1, -1)]
+        parts += [to_section(own[:, :model], 1, 0), to_section(own[:, model:], -1, 0)]
         sides = [[residuals[k]] + parts[k::2] for k in range(2)]
         forward_next, backward_next = [
             sum(part.astype(jnp.float32) for part in side).astype(jnp.bfloat16) for side in sides

time: 174 us -> 177 us (1.017)
  waiting for transfers between devices: 48.4 us -> 52.5 us
  starting transfers between devices: 104 us -> 102 us
    ppermute x8, waiting for transfers between devices: 17 us -> 21.1 us  [to_section(): return lax.ppermute(block, ('pipe', 'expert'), route)]
  transfers between devices with their start and end apart: 17 -> 17, of which waited for: 12 -> 11; matrix products, arithmetic and copies ran while one was open for 1% -> 1% of each run, Pallas kernels for 5% -> 5%
where the time goes in v13:
time: 177 us; the launch traced here: 176 us
  starting transfers between devices  102 us (58%)
  waiting for transfers between devices  52.5 us (30%)
  Pallas kernels  16.7 us (9%)
  other arithmetic  3.26 us (2%)
    ppermute x4, starting transfers between devices, along_z(): return lax.ppermute(block, 'expert', route)  51.6 us
    ppermute x8, starting transfers between devices, to_section(): return lax.ppermute(block, ('pipe', 'expert'), route)  37.6 us
    ppermute x8, waiting for transfers between devices, to_section(): return lax.ppermute(block, ('pipe', 'expert'), route)  21.1 us
    ppermute x4, waiting for transfers between devices, along_z(): return lax.ppermute(block, 'expert', route)  18.4 us
    pallas_call x2, Pallas kernels, run_kernel(): pl.pallas_call(kernel, out_shape=outs, in_specs=[whole] * len(operands),...  13.2 us
    ppermute x3, starting transfers between devices, along_x(): return lax.ppermute(block, 'expert', route)  9.25 us
    ppermute x3, waiting for transfers between devices, along_x(): return lax.ppermute(block, 'expert', route)  7.35 us
    ppermute x2, waiting for transfers between devices, other_core(): lax.ppermute(block, 'expert', expert_route(lambda x, z, c: (x, z, 1 - c)))  5.58 us
  transfers between devices with their start and end apart: 17, of which 11 were waited for; matrix products, arithmetic and copies ran while one was open for 1% of the time, Pallas kernels for 5%

profile of v13, /device:TPU:24, one launch (start us, length us, event | category | flops | bytes accessed | tf_op | source)
XLA Modules:
  0.0 176.1 jit_solution(616670720776112007)
XLA Ops:
  0.7 3.4 %gather_weights.1.refs_0_ = bf16[5376,256]{1,0:T(8,128)(2,1)} custom-call(bf16[3584,256]{1,0:T(8,128)(2,1)} %bitcast.21, bf16[128,3584]{1,0:T(8,128)(2,1)} %bitcast.22), custom_call_target="tpu_custom_call" | custom-call | tf_op jit(solution)/shard_map/gather_weights/pallas_call | solution.py:123
  4.1 4.7 %collective-permute-start.1 = (bf16[5376,256]{1,0:T(8,128)(2,1)}, bf16[5376,256]{1,0:T(8,128)(2,1)}, u32[]{:S(2)}, u32[]{:S(2)}) collective-permute-start(bf16[5376,256]{1,0:T(8,128)(2,1)} %gather_weights.1.refs_0_), channel_id=1, source_target_pairs={{0,24},{1,9},{2,26},{3,11},{4,28},{5,13},{6,30},{7,15},{8,0},{9,17... | collective-permute-start | bytes 8257544 | tf_op jit(solution)/shard_map/gather_weights/ppermute | solution.py:41
  8.8 1.9 %collective-permute-start = (bf16[5376,256]{1,0:T(8,128)(2,1)}, bf16[5376,256]{1,0:T(8,128)(2,1)}, u32[]{:S(2)}, u32[]{:S(2)}) collective-permute-start(bf16[5376,256]{1,0:T(8,128)(2,1)} %gather_weights.1.refs_0_), channel_id=1, source_target_pairs={{0,8},{1,25},{2,10},{3,27},{4,12},{5,29},{6,14},{7,31},{8,16},{9,1... | collective-permute-start | bytes 8257544 | tf_op jit(solution)/shard_map/gather_weights/ppermute | solution.py:41
  10.8 0.1 copy.18
  10.9 0.1 copy.17
  11.0 0.1 reduce-precision_convert_fusion.1
  11.1 0.1 fusion.8
  11.2 9.4 %collective-permute-start.2 = (bf16[16,10880]{1,0:T(8,128)(2,1)S(1)}, bf16[16,10880]{1,0:T(8,128)(2,1)S(1)}, u32[]{:S(2)}, u32[]{:S(2)}) collective-permute-start(bf16[16,10880]{1,0:T(8,128)(2,1)S(1)} %pad_maximum_fusion.1), channel_id=1, source_target_pairs={{0,2},{1,7},{2,4},{3,1},{4,6},{5,3},{6,0},{7,5},{8,10},{9,15},{10,... | collective-permute-start | bytes 1044488 | tf_op jit(solution)/shard_map/gather_rows/ppermute | solution.py:36
  20.6 5.6 %collective-permute-start.3 = (bf16[16,10880]{1,0:T(8,128)(2,1)S(1)}, bf16[16,10880]{1,0:T(8,128)(2,1)S(1)}, u32[]{:S(2)}, u32[]{:S(2)}) collective-permute-start(bf16[16,10880]{1,0:T(8,128)(2,1)S(1)} %pad_maximum_fusion.1), channel_id=1, source_target_pairs={{0,6},{1,3},{2,0},{3,5},{4,2},{5,7},{6,4},{7,1},{8,14},{9,11},{10,... | collective-permute-start | bytes 1044488 | tf_op jit(solution)/shard_map/gather_rows/ppermute | solution.py:36
  26.1 3.6 %collective-permute-done.2 = bf16[16,10880]{1,0:T(8,128)(2,1)S(1)} collective-permute-done((bf16[16,10880]{1,0:T(8,128)(2,1)S(1)}, bf16[16,10880]{1,0:T(8,128)(2,1)S(1)}, u32[]{:S(2)}, u32[]{:S(2)}) %collective-permute-start.2) | collective-permute-done | bytes 348192 | tf_op jit(solution)/shard_map/gather_rows/ppermute | solution.py:36
  29.8 30.4 %collective-permute-start.4 = (bf16[16,10880]{1,0:T(8,128)(2,1)S(1)}, bf16[16,10880]{1,0:T(8,128)(2,1)S(1)}, u32[]{:S(2)}, u32[]{:S(2)}) collective-permute-start(bf16[16,10880]{1,0:T(8,128)(2,1)S(1)} %collective-permute-done.2), channel_id=1, source_target_pairs={{0,2},{1,7},{2,4},{3,1},{4,6},{5,3},{6,0},{7,5},{8,10},{9,15},{10,... | collective-permute-start | bytes 1044488 | tf_op jit(solution)/shard_map/gather_rows/ppermute | solution.py:36
  60.2 0.0 collective-permute-done.3
  60.2 14.8 %collective-permute-done.4 = bf16[16,10880]{1,0:T(8,128)(2,1)S(1)} collective-permute-done((bf16[16,10880]{1,0:T(8,128)(2,1)S(1)}, bf16[16,10880]{1,0:T(8,128)(2,1)S(1)}, u32[]{:S(2)}, u32[]{:S(2)}) %collective-permute-start.4) | collective-permute-done | bytes 348192 | tf_op jit(solution)/shard_map/gather_rows/ppermute | solution.py:36
  75.0 0.0 collective-permute-done.1.refs_2_
  75.0 0.0 collective-permute-done.refs_1_
  75.0 2.7 %collective-permute-start.8 = (bf16[5376,256]{1,0:T(8,128)(2,1)}, bf16[5376,256]{1,0:T(8,128)(2,1)}, u32[]{:S(2)}, u32[]{:S(2)}) collective-permute-start(bf16[5376,256]{1,0:T(8,128)(2,1)} %collective-permute-done.refs_1_), channel_id=1, source_target_pairs={{0,8},{1,25},{2,10},{3,27},{4,12},{5,29},{6,14},{7,31},{8,16},{9,1... | collective-permute-start | bytes 8257544 | tf_op jit(solution)/shard_map/gather_opposite/ppermute | solution.py:41
  77.7 1.2 pad_maximum_fusion.mine
  78.9 1.9 %collective-permute-start.5 = (bf16[64,10880]{1,0:T(8,128)(2,1)}, bf16[64,10880]{1,0:T(8,128)(2,1)}, u32[]{:S(2)}, u32[]{:S(2)}) collective-permute-start(bf16[64,10880]{1,0:T(8,128)(2,1)} %pad_maximum_fusion.mine), channel_id=1, source_target_pairs={{0,1},{1,0},{2,3},{3,2},{4,5},{5,4},{6,7},{7,6},{8,9},{9,8},{10,11... | collective-permute-start | bytes 4177928 | tf_op jit(solution)/shard_map/gather_opposite/ppermute | solution.py:45
  80.9 0.1 stack.35
  81.0 0.1 compare_and_fusion
  81.1 3.1 %collective-permute-done.5.other = bf16[64,10880]{1,0:T(8,128)(2,1)} collective-permute-done((bf16[64,10880]{1,0:T(8,128)(2,1)}, bf16[64,10880]{1,0:T(8,128)(2,1)}, u32[]{:S(2)}, u32[]{:S(2)}) %collective-permute-start.5) | collective-permute-done | bytes 1392672 | tf_op jit(solution)/shard_map/gather_opposite/ppermute | solution.py:45
  84.3 9.3 %experts.1 = (f32[128,3584]{1,0:T(8,128)S(1)}, f32[128,3584]{1,0:T(8,128)S(1)}, bf16[128,3584]{1,0:T(8,128)(2,1)S(1)}, bf16[128,3584]{1,0:T(8,128)(2,1)S(1)}, bf...) custom-call(bf16[64,10880]{1,0:T(8,128)(2,1)} %pad_maximum_fusion.mine, ...), custom_call_target="tpu_custom_call" | custom-call | flops 1000 | bytes 1000 | tf_op jit(solution)/shard_map/experts/pallas_call | solution.py:189
  93.6 1.9 %collective-permute-start.6 = (bf16[16,3584]{1,0:T(8,128)(2,1)S(1)}, bf16[16,3584]{1,0:T(8,128)(2,1)S(1)}, u32[]{:S(2)}, u32[]{:S(2)}) collective-permute-start(bf16[16,3584]{1,0:T(8,128)(2,1)S(1)} %bitcast.27), channel_id=1, source_target_pairs={{0,32},{1,33},{2,34},{3,35},{4,36},{5,37},{6,38},{7,39},{8,40},{9,... | collective-permute-start | bytes 344072 | tf_op jit(solution)/shard_map/residual/ppermute | solution.py:57
  95.5 6.6 %collective-permute-start.7 = (bf16[16,3584]{1,0:T(8,128)(2,1)S(1)}, bf16[16,3584]{1,0:T(8,128)(2,1)S(1)}, u32[]{:S(2)}, u32[]{:S(2)}) collective-permute-start(bf16[16,3584]{1,0:T(8,128)(2,1)S(1)} %bitcast.30), channel_id=1, source_target_pairs={{32,0},{33,1},{34,2},{35,3},{36,4},{37,5},{38,6},{39,7},{40,8},{41... | collective-permute-start | bytes 344072 | tf_op jit(solution)/shard_map/residual/ppermute | solution.py:57
  102.2 1.8 %collective-permute-done.6 = bf16[16,3584]{1,0:T(8,128)(2,1)S(1)} collective-permute-done((bf16[16,3584]{1,0:T(8,128)(2,1)S(1)}, bf16[16,3584]{1,0:T(8,128)(2,1)S(1)}, u32[]{:S(2)}, u32[]{:S(2)}) %collective-permute-start.6) | collective-permute-done | bytes 114720 | tf_op jit(solution)/shard_map/residual/ppermute | solution.py:57
  104.0 0.6 collective-permute-done.7
  104.6 7.3 %collective-permute-done.8.weight = bf16[5376,256]{1,0:T(8,128)(2,1)} collective-permute-done((bf16[5376,256]{1,0:T(8,128)(2,1)}, bf16[5376,256]{1,0:T(8,128)(2,1)}, u32[]{:S(2)}, u32[]{:S(2)}) %collective-permute-start.8) | collective-permute-done | bytes 2752544 | tf_op jit(solution)/shard_map/gather_opposite/ppermute | solution.py:41
  111.9 3.9 %last_expert.1 = (f32[64,7168]{1,0:T(8,128)S(1)}, bf16[64,7168]{1,0:T(8,128)(2,1)S(1)}) custom-call(f32[128,3584]{1,0:T(8,128)S(1)} %get-tuple-element.43.total, f32[128,3584]{1,0:T(8,128)S(1)} %get-tuple-element.44.back_total, bf16[128,3584]{1,0:T(8,128)(2,1)S(1)} %get-tuple-element.45.token, bf16[128,3584]{1,0:T(8,128)(2,1)S(1)} %get-tuple-element.46.saved, ...), custom_call_target="tpu_custom_call" | custom-call | flops 1000 | bytes 1000 | tf_op jit(solution)/shard_map/last_expert/pallas_call | solution.py:189
  115.8 1.9 %collective-permute-start.9 = (bf16[64,7168]{1,0:T(8,128)(2,1)S(1)}, bf16[64,7168]{1,0:T(8,128)(2,1)S(1)}, u32[]{:S(2)}, u32[]{:S(2)}) collective-permute-start(bf16[64,7168]{1,0:T(8,128)(2,1)S(1)} %get-tuple-element.51), channel_id=1, source_target_pairs={{0,1},{1,0},{2,3},{3,2},{4,5},{5,4},{6,7},{7,6},{8,9},{9,8},{10,11... | collective-permute-start | bytes 2752520 | tf_op jit(solution)/shard_map/cores/ppermute | solution.py:45
  117.8 2.4 %collective-permute-done.9 = bf16[64,7168]{1,0:T(8,128)(2,1)S(1)} collective-permute-done((bf16[64,7168]{1,0:T(8,128)(2,1)S(1)}, bf16[64,7168]{1,0:T(8,128)(2,1)S(1)}, u32[]{:S(2)}, u32[]{:S(2)}) %collective-permute-start.9) | collective-permute-done | bytes 917536 | tf_op jit(solution)/shard_map/cores/ppermute | solution.py:45
  120.2 0.2 fusion.9
  120.5 6.3 %collective-permute-start.10 = (bf16[16,7168]{1,0:T(8,128)(2,1)S(1)}, bf16[16,7168]{1,0:T(8,128)(2,1)S(1)}, u32[]{:S(2)}, u32[]{:S(2)}) collective-permute-start(bf16[16,7168]{1,0:T(8,128)(2,1)S(1)} %split.13), channel_id=1, source_target_pairs={{0,6},{1,3},{2,0},{3,5},{4,2},{5,7},{6,4},{7,1},{8,14},{9,11},{10,... | collective-permute-start | bytes 688136 | tf_op jit(solution)/shard_map/home/ppermute | solution.py:36
  126.8 4.5 %collective-permute-start.12 = (bf16[16,3584]{1,0:T(8,128)(2,1)S(1)}, bf16[16,3584]{1,0:T(8,128)(2,1)S(1)}, u32[]{:S(2)}, u32[]{:S(2)}) collective-permute-start(bf16[16,3584]{1,0:T(8,128)(2,1)S(1)} %get-tuple-element.60), channel_id=1, source_target_pairs={{32,2},{33,7},{34,4},{35,1},{36,6},{37,3},{38,0},{39,5},{40,10},{4... | collective-permute-start | bytes 344072 | tf_op jit(solution)/shard_map/home/ppermute | solution.py:57
  131.4 7.2 %collective-permute-start.11 = (bf16[16,3584]{1,0:T(8,128)(2,1)S(1)}, bf16[16,3584]{1,0:T(8,128)(2,1)S(1)}, u32[]{:S(2)}, u32[]{:S(2)}) collective-permute-start(bf16[16,3584]{1,0:T(8,128)(2,1)S(1)} %get-tuple-element.61), channel_id=1, source_target_pairs={{0,34},{1,39},{2,36},{3,33},{4,38},{5,35},{6,32},{7,37},{8,42},{9,... | collective-permute-start | bytes 344072 | tf_op jit(solution)/shard_map/home/ppermute | solution.py:57
  138.6 2.0 %collective-permute-start.16 = (bf16[16,3584]{1,0:T(8,128)(2,1)S(1)}, bf16[16,3584]{1,0:T(8,128)(2,1)S(1)}, u32[]{:S(2)}, u32[]{:S(2)}) collective-permute-start(bf16[16,3584]{1,0:T(8,128)(2,1)S(1)} %get-tuple-element.58), channel_id=1, source_target_pairs={{32,0},{33,1},{34,2},{35,3},{36,4},{37,5},{38,6},{39,7},{40,8},{41... | collective-permute-start | bytes 344072 | tf_op jit(solution)/shard_map/home/ppermute | solution.py:57
  140.6 4.9 %collective-permute-done.12 = bf16[16,3584]{1,0:T(8,128)(2,1)S(1)} collective-permute-done((bf16[16,3584]{1,0:T(8,128)(2,1)S(1)}, bf16[16,3584]{1,0:T(8,128)(2,1)S(1)}, u32[]{:S(2)}, u32[]{:S(2)}) %collective-permute-start.12) | collective-permute-done | bytes 114720 | tf_op jit(solution)/shard_map/home/ppermute | solution.py:57
  145.5 2.3 %collective-permute-done.11 = bf16[16,3584]{1,0:T(8,128)(2,1)S(1)} collective-permute-done((bf16[16,3584]{1,0:T(8,128)(2,1)S(1)}, bf16[16,3584]{1,0:T(8,128)(2,1)S(1)}, u32[]{:S(2)}, u32[]{:S(2)}) %collective-permute-start.11) | collective-permute-done | bytes 114720 | tf_op jit(solution)/shard_map/home/ppermute | solution.py:57
  147.8 0.0 collective-permute-done.10
  147.8 0.1 fusion
  147.9 9.0 %collective-permute-start.15 = (bf16[16,3584]{1,0:T(8,128)(2,1)S(1)}, bf16[16,3584]{1,0:T(8,128)(2,1)S(1)}, u32[]{:S(2)}, u32[]{:S(2)}) collective-permute-start(bf16[16,3584]{1,0:T(8,128)(2,1)S(1)} %get-tuple-element.62), channel_id=1, source_target_pairs={{32,6},{33,3},{34,0},{35,5},{36,2},{37,7},{38,4},{39,1},{40,14},{4... | collective-permute-start | bytes 344072 | tf_op jit(solution)/shard_map/home/ppermute | solution.py:57
  156.9 1.9 %collective-permute-start.14 = (bf16[16,3584]{1,0:T(8,128)(2,1)S(1)}, bf16[16,3584]{1,0:T(8,128)(2,1)S(1)}, u32[]{:S(2)}, u32[]{:S(2)}) collective-permute-start(bf16[16,3584]{1,0:T(8,128)(2,1)S(1)} %get-tuple-element.59), channel_id=1, source_target_pairs={{0,32},{1,33},{2,34},{3,35},{4,36},{5,37},{6,38},{7,39},{8,40},{9,... | collective-permute-start | bytes 344072 | tf_op jit(solution)/shard_map/home/ppermute | solution.py:57
  158.9 4.3 %collective-permute-start.13 = (bf16[16,3584]{1,0:T(8,128)(2,1)S(1)}, bf16[16,3584]{1,0:T(8,128)(2,1)S(1)}, u32[]{:S(2)}, u32[]{:S(2)}) collective-permute-start(bf16[16,3584]{1,0:T(8,128)(2,1)S(1)} %get-tuple-element.63), channel_id=1, source_target_pairs={{0,38},{1,35},{2,32},{3,37},{4,34},{5,39},{6,36},{7,33},{8,46},{9,... | collective-permute-start | bytes 344072 | tf_op jit(solution)/shard_map/home/ppermute | solution.py:57
  163.2 0.0 collective-permute-done.16
  163.2 0.0 collective-permute-done.15
  163.2 0.7 fusion.2
  164.0 2.4 %collective-permute-done.14 = bf16[16,3584]{1,0:T(8,128)(2,1)S(1)} collective-permute-done((bf16[16,3584]{1,0:T(8,128)(2,1)S(1)}, bf16[16,3584]{1,0:T(8,128)(2,1)S(1)}, u32[]{:S(2)}, u32[]{:S(2)}) %collective-permute-start.14) | collective-permute-done | bytes 114720 | tf_op jit(solution)/shard_map/home/ppermute | solution.py:57
  166.3 9.1 %collective-permute-done.13 = bf16[16,3584]{1,0:T(8,128)(2,1)S(1)} collective-permute-done((bf16[16,3584]{1,0:T(8,128)(2,1)S(1)}, bf16[16,3584]{1,0:T(8,128)(2,1)S(1)}, u32[]{:S(2)}, u32[]{:S(2)}) %collective-permute-start.13) | collective-permute-done | bytes 114720 | tf_op jit(solution)/shard_map/home/ppermute | solution.py:57
  175.4 0.7 fusion.1
  (25 shorter events, 0.2 us)
Async XLA Ops:
  0.6 10.1 %copy-start.4 = (f32[1,16,2]{1,2,0:T(2,128)S(1)}, f32[1,16,2]{1,2,0:T(2,128)}, u32[]{:S(2)}) copy-start(f32[1,16,2]{1,2,0:T(2,128)} %param.17) | copy-start | bytes 388
  0.6 10.1 %copy-start.5 = (s32[1,16,2]{1,2,0:T(2,128)S(1)}, s32[1,16,2]{1,2,0:T(2,128)}, u32[]{:S(2)}) copy-start(s32[1,16,2]{1,2,0:T(2,128)} %param.15) | copy-start | bytes 388
  0.7 10.2 %copy-start.6 = (f32[1,16,2]{1,2,0:T(2,128)S(1)}, f32[1,16,2]{1,2,0:T(2,128)}, u32[]{:S(2)}) copy-start(f32[1,16,2]{1,2,0:T(2,128)} %param.16) | copy-start | bytes 388
  0.7 10.2 %copy-start.7 = (s32[1,16,2]{1,2,0:T(2,128)S(1)}, s32[1,16,2]{1,2,0:T(2,128)}, u32[]{:S(2)}) copy-start(s32[1,16,2]{1,2,0:T(2,128)} %param.14) | copy-start | bytes 388
  0.7 10.5 %copy-start.1 = (bf16[1,16,3584]{2,1,0:T(8,128)(2,1)S(1)}, bf16[1,16,3584]{2,1,0:T(8,128)(2,1)}, u32[]{:S(2)}) copy-start(bf16[1,16,3584]{2,1,0:T(8,128)(2,1)} %param.10) | copy-start | bytes 344068
  0.7 10.5 %copy-start.2 = (bf16[1,16,3584]{2,1,0:T(8,128)(2,1)S(1)}, bf16[1,16,3584]{2,1,0:T(8,128)(2,1)}, u32[]{:S(2)}) copy-start(bf16[1,16,3584]{2,1,0:T(8,128)(2,1)} %param.9) | copy-start | bytes 344068
  0.7 10.5 %copy-start.3 = (bf16[1,16,3584]{2,1,0:T(8,128)(2,1)S(1)}, bf16[1,16,3584]{2,1,0:T(8,128)(2,1)}, u32[]{:S(2)}) copy-start(bf16[1,16,3584]{2,1,0:T(8,128)(2,1)} %param.11) | copy-start | bytes 344068
  4.1 70.9 %collective-permute-start.1 = (bf16[5376,256]{1,0:T(8,128)(2,1)}, bf16[5376,256]{1,0:T(8,128)(2,1)}, u32[]{:S(2)}, u32[]{:S(2)}) collective-permute-start(bf16[5376,256]{1,0:T(8,128)(2,1)} %gather_weights.1.refs_0_), channel_id=1, source_target_pairs={{0,24},{1,9},{2,26},{3,11},{4,28},{5,13},{6,30},{7,15},{8,0},{9,17... | collective-permute-start | bytes 8257544 | tf_op jit(solution)/shard_map/gather_weights/ppermute | solution.py:41
  8.8 66.2 %collective-permute-start = (bf16[5376,256]{1,0:T(8,128)(2,1)}, bf16[5376,256]{1,0:T(8,128)(2,1)}, u32[]{:S(2)}, u32[]{:S(2)}) collective-permute-start(bf16[5376,256]{1,0:T(8,128)(2,1)} %gather_weights.1.refs_0_), channel_id=1, source_target_pairs={{0,8},{1,25},{2,10},{3,27},{4,12},{5,29},{6,14},{7,31},{8,16},{9,1... | collective-permute-start | bytes 8257544 | tf_op jit(solution)/shard_map/gather_weights/ppermute | solution.py:41
  11.2 73.1 %copy-start = (bf16[5376,256]{1,0:T(8,128)(2,1)S(1)}, bf16[5376,256]{1,0:T(8,128)(2,1)}, u32[]{:S(2)}) copy-start(bf16[5376,256]{1,0:T(8,128)(2,1)} %gather_weights.1.refs_0_) | copy-start | bytes 8257540
  11.2 18.6 %collective-permute-start.2 = (bf16[16,10880]{1,0:T(8,128)(2,1)S(1)}, bf16[16,10880]{1,0:T(8,128)(2,1)S(1)}, u32[]{:S(2)}, u32[]{:S(2)}) collective-permute-start(bf16[16,10880]{1,0:T(8,128)(2,1)S(1)} %pad_maximum_fusion.1), channel_id=1, source_target_pairs={{0,2},{1,7},{2,4},{3,1},{4,6},{5,3},{6,0},{7,5},{8,10},{9,15},{10,... | collective-permute-start | bytes 1044488 | tf_op jit(solution)/shard_map/gather_rows/ppermute | solution.py:36
  20.6 39.6 %collective-permute-start.3 = (bf16[16,10880]{1,0:T(8,128)(2,1)S(1)}, bf16[16,10880]{1,0:T(8,128)(2,1)S(1)}, u32[]{:S(2)}, u32[]{:S(2)}) collective-permute-start(bf16[16,10880]{1,0:T(8,128)(2,1)S(1)} %pad_maximum_fusion.1), channel_id=1, source_target_pairs={{0,6},{1,3},{2,0},{3,5},{4,2},{5,7},{6,4},{7,1},{8,14},{9,11},{10,... | collective-permute-start | bytes 1044488 | tf_op jit(solution)/shard_map/gather_rows/ppermute | solution.py:36
  29.8 45.3 %collective-permute-start.4 = (bf16[16,10880]{1,0:T(8,128)(2,1)S(1)}, bf16[16,10880]{1,0:T(8,128)(2,1)S(1)}, u32[]{:S(2)}, u32[]{:S(2)}) collective-permute-start(bf16[16,10880]{1,0:T(8,128)(2,1)S(1)} %collective-permute-done.2), channel_id=1, source_target_pairs={{0,2},{1,7},{2,4},{3,1},{4,6},{5,3},{6,0},{7,5},{8,10},{9,15},{10,... | collective-permute-start | bytes 1044488 | tf_op jit(solution)/shard_map/gather_rows/ppermute | solution.py:36
  75.0 36.9 %collective-permute-start.8 = (bf16[5376,256]{1,0:T(8,128)(2,1)}, bf16[5376,256]{1,0:T(8,128)(2,1)}, u32[]{:S(2)}, u32[]{:S(2)}) collective-permute-start(bf16[5376,256]{1,0:T(8,128)(2,1)} %collective-permute-done.refs_1_), channel_id=1, source_target_pairs={{0,8},{1,25},{2,10},{3,27},{4,12},{5,29},{6,14},{7,31},{8,16},{9,1... | collective-permute-start | bytes 8257544 | tf_op jit(solution)/shard_map/gather_opposite/ppermute | solution.py:41
  78.9 5.4 %collective-permute-start.5 = (bf16[64,10880]{1,0:T(8,128)(2,1)}, bf16[64,10880]{1,0:T(8,128)(2,1)}, u32[]{:S(2)}, u32[]{:S(2)}) collective-permute-start(bf16[64,10880]{1,0:T(8,128)(2,1)} %pad_maximum_fusion.mine), channel_id=1, source_target_pairs={{0,1},{1,0},{2,3},{3,2},{4,5},{5,4},{6,7},{7,6},{8,9},{9,8},{10,11... | collective-permute-start | bytes 4177928 | tf_op jit(solution)/shard_map/gather_opposite/ppermute | solution.py:45
  93.6 10.4 %collective-permute-start.6 = (bf16[16,3584]{1,0:T(8,128)(2,1)S(1)}, bf16[16,3584]{1,0:T(8,128)(2,1)S(1)}, u32[]{:S(2)}, u32[]{:S(2)}) collective-permute-start(bf16[16,3584]{1,0:T(8,128)(2,1)S(1)} %bitcast.27), channel_id=1, source_target_pairs={{0,32},{1,33},{2,34},{3,35},{4,36},{5,37},{6,38},{7,39},{8,40},{9,... | collective-permute-start | bytes 344072 | tf_op jit(solution)/shard_map/residual/ppermute | solution.py:57
  95.5 9.0 %collective-permute-start.7 = (bf16[16,3584]{1,0:T(8,128)(2,1)S(1)}, bf16[16,3584]{1,0:T(8,128)(2,1)S(1)}, u32[]{:S(2)}, u32[]{:S(2)}) collective-permute-start(bf16[16,3584]{1,0:T(8,128)(2,1)S(1)} %bitcast.30), channel_id=1, source_target_pairs={{32,0},{33,1},{34,2},{35,3},{36,4},{37,5},{38,6},{39,7},{40,8},{41... | collective-permute-start | bytes 344072 | tf_op jit(solution)/shard_map/residual/ppermute | solution.py:57
  115.8 4.4 %collective-permute-start.9 = (bf16[64,7168]{1,0:T(8,128)(2,1)S(1)}, bf16[64,7168]{1,0:T(8,128)(2,1)S(1)}, u32[]{:S(2)}, u32[]{:S(2)}) collective-permute-start(bf16[64,7168]{1,0:T(8,128)(2,1)S(1)} %get-tuple-element.51), channel_id=1, source_target_pairs={{0,1},{1,0},{2,3},{3,2},{4,5},{5,4},{6,7},{7,6},{8,9},{9,8},{10,11... | collective-permute-start | bytes 2752520 | tf_op jit(solution)/shard_map/cores/ppermute | solution.py:45
  120.5 27.3 %collective-permute-start.10 = (bf16[16,7168]{1,0:T(8,128)(2,1)S(1)}, bf16[16,7168]{1,0:T(8,128)(2,1)S(1)}, u32[]{:S(2)}, u32[]{:S(2)}) collective-permute-start(bf16[16,7168]{1,0:T(8,128)(2,1)S(1)} %split.13), channel_id=1, source_target_pairs={{0,6},{1,3},{2,0},{3,5},{4,2},{5,7},{6,4},{7,1},{8,14},{9,11},{10,... | collective-permute-start | bytes 688136 | tf_op jit(solution)/shard_map/home/ppermute | solution.py:36
  126.8 18.7 %collective-permute-start.12 = (bf16[16,3584]{1,0:T(8,128)(2,1)S(1)}, bf16[16,3584]{1,0:T(8,128)(2,1)S(1)}, u32[]{:S(2)}, u32[]{:S(2)}) collective-permute-start(bf16[16,3584]{1,0:T(8,128)(2,1)S(1)} %get-tuple-element.60), channel_id=1, source_target_pairs={{32,2},{33,7},{34,4},{35,1},{36,6},{37,3},{38,0},{39,5},{40,10},{4... | collective-permute-start | bytes 344072 | tf_op jit(solution)/shard_map/home/ppermute | solution.py:57
  131.4 16.5 %collective-permute-start.11 = (bf16[16,3584]{1,0:T(8,128)(2,1)S(1)}, bf16[16,3584]{1,0:T(8,128)(2,1)S(1)}, u32[]{:S(2)}, u32[]{:S(2)}) collective-permute-start(bf16[16,3584]{1,0:T(8,128)(2,1)S(1)} %get-tuple-element.61), channel_id=1, source_target_pairs={{0,34},{1,39},{2,36},{3,33},{4,38},{5,35},{6,32},{7,37},{8,42},{9,... | collective-permute-start | bytes 344072 | tf_op jit(solution)/shard_map/home/ppermute | solution.py:57
  138.6 24.6 %collective-permute-start.16 = (bf16[16,3584]{1,0:T(8,128)(2,1)S(1)}, bf16[16,3584]{1,0:T(8,128)(2,1)S(1)}, u32[]{:S(2)}, u32[]{:S(2)}) collective-permute-start(bf16[16,3584]{1,0:T(8,128)(2,1)S(1)} %get-tuple-element.58), channel_id=1, source_target_pairs={{32,0},{33,1},{34,2},{35,3},{36,4},{37,5},{38,6},{39,7},{40,8},{41... | collective-permute-start | bytes 344072 | tf_op jit(solution)/shard_map/home/ppermute | solution.py:57
  147.9 15.4 %collective-permute-start.15 = (bf16[16,3584]{1,0:T(8,128)(2,1)S(1)}, bf16[16,3584]{1,0:T(8,128)(2,1)S(1)}, u32[]{:S(2)}, u32[]{:S(2)}) collective-permute-start(bf16[16,3584]{1,0:T(8,128)(2,1)S(1)} %get-tuple-element.62), channel_id=1, source_target_pairs={{32,6},{33,3},{34,0},{35,5},{36,2},{37,7},{38,4},{39,1},{40,14},{4... | collective-permute-start | bytes 344072 | tf_op jit(solution)/shard_map/home/ppermute | solution.py:57
  156.9 9.4 %collective-permute-start.14 = (bf16[16,3584]{1,0:T(8,128)(2,1)S(1)}, bf16[16,3584]{1,0:T(8,128)(2,1)S(1)}, u32[]{:S(2)}, u32[]{:S(2)}) collective-permute-start(bf16[16,3584]{1,0:T(8,128)(2,1)S(1)} %get-tuple-element.59), channel_id=1, source_target_pairs={{0,32},{1,33},{2,34},{3,35},{4,36},{5,37},{6,38},{7,39},{8,40},{9,... | collective-permute-start | bytes 344072 | tf_op jit(solution)/shard_map/home/ppermute | solution.py:57
  158.9 16.5 %collective-permute-start.13 = (bf16[16,3584]{1,0:T(8,128)(2,1)S(1)}, bf16[16,3584]{1,0:T(8,128)(2,1)S(1)}, u32[]{:S(2)}, u32[]{:S(2)}) collective-permute-start(bf16[16,3584]{1,0:T(8,128)(2,1)S(1)} %get-tuple-element.63), channel_id=1, source_target_pairs={{0,38},{1,35},{2,32},{3,37},{4,34},{5,39},{6,36},{7,33},{8,46},{9,... | collective-permute-start | bytes 344072 | tf_op jit(solution)/shard_map/home/ppermute | solution.py:57

commit v14 on v13

--- a/solution.py
+++ b/solution.py
@@ -254,10 +254,10 @@
         passed = along_z(passed.astype(jnp.bfloat16), -1)
         own, far = own.astype(jnp.bfloat16), far.astype(jnp.bfloat16)
         parts = [to_section(far[:, :model], 1, 1), to_section(far[:, model:], -1, 1)]
+        parts += [to_section(own[:, :model], 1, 0), to_section(own[:, model:], -1, 0)]
         passed, *parts = together(passed, *parts)
         near = (near + passed.astype(jnp.float32)).astype(jnp.bfloat16)
         parts += [to_section(near[:, :model], 1, -1), to_section(near[:, model:], -1, -1)]
-        parts += [to_section(own[:, :model], 1, 0), to_section(own[:, model:], -1, 0)]
         sides = [[residuals[k]] + parts[k::2] for k in range(2)]
         forward_next, backward_next = [
             sum(part.astype(jnp.float32) for part in side).astype(jnp.bfloat16) for side in sides

time: 177 us -> 177 us (level)
  starting transfers between devices: 102 us -> 104 us
  waiting for transfers between devices: 52.5 us -> 50.5 us
    ppermute x8, waiting for transfers between devices: 21.1 us -> 19.2 us  [to_section(): return lax.ppermute(block, ('pipe', 'expert'), route)]
    ppermute x8, starting transfers between devices: 37.6 us -> 39.4 us  [to_section(): return lax.ppermute(block, ('pipe', 'expert'), route)]
  transfers between devices with their start and end apart: 17 -> 17, of which waited for: 11 -> 12; matrix products, arithmetic and copies ran while one was open for 1% -> 1% of each run, Pallas kernels for 5% -> 5%
where the time goes in v14:
time: 177 us; the launch traced here: 176 us
  starting transfers between devices  104 us (59%)
  waiting for transfers between devices  50.5 us (29%)
  Pallas kernels  16.7 us (9%)
  other arithmetic  3.26 us (2%)
    ppermute x4, starting transfers between devices, along_z(): return lax.ppermute(block, 'expert', route)  51.6 us
    ppermute x8, starting transfers between devices, to_section(): return lax.ppermute(block, ('pipe', 'expert'), route)  39.4 us
    ppermute x8, waiting for transfers between devices, to_section(): return lax.ppermute(block, ('pipe', 'expert'), route)  19.2 us
    ppermute x4, waiting for transfers between devices, along_z(): return lax.ppermute(block, 'expert', route)  18.4 us
    pallas_call x2, Pallas kernels, run_kernel(): pl.pallas_call(kernel, out_shape=outs, in_specs=[whole] * len(operands),...  13.2 us
    ppermute x3, starting transfers between devices, along_x(): return lax.ppermute(block, 'expert', route)  9.25 us
    ppermute x3, waiting for transfers between devices, along_x(): return lax.ppermute(block, 'expert', route)  7.35 us
    ppermute x2, waiting for transfers between devices, other_core(): lax.ppermute(block, 'expert', expert_route(lambda x, z, c: (x, z, 1 - c)))  5.58 us
  transfers between devices with their start and end apart: 17, of which 12 were waited for; matrix products, arithmetic and copies ran while one was open for 1% of the time, Pallas kernels for 5%

profile of v14, /device:TPU:24, one launch (start us, length us, event | category | flops | bytes accessed | tf_op | source)
XLA Modules:
  0.0 176.0 jit_solution(1936681060158539806)
XLA Ops:
  0.7 3.4 %gather_weights.1.refs_0_ = bf16[5376,256]{1,0:T(8,128)(2,1)} custom-call(bf16[3584,256]{1,0:T(8,128)(2,1)} %bitcast.21, bf16[128,3584]{1,0:T(8,128)(2,1)} %bitcast.22), custom_call_target="tpu_custom_call" | custom-call | tf_op jit(solution)/shard_map/gather_weights/pallas_call | solution.py:123
  4.1 4.7 %collective-permute-start.1 = (bf16[5376,256]{1,0:T(8,128)(2,1)}, bf16[5376,256]{1,0:T(8,128)(2,1)}, u32[]{:S(2)}, u32[]{:S(2)}) collective-permute-start(bf16[5376,256]{1,0:T(8,128)(2,1)} %gather_weights.1.refs_0_), channel_id=1, source_target_pairs={{0,24},{1,9},{2,26},{3,11},{4,28},{5,13},{6,30},{7,15},{8,0},{9,17... | collective-permute-start | bytes 8257544 | tf_op jit(solution)/shard_map/gather_weights/ppermute | solution.py:41
  8.8 1.9 %collective-permute-start = (bf16[5376,256]{1,0:T(8,128)(2,1)}, bf16[5376,256]{1,0:T(8,128)(2,1)}, u32[]{:S(2)}, u32[]{:S(2)}) collective-permute-start(bf16[5376,256]{1,0:T(8,128)(2,1)} %gather_weights.1.refs_0_), channel_id=1, source_target_pairs={{0,8},{1,25},{2,10},{3,27},{4,12},{5,29},{6,14},{7,31},{8,16},{9,1... | collective-permute-start | bytes 8257544 | tf_op jit(solution)/shard_map/gather_weights/ppermute | solution.py:41
  10.8 0.1 copy.18
  10.9 0.1 copy.17
  11.0 0.1 reduce-precision_convert_fusion.1
  11.1 0.1 fusion.8
  11.2 9.4 %collective-permute-start.2 = (bf16[16,10880]{1,0:T(8,128)(2,1)S(1)}, bf16[16,10880]{1,0:T(8,128)(2,1)S(1)}, u32[]{:S(2)}, u32[]{:S(2)}) collective-permute-start(bf16[16,10880]{1,0:T(8,128)(2,1)S(1)} %pad_maximum_fusion.1), channel_id=1, source_target_pairs={{0,2},{1,7},{2,4},{3,1},{4,6},{5,3},{6,0},{7,5},{8,10},{9,15},{10,... | collective-permute-start | bytes 1044488 | tf_op jit(solution)/shard_map/gather_rows/ppermute | solution.py:36
  20.6 5.6 %collective-permute-start.3 = (bf16[16,10880]{1,0:T(8,128)(2,1)S(1)}, bf16[16,10880]{1,0:T(8,128)(2,1)S(1)}, u32[]{:S(2)}, u32[]{:S(2)}) collective-permute-start(bf16[16,10880]{1,0:T(8,128)(2,1)S(1)} %pad_maximum_fusion.1), channel_id=1, source_target_pairs={{0,6},{1,3},{2,0},{3,5},{4,2},{5,7},{6,4},{7,1},{8,14},{9,11},{10,... | collective-permute-start | bytes 1044488 | tf_op jit(solution)/shard_map/gather_rows/ppermute | solution.py:36
  26.1 3.6 %collective-permute-done.2 = bf16[16,10880]{1,0:T(8,128)(2,1)S(1)} collective-permute-done((bf16[16,10880]{1,0:T(8,128)(2,1)S(1)}, bf16[16,10880]{1,0:T(8,128)(2,1)S(1)}, u32[]{:S(2)}, u32[]{:S(2)}) %collective-permute-start.2) | collective-permute-done | bytes 348192 | tf_op jit(solution)/shard_map/gather_rows/ppermute | solution.py:36
  29.8 30.4 %collective-permute-start.4 = (bf16[16,10880]{1,0:T(8,128)(2,1)S(1)}, bf16[16,10880]{1,0:T(8,128)(2,1)S(1)}, u32[]{:S(2)}, u32[]{:S(2)}) collective-permute-start(bf16[16,10880]{1,0:T(8,128)(2,1)S(1)} %collective-permute-done.2), channel_id=1, source_target_pairs={{0,2},{1,7},{2,4},{3,1},{4,6},{5,3},{6,0},{7,5},{8,10},{9,15},{10,... | collective-permute-start | bytes 1044488 | tf_op jit(solution)/shard_map/gather_rows/ppermute | solution.py:36
  60.2 0.0 collective-permute-done.3
  60.2 14.8 %collective-permute-done.4 = bf16[16,10880]{1,0:T(8,128)(2,1)S(1)} collective-permute-done((bf16[16,10880]{1,0:T(8,128)(2,1)S(1)}, bf16[16,10880]{1,0:T(8,128)(2,1)S(1)}, u32[]{:S(2)}, u32[]{:S(2)}) %collective-permute-start.4) | collective-permute-done | bytes 348192 | tf_op jit(solution)/shard_map/gather_rows/ppermute | solution.py:36
  75.0 0.0 collective-permute-done.1.refs_2_
  75.0 0.0 collective-permute-done.refs_1_
  75.0 2.7 %collective-permute-start.8 = (bf16[5376,256]{1,0:T(8,128)(2,1)}, bf16[5376,256]{1,0:T(8,128)(2,1)}, u32[]{:S(2)}, u32[]{:S(2)}) collective-permute-start(bf16[5376,256]{1,0:T(8,128)(2,1)} %collective-permute-done.refs_1_), channel_id=1, source_target_pairs={{0,8},{1,25},{2,10},{3,27},{4,12},{5,29},{6,14},{7,31},{8,16},{9,1... | collective-permute-start | bytes 8257544 | tf_op jit(solution)/shard_map/gather_opposite/ppermute | solution.py:41
  77.7 1.2 pad_maximum_fusion.mine
  78.9 1.9 %collective-permute-start.5 = (bf16[64,10880]{1,0:T(8,128)(2,1)}, bf16[64,10880]{1,0:T(8,128)(2,1)}, u32[]{:S(2)}, u32[]{:S(2)}) collective-permute-start(bf16[64,10880]{1,0:T(8,128)(2,1)} %pad_maximum_fusion.mine), channel_id=1, source_target_pairs={{0,1},{1,0},{2,3},{3,2},{4,5},{5,4},{6,7},{7,6},{8,9},{9,8},{10,11... | collective-permute-start | bytes 4177928 | tf_op jit(solution)/shard_map/gather_opposite/ppermute | solution.py:45
  80.9 0.1 stack.35
  81.0 0.1 compare_and_fusion
  81.1 3.1 %collective-permute-done.5.other = bf16[64,10880]{1,0:T(8,128)(2,1)} collective-permute-done((bf16[64,10880]{1,0:T(8,128)(2,1)}, bf16[64,10880]{1,0:T(8,128)(2,1)}, u32[]{:S(2)}, u32[]{:S(2)}) %collective-permute-start.5) | collective-permute-done | bytes 1392672 | tf_op jit(solution)/shard_map/gather_opposite/ppermute | solution.py:45
  84.3 9.3 %experts.1 = (f32[128,3584]{1,0:T(8,128)S(1)}, f32[128,3584]{1,0:T(8,128)S(1)}, bf16[128,3584]{1,0:T(8,128)(2,1)S(1)}, bf16[128,3584]{1,0:T(8,128)(2,1)S(1)}, bf...) custom-call(bf16[64,10880]{1,0:T(8,128)(2,1)} %pad_maximum_fusion.mine, ...), custom_call_target="tpu_custom_call" | custom-call | flops 1000 | bytes 1000 | tf_op jit(solution)/shard_map/experts/pallas_call | solution.py:189
  93.6 1.9 %collective-permute-start.6 = (bf16[16,3584]{1,0:T(8,128)(2,1)S(1)}, bf16[16,3584]{1,0:T(8,128)(2,1)S(1)}, u32[]{:S(2)}, u32[]{:S(2)}) collective-permute-start(bf16[16,3584]{1,0:T(8,128)(2,1)S(1)} %bitcast.27), channel_id=1, source_target_pairs={{0,32},{1,33},{2,34},{3,35},{4,36},{5,37},{6,38},{7,39},{8,40},{9,... | collective-permute-start | bytes 344072 | tf_op jit(solution)/shard_map/residual/ppermute | solution.py:57
  95.5 6.6 %collective-permute-start.7 = (bf16[16,3584]{1,0:T(8,128)(2,1)S(1)}, bf16[16,3584]{1,0:T(8,128)(2,1)S(1)}, u32[]{:S(2)}, u32[]{:S(2)}) collective-permute-start(bf16[16,3584]{1,0:T(8,128)(2,1)S(1)} %bitcast.30), channel_id=1, source_target_pairs={{32,0},{33,1},{34,2},{35,3},{36,4},{37,5},{38,6},{39,7},{40,8},{41... | collective-permute-start | bytes 344072 | tf_op jit(solution)/shard_map/residual/ppermute | solution.py:57
  102.2 1.8 %collective-permute-done.6 = bf16[16,3584]{1,0:T(8,128)(2,1)S(1)} collective-permute-done((bf16[16,3584]{1,0:T(8,128)(2,1)S(1)}, bf16[16,3584]{1,0:T(8,128)(2,1)S(1)}, u32[]{:S(2)}, u32[]{:S(2)}) %collective-permute-start.6) | collective-permute-done | bytes 114720 | tf_op jit(solution)/shard_map/residual/ppermute | solution.py:57
  104.0 0.6 collective-permute-done.7
  104.6 7.3 %collective-permute-done.8.weight = bf16[5376,256]{1,0:T(8,128)(2,1)} collective-permute-done((bf16[5376,256]{1,0:T(8,128)(2,1)}, bf16[5376,256]{1,0:T(8,128)(2,1)}, u32[]{:S(2)}, u32[]{:S(2)}) %collective-permute-start.8) | collective-permute-done | bytes 2752544 | tf_op jit(solution)/shard_map/gather_opposite/ppermute | solution.py:41
  111.9 3.9 %last_expert.1 = (f32[64,7168]{1,0:T(8,128)S(1)}, bf16[64,7168]{1,0:T(8,128)(2,1)S(1)}) custom-call(f32[128,3584]{1,0:T(8,128)S(1)} %get-tuple-element.45.total, f32[128,3584]{1,0:T(8,128)S(1)} %get-tuple-element.46.back_total, bf16[128,3584]{1,0:T(8,128)(2,1)S(1)} %get-tuple-element.47.token, bf16[128,3584]{1,0:T(8,128)(2,1)S(1)} %get-tuple-element.48.saved, ...), custom_call_target="tpu_custom_call" | custom-call | flops 1000 | bytes 1000 | tf_op jit(solution)/shard_map/last_expert/pallas_call | solution.py:189
  115.8 1.9 %collective-permute-start.9 = (bf16[64,7168]{1,0:T(8,128)(2,1)S(1)}, bf16[64,7168]{1,0:T(8,128)(2,1)S(1)}, u32[]{:S(2)}, u32[]{:S(2)}) collective-permute-start(bf16[64,7168]{1,0:T(8,128)(2,1)S(1)} %get-tuple-element.53), channel_id=1, source_target_pairs={{0,1},{1,0},{2,3},{3,2},{4,5},{5,4},{6,7},{7,6},{8,9},{9,8},{10,11... | collective-permute-start | bytes 2752520 | tf_op jit(solution)/shard_map/cores/ppermute | solution.py:45
  117.8 2.4 %collective-permute-done.9 = bf16[64,7168]{1,0:T(8,128)(2,1)S(1)} collective-permute-done((bf16[64,7168]{1,0:T(8,128)(2,1)S(1)}, bf16[64,7168]{1,0:T(8,128)(2,1)S(1)}, u32[]{:S(2)}, u32[]{:S(2)}) %collective-permute-start.9) | collective-permute-done | bytes 917536 | tf_op jit(solution)/shard_map/cores/ppermute | solution.py:45
  120.2 0.2 fusion.9
  120.5 6.3 %collective-permute-start.10 = (bf16[16,7168]{1,0:T(8,128)(2,1)S(1)}, bf16[16,7168]{1,0:T(8,128)(2,1)S(1)}, u32[]{:S(2)}, u32[]{:S(2)}) collective-permute-start(bf16[16,7168]{1,0:T(8,128)(2,1)S(1)} %split.13), channel_id=1, source_target_pairs={{0,6},{1,3},{2,0},{3,5},{4,2},{5,7},{6,4},{7,1},{8,14},{9,11},{10,... | collective-permute-start | bytes 688136 | tf_op jit(solution)/shard_map/home/ppermute | solution.py:36
  126.8 4.0 %collective-permute-start.14 = (bf16[16,3584]{1,0:T(8,128)(2,1)S(1)}, bf16[16,3584]{1,0:T(8,128)(2,1)S(1)}, u32[]{:S(2)}, u32[]{:S(2)}) collective-permute-start(bf16[16,3584]{1,0:T(8,128)(2,1)S(1)} %get-tuple-element.62), channel_id=1, source_target_pairs={{32,0},{33,1},{34,2},{35,3},{36,4},{37,5},{38,6},{39,7},{40,8},{41... | collective-permute-start | bytes 344072 | tf_op jit(solution)/shard_map/home/ppermute | solution.py:57
  130.8 1.9 %collective-permute-start.13 = (bf16[16,3584]{1,0:T(8,128)(2,1)S(1)}, bf16[16,3584]{1,0:T(8,128)(2,1)S(1)}, u32[]{:S(2)}, u32[]{:S(2)}) collective-permute-start(bf16[16,3584]{1,0:T(8,128)(2,1)S(1)} %get-tuple-element.63), channel_id=1, source_target_pairs={{0,32},{1,33},{2,34},{3,35},{4,36},{5,37},{6,38},{7,39},{8,40},{9,... | collective-permute-start | bytes 344072 | tf_op jit(solution)/shard_map/home/ppermute | solution.py:57
  132.8 7.1 %collective-permute-start.12 = (bf16[16,3584]{1,0:T(8,128)(2,1)S(1)}, bf16[16,3584]{1,0:T(8,128)(2,1)S(1)}, u32[]{:S(2)}, u32[]{:S(2)}) collective-permute-start(bf16[16,3584]{1,0:T(8,128)(2,1)S(1)} %get-tuple-element.64), channel_id=1, source_target_pairs={{32,2},{33,7},{34,4},{35,1},{36,6},{37,3},{38,0},{39,5},{40,10},{4... | collective-permute-start | bytes 344072 | tf_op jit(solution)/shard_map/home/ppermute | solution.py:57
  139.9 4.5 %collective-permute-start.11 = (bf16[16,3584]{1,0:T(8,128)(2,1)S(1)}, bf16[16,3584]{1,0:T(8,128)(2,1)S(1)}, u32[]{:S(2)}, u32[]{:S(2)}) collective-permute-start(bf16[16,3584]{1,0:T(8,128)(2,1)S(1)} %get-tuple-element.65), channel_id=1, source_target_pairs={{0,34},{1,39},{2,36},{3,33},{4,38},{5,35},{6,32},{7,37},{8,42},{9,... | collective-permute-start | bytes 344072 | tf_op jit(solution)/shard_map/home/ppermute | solution.py:57
  144.5 3.5 %collective-permute-done.14 = bf16[16,3584]{1,0:T(8,128)(2,1)S(1)} collective-permute-done((bf16[16,3584]{1,0:T(8,128)(2,1)S(1)}, bf16[16,3584]{1,0:T(8,128)(2,1)S(1)}, u32[]{:S(2)}, u32[]{:S(2)}) %collective-permute-start.14) | collective-permute-done | bytes 114720 | tf_op jit(solution)/shard_map/home/ppermute | solution.py:57
  148.0 0.0 collective-permute-done.13
  148.0 2.4 %collective-permute-done.12 = bf16[16,3584]{1,0:T(8,128)(2,1)S(1)} collective-permute-done((bf16[16,3584]{1,0:T(8,128)(2,1)S(1)}, bf16[16,3584]{1,0:T(8,128)(2,1)S(1)}, u32[]{:S(2)}, u32[]{:S(2)}) %collective-permute-start.12) | collective-permute-done | bytes 114720 | tf_op jit(solution)/shard_map/home/ppermute | solution.py:57
  150.3 1.2 collective-permute-done.11
  151.6 0.0 collective-permute-done.10
  151.6 0.1 fusion
  151.6 7.3 %collective-permute-start.16 = (bf16[16,3584]{1,0:T(8,128)(2,1)S(1)}, bf16[16,3584]{1,0:T(8,128)(2,1)S(1)}, u32[]{:S(2)}, u32[]{:S(2)}) collective-permute-start(bf16[16,3584]{1,0:T(8,128)(2,1)S(1)} %get-tuple-element.66), channel_id=1, source_target_pairs={{32,6},{33,3},{34,0},{35,5},{36,2},{37,7},{38,4},{39,1},{40,14},{4... | collective-permute-start | bytes 344072 | tf_op jit(solution)/shard_map/home/ppermute | solution.py:57
  159.0 5.9 %collective-permute-start.15 = (bf16[16,3584]{1,0:T(8,128)(2,1)S(1)}, bf16[16,3584]{1,0:T(8,128)(2,1)S(1)}, u32[]{:S(2)}, u32[]{:S(2)}) collective-permute-start(bf16[16,3584]{1,0:T(8,128)(2,1)S(1)} %get-tuple-element.67), channel_id=1, source_target_pairs={{0,38},{1,35},{2,32},{3,37},{4,34},{5,39},{6,36},{7,33},{8,46},{9,... | collective-permute-start | bytes 344072 | tf_op jit(solution)/shard_map/home/ppermute | solution.py:57
  164.9 0.5 collective-permute-done.16
  165.5 0.7 fusion.2
  166.2 9.1 %collective-permute-done.15 = bf16[16,3584]{1,0:T(8,128)(2,1)S(1)} collective-permute-done((bf16[16,3584]{1,0:T(8,128)(2,1)S(1)}, bf16[16,3584]{1,0:T(8,128)(2,1)S(1)}, u32[]{:S(2)}, u32[]{:S(2)}) %collective-permute-start.15) | collective-permute-done | bytes 114720 | tf_op jit(solution)/shard_map/home/ppermute | solution.py:57
  175.3 0.7 fusion.1
  (25 shorter events, 0.2 us)
Async XLA Ops:
  0.6 10.1 %copy-start.4 = (f32[1,16,2]{1,2,0:T(2,128)S(1)}, f32[1,16,2]{1,2,0:T(2,128)}, u32[]{:S(2)}) copy-start(f32[1,16,2]{1,2,0:T(2,128)} %param.17) | copy-start | bytes 388
  0.6 10.1 %copy-start.5 = (s32[1,16,2]{1,2,0:T(2,128)S(1)}, s32[1,16,2]{1,2,0:T(2,128)}, u32[]{:S(2)}) copy-start(s32[1,16,2]{1,2,0:T(2,128)} %param.15) | copy-start | bytes 388
  0.7 10.2 %copy-start.6 = (f32[1,16,2]{1,2,0:T(2,128)S(1)}, f32[1,16,2]{1,2,0:T(2,128)}, u32[]{:S(2)}) copy-start(f32[1,16,2]{1,2,0:T(2,128)} %param.16) | copy-start | bytes 388
  0.7 10.2 %copy-start.7 = (s32[1,16,2]{1,2,0:T(2,128)S(1)}, s32[1,16,2]{1,2,0:T(2,128)}, u32[]{:S(2)}) copy-start(s32[1,16,2]{1,2,0:T(2,128)} %param.14) | copy-start | bytes 388
  0.7 10.5 %copy-start.1 = (bf16[1,16,3584]{2,1,0:T(8,128)(2,1)S(1)}, bf16[1,16,3584]{2,1,0:T(8,128)(2,1)}, u32[]{:S(2)}) copy-start(bf16[1,16,3584]{2,1,0:T(8,128)(2,1)} %param.10) | copy-start | bytes 344068
  0.7 10.5 %copy-start.2 = (bf16[1,16,3584]{2,1,0:T(8,128)(2,1)S(1)}, bf16[1,16,3584]{2,1,0:T(8,128)(2,1)}, u32[]{:S(2)}) copy-start(bf16[1,16,3584]{2,1,0:T(8,128)(2,1)} %param.9) | copy-start | bytes 344068
  0.7 10.5 %copy-start.3 = (bf16[1,16,3584]{2,1,0:T(8,128)(2,1)S(1)}, bf16[1,16,3584]{2,1,0:T(8,128)(2,1)}, u32[]{:S(2)}) copy-start(bf16[1,16,3584]{2,1,0:T(8,128)(2,1)} %param.11) | copy-start | bytes 344068
  4.1 70.9 %collective-permute-start.1 = (bf16[5376,256]{1,0:T(8,128)(2,1)}, bf16[5376,256]{1,0:T(8,128)(2,1)}, u32[]{:S(2)}, u32[]{:S(2)}) collective-permute-start(bf16[5376,256]{1,0:T(8,128)(2,1)} %gather_weights.1.refs_0_), channel_id=1, source_target_pairs={{0,24},{1,9},{2,26},{3,11},{4,28},{5,13},{6,30},{7,15},{8,0},{9,17... | collective-permute-start | bytes 8257544 | tf_op jit(solution)/shard_map/gather_weights/ppermute | solution.py:41
  8.8 66.2 %collective-permute-start = (bf16[5376,256]{1,0:T(8,128)(2,1)}, bf16[5376,256]{1,0:T(8,128)(2,1)}, u32[]{:S(2)}, u32[]{:S(2)}) collective-permute-start(bf16[5376,256]{1,0:T(8,128)(2,1)} %gather_weights.1.refs_0_), channel_id=1, source_target_pairs={{0,8},{1,25},{2,10},{3,27},{4,12},{5,29},{6,14},{7,31},{8,16},{9,1... | collective-permute-start | bytes 8257544 | tf_op jit(solution)/shard_map/gather_weights/ppermute | solution.py:41
  11.2 73.1 %copy-start = (bf16[5376,256]{1,0:T(8,128)(2,1)S(1)}, bf16[5376,256]{1,0:T(8,128)(2,1)}, u32[]{:S(2)}) copy-start(bf16[5376,256]{1,0:T(8,128)(2,1)} %gather_weights.1.refs_0_) | copy-start | bytes 8257540
  11.2 18.6 %collective-permute-start.2 = (bf16[16,10880]{1,0:T(8,128)(2,1)S(1)}, bf16[16,10880]{1,0:T(8,128)(2,1)S(1)}, u32[]{:S(2)}, u32[]{:S(2)}) collective-permute-start(bf16[16,10880]{1,0:T(8,128)(2,1)S(1)} %pad_maximum_fusion.1), channel_id=1, source_target_pairs={{0,2},{1,7},{2,4},{3,1},{4,6},{5,3},{6,0},{7,5},{8,10},{9,15},{10,... | collective-permute-start | bytes 1044488 | tf_op jit(solution)/shard_map/gather_rows/ppermute | solution.py:36
  20.6 39.6 %collective-permute-start.3 = (bf16[16,10880]{1,0:T(8,128)(2,1)S(1)}, bf16[16,10880]{1,0:T(8,128)(2,1)S(1)}, u32[]{:S(2)}, u32[]{:S(2)}) collective-permute-start(bf16[16,10880]{1,0:T(8,128)(2,1)S(1)} %pad_maximum_fusion.1), channel_id=1, source_target_pairs={{0,6},{1,3},{2,0},{3,5},{4,2},{5,7},{6,4},{7,1},{8,14},{9,11},{10,... | collective-permute-start | bytes 1044488 | tf_op jit(solution)/shard_map/gather_rows/ppermute | solution.py:36
  29.8 45.3 %collective-permute-start.4 = (bf16[16,10880]{1,0:T(8,128)(2,1)S(1)}, bf16[16,10880]{1,0:T(8,128)(2,1)S(1)}, u32[]{:S(2)}, u32[]{:S(2)}) collective-permute-start(bf16[16,10880]{1,0:T(8,128)(2,1)S(1)} %collective-permute-done.2), channel_id=1, source_target_pairs={{0,2},{1,7},{2,4},{3,1},{4,6},{5,3},{6,0},{7,5},{8,10},{9,15},{10,... | collective-permute-start | bytes 1044488 | tf_op jit(solution)/shard_map/gather_rows/ppermute | solution.py:36
  75.0 36.9 %collective-permute-start.8 = (bf16[5376,256]{1,0:T(8,128)(2,1)}, bf16[5376,256]{1,0:T(8,128)(2,1)}, u32[]{:S(2)}, u32[]{:S(2)}) collective-permute-start(bf16[5376,256]{1,0:T(8,128)(2,1)} %collective-permute-done.refs_1_), channel_id=1, source_target_pairs={{0,8},{1,25},{2,10},{3,27},{4,12},{5,29},{6,14},{7,31},{8,16},{9,1... | collective-permute-start | bytes 8257544 | tf_op jit(solution)/shard_map/gather_opposite/ppermute | solution.py:41
  78.9 5.4 %collective-permute-start.5 = (bf16[64,10880]{1,0:T(8,128)(2,1)}, bf16[64,10880]{1,0:T(8,128)(2,1)}, u32[]{:S(2)}, u32[]{:S(2)}) collective-permute-start(bf16[64,10880]{1,0:T(8,128)(2,1)} %pad_maximum_fusion.mine), channel_id=1, source_target_pairs={{0,1},{1,0},{2,3},{3,2},{4,5},{5,4},{6,7},{7,6},{8,9},{9,8},{10,11... | collective-permute-start | bytes 4177928 | tf_op jit(solution)/shard_map/gather_opposite/ppermute | solution.py:45
  93.6 10.4 %collective-permute-start.6 = (bf16[16,3584]{1,0:T(8,128)(2,1)S(1)}, bf16[16,3584]{1,0:T(8,128)(2,1)S(1)}, u32[]{:S(2)}, u32[]{:S(2)}) collective-permute-start(bf16[16,3584]{1,0:T(8,128)(2,1)S(1)} %bitcast.27), channel_id=1, source_target_pairs={{0,32},{1,33},{2,34},{3,35},{4,36},{5,37},{6,38},{7,39},{8,40},{9,... | collective-permute-start | bytes 344072 | tf_op jit(solution)/shard_map/residual/ppermute | solution.py:57
  95.5 9.0 %collective-permute-start.7 = (bf16[16,3584]{1,0:T(8,128)(2,1)S(1)}, bf16[16,3584]{1,0:T(8,128)(2,1)S(1)}, u32[]{:S(2)}, u32[]{:S(2)}) collective-permute-start(bf16[16,3584]{1,0:T(8,128)(2,1)S(1)} %bitcast.30), channel_id=1, source_target_pairs={{32,0},{33,1},{34,2},{35,3},{36,4},{37,5},{38,6},{39,7},{40,8},{41... | collective-permute-start | bytes 344072 | tf_op jit(solution)/shard_map/residual/ppermute | solution.py:57
  115.8 4.4 %collective-permute-start.9 = (bf16[64,7168]{1,0:T(8,128)(2,1)S(1)}, bf16[64,7168]{1,0:T(8,128)(2,1)S(1)}, u32[]{:S(2)}, u32[]{:S(2)}) collective-permute-start(bf16[64,7168]{1,0:T(8,128)(2,1)S(1)} %get-tuple-element.53), channel_id=1, source_target_pairs={{0,1},{1,0},{2,3},{3,2},{4,5},{5,4},{6,7},{7,6},{8,9},{9,8},{10,11... | collective-permute-start | bytes 2752520 | tf_op jit(solution)/shard_map/cores/ppermute | solution.py:45
  120.5 31.1 %collective-permute-start.10 = (bf16[16,7168]{1,0:T(8,128)(2,1)S(1)}, bf16[16,7168]{1,0:T(8,128)(2,1)S(1)}, u32[]{:S(2)}, u32[]{:S(2)}) collective-permute-start(bf16[16,7168]{1,0:T(8,128)(2,1)S(1)} %split.13), channel_id=1, source_target_pairs={{0,6},{1,3},{2,0},{3,5},{4,2},{5,7},{6,4},{7,1},{8,14},{9,11},{10,... | collective-permute-start | bytes 688136 | tf_op jit(solution)/shard_map/home/ppermute | solution.py:36
  126.8 21.2 %collective-permute-start.14 = (bf16[16,3584]{1,0:T(8,128)(2,1)S(1)}, bf16[16,3584]{1,0:T(8,128)(2,1)S(1)}, u32[]{:S(2)}, u32[]{:S(2)}) collective-permute-start(bf16[16,3584]{1,0:T(8,128)(2,1)S(1)} %get-tuple-element.62), channel_id=1, source_target_pairs={{32,0},{33,1},{34,2},{35,3},{36,4},{37,5},{38,6},{39,7},{40,8},{41... | collective-permute-start | bytes 344072 | tf_op jit(solution)/shard_map/home/ppermute | solution.py:57
  130.8 17.1 %collective-permute-start.13 = (bf16[16,3584]{1,0:T(8,128)(2,1)S(1)}, bf16[16,3584]{1,0:T(8,128)(2,1)S(1)}, u32[]{:S(2)}, u32[]{:S(2)}) collective-permute-start(bf16[16,3584]{1,0:T(8,128)(2,1)S(1)} %get-tuple-element.63), channel_id=1, source_target_pairs={{0,32},{1,33},{2,34},{3,35},{4,36},{5,37},{6,38},{7,39},{8,40},{9,... | collective-permute-start | bytes 344072 | tf_op jit(solution)/shard_map/home/ppermute | solution.py:57
  132.8 17.6 %collective-permute-start.12 = (bf16[16,3584]{1,0:T(8,128)(2,1)S(1)}, bf16[16,3584]{1,0:T(8,128)(2,1)S(1)}, u32[]{:S(2)}, u32[]{:S(2)}) collective-permute-start(bf16[16,3584]{1,0:T(8,128)(2,1)S(1)} %get-tuple-element.64), channel_id=1, source_target_pairs={{32,2},{33,7},{34,4},{35,1},{36,6},{37,3},{38,0},{39,5},{40,10},{4... | collective-permute-start | bytes 344072 | tf_op jit(solution)/shard_map/home/ppermute | solution.py:57
  139.9 11.7 %collective-permute-start.11 = (bf16[16,3584]{1,0:T(8,128)(2,1)S(1)}, bf16[16,3584]{1,0:T(8,128)(2,1)S(1)}, u32[]{:S(2)}, u32[]{:S(2)}) collective-permute-start(bf16[16,3584]{1,0:T(8,128)(2,1)S(1)} %get-tuple-element.65), channel_id=1, source_target_pairs={{0,34},{1,39},{2,36},{3,33},{4,38},{5,35},{6,32},{7,37},{8,42},{9,... | collective-permute-start | bytes 344072 | tf_op jit(solution)/shard_map/home/ppermute | solution.py:57
  151.6 13.8 %collective-permute-start.16 = (bf16[16,3584]{1,0:T(8,128)(2,1)S(1)}, bf16[16,3584]{1,0:T(8,128)(2,1)S(1)}, u32[]{:S(2)}, u32[]{:S(2)}) collective-permute-start(bf16[16,3584]{1,0:T(8,128)(2,1)S(1)} %get-tuple-element.66), channel_id=1, source_target_pairs={{32,6},{33,3},{34,0},{35,5},{36,2},{37,7},{38,4},{39,1},{40,14},{4... | collective-permute-start | bytes 344072 | tf_op jit(solution)/shard_map/home/ppermute | solution.py:57
  159.0 16.3 %collective-permute-start.15 = (bf16[16,3584]{1,0:T(8,128)(2,1)S(1)}, bf16[16,3584]{1,0:T(8,128)(2,1)S(1)}, u32[]{:S(2)}, u32[]{:S(2)}) collective-permute-start(bf16[16,3584]{1,0:T(8,128)(2,1)S(1)} %get-tuple-element.67), channel_id=1, source_target_pairs={{0,38},{1,35},{2,32},{3,37},{4,34},{5,39},{6,36},{7,33},{8,46},{9,... | collective-permute-start | bytes 344072 | tf_op jit(solution)/shard_map/home/ppermute | solution.py:57
